TPU v7x, 32 devices: a whole 2x2x4 slice. The times are simulated.
32 devices in a mesh: ens: 4 (over x, core), pix: 8 (over z, y).
Axes of the slice: x: 2, y: 2, z: 4, core: 2. Of those that a mesh axis runs over, the one named last changes fastest.
Arguments:
- sample_layer_feed: bfloat16 [4, 1024, 1024], P('ens', 'pix'), may hold values from -54 to 54
- gain: float32 [1024], replicated, may hold values from 0.1 to 1.9
- w_query: bfloat16 [1024, 512], P('ens'), may hold values from -15 to 15
- w_key: bfloat16 [1024, 512], P('ens'), may hold values from -0.1875 to 0.1875
- w_value: bfloat16 [1024, 512], P('ens'), may hold values from -0.1875 to 0.1875
- w_out: bfloat16 [512, 1024], P(None, 'ens'), may hold values from -0.25 to 0.25
- readout_matrix: bfloat16 [1024, 128], replicated, may hold values from -0.1875 to 0.1875
- target: float32 [1024, 128], P('pix'), may hold values from -6 to 6
- pixel_weight: float32 [1024], P('pix'), may hold values from 0.25 to 6
- pix_mask: int32 [1024], replicated, may hold values from 0 to 1, as said below
- neighbours: int32 [8, 9], P('pix'), may hold values from 0 to 7, as said below
- neighbour_mask: int32 [8, 9], P('pix'), may hold values from 0 to 1, as said below
Outputs:
- loss: float32 [], replicated
- grad_w_out: float32 [512, 1024], P(None, 'ens')
- grad_w_value: float32 [1024, 512], P('ens')
Inputs may be any that keep to these rules, and one draw needn't show every extreme that they name: `neighbours`: slot 0 of tile t names t itself; every slot names tile t, t - 1 or t + 1 (the tiles of the same and the neighbouring pix devices). `neighbour_mask`: slot 0 is live in every tile. `pix_mask`: in every tile the real pixels come first, and they are half of the tile or more.
All inputs are finite; a program needn't handle non-finite values.
Results may differ from a plain program's by a relative error of at most 0.025.
The roundings to bfloat16 on the way count: a program that leaves them out, or rounds other values in their place, can miss the bound.
Values may be sent and summed in bfloat16 or wider, within the bound.
No kernel may reach another device: no remote copies, remote signals or barrier semaphores. Data moves between devices by JAX's collectives and lax.ppermute only.
A program may use at most 64 MiB of HBM per device.

v0:
```python
import math

import jax
import jax.numpy as jnp
from jax import lax
from jax.sharding import PartitionSpec as P

HEADS = 8
HD = 64
TILE = 128
NB = 9


eps_norm = 1e-06
easing_breadth = 0.1


def padded(value, sides, width):
    for axis, dim in sides:
        size, length = (lax.axis_size(axis), value.shape[dim])
        up = [(i, (i + 1) % size) for i in range(size - 1)]
        down = [(j, i) for i, j in up]
        last = lax.slice_in_dim(value, length - width, length, axis=dim)
        initial = lax.slice_in_dim(value, 0, width, axis=dim)
        before = lax.ppermute(last, axis, up)
        after = lax.ppermute(initial, axis, down)
        value = jnp.concatenate([before, value, after], axis=dim)
    return value


def passed_along(value, axis, steps):
    count = lax.axis_size(axis)
    initial, last = (max(0, -steps), min(count, count - steps))
    return lax.ppermute(value, axis, [(source, source + steps) for source in range(initial, last)])


def rms_scaled(member_rows, gain):
    values_f = member_rows.astype(jnp.float32)
    inverse = lax.rsqrt(jnp.mean(values_f * values_f, axis=-1, keepdims=True) + eps_norm)
    return (values_f * inverse * gain).astype(jnp.bfloat16)


def eased_magnitude(sample_dispersion):
    return easing_breadth * (
        jax.nn.softplus(sample_dispersion / easing_breadth)
        + jax.nn.softplus(-sample_dispersion / easing_breadth)
    )


def tile_weights(query_tile, near_keys, live_keys):
    scores = jnp.einsum(
        "qhd,khd->hqk",
        query_tile.reshape(TILE, HEADS, HD),
        near_keys.reshape(-1, HEADS, HD),
        preferred_element_type=jnp.float32,
    ) * HD ** (-0.5)
    scores = jnp.where(live_keys[None, None, :], scores, -1e30)
    row_max = jnp.max(scores, axis=-1, keepdims=True)
    expos = jnp.exp(scores - row_max)
    return (expos / jnp.sum(expos, axis=-1, keepdims=True)).astype(jnp.bfloat16)


def pair_terms(
    own_rows,
    ensemble_wide_entries,
    observed_entries,
    loss_scale_weight,
    sample_sequence,
    derivative_factor,
):
    own_f = own_rows.astype(jnp.float32)

    def extend_sample_entries(totals, sample_ordinal):
        eased_aggregate, accrued_tangent_amount = totals
        sample_dispersion = own_f - sample_ordinal.astype(jnp.float32)[None]
        return (
            (
                eased_aggregate + eased_magnitude(sample_dispersion),
                accrued_tangent_amount + jnp.tanh(sample_dispersion / (2.0 * easing_breadth)),
            ),
            None,
        )

    blank_tile_filler = jnp.zeros_like(own_f)
    (eased_aggregate, accrued_tangent_amount), discarded_yield = lax.scan(
        extend_sample_entries, (blank_tile_filler, blank_tile_filler), ensemble_wide_entries
    )
    null_discrepancy = eased_magnitude(jnp.zeros((), jnp.float32))
    matrix_vertical_vector = loss_scale_weight[None, :, None]
    penalty_term_series = matrix_vertical_vector * (
        eased_magnitude(own_f - observed_entries[None])
        - (eased_aggregate - null_discrepancy) / (2.0 * (sample_sequence - 1))
    )
    grads = (
        matrix_vertical_vector
        * (
            jnp.tanh((own_f - observed_entries[None]) / (2.0 * easing_breadth))
            - accrued_tangent_amount / (sample_sequence - 1)
        )
        * derivative_factor
    ).astype(jnp.bfloat16)
    return (jnp.sum(penalty_term_series), grads)


def per_device(
    sample_layer_feed,
    gain,
    w_query,
    w_key,
    w_value,
    w_out,
    readout_matrix,
    target,
    pixel_weight,
    pix_mask,
    neighbours,
    neighbour_mask,
):
    member_rows = sample_layer_feed[0]
    sample_sequence = lax.axis_size("ens")
    pixels_dev = member_rows.shape[0]
    inner = w_query.shape[1]
    normed = rms_scaled(member_rows, gain)
    pieces = (
        lax.all_gather(w_query, "ens", axis=0, tiled=True),
        lax.all_gather(w_key, "ens", axis=0, tiled=True),
        lax.all_gather(w_value, "ens", axis=0, tiled=True),
    )
    columns = normed
    queries, key_rows, value_rows = tuple(
        (
            jnp.dot(columns, shard_piece, preferred_element_type=jnp.float32)
            for shard_piece in pieces
        )
    )
    queries = queries.astype(jnp.bfloat16)
    key_rows = key_rows.astype(jnp.bfloat16)
    value_rows = value_rows.astype(jnp.bfloat16)
    key_window = padded(jnp.stack([key_rows, value_rows]), (("pix", 1),), pixels_dev)
    position = lax.axis_index("pix")
    per_dev = pixels_dev // TILE
    local_slots = neighbours - (position - 1) * per_dev
    padded_mask = jnp.pad(pix_mask, (pixels_dev, pixels_dev))
    live_window = (
        lax.dynamic_slice_in_dim(padded_mask, position * pixels_dev, 3 * pixels_dev, 0).reshape(
            3 * per_dev, TILE
        )
        > 0
    )
    key_tiles = key_window[0].reshape(3 * per_dev, TILE, inner)
    value_tiles = key_window[1].reshape(3 * per_dev, TILE, inner)
    query_tiles = queries.reshape(per_dev, TILE, inner)

    def attend(inputs):
        query_tile, slots, slot_live = inputs
        live_keys = (live_window[slots] & (slot_live[:, None] > 0)).reshape(NB * TILE)
        near_keys = key_tiles[slots].reshape(NB * TILE, inner)
        weights = tile_weights(query_tile, near_keys, live_keys)
        near_values = value_tiles[slots].reshape(NB * TILE, HEADS, HD)
        mixture = jnp.einsum(
            "hqk,khd->qhd", weights, near_values, preferred_element_type=jnp.float32
        )
        return (mixture.reshape(TILE, inner).astype(jnp.bfloat16), weights)

    mixed_tiles, stored_weights = lax.map(attend, (query_tiles, local_slots, neighbour_mask))
    neighbour_mixing_vector = mixed_tiles.reshape(pixels_dev, inner)
    projected = jnp.dot(
        neighbour_mixing_vector,
        lax.all_gather(w_out, "ens", axis=1, tiled=True),
        preferred_element_type=jnp.float32,
    )
    hidden_state = (member_rows.astype(jnp.float32) + projected).astype(jnp.bfloat16)
    sample_prediction = jnp.dot(
        hidden_state, readout_matrix, preferred_element_type=jnp.float32
    ).astype(jnp.bfloat16)
    own_mask = live_window[per_dev : 2 * per_dev].reshape(pixels_dev)
    loss_scale_weight = pixel_weight * own_mask.astype(jnp.float32)
    grid_cell_number = pixels_dev * lax.axis_size("pix")
    derivative_factor = 1.0 / math.sqrt(sample_sequence * grid_cell_number)
    ensemble_wide_entries = lax.all_gather(sample_prediction[None], "ens", axis=0, tiled=True)
    loss_partial_sum, entry_derivatives = pair_terms(
        sample_prediction[None],
        ensemble_wide_entries,
        target,
        loss_scale_weight,
        sample_sequence,
        derivative_factor,
    )
    prediction_derivative = entry_derivatives[0]
    loss = lax.psum(loss_partial_sum, ("ens", "pix")) / (
        sample_sequence * grid_cell_number * sample_prediction.shape[1]
    )
    latent_derivative = lax.dot_general(
        prediction_derivative,
        readout_matrix,
        (((1,), (1,)), ((), ())),
        preferred_element_type=jnp.float32,
    ).astype(jnp.bfloat16)
    columns = latent_derivative
    grad_attended = lax.dot_general(
        columns,
        lax.all_gather(w_out, "ens", axis=1, tiled=True),
        (((1,), (1,)), ((), ())),
        preferred_element_type=jnp.float32,
    )
    grad_attended = grad_attended.astype(jnp.bfloat16)
    grad_tiles = grad_attended.reshape(per_dev, TILE, HEADS, HD)

    def collect(accumulated, inputs):
        weights, slots, grad_tile = inputs
        contrib = jnp.einsum(
            "hqk,qhd->khd", weights, grad_tile, preferred_element_type=jnp.float32
        ).reshape(NB, TILE, inner)
        return (accumulated.at[slots].add(contrib), None)

    start_acc = jnp.zeros((3 * per_dev, TILE, inner), jnp.float32)
    accumulated, discarded_yield = lax.scan(
        collect, start_acc, (stored_weights, local_slots, grad_tiles)
    )
    accumulated = accumulated.reshape(3 * pixels_dev, inner)
    from_above = passed_along(accumulated[:pixels_dev].astype(jnp.bfloat16), "pix", -1).astype(
        jnp.float32
    )
    from_below = passed_along(accumulated[2 * pixels_dev :].astype(jnp.bfloat16), "pix", 1).astype(
        jnp.float32
    )
    grad_values = (accumulated[pixels_dev : 2 * pixels_dev] + from_above + from_below).astype(
        jnp.bfloat16
    )
    value_term = lax.dot_general(
        normed, grad_values, (((0,), (0,)), ((), ())), preferred_element_type=jnp.float32
    )
    output_term = lax.dot_general(
        latent_derivative,
        neighbour_mixing_vector,
        (((0,), (0,)), ((), ())),
        preferred_element_type=jnp.float32,
    )
    owned_rows = lax.psum_scatter(
        jnp.concatenate([value_term, output_term], axis=1).astype(jnp.bfloat16),
        "ens",
        scatter_dimension=0,
        tiled=True,
    )
    summed = lax.psum(owned_rows, "pix").astype(jnp.float32)
    grad_w_value = summed[:, :inner]
    grad_w_out = summed[:, inner:].T
    return (loss, grad_w_out, grad_w_value)


def solution(mesh):
    in_specs = (
        P("ens", "pix", None),
        P(),
        P("ens", None),
        P("ens", None),
        P("ens", None),
        P(None, "ens"),
        P(),
        P("pix", None),
        P("pix"),
        P(),
        P("pix", None),
        P("pix", None),
    )
    out_specs = (P(), P(None, "ens"), P("ens", None))
    return jax.shard_map(
        per_device, mesh=mesh, in_specs=in_specs, out_specs=out_specs, check_vma=False
    )
```

profile of v0, /device:TPU:0, one launch (start us, length us, event | category | flops | bytes accessed | tf_op | source)
XLA Modules:
  0.0 239.7 jit_solution(1672874567291596875)
XLA Ops:
  7.3 0.7 all-gather.6.cloned.1.call-update
  7.9 0.0 all-gather.8.cloned.1.call-start
  8.0 0.7 all-gather.8.cloned.1.call-update
  8.7 0.0 all-gather.10.cloned.1.call-start
  8.7 0.7 all-gather.10.cloned.1.call-update
  9.5 0.5 all-gather.12.cloned.1.call-update
  10.0 0.0 reduce-scatter.2.cloned.1.call-start
  10.1 0.8 fusion.75
  10.8 0.8 fusion.43
  11.6 1.1 fusion.18
  12.7 0.7 fusion.44
  13.4 0.7 compare_bitcast_fusion
  14.0 0.6 gather_fusion.1
  14.6 0.1 and_bitcast_fusion
  14.7 14.4 %all-gather.6.cloned.1.call-done = bf16[1024,512]{1,0:T(8,128)(2,1)} async-done(((bf16[256,512]{1,0:T(8,128)(2,1)}), bf16[1024,512]{1,0:T(8,128)(2,1)}) %all-gather.6.cloned.1.call-update) | async-done | bytes 1048592 | tf_op jit(solution)/shard_map/all_gather | solution.py:126
  29.1 1.7 fusion.14
  30.7 16.6 %all-gather.8.cloned.1.call-done = bf16[1024,512]{1,0:T(8,128)(2,1)} async-done(((bf16[256,512]{1,0:T(8,128)(2,1)}), bf16[1024,512]{1,0:T(8,128)(2,1)}) %all-gather.8.cloned.1.call-update) | async-done | bytes 1048592 | tf_op jit(solution)/shard_map/all_gather | solution.py:127
  47.4 1.6 fusion.15
  49.0 3.4 %collective-permute-start = (bf16[2,128,512]{2,1,0:T(8,128)(2,1)S(1)}, bf16[2,128,512]{2,1,0:T(8,128)(2,1)S(1)}, u32[]{:S(2)}, u32[]{:S(2)}) collective-permute-start(bf16[2,128,512]{2,1,0:T(8,128)(2,1)S(1)} %pad_maximum_fusion.2), channel_id=1, source_target_pairs={{0,1},{1,2},{2,3},{3,4},{4,5},{5,6},{6,7},{8,9},{9,10},{10,11},{11... | collective-permute-start | bytes 786440 | tf_op jit(solution)/shard_map/ppermute | solution.py:25
  52.4 1.3 collective-permute-start.1
  53.7 12.0 %all-gather.10.cloned.1.call-done = bf16[1024,512]{1,0:T(8,128)(2,1)} async-done(((bf16[256,512]{1,0:T(8,128)(2,1)}), bf16[1024,512]{1,0:T(8,128)(2,1)}) %all-gather.10.cloned.1.call-update) | async-done | bytes 1048592 | tf_op jit(solution)/shard_map/all_gather | solution.py:125
  65.7 1.6 convolution_convert_fusion.4
  67.3 0.1 copy.25
  67.4 0.1 pad_maximum_fusion.1
  67.5 0.1 fusion.57
  67.6 0.6 gather_fusion.2
  68.2 2.7 %reshape.204 = bf16[1152,8,64]{2,1,0:T(8,128)(2,1)} reshape(bf16[9,128,512]{2,1,0:T(8,128)(2,1)S(1)} %gather_fusion.2) | data formatting | bytes 2359296 | tf_op jit(solution)/shard_map/while/body/eval_jaxpr/reshape;while/body/eval_jaxpr/reshape | solution.py:54
  70.9 0.6 gather_fusion
  71.5 2.6 %reshape.203 = bf16[1152,8,64]{2,1,0:T(8,128)(2,1)} reshape(bf16[9,128,512]{2,1,0:T(8,128)(2,1)S(1)} %gather_fusion) | data formatting | bytes 2359296 | tf_op jit(solution)/shard_map/while/body/eval_jaxpr/reshape | solution.py:159
  74.1 5.8 %exponential_reduce_fusion = (f32[8,128]{1,0:T(8,128)S(1)}, f32[8,128,1152]{2,1,0:T(8,128)}) fusion(bf16[128,8,64]{0,2,1:T(8,128)(2,1)S(1)} %bitcast.98, bf16[1152,8,64]{2,1,0:T(8,128)(2,1)} %reshape.204, pred[1152]{0:T(1024)(128)(4,1)S(1)} %and_bitcast_fusion), kind=kOutput, calls=%fused_computation.17 | convolution fusion | flops 155714688 | bytes 6034560 | tf_op jit(solution)/shard_map/while/body/eval_jaxpr/sub | solution.py:59
  79.9 3.6 %divide_convert_fusion = bf16[8,128,1152]{2,1,0:T(8,128)(2,1)S(1)} fusion(f32[8,128,1152]{2,1,0:T(8,128)} %get-tuple-element.119, f32[8,128]{1,0:T(8,128)S(1)} %get-tuple-element.118), kind=kLoop, calls=%fused_computation.16 | loop fusion | flops 2359296 | bytes 7081984 | tf_op jit(solution)/shard_map/while/body/eval_jaxpr/convert_element_type | solution.py:60
  83.5 1.1 fusion.11
  84.7 1.7 fusion.16
  86.4 5.4 %all-gather = bf16[512,128]{1,0:T(8,128)(2,1)S(1)} all-gather(bf16[128,128]{1,0:T(8,128)(2,1)S(1)} %fusion.16), channel_id=2, replica_groups=mesh['ens'=4,'pix'=8] {'ens'}, dimensions={0}, use_global_device_ids=true | all-gather | bytes 163840 | tf_op jit(solution)/shard_map/all_gather | solution.py:180
  91.8 0.5 while.3
  91.8 0.1 select_add_fusion.2
  92.0 0.1 select_add_fusion.2
  92.1 0.1 select_add_fusion.2
  92.2 0.1 select_add_fusion.2
  92.4 0.3 convolution_convert_fusion.2
  92.7 0.7 copy-done.4
  93.3 1.7 convolution_convert_fusion.3
  95.1 0.1 copy.27
  95.2 1.9 convolution_bitcast_fusion
  97.1 4.3 %reshape.198 = f32[9,128,512]{1,0,2:T(8,128)} reshape(f32[1152,8,64]{0,2,1:T(8,128)} %convolution_bitcast_fusion) | data formatting | bytes 4718592 | tf_op jit(solution)/shard_map/while/body/eval_jaxpr/reshape | solution.py:213
  101.4 3.3 %copy.28 = f32[9,128,512]{2,1,0:T(8,128)S(1)} copy(f32[9,128,512]{1,0,2:T(8,128)} %reshape.198) | data formatting | bytes 4718592 | tf_op jit(solution)/shard_map/while/body/eval_jaxpr/reshape | solution.py:213
  104.8 0.1 broadcast_in_dim.53
  104.8 3.1 %scatter_fusion = f32[3,128,512]{2,1,0:T(8,128)S(1)} fusion(f32[3,128,512]{2,1,0:T(8,128)S(1)} %broadcast_in_dim.53, s32[9]{0:T(128)S(1)} %fusion.44, f32[9,128,512]{2,1,0:T(8,128)S(1)} %copy.28), kind=kCustom, calls=%fused_computation.3 | custom fusion | flops 589824 | bytes 7077924 | tf_op jit(solution)/shard_map/while/body/eval_jaxpr/scatter-add | solution.py:214
  107.9 0.1 convert.11
  108.0 1.3 collective-permute-start.2
  109.3 4.6 %collective-permute-start.3 = (bf16[128,512]{1,0:T(8,128)(2,1)S(1)}, bf16[128,512]{1,0:T(8,128)(2,1)S(1)}, u32[]{:S(2)}, u32[]{:S(2)}) collective-permute-start(bf16[128,512]{1,0:T(8,128)(2,1)S(1)} %get-tuple-element.117), channel_id=1, source_target_pairs={{0,1},{1,2},{2,3},{3,4},{4,5},{5,6},{6,7},{8,9},{9,10},{10,11},{11... | collective-permute-start | bytes 393224 | tf_op jit(solution)/shard_map/ppermute | solution.py:34
  113.9 1.4 convolution_convert_fusion
  115.3 0.3 collective-permute-done.2
  115.7 2.7 %collective-permute-done.3 = bf16[128,512]{1,0:T(8,128)(2,1)S(1)} collective-permute-done((bf16[128,512]{1,0:T(8,128)(2,1)S(1)}, bf16[128,512]{1,0:T(8,128)(2,1)S(1)}, u32[]{:S(2)}, u32[]{:S(2)}) %collective-permute-start.3) | collective-permute-done | bytes 131104 | tf_op jit(solution)/shard_map/ppermute | solution.py:34
  118.4 0.5 convolution_convert_fusion.1
  118.9 1.5 pad_maximum_fusion
  120.5 0.0 all-reduce.3.cloned.1.call-start
  120.5 31.9 %reduce-scatter.2.cloned.1.call-done = bf16[256,1024]{0,1:T(8,128)(2,1)} async-done(((bf16[1024,1024]{0,1:T(8,128)(2,1)}), bf16[256,1024]{0,1:T(8,128)(2,1)}) %reduce-scatter.2.cloned.1.call-update) | async-done | bytes 524304 | tf_op jit(solution)/shard_map/reduce_scatter | solution.py:239
  152.5 0.7 fusion.33
  153.2 39.8 %psum.14 = f32[]{:T(128)} all-reduce(f32[]{:T(128)} %fusion.33), channel_id=1, replica_groups=mesh['ens'=4,'pix'=8] {'ens','pix'}, use_global_device_ids=true, to_apply=%region_6.7 | all-reduce | flops 1 | bytes 8 | tf_op jit(solution)/shard_map/psum | solution.py:190
  193.6 35.1 %all-reduce.3.cloned.1.call-done = bf16[256,1024]{0,1:T(8,128)(2,1)} async-done(((bf16[256,1024]{0,1:T(8,128)(2,1)}), bf16[256,1024]{0,1:T(8,128)(2,1)}) %all-reduce.3.cloned.1.call-update) | async-done | bytes 524304 | tf_op jit(solution)/shard_map/psum | solution.py:245
  228.7 1.2 convert_element_type.103
  229.9 0.8 slice_bitcast_fusion
  230.8 1.0 copy.29
  (37 shorter events, 0.3 us)
Async XLA Ops:
  7.2 77.5 %copy-start = (bf16[1024,128]{1,0:T(8,128)(2,1)S(1)}, bf16[1024,128]{1,0:T(8,128)(2,1)}, u32[]{:S(2)}) copy-start(bf16[1024,128]{1,0:T(8,128)(2,1)} %param.20) | copy-start | bytes 786436
  7.2 40.2 %copy-start.1 = (bf16[1,128,1024]{2,1,0:T(8,128)(2,1)S(1)}, bf16[1,128,1024]{2,1,0:T(8,128)(2,1)}, u32[]{:S(2)}) copy-start(bf16[1,128,1024]{2,1,0:T(8,128)(2,1)} %param.14) | copy-start | bytes 786436
  7.2 40.2 %copy-start.9 = (f32[1024]{0:T(1024)S(1)}, f32[1024]{0:T(1024)}, u32[]{:S(2)}) copy-start(f32[1024]{0:T(1024)} %param.15) | copy-start | bytes 12292
  7.2 46.5 %copy-start.10 = (f32[128]{0:T(128)S(1)}, f32[128]{0:T(128)}, u32[]{:S(2)}) copy-start(f32[128]{0:T(128)} %param.22) | copy-start | bytes 1540
  7.2 21.8 %all-gather.6.cloned.1.call-start = ((), (), s32[]{:S(2)}) async-start(), calls=%async_computation.1 | async-start | bytes 1310720 | tf_op jit(solution)/shard_map/all_gather | solution.py:126
  7.9 39.4 %all-gather.8.cloned.1.call-start = ((), (), s32[]{:S(2)}) async-start(), calls=%async_computation.2 | async-start | bytes 1310720 | tf_op jit(solution)/shard_map/all_gather | solution.py:127
  8.7 57.0 %all-gather.10.cloned.1.call-start = ((), (), s32[]{:S(2)}) async-start(), calls=%async_computation.3 | async-start | bytes 1310720 | tf_op jit(solution)/shard_map/all_gather | solution.py:125
  9.4 75.2 %all-gather.12.cloned.1.call-start = ((), (), s32[]{:S(2)}) async-start(), calls=%async_computation.4 | async-start | bytes 1310720 | tf_op jit(solution)/shard_map/all_gather | solution.py:169
  10.0 142.4 %reduce-scatter.2.cloned.1.call-start = ((), (), s32[]{:S(2)}) async-start(), calls=%async_computation.5 | async-start | bytes 2621440 | tf_op jit(solution)/shard_map/reduce_scatter | solution.py:239
  49.0 18.4 %collective-permute-start = (bf16[2,128,512]{2,1,0:T(8,128)(2,1)S(1)}, bf16[2,128,512]{2,1,0:T(8,128)(2,1)S(1)}, u32[]{:S(2)}, u32[]{:S(2)}) collective-permute-start(bf16[2,128,512]{2,1,0:T(8,128)(2,1)S(1)} %pad_maximum_fusion.2), channel_id=1, source_target_pairs={{0,1},{1,2},{2,3},{3,4},{4,5},{5,6},{6,7},{8,9},{9,10},{10,11},{11... | collective-permute-start | bytes 786440 | tf_op jit(solution)/shard_map/ppermute | solution.py:25
  52.4 15.0 %collective-permute-start.1 = (bf16[2,128,512]{2,1,0:T(8,128)(2,1)S(1)}, bf16[2,128,512]{2,1,0:T(8,128)(2,1)S(1)}, u32[]{:S(2)}, u32[]{:S(2)}) collective-permute-start(bf16[2,128,512]{2,1,0:T(8,128)(2,1)S(1)} %pad_maximum_fusion.2), channel_id=1, source_target_pairs={{1,0},{2,1},{3,2},{4,3},{5,4},{6,5},{7,6},{9,8},{10,9},{11,10},{12... | collective-permute-start | bytes 786440 | tf_op jit(solution)/shard_map/ppermute | solution.py:26
  79.9 3.6 %copy-start.3 = (bf16[1152,8,64]{2,1,0:T(8,128)(2,1)S(1)}, bf16[1152,8,64]{2,1,0:T(8,128)(2,1)}, u32[]{:S(2)}) copy-start(bf16[1152,8,64]{2,1,0:T(8,128)(2,1)} %reshape.203) | copy-start | bytes 3538948
  84.6 10.5 %copy-start.6 = (bf16[8,64,128]{2,1,0:T(8,128)(2,1)}, bf16[8,64,128]{2,1,0:T(8,128)(2,1)S(1)}, u32[]{:S(2)}) copy-start(bf16[8,64,128]{2,1,0:T(8,128)(2,1)S(1)} %fusion.11) | copy-start | bytes 393220
  84.6 7.7 %copy-start.7 = (f32[128,128]{1,0:T(8,128)S(1)}, f32[128,128]{1,0:T(8,128)}, u32[]{:S(2)}) copy-start(f32[128,128]{1,0:T(8,128)} %param.21) | copy-start | bytes 196612
  92.6 0.7 copy-start.4
  107.9 10.5 %copy-start.2 = (bf16[1,128,1024]{2,1,0:T(8,128)(2,1)S(1)}, bf16[1,128,1024]{2,1,0:T(8,128)(2,1)}, u32[]{:S(2)}) copy-start(bf16[1,128,1024]{2,1,0:T(8,128)(2,1)} %param.14) | copy-start | bytes 786436
  108.0 7.7 %collective-permute-start.2 = (bf16[128,512]{1,0:T(8,128)(2,1)S(1)}, bf16[128,512]{1,0:T(8,128)(2,1)S(1)}, u32[]{:S(2)}, u32[]{:S(2)}) collective-permute-start(bf16[128,512]{1,0:T(8,128)(2,1)S(1)} %get-tuple-element.116), channel_id=1, source_target_pairs={{1,0},{2,1},{3,2},{4,3},{5,4},{6,5},{7,6},{9,8},{10,9},{11,10},{12... | collective-permute-start | bytes 393224 | tf_op jit(solution)/shard_map/ppermute | solution.py:34
  109.3 9.1 %collective-permute-start.3 = (bf16[128,512]{1,0:T(8,128)(2,1)S(1)}, bf16[128,512]{1,0:T(8,128)(2,1)S(1)}, u32[]{:S(2)}, u32[]{:S(2)}) collective-permute-start(bf16[128,512]{1,0:T(8,128)(2,1)S(1)} %get-tuple-element.117), channel_id=1, source_target_pairs={{0,1},{1,2},{2,3},{3,4},{4,5},{5,6},{6,7},{8,9},{9,10},{10,11},{11... | collective-permute-start | bytes 393224 | tf_op jit(solution)/shard_map/ppermute | solution.py:34
  120.5 32.0 %copy-start.8 = (f32[128,128]{1,0:T(8,128)S(1)}, f32[128,128]{1,0:T(8,128)}, u32[]{:S(2)}) copy-start(f32[128,128]{1,0:T(8,128)} %param.21) | copy-start | bytes 196612
  120.5 108.2 %all-reduce.3.cloned.1.call-start = ((), (), s32[]{:S(2)}) async-start(), calls=%async_computation.6 | async-start | bytes 1048576 | tf_op jit(solution)/shard_map/psum | solution.py:245
  228.7 2.0 copy-start.5
Sparse Core Ops, SparseCore 0:
  9.6 19.4 all-gather.5
  30.6 16.7 all-gather.7
  48.9 16.7 all-gather.9
  67.1 16.8 all-gather.11
  120.6 31.8 reduce-scatter.1
  156.1 72.5 all-reduce.2
where the time goes:
time: 241 us; the launch traced here: 240 us
  waiting for transfers between devices  116 us (48%)
  blocking collectives  45.2 us (19%)
  matrix products  19.3 us (8%)
  local copies, waits for them, and re-layouts  17.7 us (7%)
  between operations  16.3 us (7%)
  other arithmetic  14.7 us (6%)
  starting transfers between devices  10.8 us (4%)
    psum x1, blocking collectives, per_device(): lax.psum(loss_partial_sum, ('ens', 'pix'))  39.8 us
    psum x1, waiting for transfers between devices, per_device(): summed = lax.psum(owned_rows, 'pix').astype(jnp.float32)  35.1 us
    reduce_scatter x1, waiting for transfers between devices, per_device(): lax.psum_scatter(jnp.concatenate([value_term, output_term], axis=1).astyp...  31.9 us
    all_gather x1, waiting for transfers between devices, per_device(): lax.all_gather(w_value, 'ens', axis=0, tiled=True)  16.6 us
    all_gather x1, waiting for transfers between devices, per_device(): lax.all_gather(w_key, 'ens', axis=0, tiled=True)  14.4 us
    all_gather x1, waiting for transfers between devices, per_device(): lax.all_gather(w_query, 'ens', axis=0, tiled=True)  12 us
    reshape x2, local copies, waits for them, and re-layouts, collect(): contrib = jnp.einsum('hqk,qhd->khd', weights, grad_tile, preferred_elemen...  7.61 us
    ppermute x2, starting transfers between devices, passed_along(): lax.ppermute(value, axis, [(source, source + steps) for source in range(i...  5.86 us
  transfers between devices with their start and end apart: 10, of which 7 were waited for; matrix products, arithmetic and copies ran while one was open for 12% of the time, Pallas kernels for 0%

commit v1 on v0

v1 whole, which is shorter than its diff:
```python
import functools
import math

import jax
import jax.numpy as jnp
from jax import lax
from jax.experimental import pallas as pl
from jax.experimental.pallas import tpu as pltpu
from jax.sharding import PartitionSpec as P

HEADS = 8
HD = 64
TILE = 128
NB = 9
LANES = 128
EPS = 1e-06
BREADTH = 0.1

F32 = jnp.float32
BF16 = jnp.bfloat16
VMEM = pl.BlockSpec(memory_space=pltpu.VMEM)
SMEM = pl.BlockSpec(memory_space=pltpu.SMEM)
NN = (((1,), (0,)), ((), ()))
NT = (((1,), (1,)), ((), ()))
TN = (((0,), (0,)), ((), ()))


def dot(a, b, dims=NN):
    return lax.dot_general(a, b, dims, preferred_element_type=F32)


def call(body, outs, ins, flops, name, scratch=(), vmem=32):
    specs = [SMEM if s == "s" else VMEM for s, _ in ins]
    return pl.pallas_call(
        body,
        out_shape=[jax.ShapeDtypeStruct(s, d) for s, d in outs],
        in_specs=specs,
        out_specs=[VMEM] * len(outs),
        scratch_shapes=list(scratch),
        compiler_params=pltpu.CompilerParams(vmem_limit_bytes=vmem * 2**20),
        cost_estimate=pl.CostEstimate(flops=flops, bytes_accessed=2**20, transcendentals=0),
        name=name,
    )(*[a for _, a in ins])


def xor_permute(value, axis, mask):
    size = lax.axis_size(axis)
    return lax.ppermute(value, axis, [(i, i ^ mask) for i in range(size)])


def normed_body(n_ens, dsh, x_ref, up_ref, down_ref, gain_ref, n_ref, keep_ref, send_ref, turned_ref):
    core = lax.axis_index("ens") % 2
    gain = gain_ref[...]
    for i, ref in enumerate((up_ref, x_ref, down_ref)):
        rows = ref[0].astype(F32)
        inv = lax.rsqrt(jnp.mean(rows * rows, axis=-1, keepdims=True) + EPS)
        n_ref[i * TILE : (i + 1) * TILE, :] = (rows * inv * gain).astype(BF16)
    turned_ref[...] = n_ref[...].T
    for b in range(n_ens // 2):
        mine = pl.multiple_of((2 * b + core) * dsh, dsh)
        theirs = pl.multiple_of((2 * b + 1 - core) * dsh, dsh)
        keep_ref[b * dsh : (b + 1) * dsh, :] = turned_ref[pl.ds(mine, dsh), :]
        send_ref[b * dsh : (b + 1) * dsh, :] = turned_ref[pl.ds(theirs, dsh), :]


def counts_of(nb_ref, nm_ref, position):
    counts = []
    for d in (-1, 0, 1):
        total = jnp.int32(0)
        for s in range(NB):
            hit = (nb_ref[0, s] == position + d) & (nm_ref[0, s] > 0)
            total = total + jnp.where(hit, 1, 0)
        counts.append(total.astype(F32))
    return counts


def assembled(pieces, scratch, dsh):
    me = lax.axis_index("ens")
    for j, ref in enumerate(pieces):
        start = pl.multiple_of((me ^ j) * dsh, dsh)
        scratch[pl.ds(start, dsh), :] = ref[...]
    return scratch[...]


def weights_body(n_ens, dsh, n_ref, *refs):
    q_refs, k_refs = refs[:n_ens], refs[n_ens : 2 * n_ens]
    mask_ref, nb_ref, nm_ref, w_ref, scratch = refs[2 * n_ens :]
    position = lax.axis_index("pix")
    n_pix = mask_ref.shape[0]
    counts = counts_of(nb_ref, nm_ref, position)
    lanes = []
    for i, d in enumerate((-1, 0, 1)):
        row = jnp.clip(position + d, 0, n_pix - 1)
        lanes.append(jnp.where(mask_ref[pl.ds(row, 1), :] > 0, 1.0, 0.0) * counts[i])
    times = jnp.concatenate(lanes, axis=1)
    bias = jnp.where(times > 0, 0.0, -1e30)
    queries = dot(n_ref[TILE : 2 * TILE, :], assembled(q_refs, scratch, dsh)).astype(BF16)
    keys = dot(n_ref[...], assembled(k_refs, scratch, dsh)).astype(BF16)
    lane = lax.broadcasted_iota(jnp.int32, (TILE, LANES), 1)
    for h in range(HEADS):
        cols = slice(h // 2 * LANES, (h // 2 + 1) * LANES)
        own = (lane < HD) if h % 2 == 0 else (lane >= HD)
        query = jnp.where(own, queries[:, cols], jnp.zeros((), BF16))
        scores = dot(query, keys[:, cols], NT) * HD ** (-0.5) + bias
        top = jnp.max(scores, axis=-1, keepdims=True)
        expos = jnp.exp(scores - top)
        total = jnp.sum(expos * times, axis=-1, keepdims=True)
        w_ref[h] = (expos / total).astype(BF16)


def attend_body(n_ens, dsh, n_ref, *refs):
    v_refs = refs[:n_ens]
    w_ref, nb_ref, nm_ref, att_ref, scratch = refs[n_ens:]
    counts = counts_of(nb_ref, nm_ref, lax.axis_index("pix"))
    values = dot(n_ref[...], assembled(v_refs, scratch, dsh)).astype(BF16)
    lane = lax.broadcasted_iota(jnp.int32, (TILE, LANES), 1)
    for g in range(HEADS // 2):
        cols = slice(g * LANES, (g + 1) * LANES)
        halves = []
        for h in (2 * g, 2 * g + 1):
            total = jnp.zeros((TILE, LANES), F32)
            for i in range(3):
                rows = slice(i * TILE, (i + 1) * TILE)
                total = total + counts[i] * dot(w_ref[h, :, rows], values[rows, cols])
            halves.append(total)
        att_ref[:, cols] = jnp.where(lane < HD, halves[0], halves[1]).astype(BF16)


def forecast_body(n_ens, dsh, x_ref, att_ref, read_ref, *refs):
    o_refs = refs[:n_ens]
    f_ref, scratch = refs[n_ens:]
    hidden = x_ref[0].astype(F32) + dot(att_ref[...], assembled(o_refs, scratch, dsh), NT)
    f_ref[...] = dot(hidden.astype(BF16), read_ref[...]).astype(BF16)


def sabs(a):
    mag = jnp.abs(a)
    return mag + 2.0 * BREADTH * jnp.log1p(jnp.exp(mag * (-1.0 / BREADTH)))


def backward_body(n_ens, dsh, factor, *refs):
    f_refs, o_refs = refs[:n_ens], refs[n_ens : 2 * n_ens]
    target_ref, pw_ref, mask_ref, read_ref, w_ref, nb_ref, nm_ref = refs[2 * n_ens : 2 * n_ens + 7]
    gf_ref, con_ref, loss_ref, scratch = refs[2 * n_ens + 7 :]
    position = lax.axis_index("pix")
    counts = counts_of(nb_ref, nm_ref, position)
    live = jnp.where(mask_ref[pl.ds(position, 1), :] > 0, 1.0, 0.0)
    lw = jnp.broadcast_to(pw_ref[...] * live, (LANES, TILE)).T
    target = target_ref[...]
    fc = [ref[...].astype(F32) for ref in f_refs]
    sums = [jnp.zeros((TILE, LANES), F32) for _ in range(n_ens)]
    for i in range(n_ens):
        for j in range(i + 1, n_ens):
            t = jnp.tanh((fc[i] - fc[j]) / (2.0 * BREADTH))
            sums[i] = sums[i] + t
            sums[j] = sums[j] - t
    for i in range(n_ens):
        t = jnp.tanh((fc[i] - target) / (2.0 * BREADTH))
        gf_ref[i * TILE : (i + 1) * TILE, :] = (lw * (t - sums[i] / (n_ens - 1)) * factor).astype(BF16)
    others = jnp.zeros((TILE, LANES), F32)
    for j in range(1, n_ens):
        others = others + sabs(fc[0] - fc[j])
    terms = lw * (sabs(fc[0] - target) - others / (2.0 * (n_ens - 1)))
    loss_ref[...] = jnp.full((8, LANES), jnp.sum(terms), F32)
    grad_hidden = dot(gf_ref[:TILE, :], read_ref[...], NT).astype(BF16)
    grad_att = dot(grad_hidden, assembled(o_refs, scratch, dsh)).astype(BF16)
    lane = lax.broadcasted_iota(jnp.int32, (TILE, LANES), 1)
    zero = jnp.zeros((), BF16)
    for g in range(HEADS // 2):
        cols = slice(g * LANES, (g + 1) * LANES)
        pair = grad_att[:, cols]
        both = dot(w_ref[2 * g], jnp.where(lane < HD, pair, zero), TN)
        both = both + dot(w_ref[2 * g + 1], jnp.where(lane < HD, zero, pair), TN)
        for i in range(3):
            rows = slice(i * TILE, (i + 1) * TILE)
            con_ref[rows, cols] = (both[rows] * counts[i]).astype(BF16)


def value_body(blocks, dsh, keep_ref, sib_ref, own_con, sib_con, v_ref):
    term = dot(keep_ref[...], own_con[...]) + dot(sib_ref[...], sib_con[...])
    for b in range(blocks):
        for cb in range(term.shape[1] // LANES):
            v_ref[b, cb * dsh : (cb + 1) * dsh, :] = term[
                b * dsh : (b + 1) * dsh, cb * LANES : (cb + 1) * LANES
            ]


def output_body(n_ens, dsh, gf_ref, read_ref, *refs):
    att_refs = refs[:n_ens]
    o_ref, scratch = refs[n_ens:]
    start = pl.multiple_of(lax.axis_index("ens") * dsh, dsh)
    for j in range(n_ens):
        scratch[j * TILE : (j + 1) * TILE, :] = att_refs[j][...]
    turned = dot(read_ref[pl.ds(start, dsh), :], gf_ref[...], NT).astype(BF16)
    term = dot(turned, scratch[...])
    for cb in range(term.shape[1] // LANES):
        o_ref[cb * dsh : (cb + 1) * dsh, :] = term[:, cb * LANES : (cb + 1) * LANES]


def finish_body(n_pix, dsh, *refs):
    pieces = refs[:n_pix]
    gv_ref, go_ref, scratch = refs[n_pix:]
    rows = scratch.shape[1] // n_pix
    position = lax.axis_index("pix")
    for j in range(n_pix):
        start = pl.multiple_of((position ^ j) * rows, rows)
        scratch[:, pl.ds(start, rows), :] = pieces[j][...].astype(F32)
    for cb in range(scratch.shape[1] // dsh):
        gv_ref[:, cb * LANES : (cb + 1) * LANES] = scratch[0, cb * dsh : (cb + 1) * dsh, :]
        go_ref[cb * LANES : (cb + 1) * LANES, :] = scratch[1, cb * dsh : (cb + 1) * dsh, :].T


def in_parts(total):
    first = lax.reduce_precision(total, 8, 7)
    second = lax.reduce_precision(total - first, 8, 7)
    third = total - first - second
    return jnp.stack([first, second, third]).astype(BF16)


def from_parts(parts):
    parts = parts.astype(F32)
    return parts[0] + parts[1] + parts[2]


def gathered(value, axis, bits):
    pieces = {0: value}
    for bit in bits:
        pieces.update({j ^ bit: xor_permute(piece, axis, bit) for j, piece in list(pieces.items())})
    return [pieces[j] for j in sorted(pieces)]


def at(blocks, index):
    return lax.dynamic_index_in_dim(blocks, index, 0, keepdims=False)


def part_of(split, index):
    return lax.dynamic_index_in_dim(split, index, 1, keepdims=False).reshape(-1, LANES)


def with_loss(block, total):
    rows = jnp.broadcast_to(in_parts(total)[:, None], (3, LANES))
    rows = jnp.pad(rows, ((0, 13), (0, 0)))
    return jnp.concatenate([block.reshape(-1, LANES).astype(BF16), rows], axis=0)


def split_loss(message):
    return message[:-16], from_parts(message[-16:-13, 0])


def per_device(
    sample_layer_feed,
    gain,
    w_query,
    w_key,
    w_value,
    w_out,
    readout_matrix,
    target,
    pixel_weight,
    pix_mask,
    neighbours,
    neighbour_mask,
):
    n_ens, n_pix = lax.axis_size("ens"), lax.axis_size("pix")
    dsh, inner = w_query.shape
    d_model = dsh * n_ens
    n_out = readout_matrix.shape[1]
    ens_bits = [1 << b for b in reversed(range(n_ens.bit_length() - 1))]
    e, p = lax.axis_index("ens"), lax.axis_index("pix")
    rows = sample_layer_feed.shape[1]
    assert rows == TILE and n_out == LANES

    q_parts = gathered(w_query, "ens", ens_bits)
    k_parts = gathered(w_key, "ens", ens_bits)
    up = lax.ppermute(sample_layer_feed, "pix", [(i, i + 1) for i in range(n_pix - 1)])
    down = lax.ppermute(sample_layer_feed, "pix", [(i + 1, i) for i in range(n_pix - 1)])
    v_parts = gathered(w_value, "ens", ens_bits)
    o_parts = gathered(w_out.T, "ens", ens_bits)

    mask_rows = pix_mask.reshape(n_pix, TILE)
    half = ((d_model // 2, 3 * TILE), BF16)
    normed, turned_keep, turned_send = call(
        functools.partial(normed_body, n_ens, dsh),
        [((3 * TILE, d_model), BF16), half, half],
        [("v", sample_layer_feed), ("v", up), ("v", down), ("v", gain.reshape(1, -1))],
        10**7,
        "normed",
        scratch=[pltpu.VMEM((d_model, 3 * TILE), BF16)],
    )
    turned_sib = xor_permute(turned_send, "ens", 1)

    full = pltpu.VMEM((d_model, inner), BF16)
    (weights,) = call(
        functools.partial(weights_body, n_ens, dsh),
        [((HEADS, TILE, 3 * TILE), BF16)],
        [("v", normed)]
        + [("v", a) for a in q_parts + k_parts]
        + [("v", mask_rows), ("s", neighbours), ("s", neighbour_mask)],
        2 * 10**9,
        "weights",
        scratch=[full],
    )
    (attended,) = call(
        functools.partial(attend_body, n_ens, dsh),
        [((TILE, inner), BF16)],
        [("v", normed)]
        + [("v", a) for a in v_parts]
        + [("v", weights), ("s", neighbours), ("s", neighbour_mask)],
        10**9,
        "attend",
        scratch=[full],
    )
    (forecast,) = call(
        functools.partial(forecast_body, n_ens, dsh),
        [((TILE, LANES), BF16)],
        [("v", sample_layer_feed), ("v", attended), ("v", readout_matrix)] + [("v", a) for a in o_parts],
        10**9,
        "forecast",
        scratch=[full],
    )
    forecasts = gathered(forecast, "ens", ens_bits)
    attended_all = gathered(attended, "ens", ens_bits)

    factor = 1.0 / math.sqrt(n_ens * n_pix * TILE)
    grads, contrib, loss_rows = call(
        functools.partial(backward_body, n_ens, dsh, factor),
        [((n_ens * TILE, LANES), BF16), ((3 * TILE, inner), BF16), ((8, LANES), F32)],
        [("v", a) for a in forecasts + o_parts]
        + [("v", target), ("v", pixel_weight.reshape(1, TILE)), ("v", mask_rows), ("v", readout_matrix)]
        + [("v", weights), ("s", neighbours), ("s", neighbour_mask)],
        10**9,
        "backward",
        scratch=[full],
    )
    contrib_sib = xor_permute(contrib, "ens", 1)
    blocks = n_ens // 2
    (value_term,) = call(
        functools.partial(value_body, blocks, dsh),
        [((blocks, dsh * inner // LANES, LANES), F32)],
        [("v", turned_keep), ("v", turned_sib), ("v", contrib), ("v", contrib_sib)],
        10**9,
        "value_term",
    )
    (output_term,) = call(
        functools.partial(output_body, n_ens, dsh),
        [((dsh * inner // LANES, LANES), F32)],
        [("v", grads), ("v", readout_matrix)] + [("v", a) for a in attended_all],
        10**9,
        "output_term",
        scratch=[pltpu.VMEM((n_ens * TILE, inner), BF16)],
    )

    loss = loss_rows[0, 0]
    loss = loss + xor_permute(loss.reshape(1, 1), "ens", 1)[0, 0]
    for bit in ens_bits[:-1]:
        upper = (e // bit) % 2
        halves = value_term.reshape(2, -1, LANES)
        kept = at(halves, upper)
        message = with_loss(at(halves, 1 - upper), loss)
        got, other = split_loss(xor_permute(message, "ens", bit))
        value_term = kept + got.astype(F32)
        loss = loss + other
    value_term = value_term.reshape(-1, LANES)

    n_bits = n_pix.bit_length() - 1
    groups = [[1]] + [[1 << b for b in range(s, min(s + 2, n_bits))] for s in range(1, n_bits, 2)]
    terms = [value_term, output_term]
    for group in groups:
        size = 1 << len(group)
        low = group[0]
        pos = (p // low) % size
        shape = (n_pix // (low * size), size, -1, LANES)
        split = [t.reshape(shape) for t in terms]
        kept = [part_of(s, pos) for s in split]
        losses = [None] * size
        for d in range(1, size):
            message = with_loss(jnp.concatenate([part_of(s, pos ^ d) for s in split], axis=0), loss)
            got, other = split_loss(xor_permute(message, "pix", d * low))
            got = got.astype(F32).reshape(2, -1, LANES)
            kept = [kept[0] + got[0], kept[1] + got[1]]
            losses[d] = other
        losses[0] = loss
        ordered = jnp.stack(losses)
        loss = functools.reduce(jnp.add, [at(ordered, pos ^ i) for i in range(size)])
        terms = kept
    piece = jnp.stack(terms).astype(BF16)
    pieces = {0: piece}
    for group in reversed(groups):
        stack = jnp.stack([pieces[j] for j in sorted(pieces)])
        keys = sorted(pieces)
        new = dict(pieces)
        for d in range(1, 1 << len(group)):
            got = xor_permute(stack, "pix", d * group[0])
            for i, j in enumerate(keys):
                new[j ^ (d * group[0])] = got[i]
        pieces = new
    grad_w_value, grad_w_out = call(
        functools.partial(finish_body, n_pix, dsh),
        [((dsh, inner), F32), ((inner, dsh), F32)],
        [("v", pieces[j]) for j in range(n_pix)],
        10**6,
        "finish",
        scratch=[pltpu.VMEM((2, dsh * inner // LANES, LANES), F32)],
    )
    loss = loss / (n_ens * n_pix * TILE * n_out)
    return (loss, grad_w_out, grad_w_value)


def solution(mesh):
    in_specs = (
        P("ens", "pix", None),
        P(),
        P("ens", None),
        P("ens", None),
        P("ens", None),
        P(None, "ens"),
        P(),
        P("pix", None),
        P("pix"),
        P(),
        P("pix", None),
        P("pix", None),
    )
    out_specs = (P(), P(None, "ens"), P("ens", None))
    return jax.shard_map(
        per_device, mesh=mesh, in_specs=in_specs, out_specs=out_specs, check_vma=False
    )
```

time: 241 us -> 119 us (0.49)
  waiting for transfers between devices: 116 us -> 43.5 us
  blocking collectives: 45.2 us -> 0 us
  matrix products: 19.3 us -> 0 us
  starting transfers between devices: 10.8 us -> 29.5 us
  other arithmetic: 14.7 us -> 1.21 us
  between operations: 16.3 us -> 28 us
  local copies, waits for them, and re-layouts: 17.7 us -> 7.42 us
  Pallas kernels: 0 us -> 8.98 us
    all_gather x4 -> x0, waiting for transfers between devices: 43 us -> none  [the longest x1 16.6 us: per_device(): lax.all_gather(w_value, 'ens', axis=0, tiled=True)]
    ppermute x4 -> x32, waiting for transfers between devices: 3.08 us -> 43.5 us  [the longest x30 35.4 us: xor_permute(): return lax.ppermute(value, axis, [(i, i ^ mask) for i in range(size)])]
    psum x1 -> x0, blocking collectives: 39.8 us -> none  [per_device(): lax.psum(loss_partial_sum, ('ens', 'pix'))]
    psum x1 -> x0, waiting for transfers between devices: 35.1 us -> none  [per_device(): summed = lax.psum(owned_rows, 'pix').astype(jnp.float32)]
    reduce_scatter x1 -> x0, waiting for transfers between devices: 31.9 us -> none  [per_device(): lax.psum_scatter(jnp.concatenate([value_term, output_term], axis=1).astyp...]
    ppermute x4 -> x32, starting transfers between devices: 10.5 us -> 29.5 us  [the longest x30 23.2 us: xor_permute(): return lax.ppermute(value, axis, [(i, i ^ mask) for i in range(size)])]
    dot_general x10 -> x0, matrix products: 13.5 us -> none  [the longest x3 4.83 us: per_device(): jnp.dot(columns, shard_piece, preferred_element_type=jnp.float32)]
    reshape x4 -> x2, local copies, waits for them, and re-layouts: 12.9 us -> 0.05 us  [part_of(): lax.dynamic_index_in_dim(split, index, 1, keepdims=False).reshape(-1, LANES)]
  transfers between devices with their start and end apart: 10 -> 32, of which waited for: 7 -> 15; matrix products, arithmetic and copies ran while one was open for 12% -> 4% of each run, Pallas kernels for 0% -> 6%
where the time goes in v1:
time: 119 us
  waiting for transfers between devices  43.5 us (37%)
  starting transfers between devices  29.5 us (25%)
  between operations  28 us (24%)
  Pallas kernels  8.98 us (8%)
  local copies, waits for them, and re-layouts  7.42 us (6%)
  other arithmetic  1.21 us (1%)
    ppermute x30, waiting for transfers between devices, xor_permute(): return lax.ppermute(value, axis, [(i, i ^ mask) for i in range(size)])  35.4 us
    ppermute x30, starting transfers between devices, xor_permute(): return lax.ppermute(value, axis, [(i, i ^ mask) for i in range(size)])  23.2 us
    pallas_call x8, Pallas kernels, call(): pl.pallas_call(body, out_shape=[jax.ShapeDtypeStruct(s, d) for s, d in ou...  8.98 us
    ppermute x1, waiting for transfers between devices, per_device(): lax.ppermute(sample_layer_feed, 'pix', [(i, i + 1) for i in range(n_pix -...  8.07 us
    ppermute x1, starting transfers between devices, per_device(): lax.ppermute(sample_layer_feed, 'pix', [(i, i + 1) for i in range(n_pix -...  5.02 us
    slice x5, local copies, waits for them, and re-layouts, from_parts(): return parts[0] + parts[1] + parts[2]  2.97 us
    unnamed x31, local copies, waits for them, and re-layouts  2.46 us
  transfers between devices with their start and end apart: 32, of which 15 were waited for; matrix products, arithmetic and copies ran while one was open for 4% of the time, Pallas kernels for 6%

profile of v1, /device:TPU:0, one launch (start us, length us, event | category | flops | bytes accessed | tf_op | source)
XLA Modules:
  0.0 118.6 jit_solution(1273103815713949146)
XLA Ops:
  0.6 5.0 %collective-permute-start = (bf16[1,128,1024]{2,1,0:T(8,128)(2,1)}, bf16[1,128,1024]{2,1,0:T(8,128)(2,1)S(1)}, u32[]{:S(2)}, u32[]{:S(2)}) collective-permute-start(bf16[1,128,1024]{2,1,0:T(8,128)(2,1)} %x_ref.3), channel_id=1, source_target_pairs={{0,1},{1,2},{2,3},{3,4},{4,5},{5,6},{6,7},{8,9},{9,10},{10,11},{11... | collective-permute-start | bytes 786440 | tf_op jit(solution)/shard_map/ppermute | solution.py:275
  5.7 1.3 %collective-permute-start.1 = (bf16[1,128,1024]{2,1,0:T(8,128)(2,1)}, bf16[1,128,1024]{2,1,0:T(8,128)(2,1)S(1)}, u32[]{:S(2)}, u32[]{:S(2)}) collective-permute-start(bf16[1,128,1024]{2,1,0:T(8,128)(2,1)} %x_ref.3), channel_id=1, source_target_pairs={{1,0},{2,1},{3,2},{4,3},{5,4},{6,5},{7,6},{9,8},{10,9},{11,10},{12... | collective-permute-start | bytes 786440 | tf_op jit(solution)/shard_map/ppermute | solution.py:276
  7.0 1.6 %collective-permute-start.9 = (bf16[256,512]{1,0:T(8,128)(2,1)}, bf16[256,512]{1,0:T(8,128)(2,1)S(1)}, u32[]{:S(2)}, u32[]{:S(2)}) collective-permute-start(bf16[256,512]{1,0:T(8,128)(2,1)} %refs_4_.1), channel_id=1, source_target_pairs={{0,16},{8,24},{16,0},{24,8},{1,17},{9,25},{17,1},{25,9},{2,18},{10... | collective-permute-start | bytes 786440 | tf_op jit(solution)/shard_map/ppermute | solution.py:48
  8.5 0.5 collective-permute-start.6
  9.1 8.1 %collective-permute-done.up_ref = bf16[1,128,1024]{2,1,0:T(8,128)(2,1)S(1)} collective-permute-done((bf16[1,128,1024]{2,1,0:T(8,128)(2,1)}, bf16[1,128,1024]{2,1,0:T(8,128)(2,1)S(1)}, u32[]{:S(2)}, u32[]{:S(2)}) %collective-permute-start) | collective-permute-done | bytes 262176 | tf_op jit(solution)/shard_map/ppermute | solution.py:275
  17.1 1.5 %collective-permute-start.3 = (bf16[256,512]{1,0:T(8,128)(2,1)}, bf16[256,512]{1,0:T(8,128)(2,1)S(1)}, u32[]{:S(2)}, u32[]{:S(2)}) collective-permute-start(bf16[256,512]{1,0:T(8,128)(2,1)} %refs_0_.3), channel_id=1, source_target_pairs={{0,16},{8,24},{16,0},{24,8},{1,17},{9,25},{17,1},{25,9},{2,18},{10... | collective-permute-start | bytes 786440 | tf_op jit(solution)/shard_map/ppermute | solution.py:48
  18.6 1.1 copy.15
  19.8 0.6 collective-permute-start.12
  20.4 0.4 collective-permute-done.6.refs_2_
  20.7 0.5 collective-permute-start.7
  21.3 0.1 collective-permute-start.2
  21.3 5.2 %collective-permute-done.3.refs_2_ = bf16[256,512]{1,0:T(8,128)(2,1)S(1)} collective-permute-done((bf16[256,512]{1,0:T(8,128)(2,1)}, bf16[256,512]{1,0:T(8,128)(2,1)S(1)}, u32[]{:S(2)}, u32[]{:S(2)}) %collective-permute-start.3) | collective-permute-done | bytes 262176 | tf_op jit(solution)/shard_map/ppermute | solution.py:48
  26.6 0.6 normed.1
  27.2 4.7 %collective-permute-done.12.refs_2_.refs_6_ = bf16[256,512]{1,0:T(8,128)(2,1)S(1)} collective-permute-done((bf16[256,512]{1,0:T(8,128)(2,1)S(1)}, bf16[256,512]{1,0:T(8,128)(2,1)S(1)}, u32[]{:S(2)}, u32[]{:S(2)}) %collective-permute-start.12) | collective-permute-done | bytes 262176 | tf_op jit(solution)/shard_map/ppermute | solution.py:48
  31.9 0.5 collective-permute-start.13
  32.4 0.6 copy-done.10
  33.1 2.2 %weights.1.refs_4_.refs_12_ = bf16[8,128,384]{2,1,0:T(8,128)(2,1)S(1)} custom-call(bf16[384,1024]{1,0:T(8,128)(2,1)S(1)} %get-tuple-element.11.n_ref, bf16[256,512]{1,0:T(8,128)(2,1)S(1)} %copy-done.2, bf16[256,512]{1,0:T(8,128)(2,1)S(1)} %collective-permute-done.5.refs_1_, bf16[256,512]{1,0:T(8,128)(2,1)S(1)} %collective-permute-done.6.refs_2_, ...), custom_call_target="tpu_custom_call" | custom-call | flops 2000000000 | bytes 1048576 | tf_op jit(solution)/shard_map/weights/pallas_call | solution.py:34
  35.3 1.5 %attend.1.att_ref.refs_0_ = bf16[128,512]{1,0:T(8,128)(2,1)S(1)} custom-call(bf16[384,1024]{1,0:T(8,128)(2,1)S(1)} %get-tuple-element.11.n_ref, bf16[256,512]{1,0:T(8,128)(2,1)S(1)} %copy-done.4, bf16[256,512]{1,0:T(8,128)(2,1)S(1)} %collective-permute-done.2.refs_1_, bf16[256,512]{1,0:T(8,128)(2,1)S(1)} %collective-permute-done.3.refs_2_, ...), custom_call_target="tpu_custom_call" | custom-call | flops 1000000000 | bytes 1048576 | tf_op jit(solution)/shard_map/attend/pallas_call | solution.py:34
  36.9 0.7 forecast.1.refs_0_
  37.6 1.6 %collective-permute-start.15 = (bf16[128,128]{1,0:T(8,128)(2,1)S(1)}, bf16[128,128]{1,0:T(8,128)(2,1)S(1)}, u32[]{:S(2)}, u32[]{:S(2)}) collective-permute-start(bf16[128,128]{1,0:T(8,128)(2,1)S(1)} %forecast.1.refs_0_), channel_id=1, source_target_pairs={{0,16},{8,24},{16,0},{24,8},{1,17},{9,25},{17,1},{25,9},{2,18},{10... | collective-permute-start | bytes 98312 | tf_op jit(solution)/shard_map/ppermute | solution.py:48
  39.2 2.4 %collective-permute-done.15.refs_2_ = bf16[128,128]{1,0:T(8,128)(2,1)S(1)} collective-permute-done((bf16[128,128]{1,0:T(8,128)(2,1)S(1)}, bf16[128,128]{1,0:T(8,128)(2,1)S(1)}, u32[]{:S(2)}, u32[]{:S(2)}) %collective-permute-start.15) | collective-permute-done | bytes 32800 | tf_op jit(solution)/shard_map/ppermute | solution.py:48
  41.6 0.5 collective-permute-start.18
  42.1 0.7 collective-permute-done.16.refs_3_
  42.8 1.6 %backward.1 = (bf16[512,128]{1,0:T(8,128)(2,1)S(1)}, bf16[384,512]{1,0:T(8,128)(2,1)S(1)}, f32[8,128]{1,0:T(8,128)S(1)}) custom-call(bf16[128,128]{1,0:T(8,128)(2,1)S(1)} %forecast.1.refs_0_, bf16[128,128]{1,0:T(8,128)(2,1)S(1)} %collective-permute-done.14.refs_1_, bf16[128,128]{1,0:T(8,128)(2,1)S(1)} %collective-permute-done.15.refs_2_, ...), custom_call_target="tpu_custom_call" | custom-call | flops 1000000000 | bytes 1048576 | tf_op jit(solution)/shard_map/backward/pallas_call | solution.py:34
  44.4 0.6 copy-done.13
  45.1 0.2 collective-permute-start.19
  45.3 1.5 %collective-permute-start.22 = (bf16[128,512]{1,0:T(8,128)(2,1)S(1)}, bf16[128,512]{1,0:T(8,128)(2,1)S(1)}, u32[]{:S(2)}, u32[]{:S(2)}) collective-permute-start(bf16[128,512]{1,0:T(8,128)(2,1)S(1)} %copy-done.7), channel_id=1, source_target_pairs={{0,16},{8,24},{16,0},{24,8},{1,17},{9,25},{17,1},{25,9},{2,18},{10... | collective-permute-start | bytes 393224 | tf_op jit(solution)/shard_map/ppermute | solution.py:48
  46.8 0.5 slice.137
  47.3 1.2 collective-permute-done.17
  53.5 0.1 select_maximum_fusion.4
  53.6 0.7 value_term.1
  54.3 0.2 pad_maximum_fusion
  54.5 0.6 collective-permute-start.20
  55.1 0.5 collective-permute-start.23
  55.6 0.8 collective-permute-done.21.refs_1_
  56.5 0.2 collective-permute-done.23.refs_3_
  56.7 0.4 output_term.1
  57.1 6.0 %collective-permute-done.20 = bf16[1040,128]{1,0:T(8,128)(2,1)S(1)} collective-permute-done((bf16[1040,128]{1,0:T(8,128)(2,1)S(1)}, bf16[1040,128]{1,0:T(8,128)(2,1)S(1)}, u32[]{:S(2)}, u32[]{:S(2)}) %collective-permute-start.20) | collective-permute-done | bytes 266272 | tf_op jit(solution)/shard_map/ppermute | solution.py:48
  63.1 0.6 fusion.14
  69.3 0.1 select_maximum_fusion.2
  69.5 0.2 maximum_maximum_fusion
  69.7 2.4 %collective-permute-start.24 = (bf16[1040,128]{1,0:T(8,128)(2,1)S(1)}, bf16[1040,128]{1,0:T(8,128)(2,1)S(1)}, u32[]{:S(2)}, u32[]{:S(2)}) collective-permute-start(bf16[1040,128]{1,0:T(8,128)(2,1)S(1)} %maximum_maximum_fusion), channel_id=1, source_target_pairs={{0,1},{1,0},{2,3},{3,2},{4,5},{5,4},{6,7},{7,6},{8,9},{9,8},{10,11... | collective-permute-start | bytes 798728 | tf_op jit(solution)/shard_map/ppermute | solution.py:48
  72.2 6.0 %collective-permute-done.24 = bf16[1040,128]{1,0:T(8,128)(2,1)S(1)} collective-permute-done((bf16[1040,128]{1,0:T(8,128)(2,1)S(1)}, bf16[1040,128]{1,0:T(8,128)(2,1)S(1)}, u32[]{:S(2)}, u32[]{:S(2)}) %collective-permute-start.24) | collective-permute-done | bytes 266272 | tf_op jit(solution)/shard_map/ppermute | solution.py:48
  78.1 0.6 fusion.13
  80.7 0.1 pad_maximum_fusion.4
  80.8 0.6 fusion.16
  86.3 0.1 select_maximum_fusion
  86.6 0.1 maximum_maximum_fusion.1
  86.8 4.8 %collective-permute-start.27 = (bf16[272,128]{1,0:T(8,128)(2,1)S(1)}, bf16[272,128]{1,0:T(8,128)(2,1)S(1)}, u32[]{:S(2)}, u32[]{:S(2)}) collective-permute-start(bf16[272,128]{1,0:T(8,128)(2,1)S(1)} %get-tuple-element.50), channel_id=1, source_target_pairs={{0,6},{1,7},{2,4},{3,5},{4,2},{5,3},{6,0},{7,1},{8,14},{9,15},{10,... | collective-permute-start | bytes 208904 | tf_op jit(solution)/shard_map/ppermute | solution.py:48
  91.5 0.6 collective-permute-start.25
  92.2 1.6 %collective-permute-done.27 = bf16[272,128]{1,0:T(8,128)(2,1)S(1)} collective-permute-done((bf16[272,128]{1,0:T(8,128)(2,1)S(1)}, bf16[272,128]{1,0:T(8,128)(2,1)S(1)}, u32[]{:S(2)}, u32[]{:S(2)}) %collective-permute-start.27) | collective-permute-done | bytes 69664 | tf_op jit(solution)/shard_map/ppermute | solution.py:48
  93.9 2.9 %collective-permute-done.26 = bf16[272,128]{1,0:T(8,128)(2,1)S(1)} collective-permute-done((bf16[272,128]{1,0:T(8,128)(2,1)S(1)}, bf16[272,128]{1,0:T(8,128)(2,1)S(1)}, u32[]{:S(2)}, u32[]{:S(2)}) %collective-permute-start.26) | collective-permute-done | bytes 69664 | tf_op jit(solution)/shard_map/ppermute | solution.py:48
  96.8 0.7 collective-permute-start.28
  97.5 2.2 %collective-permute-start.29 = (bf16[1,2,128,128]{3,2,1,0:T(8,128)(2,1)S(1)}, bf16[1,2,128,128]{3,2,1,0:T(8,128)(2,1)S(1)}, u32[]{:S(2)}, u32[]{:S(2)}) collective-permute-start(bf16[1,2,128,128]{3,2,1,0:T(8,128)(2,1)S(1)} %pad_maximum_fusion.3), channel_id=1, source_target_pairs={{0,4},{1,5},{2,6},{3,7},{4,0},{5,1},{6,2},{7,3},{8,12},{9,13},{10,... | collective-permute-start | bytes 196616 | tf_op jit(solution)/shard_map/ppermute | solution.py:48
  99.7 1.6 %collective-permute-start.30 = (bf16[1,2,128,128]{3,2,1,0:T(8,128)(2,1)S(1)}, bf16[1,2,128,128]{3,2,1,0:T(8,128)(2,1)S(1)}, u32[]{:S(2)}, u32[]{:S(2)}) collective-permute-start(bf16[1,2,128,128]{3,2,1,0:T(8,128)(2,1)S(1)} %pad_maximum_fusion.3), channel_id=1, source_target_pairs={{0,6},{1,7},{2,4},{3,5},{4,2},{5,3},{6,0},{7,1},{8,14},{9,15},{10,... | collective-permute-start | bytes 196616 | tf_op jit(solution)/shard_map/ppermute | solution.py:48
  101.3 0.6 fusion.10
  101.9 0.6 fusion.11
  102.5 1.3 %collective-permute-done.29 = bf16[1,2,128,128]{3,2,1,0:T(8,128)(2,1)S(1)} collective-permute-done((bf16[1,2,128,128]{3,2,1,0:T(8,128)(2,1)S(1)}, bf16[1,2,128,128]{3,2,1,0:T(8,128)(2,1)S(1)}, u32[]{:S(2)}, u32[]{:S(2)}) %collective-permute-start.29) | collective-permute-done | bytes 65568 | tf_op jit(solution)/shard_map/ppermute | solution.py:48
  103.7 2.0 %collective-permute-done.30 = bf16[1,2,128,128]{3,2,1,0:T(8,128)(2,1)S(1)} collective-permute-done((bf16[1,2,128,128]{3,2,1,0:T(8,128)(2,1)S(1)}, bf16[1,2,128,128]{3,2,1,0:T(8,128)(2,1)S(1)}, u32[]{:S(2)}, u32[]{:S(2)}) %collective-permute-start.30) | collective-permute-done | bytes 65568 | tf_op jit(solution)/shard_map/ppermute | solution.py:48
  105.8 0.7 collective-permute-start.31
  106.5 0.6 fusion.12
  112.8 0.1 pad_maximum_fusion.5
  112.9 0.7 fusion.15
  116.2 1.2 %finish.1 = (f32[256,512]{1,0:T(8,128)}, f32[512,256]{1,0:T(8,128)}) custom-call(bf16[2,128,128]{2,1,0:T(8,128)(2,1)S(1)} %pad_maximum_fusion.2.refs_0_, bf16[2,128,128]{2,1,0:T(8,128)(2,1)S(1)} %get-tuple-element.26.refs_1_, bf16[2,128,128]{2,1,0:T(8,128)(2,1)S(1)} %bitcast.77, bf16[2,128,128]{2,1,0:T(8,128)(2,1)S(1)} %get-tuple-element.25.refs_3_, ...), custom_call_target="tpu_custom_call" | custom-call | flops 1000000 | bytes 1048576 | tf_op jit(solution)/shard_map/finish/pallas_call | solution.py:34
  (80 shorter events, 0.8 us)
Async XLA Ops:
  0.6 25.9 %copy-start = (bf16[1,128,1024]{2,1,0:T(8,128)(2,1)S(1)}, bf16[1,128,1024]{2,1,0:T(8,128)(2,1)}, u32[]{:S(2)}) copy-start(bf16[1,128,1024]{2,1,0:T(8,128)(2,1)} %x_ref.3) | copy-start | bytes 786436
  0.6 16.5 %collective-permute-start = (bf16[1,128,1024]{2,1,0:T(8,128)(2,1)}, bf16[1,128,1024]{2,1,0:T(8,128)(2,1)S(1)}, u32[]{:S(2)}, u32[]{:S(2)}) collective-permute-start(bf16[1,128,1024]{2,1,0:T(8,128)(2,1)} %x_ref.3), channel_id=1, source_target_pairs={{0,1},{1,2},{2,3},{3,4},{4,5},{5,6},{6,7},{8,9},{9,10},{10,11},{11... | collective-permute-start | bytes 786440 | tf_op jit(solution)/shard_map/ppermute | solution.py:275
  5.7 11.5 %collective-permute-start.1 = (bf16[1,128,1024]{2,1,0:T(8,128)(2,1)}, bf16[1,128,1024]{2,1,0:T(8,128)(2,1)S(1)}, u32[]{:S(2)}, u32[]{:S(2)}) collective-permute-start(bf16[1,128,1024]{2,1,0:T(8,128)(2,1)} %x_ref.3), channel_id=1, source_target_pairs={{1,0},{2,1},{3,2},{4,3},{5,4},{6,5},{7,6},{9,8},{10,9},{11,10},{12... | collective-permute-start | bytes 786440 | tf_op jit(solution)/shard_map/ppermute | solution.py:276
  7.0 12.8 %collective-permute-start.9 = (bf16[256,512]{1,0:T(8,128)(2,1)}, bf16[256,512]{1,0:T(8,128)(2,1)S(1)}, u32[]{:S(2)}, u32[]{:S(2)}) collective-permute-start(bf16[256,512]{1,0:T(8,128)(2,1)} %refs_4_.1), channel_id=1, source_target_pairs={{0,16},{8,24},{16,0},{24,8},{1,17},{9,25},{17,1},{25,9},{2,18},{10... | collective-permute-start | bytes 786440 | tf_op jit(solution)/shard_map/ppermute | solution.py:48
  8.5 12.2 %collective-permute-start.6 = (bf16[256,512]{1,0:T(8,128)(2,1)}, bf16[256,512]{1,0:T(8,128)(2,1)S(1)}, u32[]{:S(2)}, u32[]{:S(2)}) collective-permute-start(bf16[256,512]{1,0:T(8,128)(2,1)} %refs_0_.2), channel_id=1, source_target_pairs={{0,16},{8,24},{16,0},{24,8},{1,17},{9,25},{17,1},{25,9},{2,18},{10... | collective-permute-start | bytes 786440 | tf_op jit(solution)/shard_map/ppermute | solution.py:48
  9.1 11.7 %collective-permute-start.5 = (bf16[256,512]{1,0:T(8,128)(2,1)}, bf16[256,512]{1,0:T(8,128)(2,1)S(1)}, u32[]{:S(2)}, u32[]{:S(2)}) collective-permute-start(bf16[256,512]{1,0:T(8,128)(2,1)} %refs_0_.2), channel_id=1, source_target_pairs={{0,8},{8,0},{16,24},{24,16},{1,9},{9,1},{17,25},{25,17},{2,10},{10... | collective-permute-start | bytes 786440 | tf_op jit(solution)/shard_map/ppermute | solution.py:48
  17.1 4.1 %collective-permute-start.8 = (bf16[256,512]{1,0:T(8,128)(2,1)}, bf16[256,512]{1,0:T(8,128)(2,1)S(1)}, u32[]{:S(2)}, u32[]{:S(2)}) collective-permute-start(bf16[256,512]{1,0:T(8,128)(2,1)} %refs_4_.1), channel_id=1, source_target_pairs={{0,8},{8,0},{16,24},{24,16},{1,9},{9,1},{17,25},{25,17},{2,10},{10... | collective-permute-start | bytes 786440 | tf_op jit(solution)/shard_map/ppermute | solution.py:48
  17.1 9.4 %collective-permute-start.3 = (bf16[256,512]{1,0:T(8,128)(2,1)}, bf16[256,512]{1,0:T(8,128)(2,1)S(1)}, u32[]{:S(2)}, u32[]{:S(2)}) collective-permute-start(bf16[256,512]{1,0:T(8,128)(2,1)} %refs_0_.3), channel_id=1, source_target_pairs={{0,16},{8,24},{16,0},{24,8},{1,17},{9,25},{17,1},{25,9},{2,18},{10... | collective-permute-start | bytes 786440 | tf_op jit(solution)/shard_map/ppermute | solution.py:48
  18.6 7.9 %copy-start.1 = (f32[1024]{0:T(1024)S(1)}, f32[1024]{0:T(1024)}, u32[]{:S(2)}) copy-start(f32[1024]{0:T(1024)} %param.13) | copy-start | bytes 12292
  19.8 12.1 %collective-permute-start.12 = (bf16[256,512]{1,0:T(8,128)(2,1)S(1)}, bf16[256,512]{1,0:T(8,128)(2,1)S(1)}, u32[]{:S(2)}, u32[]{:S(2)}) collective-permute-start(bf16[256,512]{1,0:T(8,128)(2,1)S(1)} %bitcast.73), channel_id=1, source_target_pairs={{0,16},{8,24},{16,0},{24,8},{1,17},{9,25},{17,1},{25,9},{2,18},{10... | collective-permute-start | bytes 786440 | tf_op jit(solution)/shard_map/ppermute | solution.py:48
  20.7 11.1 %collective-permute-start.10 = (bf16[256,512]{1,0:T(8,128)(2,1)S(1)}, bf16[256,512]{1,0:T(8,128)(2,1)S(1)}, u32[]{:S(2)}, u32[]{:S(2)}) collective-permute-start(bf16[256,512]{1,0:T(8,128)(2,1)S(1)} %collective-permute-done.9.refs_6_), channel_id=1, source_target_pairs={{0,8},{8,0},{16,24},{24,16},{1,9},{9,1},{17,25},{25,17},{2,10},{10... | collective-permute-start | bytes 786440 | tf_op jit(solution)/shard_map/ppermute | solution.py:48
  20.7 11.6 %collective-permute-start.7 = (bf16[256,512]{1,0:T(8,128)(2,1)S(1)}, bf16[256,512]{1,0:T(8,128)(2,1)S(1)}, u32[]{:S(2)}, u32[]{:S(2)}) collective-permute-start(bf16[256,512]{1,0:T(8,128)(2,1)S(1)} %collective-permute-done.6.refs_2_), channel_id=1, source_target_pairs={{0,8},{8,0},{16,24},{24,16},{1,9},{9,1},{17,25},{25,17},{2,10},{10... | collective-permute-start | bytes 786440 | tf_op jit(solution)/shard_map/ppermute | solution.py:48
  21.3 14.0 %collective-permute-start.2 = (bf16[256,512]{1,0:T(8,128)(2,1)}, bf16[256,512]{1,0:T(8,128)(2,1)S(1)}, u32[]{:S(2)}, u32[]{:S(2)}) collective-permute-start(bf16[256,512]{1,0:T(8,128)(2,1)} %refs_0_.3), channel_id=1, source_target_pairs={{0,8},{8,0},{16,24},{24,16},{1,9},{9,1},{17,25},{25,17},{2,10},{10... | collective-permute-start | bytes 786440 | tf_op jit(solution)/shard_map/ppermute | solution.py:48
  26.5 8.8 %collective-permute-start.4 = (bf16[256,512]{1,0:T(8,128)(2,1)S(1)}, bf16[256,512]{1,0:T(8,128)(2,1)S(1)}, u32[]{:S(2)}, u32[]{:S(2)}) collective-permute-start(bf16[256,512]{1,0:T(8,128)(2,1)S(1)} %collective-permute-done.3.refs_2_), channel_id=1, source_target_pairs={{0,8},{8,0},{16,24},{24,16},{1,9},{9,1},{17,25},{25,17},{2,10},{10... | collective-permute-start | bytes 786440 | tf_op jit(solution)/shard_map/ppermute | solution.py:48
  26.5 5.8 %copy-start.2 = (bf16[256,512]{1,0:T(8,128)(2,1)S(1)}, bf16[256,512]{1,0:T(8,128)(2,1)}, u32[]{:S(2)}) copy-start(bf16[256,512]{1,0:T(8,128)(2,1)} %refs_0_.2) | copy-start | bytes 786436
  26.6 5.8 %copy-start.3 = (bf16[256,512]{1,0:T(8,128)(2,1)S(1)}, bf16[256,512]{1,0:T(8,128)(2,1)}, u32[]{:S(2)}) copy-start(bf16[256,512]{1,0:T(8,128)(2,1)} %refs_4_.1) | copy-start | bytes 786436
  26.6 5.8 %copy-start.9 = (s32[1024]{0:T(1024)S(1)}, s32[1024]{0:T(1024)}, u32[]{:S(2)}) copy-start(s32[1024]{0:T(1024)} %param.21) | copy-start | bytes 12292
  31.9 5.0 %collective-permute-start.11 = (bf16[256,512]{1,0:T(8,128)(2,1)S(1)}, bf16[256,512]{1,0:T(8,128)(2,1)S(1)}, u32[]{:S(2)}, u32[]{:S(2)}) collective-permute-start(bf16[256,512]{1,0:T(8,128)(2,1)S(1)} %bitcast.74), channel_id=1, source_target_pairs={{0,8},{8,0},{16,24},{24,16},{1,9},{9,1},{17,25},{25,17},{2,10},{10... | collective-permute-start | bytes 786440 | tf_op jit(solution)/shard_map/ppermute | solution.py:48
  31.9 5.0 %collective-permute-start.13 = (bf16[256,512]{1,0:T(8,128)(2,1)S(1)}, bf16[256,512]{1,0:T(8,128)(2,1)S(1)}, u32[]{:S(2)}, u32[]{:S(2)}) collective-permute-start(bf16[256,512]{1,0:T(8,128)(2,1)S(1)} %collective-permute-done.12.refs_2_.refs_6_), channel_id=1, source_target_pairs={{0,8},{8,0},{16,24},{24,16},{1,9},{9,1},{17,25},{25,17},{2,10},{10... | collective-permute-start | bytes 786440 | tf_op jit(solution)/shard_map/ppermute | solution.py:48
  32.4 0.7 copy-start.10
  32.4 0.7 copy-start.11
  33.1 2.3 %copy-start.4 = (bf16[256,512]{1,0:T(8,128)(2,1)S(1)}, bf16[256,512]{1,0:T(8,128)(2,1)}, u32[]{:S(2)}) copy-start(bf16[256,512]{1,0:T(8,128)(2,1)} %refs_0_.3) | copy-start | bytes 786436
  35.3 1.6 %copy-start.5 = (bf16[1024,128]{1,0:T(8,128)(2,1)S(1)}, bf16[1024,128]{1,0:T(8,128)(2,1)}, u32[]{:S(2)}) copy-start(bf16[1024,128]{1,0:T(8,128)(2,1)} %read_ref.3) | copy-start | bytes 786436
  36.9 0.7 copy-start.6
  36.9 5.9 %copy-start.8 = (f32[128,128]{1,0:T(8,128)S(1)}, f32[128,128]{1,0:T(8,128)}, u32[]{:S(2)}) copy-start(f32[128,128]{1,0:T(8,128)} %refs_8_.1) | copy-start | bytes 196612
  37.6 4.0 %collective-permute-start.15 = (bf16[128,128]{1,0:T(8,128)(2,1)S(1)}, bf16[128,128]{1,0:T(8,128)(2,1)S(1)}, u32[]{:S(2)}, u32[]{:S(2)}) collective-permute-start(bf16[128,128]{1,0:T(8,128)(2,1)S(1)} %forecast.1.refs_0_), channel_id=1, source_target_pairs={{0,16},{8,24},{16,0},{24,8},{1,17},{9,25},{17,1},{25,9},{2,18},{10... | collective-permute-start | bytes 98312 | tf_op jit(solution)/shard_map/ppermute | solution.py:48
  39.2 2.9 %collective-permute-start.14 = (bf16[128,128]{1,0:T(8,128)(2,1)S(1)}, bf16[128,128]{1,0:T(8,128)(2,1)S(1)}, u32[]{:S(2)}, u32[]{:S(2)}) collective-permute-start(bf16[128,128]{1,0:T(8,128)(2,1)S(1)} %forecast.1.refs_0_), channel_id=1, source_target_pairs={{0,8},{8,0},{16,24},{24,16},{1,9},{9,1},{17,25},{25,17},{2,10},{10... | collective-permute-start | bytes 98312 | tf_op jit(solution)/shard_map/ppermute | solution.py:48
  41.6 1.2 %collective-permute-start.16 = (bf16[128,128]{1,0:T(8,128)(2,1)S(1)}, bf16[128,128]{1,0:T(8,128)(2,1)S(1)}, u32[]{:S(2)}, u32[]{:S(2)}) collective-permute-start(bf16[128,128]{1,0:T(8,128)(2,1)S(1)} %collective-permute-done.15.refs_2_), channel_id=1, source_target_pairs={{0,8},{8,0},{16,24},{24,16},{1,9},{9,1},{17,25},{25,17},{2,10},{10... | collective-permute-start | bytes 98312 | tf_op jit(solution)/shard_map/ppermute | solution.py:48
  41.6 1.2 %copy-start.12 = (f32[128]{0:T(128)S(1)}, f32[128]{0:T(128)}, u32[]{:S(2)}) copy-start(f32[128]{0:T(128)} %param.20) | copy-start | bytes 1540
  41.6 12.0 %collective-permute-start.18 = (bf16[512,384]{1,0:T(8,128)(2,1)S(1)}, bf16[512,384]{1,0:T(8,128)(2,1)S(1)}, u32[]{:S(2)}, u32[]{:S(2)}) collective-permute-start(bf16[512,384]{1,0:T(8,128)(2,1)S(1)} %get-tuple-element.14), channel_id=1, source_target_pairs={{0,8},{8,0},{16,24},{24,16},{1,9},{9,1},{17,25},{25,17},{2,10},{10... | collective-permute-start | bytes 1179656 | tf_op jit(solution)/shard_map/ppermute | solution.py:48
  42.8 2.5 %copy-start.7 = (bf16[128,512]{1,0:T(8,128)(2,1)S(1)}, bf16[128,512]{1,0:T(8,128)(2,1)}, u32[]{:S(2)}) copy-start(bf16[128,512]{1,0:T(8,128)(2,1)} %copy-done.6) | copy-start | bytes 393220
  44.4 0.7 copy-start.13
  45.1 8.5 %collective-permute-start.19 = (bf16[384,512]{1,0:T(8,128)(2,1)S(1)}, bf16[384,512]{1,0:T(8,128)(2,1)S(1)}, u32[]{:S(2)}, u32[]{:S(2)}) collective-permute-start(bf16[384,512]{1,0:T(8,128)(2,1)S(1)} %get-tuple-element.15.own_con), channel_id=1, source_target_pairs={{0,8},{8,0},{16,24},{24,16},{1,9},{9,1},{17,25},{25,17},{2,10},{10... | collective-permute-start | bytes 1179656 | tf_op jit(solution)/shard_map/ppermute | solution.py:48
  45.3 9.9 %collective-permute-start.22 = (bf16[128,512]{1,0:T(8,128)(2,1)S(1)}, bf16[128,512]{1,0:T(8,128)(2,1)S(1)}, u32[]{:S(2)}, u32[]{:S(2)}) collective-permute-start(bf16[128,512]{1,0:T(8,128)(2,1)S(1)} %copy-done.7), channel_id=1, source_target_pairs={{0,16},{8,24},{16,0},{24,8},{1,17},{9,25},{17,1},{25,9},{2,18},{10... | collective-permute-start | bytes 393224 | tf_op jit(solution)/shard_map/ppermute | solution.py:48
  47.3 1.2 %collective-permute-start.17 = (f32[1,1]{1,0:T(1,128)}, f32[1,1]{1,0:T(1,128)}, u32[]{:S(2)}, u32[]{:S(2)}) collective-permute-start(f32[1,1]{1,0:T(1,128)} %slice.137), channel_id=1, source_target_pairs={{0,8},{8,0},{16,24},{24,16},{1,9},{9,1},{17,25},{25,17},{2,10},{10... | collective-permute-start | bytes 20 | tf_op jit(solution)/shard_map/ppermute | solution.py:48
  54.3 2.4 %copy-start.14 = (bf16[512,128]{1,0:T(8,128)(2,1)S(1)}, bf16[512,128]{1,0:T(8,128)(2,1)}, u32[]{:S(2)}) copy-start(bf16[512,128]{1,0:T(8,128)(2,1)} %copy-done.13) | copy-start | bytes 393220
  54.5 8.6 %collective-permute-start.20 = (bf16[1040,128]{1,0:T(8,128)(2,1)S(1)}, bf16[1040,128]{1,0:T(8,128)(2,1)S(1)}, u32[]{:S(2)}, u32[]{:S(2)}) collective-permute-start(bf16[1040,128]{1,0:T(8,128)(2,1)S(1)} %pad_maximum_fusion), channel_id=1, source_target_pairs={{0,16},{8,24},{16,0},{24,8},{1,17},{9,25},{17,1},{25,9},{2,18},{10... | collective-permute-start | bytes 798728 | tf_op jit(solution)/shard_map/ppermute | solution.py:48
  55.1 1.3 %collective-permute-start.21 = (bf16[128,512]{1,0:T(8,128)(2,1)S(1)}, bf16[128,512]{1,0:T(8,128)(2,1)S(1)}, u32[]{:S(2)}, u32[]{:S(2)}) collective-permute-start(bf16[128,512]{1,0:T(8,128)(2,1)S(1)} %copy-done.7), channel_id=1, source_target_pairs={{0,8},{8,0},{16,24},{24,16},{1,9},{9,1},{17,25},{25,17},{2,10},{10... | collective-permute-start | bytes 393224 | tf_op jit(solution)/shard_map/ppermute | solution.py:48
  55.1 1.5 %collective-permute-start.23 = (bf16[128,512]{1,0:T(8,128)(2,1)S(1)}, bf16[128,512]{1,0:T(8,128)(2,1)S(1)}, u32[]{:S(2)}, u32[]{:S(2)}) collective-permute-start(bf16[128,512]{1,0:T(8,128)(2,1)S(1)} %collective-permute-done.22.refs_2_), channel_id=1, source_target_pairs={{0,8},{8,0},{16,24},{24,16},{1,9},{9,1},{17,25},{25,17},{2,10},{10... | collective-permute-start | bytes 393224 | tf_op jit(solution)/shard_map/ppermute | solution.py:48
  69.7 8.4 %collective-permute-start.24 = (bf16[1040,128]{1,0:T(8,128)(2,1)S(1)}, bf16[1040,128]{1,0:T(8,128)(2,1)S(1)}, u32[]{:S(2)}, u32[]{:S(2)}) collective-permute-start(bf16[1040,128]{1,0:T(8,128)(2,1)S(1)} %maximum_maximum_fusion), channel_id=1, source_target_pairs={{0,1},{1,0},{2,3},{3,2},{4,5},{5,4},{6,7},{7,6},{8,9},{9,8},{10,11... | collective-permute-start | bytes 798728 | tf_op jit(solution)/shard_map/ppermute | solution.py:48
  86.8 7.1 %collective-permute-start.27 = (bf16[272,128]{1,0:T(8,128)(2,1)S(1)}, bf16[272,128]{1,0:T(8,128)(2,1)S(1)}, u32[]{:S(2)}, u32[]{:S(2)}) collective-permute-start(bf16[272,128]{1,0:T(8,128)(2,1)S(1)} %get-tuple-element.50), channel_id=1, source_target_pairs={{0,6},{1,7},{2,4},{3,5},{4,2},{5,3},{6,0},{7,1},{8,14},{9,15},{10,... | collective-permute-start | bytes 208904 | tf_op jit(solution)/shard_map/ppermute | solution.py:48
  91.5 5.2 %collective-permute-start.26 = (bf16[272,128]{1,0:T(8,128)(2,1)S(1)}, bf16[272,128]{1,0:T(8,128)(2,1)S(1)}, u32[]{:S(2)}, u32[]{:S(2)}) collective-permute-start(bf16[272,128]{1,0:T(8,128)(2,1)S(1)} %get-tuple-element.49), channel_id=1, source_target_pairs={{0,4},{1,5},{2,6},{3,7},{4,0},{5,1},{6,2},{7,3},{8,12},{9,13},{10,... | collective-permute-start | bytes 208904 | tf_op jit(solution)/shard_map/ppermute | solution.py:48
  91.5 5.2 %collective-permute-start.25 = (bf16[272,128]{1,0:T(8,128)(2,1)S(1)}, bf16[272,128]{1,0:T(8,128)(2,1)S(1)}, u32[]{:S(2)}, u32[]{:S(2)}) collective-permute-start(bf16[272,128]{1,0:T(8,128)(2,1)S(1)} %get-tuple-element.48), channel_id=1, source_target_pairs={{0,2},{1,3},{2,0},{3,1},{4,6},{5,7},{6,4},{7,5},{8,10},{9,11},{10,... | collective-permute-start | bytes 208904 | tf_op jit(solution)/shard_map/ppermute | solution.py:48
  96.8 5.6 %collective-permute-start.28 = (bf16[1,2,128,128]{3,2,1,0:T(8,128)(2,1)S(1)}, bf16[1,2,128,128]{3,2,1,0:T(8,128)(2,1)S(1)}, u32[]{:S(2)}, u32[]{:S(2)}) collective-permute-start(bf16[1,2,128,128]{3,2,1,0:T(8,128)(2,1)S(1)} %pad_maximum_fusion.3), channel_id=1, source_target_pairs={{0,2},{1,3},{2,0},{3,1},{4,6},{5,7},{6,4},{7,5},{8,10},{9,11},{10,... | collective-permute-start | bytes 196616 | tf_op jit(solution)/shard_map/ppermute | solution.py:48
  97.5 6.2 %collective-permute-start.29 = (bf16[1,2,128,128]{3,2,1,0:T(8,128)(2,1)S(1)}, bf16[1,2,128,128]{3,2,1,0:T(8,128)(2,1)S(1)}, u32[]{:S(2)}, u32[]{:S(2)}) collective-permute-start(bf16[1,2,128,128]{3,2,1,0:T(8,128)(2,1)S(1)} %pad_maximum_fusion.3), channel_id=1, source_target_pairs={{0,4},{1,5},{2,6},{3,7},{4,0},{5,1},{6,2},{7,3},{8,12},{9,13},{10,... | collective-permute-start | bytes 196616 | tf_op jit(solution)/shard_map/ppermute | solution.py:48
  99.7 6.1 %collective-permute-start.30 = (bf16[1,2,128,128]{3,2,1,0:T(8,128)(2,1)S(1)}, bf16[1,2,128,128]{3,2,1,0:T(8,128)(2,1)S(1)}, u32[]{:S(2)}, u32[]{:S(2)}) collective-permute-start(bf16[1,2,128,128]{3,2,1,0:T(8,128)(2,1)S(1)} %pad_maximum_fusion.3), channel_id=1, source_target_pairs={{0,6},{1,7},{2,4},{3,5},{4,2},{5,3},{6,0},{7,1},{8,14},{9,15},{10,... | collective-permute-start | bytes 196616 | tf_op jit(solution)/shard_map/ppermute | solution.py:48
  105.8 10.4 %collective-permute-start.31 = (bf16[4,2,128,128]{3,2,1,0:T(8,128)(2,1)S(1)}, bf16[4,2,128,128]{3,2,1,0:T(8,128)(2,1)S(1)}, u32[]{:S(2)}, u32[]{:S(2)}) collective-permute-start(bf16[4,2,128,128]{3,2,1,0:T(8,128)(2,1)S(1)} %pad_maximum_fusion.1), channel_id=1, source_target_pairs={{0,1},{1,0},{2,3},{3,2},{4,5},{5,4},{6,7},{7,6},{8,9},{9,8},{10,11... | collective-permute-start | bytes 786440 | tf_op jit(solution)/shard_map/ppermute | solution.py:48

commit v2 on v1

--- a/solution.py
+++ b/solution.py
@@ -141,7 +141,7 @@
 def backward_body(n_ens, dsh, factor, *refs):
     f_refs, o_refs = refs[:n_ens], refs[n_ens : 2 * n_ens]
     target_ref, pw_ref, mask_ref, read_ref, w_ref, nb_ref, nm_ref = refs[2 * n_ens : 2 * n_ens + 7]
-    gf_ref, con_ref, loss_ref, scratch = refs[2 * n_ens + 7 :]
+    gf_ref, con_ref, scratch = refs[2 * n_ens + 7 :]
     position = lax.axis_index("pix")
     counts = counts_of(nb_ref, nm_ref, position)
     live = jnp.where(mask_ref[pl.ds(position, 1), :] > 0, 1.0, 0.0)
@@ -161,7 +161,11 @@
     for j in range(1, n_ens):
         others = others + sabs(fc[0] - fc[j])
     terms = lw * (sabs(fc[0] - target) - others / (2.0 * (n_ens - 1)))
-    loss_ref[...] = jnp.full((8, LANES), jnp.sum(terms), F32)
+    loss = jnp.full((16, LANES), jnp.sum(terms), F32)
+    for i in range(con_ref.shape[1] // LANES):
+        part = loss.astype(BF16)
+        con_ref[3 * TILE :, i * LANES : (i + 1) * LANES] = part
+        loss = loss - part.astype(F32)
     grad_hidden = dot(gf_ref[:TILE, :], read_ref[...], NT).astype(BF16)
     grad_att = dot(grad_hidden, assembled(o_refs, scratch, dsh)).astype(BF16)
     lane = lax.broadcasted_iota(jnp.int32, (TILE, LANES), 1)
@@ -176,8 +180,14 @@
             con_ref[rows, cols] = (both[rows] * counts[i]).astype(BF16)
 
 
-def value_body(blocks, dsh, keep_ref, sib_ref, own_con, sib_con, v_ref):
-    term = dot(keep_ref[...], own_con[...]) + dot(sib_ref[...], sib_con[...])
+def value_body(blocks, dsh, keep_ref, sib_ref, own_con, sib_con, v_ref, loss_ref):
+    rows = 3 * TILE
+    term = dot(keep_ref[...], own_con[:rows, :]) + dot(sib_ref[...], sib_con[:rows, :])
+    parts = []
+    for ref in (own_con, sib_con):
+        part = ref[rows:, :].astype(F32)
+        parts.append(part[:, :LANES] + part[:, LANES : 2 * LANES] + part[:, 2 * LANES : 3 * LANES])
+    loss_ref[...] = (parts[0] + parts[1])[:8]
     for b in range(blocks):
         for cb in range(term.shape[1] // LANES):
             v_ref[b, cb * dsh : (cb + 1) * dsh, :] = term[
@@ -197,9 +207,10 @@
         o_ref[cb * dsh : (cb + 1) * dsh, :] = term[:, cb * LANES : (cb + 1) * LANES]
 
 
-def finish_body(n_pix, dsh, *refs):
+def finish_body(n_pix, dsh, scale, *refs):
     pieces = refs[:n_pix]
-    gv_ref, go_ref, scratch = refs[n_pix:]
+    total_ref, gv_ref, go_ref, loss_ref, scratch = refs[n_pix:]
+    loss_ref[...] = total_ref[:1, :1] * scale
     rows = scratch.shape[1] // n_pix
     position = lax.axis_index("pix")
     for j in range(n_pix):
@@ -214,18 +225,23 @@
     first = lax.reduce_precision(total, 8, 7)
     second = lax.reduce_precision(total - first, 8, 7)
     third = total - first - second
-    return jnp.stack([first, second, third]).astype(BF16)
-
-
-def from_parts(parts):
-    parts = parts.astype(F32)
-    return parts[0] + parts[1] + parts[2]
+    return [part.astype(BF16) for part in (first, second, third, jnp.zeros_like(total))]
+
+
+def with_loss(block, total):
+    return jnp.concatenate([block.reshape(-1, LANES).astype(BF16)] + in_parts(total), axis=0)
+
+
+def split_loss(message):
+    parts = message[-32:].astype(F32).reshape(4, 8, LANES)
+    return message[:-32], parts[0] + parts[1] + parts[2]
 
 
 def gathered(value, axis, bits):
     pieces = {0: value}
     for bit in bits:
-        pieces.update({j ^ bit: xor_permute(piece, axis, bit) for j, piece in list(pieces.items())})
+        held = lax.optimization_barrier(pieces)
+        pieces = held | {j ^ bit: xor_permute(piece, axis, bit) for j, piece in held.items()}
     return [pieces[j] for j in sorted(pieces)]
 
 
@@ -235,16 +251,6 @@
 
 def part_of(split, index):
     return lax.dynamic_index_in_dim(split, index, 1, keepdims=False).reshape(-1, LANES)
-
-
-def with_loss(block, total):
-    rows = jnp.broadcast_to(in_parts(total)[:, None], (3, LANES))
-    rows = jnp.pad(rows, ((0, 13), (0, 0)))
-    return jnp.concatenate([block.reshape(-1, LANES).astype(BF16), rows], axis=0)
-
-
-def split_loss(message):
-    return message[:-16], from_parts(message[-16:-13, 0])
 
 
 def per_device(
@@ -322,9 +328,9 @@
     attended_all = gathered(attended, "ens", ens_bits)
 
     factor = 1.0 / math.sqrt(n_ens * n_pix * TILE)
-    grads, contrib, loss_rows = call(
+    grads, contrib = call(
         functools.partial(backward_body, n_ens, dsh, factor),
-        [((n_ens * TILE, LANES), BF16), ((3 * TILE, inner), BF16), ((8, LANES), F32)],
+        [((n_ens * TILE, LANES), BF16), ((3 * TILE + 16, inner), BF16)],
         [("v", a) for a in forecasts + o_parts]
         + [("v", target), ("v", pixel_weight.reshape(1, TILE)), ("v", mask_rows), ("v", readout_matrix)]
         + [("v", weights), ("s", neighbours), ("s", neighbour_mask)],
@@ -334,9 +340,9 @@
     )
     contrib_sib = xor_permute(contrib, "ens", 1)
     blocks = n_ens // 2
-    (value_term,) = call(
+    value_term, loss = call(
         functools.partial(value_body, blocks, dsh),
-        [((blocks, dsh * inner // LANES, LANES), F32)],
+        [((blocks, dsh * inner // LANES, LANES), F32), ((8, LANES), F32)],
         [("v", turned_keep), ("v", turned_sib), ("v", contrib), ("v", contrib_sib)],
         10**9,
         "value_term",
@@ -350,8 +356,6 @@
         scratch=[pltpu.VMEM((n_ens * TILE, inner), BF16)],
     )
 
-    loss = loss_rows[0, 0]
-    loss = loss + xor_permute(loss.reshape(1, 1), "ens", 1)[0, 0]
     for bit in ens_bits[:-1]:
         upper = (e // bit) % 2
         halves = value_term.reshape(2, -1, LANES)
@@ -364,25 +368,34 @@
 
     n_bits = n_pix.bit_length() - 1
     groups = [[1]] + [[1 << b for b in range(s, min(s + 2, n_bits))] for s in range(1, n_bits, 2)]
+
+    def pieces_of(term, group):
+        size = 1 << len(group)
+        return term.reshape(n_pix // (group[0] * size), size, -1, LANES)
+
+    def exchanged(messages, group):
+        return [xor_permute(m, "pix", (d + 1) * group[0]) for d, m in enumerate(messages)]
+
+    split = pieces_of(output_term, groups[0])
+    got = exchanged([part_of(split, 1 - p % 2).astype(BF16)], groups[0])[0]
+    output_term = part_of(split, p % 2) + got.astype(F32)
+    for group in groups:
+        size, pos = 1 << len(group), (p // group[0]) % (1 << len(group))
+        moving = [value_term] if group == groups[0] else [value_term, output_term]
+        split = [pieces_of(t, group) for t in moving]
+        messages = [
+            with_loss(jnp.concatenate([part_of(s, pos ^ d) for s in split]), loss) for d in range(1, size)
+        ]
+        received = [split_loss(m) for m in exchanged(messages, group)]
+        kept = [part_of(s, pos) for s in split]
+        for block, _ in received:
+            block = block.astype(F32).reshape(len(kept), -1, LANES)
+            kept = [k + block[i] for i, k in enumerate(kept)]
+        value_term = kept[0]
+        output_term = kept[1] if len(kept) > 1 else output_term
+        losses = jnp.stack([loss] + [other for _, other in received])
+        loss = functools.reduce(jnp.add, [at(losses, pos ^ i) for i in range(size)])
     terms = [value_term, output_term]
-    for group in groups:
-        size = 1 << len(group)
-        low = group[0]
-        pos = (p // low) % size
-        shape = (n_pix // (low * size), size, -1, LANES)
-        split = [t.reshape(shape) for t in terms]
-        kept = [part_of(s, pos) for s in split]
-        losses = [None] * size
-        for d in range(1, size):
-            message = with_loss(jnp.concatenate([part_of(s, pos ^ d) for s in split], axis=0), loss)
-            got, other = split_loss(xor_permute(message, "pix", d * low))
-            got = got.astype(F32).reshape(2, -1, LANES)
-            kept = [kept[0] + got[0], kept[1] + got[1]]
-            losses[d] = other
-        losses[0] = loss
-        ordered = jnp.stack(losses)
-        loss = functools.reduce(jnp.add, [at(ordered, pos ^ i) for i in range(size)])
-        terms = kept
     piece = jnp.stack(terms).astype(BF16)
     pieces = {0: piece}
     for group in reversed(groups):
@@ -394,16 +407,16 @@
             for i, j in enumerate(keys):
                 new[j ^ (d * group[0])] = got[i]
         pieces = new
-    grad_w_value, grad_w_out = call(
-        functools.partial(finish_body, n_pix, dsh),
-        [((dsh, inner), F32), ((inner, dsh), F32)],
-        [("v", pieces[j]) for j in range(n_pix)],
+    scale = 1.0 / (n_ens * n_pix * TILE * n_out)
+    grad_w_value, grad_w_out, loss = call(
+        functools.partial(finish_body, n_pix, dsh, scale),
+        [((dsh, inner), F32), ((inner, dsh), F32), ((1, 1), F32)],
+        [("v", pieces[j]) for j in range(n_pix)] + [("v", loss)],
         10**6,
         "finish",
         scratch=[pltpu.VMEM((2, dsh * inner // LANES, LANES), F32)],
     )
-    loss = loss / (n_ens * n_pix * TILE * n_out)
-    return (loss, grad_w_out, grad_w_value)
+    return (loss.reshape(()), grad_w_out, grad_w_value)
 
 
 def solution(mesh):

time: 119 us -> 89.4 us (0.75)
  between operations: 28 us -> 1.02 us
  local copies, waits for them, and re-layouts: 7.42 us -> 2.05 us
  starting transfers between devices: 29.5 us -> 33.8 us
    ppermute x1, waiting for transfers between devices: 8.07 us -> 1.91 us  [per_device(): lax.ppermute(sample_layer_feed, 'pix', [(i, i + 1) for i in range(n_pix -...]
    ppermute x30, waiting for transfers between devices: 35.4 us -> 41 us  [xor_permute(): return lax.ppermute(value, axis, [(i, i ^ mask) for i in range(size)])]
    ppermute x30, starting transfers between devices: 23.2 us -> 28.6 us  [xor_permute(): return lax.ppermute(value, axis, [(i, i ^ mask) for i in range(size)])]
    slice x7 -> x0, local copies, waits for them, and re-layouts: 3.52 us -> none  [the longest x5 2.97 us: from_parts(): return parts[0] + parts[1] + parts[2]]
    dynamic_slice x2, local copies, waits for them, and re-layouts: 1.26 us -> 0.04 us  [part_of(): lax.dynamic_index_in_dim(split, index, 1, keepdims=False).reshape(-1, LANES)]
    unnamed x31 -> x27, local copies, waits for them, and re-layouts: 2.46 us -> 1.9 us
  transfers between devices with their start and end apart: 32 -> 32, of which waited for: 15 -> 17; matrix products, arithmetic and copies ran while one was open for 4% -> 2% of each run, Pallas kernels for 6% -> 6%
where the time goes in v2:
time: 89.4 us; the launch traced here: 89.2 us
  waiting for transfers between devices  42.9 us (48%)
  starting transfers between devices  33.8 us (38%)
  Pallas kernels  8.96 us (10%)
  local copies, waits for them, and re-layouts  2.05 us (2%)
  between operations  1.02 us (1%)
    ppermute x30, waiting for transfers between devices, xor_permute(): return lax.ppermute(value, axis, [(i, i ^ mask) for i in range(size)])  41 us
    ppermute x30, starting transfers between devices, xor_permute(): return lax.ppermute(value, axis, [(i, i ^ mask) for i in range(size)])  28.6 us
    pallas_call x8, Pallas kernels, call(): pl.pallas_call(body, out_shape=[jax.ShapeDtypeStruct(s, d) for s, d in ou...  8.96 us
    ppermute x1, starting transfers between devices, per_device(): lax.ppermute(sample_layer_feed, 'pix', [(i, i + 1) for i in range(n_pix -...  3.88 us
    ppermute x1, waiting for transfers between devices, per_device(): lax.ppermute(sample_layer_feed, 'pix', [(i, i + 1) for i in range(n_pix -...  1.91 us
    unnamed x27, local copies, waits for them, and re-layouts  1.9 us
  transfers between devices with their start and end apart: 32, of which 17 were waited for; matrix products, arithmetic and copies ran while one was open for 2% of the time, Pallas kernels for 6%

profile of v2, /device:TPU:0, one launch (start us, length us, event | category | flops | bytes accessed | tf_op | source)
XLA Modules:
  0.0 89.2 jit_solution(6562752077061087668)
XLA Ops:
  0.6 3.0 %collective-permute-start.9 = (bf16[256,512]{1,0:T(8,128)(2,1)}, bf16[256,512]{1,0:T(8,128)(2,1)S(1)}, u32[]{:S(2)}, u32[]{:S(2)}) collective-permute-start(bf16[256,512]{1,0:T(8,128)(2,1)} %refs_4_), channel_id=1, source_target_pairs={{0,16},{8,24},{16,0},{24,8},{1,17},{9,25},{17,1},{25,9},{2,18},{10... | collective-permute-start | bytes 786440 | tf_op jit(solution)/shard_map/ppermute | solution.py:48
  3.6 0.1 collective-permute-start.6
  3.7 3.9 %collective-permute-start = (bf16[1,128,1024]{2,1,0:T(8,128)(2,1)}, bf16[1,128,1024]{2,1,0:T(8,128)(2,1)S(1)}, u32[]{:S(2)}, u32[]{:S(2)}) collective-permute-start(bf16[1,128,1024]{2,1,0:T(8,128)(2,1)} %x_ref.3), channel_id=1, source_target_pairs={{0,1},{1,2},{2,3},{3,4},{4,5},{5,6},{6,7},{8,9},{9,10},{10,11},{11... | collective-permute-start | bytes 786440 | tf_op jit(solution)/shard_map/ppermute | solution.py:281
  7.6 1.3 %collective-permute-start.1 = (bf16[1,128,1024]{2,1,0:T(8,128)(2,1)}, bf16[1,128,1024]{2,1,0:T(8,128)(2,1)S(1)}, u32[]{:S(2)}, u32[]{:S(2)}) collective-permute-start(bf16[1,128,1024]{2,1,0:T(8,128)(2,1)} %x_ref.3), channel_id=1, source_target_pairs={{1,0},{2,1},{3,2},{4,3},{5,4},{6,5},{7,6},{9,8},{10,9},{11,10},{12... | collective-permute-start | bytes 786440 | tf_op jit(solution)/shard_map/ppermute | solution.py:282
  8.9 1.6 %collective-permute-start.3 = (bf16[256,512]{1,0:T(8,128)(2,1)}, bf16[256,512]{1,0:T(8,128)(2,1)S(1)}, u32[]{:S(2)}, u32[]{:S(2)}) collective-permute-start(bf16[256,512]{1,0:T(8,128)(2,1)} %refs_0_.1), channel_id=1, source_target_pairs={{0,16},{8,24},{16,0},{24,8},{1,17},{9,25},{17,1},{25,9},{2,18},{10... | collective-permute-start | bytes 786440 | tf_op jit(solution)/shard_map/ppermute | solution.py:48
  10.5 1.1 %copy.15 = bf16[512,256]{0,1:T(8,128)(2,1)S(1)} copy(bf16[512,256]{1,0:T(8,128)(2,1)} %param.17) | data formatting | bytes 524288 | tf_op args[5]
  11.6 0.0 collective-permute-done.9.refs_6_
  11.6 1.5 %collective-permute-start.12 = (bf16[256,512]{1,0:T(8,128)(2,1)S(1)}, bf16[256,512]{1,0:T(8,128)(2,1)S(1)}, u32[]{:S(2)}, u32[]{:S(2)}) collective-permute-start(bf16[256,512]{1,0:T(8,128)(2,1)S(1)} %bitcast.104), channel_id=1, source_target_pairs={{0,16},{8,24},{16,0},{24,8},{1,17},{9,25},{17,1},{25,9},{2,18},{10... | collective-permute-start | bytes 786440 | tf_op jit(solution)/shard_map/ppermute | solution.py:48
  13.0 3.6 %collective-permute-done.6.refs_2_ = bf16[256,512]{1,0:T(8,128)(2,1)S(1)} collective-permute-done((bf16[256,512]{1,0:T(8,128)(2,1)}, bf16[256,512]{1,0:T(8,128)(2,1)S(1)}, u32[]{:S(2)}, u32[]{:S(2)}) %collective-permute-start.6) | collective-permute-done | bytes 262176 | tf_op jit(solution)/shard_map/ppermute | solution.py:48
  16.6 0.0 collective-permute-start.10
  16.6 1.9 %collective-permute-done.up_ref = bf16[1,128,1024]{2,1,0:T(8,128)(2,1)S(1)} collective-permute-done((bf16[1,128,1024]{2,1,0:T(8,128)(2,1)}, bf16[1,128,1024]{2,1,0:T(8,128)(2,1)S(1)}, u32[]{:S(2)}, u32[]{:S(2)}) %collective-permute-start) | collective-permute-done | bytes 262176 | tf_op jit(solution)/shard_map/ppermute | solution.py:281
  18.5 0.0 collective-permute-start.11
  18.5 0.0 collective-permute-done.1.down_ref
  18.5 0.5 collective-permute-start.7
  19.0 3.2 %collective-permute-done.3.refs_2_ = bf16[256,512]{1,0:T(8,128)(2,1)S(1)} collective-permute-done((bf16[256,512]{1,0:T(8,128)(2,1)}, bf16[256,512]{1,0:T(8,128)(2,1)S(1)}, u32[]{:S(2)}, u32[]{:S(2)}) %collective-permute-start.3) | collective-permute-done | bytes 262176 | tf_op jit(solution)/shard_map/ppermute | solution.py:48
  22.2 4.8 %collective-permute-done.12.refs_2_.refs_6_ = bf16[256,512]{1,0:T(8,128)(2,1)S(1)} collective-permute-done((bf16[256,512]{1,0:T(8,128)(2,1)S(1)}, bf16[256,512]{1,0:T(8,128)(2,1)S(1)}, u32[]{:S(2)}, u32[]{:S(2)}) %collective-permute-start.12) | collective-permute-done | bytes 262176 | tf_op jit(solution)/shard_map/ppermute | solution.py:48
  27.0 0.0 collective-permute-start.4
  27.0 0.0 collective-permute-done.10.refs_5_
  27.0 0.5 collective-permute-start.5
  27.5 0.0 copy-start.7
  27.6 0.6 normed.1
  28.2 0.1 collective-permute-start.13
  28.3 0.0 collective-permute-done.7.refs_1_
  28.3 0.5 collective-permute-start.14
  28.8 0.6 copy-done.8
  29.4 0.0 copy-done.9
  29.4 2.2 %weights.1.refs_4_.refs_12_ = bf16[8,128,384]{2,1,0:T(8,128)(2,1)S(1)} custom-call(bf16[384,1024]{1,0:T(8,128)(2,1)S(1)} %get-tuple-element.27.n_ref, bf16[256,512]{1,0:T(8,128)(2,1)S(1)} %copy-done.2, bf16[256,512]{1,0:T(8,128)(2,1)S(1)} %collective-permute-done.7.refs_1_, bf16[256,512]{1,0:T(8,128)(2,1)S(1)} %collective-permute-done.6.refs_2_, ...), custom_call_target="tpu_custom_call" | custom-call | flops 2000000000 | bytes 1048576 | tf_op jit(solution)/shard_map/weights/pallas_call | solution.py:34
  31.6 0.0 copy-start.5
  31.7 1.5 %attend.1.att_ref.refs_0_ = bf16[128,512]{1,0:T(8,128)(2,1)S(1)} custom-call(bf16[384,1024]{1,0:T(8,128)(2,1)S(1)} %get-tuple-element.27.n_ref, bf16[256,512]{1,0:T(8,128)(2,1)S(1)} %copy-done.4, bf16[256,512]{1,0:T(8,128)(2,1)S(1)} %collective-permute-done.4.refs_1_, bf16[256,512]{1,0:T(8,128)(2,1)S(1)} %collective-permute-done.3.refs_2_, ...), custom_call_target="tpu_custom_call" | custom-call | flops 1000000000 | bytes 1048576 | tf_op jit(solution)/shard_map/attend/pallas_call | solution.py:34
  33.2 0.0 copy-start.6
  33.3 0.7 forecast.1.refs_0_
  34.0 1.8 %collective-permute-start.15 = (bf16[128,128]{1,0:T(8,128)(2,1)S(1)}, bf16[128,128]{1,0:T(8,128)(2,1)S(1)}, u32[]{:S(2)}, u32[]{:S(2)}) collective-permute-start(bf16[128,128]{1,0:T(8,128)(2,1)S(1)} %forecast.1.refs_0_), channel_id=1, source_target_pairs={{0,16},{8,24},{16,0},{24,8},{1,17},{9,25},{17,1},{25,9},{2,18},{10... | collective-permute-start | bytes 98312 | tf_op jit(solution)/shard_map/ppermute | solution.py:48
  35.8 2.2 %collective-permute-done.15.refs_2_ = bf16[128,128]{1,0:T(8,128)(2,1)S(1)} collective-permute-done((bf16[128,128]{1,0:T(8,128)(2,1)S(1)}, bf16[128,128]{1,0:T(8,128)(2,1)S(1)}, u32[]{:S(2)}, u32[]{:S(2)}) %collective-permute-start.15) | collective-permute-done | bytes 32800 | tf_op jit(solution)/shard_map/ppermute | solution.py:48
  37.9 0.5 collective-permute-start.17
  38.5 0.7 collective-permute-done.16.refs_1_
  39.2 0.2 collective-permute-done.17.refs_3_
  39.3 1.6 %backward.1 = (bf16[512,128]{1,0:T(8,128)(2,1)S(1)}, bf16[400,512]{1,0:T(8,128)(2,1)S(1)}) custom-call(bf16[128,128]{1,0:T(8,128)(2,1)S(1)} %forecast.1.refs_0_, bf16[128,128]{1,0:T(8,128)(2,1)S(1)} %collective-permute-done.16.refs_1_, bf16[128,128]{1,0:T(8,128)(2,1)S(1)} %collective-permute-done.15.refs_2_, ...), custom_call_target="tpu_custom_call" | custom-call | flops 1000000000 | bytes 1048576 | tf_op jit(solution)/shard_map/backward/pallas_call | solution.py:34
  40.9 0.4 collective-permute-start.18
  41.3 0.2 collective-permute-start.2
  41.5 1.8 %collective-permute-start.21 = (bf16[128,512]{1,0:T(8,128)(2,1)S(1)}, bf16[128,512]{1,0:T(8,128)(2,1)S(1)}, u32[]{:S(2)}, u32[]{:S(2)}) collective-permute-start(bf16[128,512]{1,0:T(8,128)(2,1)S(1)} %attend.1.att_ref.refs_0_), channel_id=1, source_target_pairs={{0,16},{8,24},{16,0},{24,8},{1,17},{9,25},{17,1},{25,9},{2,18},{10... | collective-permute-start | bytes 393224 | tf_op jit(solution)/shard_map/ppermute | solution.py:48
  43.3 4.0 %collective-permute-done.21.refs_2_ = bf16[128,512]{1,0:T(8,128)(2,1)S(1)} collective-permute-done((bf16[128,512]{1,0:T(8,128)(2,1)S(1)}, bf16[128,512]{1,0:T(8,128)(2,1)S(1)}, u32[]{:S(2)}, u32[]{:S(2)}) %collective-permute-start.21) | collective-permute-done | bytes 131104 | tf_op jit(solution)/shard_map/ppermute | solution.py:48
  47.3 0.5 collective-permute-start.23
  47.8 0.7 value_term.1
  48.6 1.8 %collective-permute-start.19 = (bf16[1056,128]{1,0:T(8,128)(2,1)S(1)}, bf16[1056,128]{1,0:T(8,128)(2,1)S(1)}, u32[]{:S(2)}, u32[]{:S(2)}) collective-permute-start(bf16[1056,128]{1,0:T(8,128)(2,1)S(1)} %constant_dynamic-update-slice_fusion), channel_id=1, source_target_pairs={{0,16},{8,24},{16,0},{24,8},{1,17},{9,25},{17,1},{25,9},{2,18},{10... | collective-permute-start | bytes 811016 | tf_op jit(solution)/shard_map/ppermute | solution.py:48
  50.4 0.4 output_term.1
  50.9 1.6 %collective-permute-start.24 = (bf16[512,128]{1,0:T(8,128)(2,1)S(1)}, bf16[512,128]{1,0:T(8,128)(2,1)S(1)}, u32[]{:S(2)}, u32[]{:S(2)}) collective-permute-start(bf16[512,128]{1,0:T(8,128)(2,1)S(1)} %bitcast.128), channel_id=1, source_target_pairs={{0,1},{1,0},{2,3},{3,2},{4,5},{5,4},{6,7},{7,6},{8,9},{9,8},{10,11... | collective-permute-start | bytes 393224 | tf_op jit(solution)/shard_map/ppermute | solution.py:48
  52.5 4.6 %collective-permute-done.19 = bf16[1056,128]{1,0:T(8,128)(2,1)S(1)} collective-permute-done((bf16[1056,128]{1,0:T(8,128)(2,1)S(1)}, bf16[1056,128]{1,0:T(8,128)(2,1)S(1)}, u32[]{:S(2)}, u32[]{:S(2)}) %collective-permute-start.19) | collective-permute-done | bytes 270368 | tf_op jit(solution)/shard_map/ppermute | solution.py:48
  57.2 1.8 %collective-permute-start.20 = (bf16[544,128]{1,0:T(8,128)(2,1)S(1)}, bf16[544,128]{1,0:T(8,128)(2,1)S(1)}, u32[]{:S(2)}, u32[]{:S(2)}) collective-permute-start(bf16[544,128]{1,0:T(8,128)(2,1)S(1)} %constant_dynamic-update-slice_fusion.4), channel_id=1, source_target_pairs={{0,1},{1,0},{2,3},{3,2},{4,5},{5,4},{6,7},{7,6},{8,9},{9,8},{10,11... | collective-permute-start | bytes 417800 | tf_op jit(solution)/shard_map/ppermute | solution.py:48
  59.1 3.2 %collective-permute-done.20 = bf16[544,128]{1,0:T(8,128)(2,1)S(1)} collective-permute-done((bf16[544,128]{1,0:T(8,128)(2,1)S(1)}, bf16[544,128]{1,0:T(8,128)(2,1)S(1)}, u32[]{:S(2)}, u32[]{:S(2)}) %collective-permute-start.20) | collective-permute-done | bytes 139296 | tf_op jit(solution)/shard_map/ppermute | solution.py:48
  62.6 2.9 %collective-permute-start.26 = (bf16[288,128]{1,0:T(8,128)(2,1)S(1)}, bf16[288,128]{1,0:T(8,128)(2,1)S(1)}, u32[]{:S(2)}, u32[]{:S(2)}) collective-permute-start(bf16[288,128]{1,0:T(8,128)(2,1)S(1)} %constant_dynamic-update-slice_fusion.15), channel_id=1, source_target_pairs={{0,4},{1,5},{2,6},{3,7},{4,0},{5,1},{6,2},{7,3},{8,12},{9,13},{10,... | collective-permute-start | bytes 221192 | tf_op jit(solution)/shard_map/ppermute | solution.py:48
  65.5 1.3 %collective-permute-start.27 = (bf16[288,128]{1,0:T(8,128)(2,1)S(1)}, bf16[288,128]{1,0:T(8,128)(2,1)S(1)}, u32[]{:S(2)}, u32[]{:S(2)}) collective-permute-start(bf16[288,128]{1,0:T(8,128)(2,1)S(1)} %constant_dynamic-update-slice_fusion.21), channel_id=1, source_target_pairs={{0,6},{1,7},{2,4},{3,5},{4,2},{5,3},{6,0},{7,1},{8,14},{9,15},{10,... | collective-permute-start | bytes 221192 | tf_op jit(solution)/shard_map/ppermute | solution.py:48
  66.8 0.3 collective-permute-start.25
  67.1 2.8 %collective-permute-done.26 = bf16[288,128]{1,0:T(8,128)(2,1)S(1)} collective-permute-done((bf16[288,128]{1,0:T(8,128)(2,1)S(1)}, bf16[288,128]{1,0:T(8,128)(2,1)S(1)}, u32[]{:S(2)}, u32[]{:S(2)}) %collective-permute-start.26) | collective-permute-done | bytes 73760 | tf_op jit(solution)/shard_map/ppermute | solution.py:48
  70.0 1.8 %collective-permute-done.27 = bf16[288,128]{1,0:T(8,128)(2,1)S(1)} collective-permute-done((bf16[288,128]{1,0:T(8,128)(2,1)S(1)}, bf16[288,128]{1,0:T(8,128)(2,1)S(1)}, u32[]{:S(2)}, u32[]{:S(2)}) %collective-permute-start.27) | collective-permute-done | bytes 73760 | tf_op jit(solution)/shard_map/ppermute | solution.py:48
  71.7 0.4 collective-permute-done.25
  72.2 0.1 collective-permute-start.28
  72.3 3.1 %collective-permute-start.29 = (bf16[1,2,128,128]{3,2,1,0:T(8,128)(2,1)S(1)}, bf16[1,2,128,128]{3,2,1,0:T(8,128)(2,1)S(1)}, u32[]{:S(2)}, u32[]{:S(2)}) collective-permute-start(bf16[1,2,128,128]{3,2,1,0:T(8,128)(2,1)S(1)} %pad_maximum_fusion.2), channel_id=1, source_target_pairs={{0,4},{1,5},{2,6},{3,7},{4,0},{5,1},{6,2},{7,3},{8,12},{9,13},{10,... | collective-permute-start | bytes 196616 | tf_op jit(solution)/shard_map/ppermute | solution.py:48
  75.5 1.2 %collective-permute-start.30 = (bf16[1,2,128,128]{3,2,1,0:T(8,128)(2,1)S(1)}, bf16[1,2,128,128]{3,2,1,0:T(8,128)(2,1)S(1)}, u32[]{:S(2)}, u32[]{:S(2)}) collective-permute-start(bf16[1,2,128,128]{3,2,1,0:T(8,128)(2,1)S(1)} %pad_maximum_fusion.2), channel_id=1, source_target_pairs={{0,6},{1,7},{2,4},{3,5},{4,2},{5,3},{6,0},{7,1},{8,14},{9,15},{10,... | collective-permute-start | bytes 196616 | tf_op jit(solution)/shard_map/ppermute | solution.py:48
  76.7 0.1 collective-permute-done.28
  76.9 0.8 collective-permute-done.29
  77.7 3.8 %collective-permute-done.30 = bf16[1,2,128,128]{3,2,1,0:T(8,128)(2,1)S(1)} collective-permute-done((bf16[1,2,128,128]{3,2,1,0:T(8,128)(2,1)S(1)}, bf16[1,2,128,128]{3,2,1,0:T(8,128)(2,1)S(1)}, u32[]{:S(2)}, u32[]{:S(2)}) %collective-permute-start.30) | collective-permute-done | bytes 65568 | tf_op jit(solution)/shard_map/ppermute | solution.py:48
  81.6 1.6 %collective-permute-start.31 = (bf16[4,2,128,128]{3,2,1,0:T(8,128)(2,1)S(1)}, bf16[4,2,128,128]{3,2,1,0:T(8,128)(2,1)S(1)}, u32[]{:S(2)}, u32[]{:S(2)}) collective-permute-start(bf16[4,2,128,128]{3,2,1,0:T(8,128)(2,1)S(1)} %pad_maximum_fusion), channel_id=1, source_target_pairs={{0,1},{1,0},{2,3},{3,2},{4,5},{5,4},{6,7},{7,6},{8,9},{9,8},{10,11... | collective-permute-start | bytes 786440 | tf_op jit(solution)/shard_map/ppermute | solution.py:48
  83.2 4.8 %collective-permute-done.31 = bf16[4,2,128,128]{3,2,1,0:T(8,128)(2,1)S(1)} collective-permute-done((bf16[4,2,128,128]{3,2,1,0:T(8,128)(2,1)S(1)}, bf16[4,2,128,128]{3,2,1,0:T(8,128)(2,1)S(1)}, u32[]{:S(2)}, u32[]{:S(2)}) %collective-permute-start.31) | collective-permute-done | bytes 262176 | tf_op jit(solution)/shard_map/ppermute | solution.py:48
  88.0 1.2 %finish.1 = (f32[256,512]{1,0:T(8,128)}, f32[512,256]{1,0:T(8,128)}, f32[1,1]{1,0:T(1,128)}) custom-call(bf16[2,128,128]{2,1,0:T(8,128)(2,1)S(1)} %pad_maximum_fusion.1.refs_0_, bf16[2,128,128]{2,1,0:T(8,128)(2,1)S(1)} %get-tuple-element.56.refs_1_, bf16[2,128,128]{2,1,0:T(8,128)(2,1)S(1)} %bitcast.108, bf16[2,128,128]{2,1,0:T(8,128)(2,1)S(1)} %get-tuple-element.55.refs_3_, ...), custom_call_target="tpu_custom_call" | custom-call | flops 1000000 | bytes 1048576 | tf_op jit(solution)/shard_map/finish/pallas_call | solution.py:34
  (77 shorter events, 0.8 us)
Async XLA Ops:
  0.6 26.9 %copy-start = (bf16[1,128,1024]{2,1,0:T(8,128)(2,1)S(1)}, bf16[1,128,1024]{2,1,0:T(8,128)(2,1)}, u32[]{:S(2)}) copy-start(bf16[1,128,1024]{2,1,0:T(8,128)(2,1)} %x_ref.3) | copy-start | bytes 786436
  0.6 10.9 %collective-permute-start.9 = (bf16[256,512]{1,0:T(8,128)(2,1)}, bf16[256,512]{1,0:T(8,128)(2,1)S(1)}, u32[]{:S(2)}, u32[]{:S(2)}) collective-permute-start(bf16[256,512]{1,0:T(8,128)(2,1)} %refs_4_), channel_id=1, source_target_pairs={{0,16},{8,24},{16,0},{24,8},{1,17},{9,25},{17,1},{25,9},{2,18},{10... | collective-permute-start | bytes 786440 | tf_op jit(solution)/shard_map/ppermute | solution.py:48
  3.6 13.0 %collective-permute-start.6 = (bf16[256,512]{1,0:T(8,128)(2,1)}, bf16[256,512]{1,0:T(8,128)(2,1)S(1)}, u32[]{:S(2)}, u32[]{:S(2)}) collective-permute-start(bf16[256,512]{1,0:T(8,128)(2,1)} %refs_0_), channel_id=1, source_target_pairs={{0,16},{8,24},{16,0},{24,8},{1,17},{9,25},{17,1},{25,9},{2,18},{10... | collective-permute-start | bytes 786440 | tf_op jit(solution)/shard_map/ppermute | solution.py:48
  3.7 14.8 %collective-permute-start = (bf16[1,128,1024]{2,1,0:T(8,128)(2,1)}, bf16[1,128,1024]{2,1,0:T(8,128)(2,1)S(1)}, u32[]{:S(2)}, u32[]{:S(2)}) collective-permute-start(bf16[1,128,1024]{2,1,0:T(8,128)(2,1)} %x_ref.3), channel_id=1, source_target_pairs={{0,1},{1,2},{2,3},{3,4},{4,5},{5,6},{6,7},{8,9},{9,10},{10,11},{11... | collective-permute-start | bytes 786440 | tf_op jit(solution)/shard_map/ppermute | solution.py:281
  7.6 10.9 %collective-permute-start.1 = (bf16[1,128,1024]{2,1,0:T(8,128)(2,1)}, bf16[1,128,1024]{2,1,0:T(8,128)(2,1)S(1)}, u32[]{:S(2)}, u32[]{:S(2)}) collective-permute-start(bf16[1,128,1024]{2,1,0:T(8,128)(2,1)} %x_ref.3), channel_id=1, source_target_pairs={{1,0},{2,1},{3,2},{4,3},{5,4},{6,5},{7,6},{9,8},{10,9},{11,10},{12... | collective-permute-start | bytes 786440 | tf_op jit(solution)/shard_map/ppermute | solution.py:282
  8.9 13.3 %collective-permute-start.3 = (bf16[256,512]{1,0:T(8,128)(2,1)}, bf16[256,512]{1,0:T(8,128)(2,1)S(1)}, u32[]{:S(2)}, u32[]{:S(2)}) collective-permute-start(bf16[256,512]{1,0:T(8,128)(2,1)} %refs_0_.1), channel_id=1, source_target_pairs={{0,16},{8,24},{16,0},{24,8},{1,17},{9,25},{17,1},{25,9},{2,18},{10... | collective-permute-start | bytes 786440 | tf_op jit(solution)/shard_map/ppermute | solution.py:48
  10.5 17.1 %copy-start.1 = (f32[1024]{0:T(1024)S(1)}, f32[1024]{0:T(1024)}, u32[]{:S(2)}) copy-start(f32[1024]{0:T(1024)} %param.13) | copy-start | bytes 12292
  11.6 15.4 %collective-permute-start.12 = (bf16[256,512]{1,0:T(8,128)(2,1)S(1)}, bf16[256,512]{1,0:T(8,128)(2,1)S(1)}, u32[]{:S(2)}, u32[]{:S(2)}) collective-permute-start(bf16[256,512]{1,0:T(8,128)(2,1)S(1)} %bitcast.104), channel_id=1, source_target_pairs={{0,16},{8,24},{16,0},{24,8},{1,17},{9,25},{17,1},{25,9},{2,18},{10... | collective-permute-start | bytes 786440 | tf_op jit(solution)/shard_map/ppermute | solution.py:48
  16.6 10.4 %collective-permute-start.10 = (bf16[256,512]{1,0:T(8,128)(2,1)}, bf16[256,512]{1,0:T(8,128)(2,1)S(1)}, u32[]{:S(2)}, u32[]{:S(2)}) collective-permute-start(bf16[256,512]{1,0:T(8,128)(2,1)} %refs_4_), channel_id=1, source_target_pairs={{0,8},{8,0},{16,24},{24,16},{1,9},{9,1},{17,25},{25,17},{2,10},{10... | collective-permute-start | bytes 786440 | tf_op jit(solution)/shard_map/ppermute | solution.py:48
  18.5 9.6 %collective-permute-start.11 = (bf16[256,512]{1,0:T(8,128)(2,1)S(1)}, bf16[256,512]{1,0:T(8,128)(2,1)S(1)}, u32[]{:S(2)}, u32[]{:S(2)}) collective-permute-start(bf16[256,512]{1,0:T(8,128)(2,1)S(1)} %collective-permute-done.9.refs_6_), channel_id=1, source_target_pairs={{0,8},{8,0},{16,24},{24,16},{1,9},{9,1},{17,25},{25,17},{2,10},{10... | collective-permute-start | bytes 786440 | tf_op jit(solution)/shard_map/ppermute | solution.py:48
  18.5 9.7 %collective-permute-start.7 = (bf16[256,512]{1,0:T(8,128)(2,1)}, bf16[256,512]{1,0:T(8,128)(2,1)S(1)}, u32[]{:S(2)}, u32[]{:S(2)}) collective-permute-start(bf16[256,512]{1,0:T(8,128)(2,1)} %refs_0_), channel_id=1, source_target_pairs={{0,8},{8,0},{16,24},{24,16},{1,9},{9,1},{17,25},{25,17},{2,10},{10... | collective-permute-start | bytes 786440 | tf_op jit(solution)/shard_map/ppermute | solution.py:48
  22.2 6.5 %collective-permute-start.8 = (bf16[256,512]{1,0:T(8,128)(2,1)S(1)}, bf16[256,512]{1,0:T(8,128)(2,1)S(1)}, u32[]{:S(2)}, u32[]{:S(2)}) collective-permute-start(bf16[256,512]{1,0:T(8,128)(2,1)S(1)} %collective-permute-done.6.refs_2_), channel_id=1, source_target_pairs={{0,8},{8,0},{16,24},{24,16},{1,9},{9,1},{17,25},{25,17},{2,10},{10... | collective-permute-start | bytes 786440 | tf_op jit(solution)/shard_map/ppermute | solution.py:48
  27.0 4.6 %collective-permute-start.4 = (bf16[256,512]{1,0:T(8,128)(2,1)}, bf16[256,512]{1,0:T(8,128)(2,1)S(1)}, u32[]{:S(2)}, u32[]{:S(2)}) collective-permute-start(bf16[256,512]{1,0:T(8,128)(2,1)} %refs_0_.1), channel_id=1, source_target_pairs={{0,8},{8,0},{16,24},{24,16},{1,9},{9,1},{17,25},{25,17},{2,10},{10... | collective-permute-start | bytes 786440 | tf_op jit(solution)/shard_map/ppermute | solution.py:48
  27.0 4.6 %collective-permute-start.5 = (bf16[256,512]{1,0:T(8,128)(2,1)S(1)}, bf16[256,512]{1,0:T(8,128)(2,1)S(1)}, u32[]{:S(2)}, u32[]{:S(2)}) collective-permute-start(bf16[256,512]{1,0:T(8,128)(2,1)S(1)} %collective-permute-done.3.refs_2_), channel_id=1, source_target_pairs={{0,8},{8,0},{16,24},{24,16},{1,9},{9,1},{17,25},{25,17},{2,10},{10... | collective-permute-start | bytes 786440 | tf_op jit(solution)/shard_map/ppermute | solution.py:48
  27.5 1.2 %copy-start.2 = (bf16[256,512]{1,0:T(8,128)(2,1)S(1)}, bf16[256,512]{1,0:T(8,128)(2,1)}, u32[]{:S(2)}) copy-start(bf16[256,512]{1,0:T(8,128)(2,1)} %refs_0_) | copy-start | bytes 786436
  27.5 1.2 %copy-start.3 = (bf16[256,512]{1,0:T(8,128)(2,1)S(1)}, bf16[256,512]{1,0:T(8,128)(2,1)}, u32[]{:S(2)}) copy-start(bf16[256,512]{1,0:T(8,128)(2,1)} %refs_4_) | copy-start | bytes 786436
  27.5 1.2 %copy-start.7 = (s32[1024]{0:T(1024)S(1)}, s32[1024]{0:T(1024)}, u32[]{:S(2)}) copy-start(s32[1024]{0:T(1024)} %param.21) | copy-start | bytes 12292
  28.2 5.1 %collective-permute-start.13 = (bf16[256,512]{1,0:T(8,128)(2,1)S(1)}, bf16[256,512]{1,0:T(8,128)(2,1)S(1)}, u32[]{:S(2)}, u32[]{:S(2)}) collective-permute-start(bf16[256,512]{1,0:T(8,128)(2,1)S(1)} %bitcast.105), channel_id=1, source_target_pairs={{0,8},{8,0},{16,24},{24,16},{1,9},{9,1},{17,25},{25,17},{2,10},{10... | collective-permute-start | bytes 786440 | tf_op jit(solution)/shard_map/ppermute | solution.py:48
  28.3 5.0 %collective-permute-start.14 = (bf16[256,512]{1,0:T(8,128)(2,1)S(1)}, bf16[256,512]{1,0:T(8,128)(2,1)S(1)}, u32[]{:S(2)}, u32[]{:S(2)}) collective-permute-start(bf16[256,512]{1,0:T(8,128)(2,1)S(1)} %collective-permute-done.12.refs_2_.refs_6_), channel_id=1, source_target_pairs={{0,8},{8,0},{16,24},{24,16},{1,9},{9,1},{17,25},{25,17},{2,10},{10... | collective-permute-start | bytes 786440 | tf_op jit(solution)/shard_map/ppermute | solution.py:48
  28.8 0.7 copy-start.8
  28.8 0.7 copy-start.9
  29.4 2.3 %copy-start.4 = (bf16[256,512]{1,0:T(8,128)(2,1)S(1)}, bf16[256,512]{1,0:T(8,128)(2,1)}, u32[]{:S(2)}) copy-start(bf16[256,512]{1,0:T(8,128)(2,1)} %refs_0_.1) | copy-start | bytes 786436
  31.6 1.6 %copy-start.5 = (bf16[1024,128]{1,0:T(8,128)(2,1)S(1)}, bf16[1024,128]{1,0:T(8,128)(2,1)}, u32[]{:S(2)}) copy-start(bf16[1024,128]{1,0:T(8,128)(2,1)} %read_ref.3) | copy-start | bytes 786436
  33.2 6.1 %copy-start.6 = (f32[128,128]{1,0:T(8,128)S(1)}, f32[128,128]{1,0:T(8,128)}, u32[]{:S(2)}) copy-start(f32[128,128]{1,0:T(8,128)} %refs_8_.1) | copy-start | bytes 196612
  34.0 5.4 %copy-start.10 = (f32[128]{0:T(128)S(1)}, f32[128]{0:T(128)}, u32[]{:S(2)}) copy-start(f32[128]{0:T(128)} %param.20) | copy-start | bytes 1540
  34.0 4.0 %collective-permute-start.15 = (bf16[128,128]{1,0:T(8,128)(2,1)S(1)}, bf16[128,128]{1,0:T(8,128)(2,1)S(1)}, u32[]{:S(2)}, u32[]{:S(2)}) collective-permute-start(bf16[128,128]{1,0:T(8,128)(2,1)S(1)} %forecast.1.refs_0_), channel_id=1, source_target_pairs={{0,16},{8,24},{16,0},{24,8},{1,17},{9,25},{17,1},{25,9},{2,18},{10... | collective-permute-start | bytes 98312 | tf_op jit(solution)/shard_map/ppermute | solution.py:48
  37.9 1.2 %collective-permute-start.16 = (bf16[128,128]{1,0:T(8,128)(2,1)S(1)}, bf16[128,128]{1,0:T(8,128)(2,1)S(1)}, u32[]{:S(2)}, u32[]{:S(2)}) collective-permute-start(bf16[128,128]{1,0:T(8,128)(2,1)S(1)} %forecast.1.refs_0_), channel_id=1, source_target_pairs={{0,8},{8,0},{16,24},{24,16},{1,9},{9,1},{17,25},{25,17},{2,10},{10... | collective-permute-start | bytes 98312 | tf_op jit(solution)/shard_map/ppermute | solution.py:48
  37.9 1.4 %collective-permute-start.17 = (bf16[128,128]{1,0:T(8,128)(2,1)S(1)}, bf16[128,128]{1,0:T(8,128)(2,1)S(1)}, u32[]{:S(2)}, u32[]{:S(2)}) collective-permute-start(bf16[128,128]{1,0:T(8,128)(2,1)S(1)} %collective-permute-done.15.refs_2_), channel_id=1, source_target_pairs={{0,8},{8,0},{16,24},{24,16},{1,9},{9,1},{17,25},{25,17},{2,10},{10... | collective-permute-start | bytes 98312 | tf_op jit(solution)/shard_map/ppermute | solution.py:48
  40.9 6.9 %collective-permute-start.18 = (bf16[400,512]{1,0:T(8,128)(2,1)S(1)}, bf16[400,512]{1,0:T(8,128)(2,1)S(1)}, u32[]{:S(2)}, u32[]{:S(2)}) collective-permute-start(bf16[400,512]{1,0:T(8,128)(2,1)S(1)} %get-tuple-element.38.own_con), channel_id=1, source_target_pairs={{0,8},{8,0},{16,24},{24,16},{1,9},{9,1},{17,25},{25,17},{2,10},{10... | collective-permute-start | bytes 1228808 | tf_op jit(solution)/shard_map/ppermute | solution.py:48
  41.3 6.4 %collective-permute-start.2 = (bf16[512,384]{1,0:T(8,128)(2,1)S(1)}, bf16[512,384]{1,0:T(8,128)(2,1)S(1)}, u32[]{:S(2)}, u32[]{:S(2)}) collective-permute-start(bf16[512,384]{1,0:T(8,128)(2,1)S(1)} %get-tuple-element.26), channel_id=1, source_target_pairs={{0,8},{8,0},{16,24},{24,16},{1,9},{9,1},{17,25},{25,17},{2,10},{10... | collective-permute-start | bytes 1179656 | tf_op jit(solution)/shard_map/ppermute | solution.py:48
  41.5 5.8 %collective-permute-start.21 = (bf16[128,512]{1,0:T(8,128)(2,1)S(1)}, bf16[128,512]{1,0:T(8,128)(2,1)S(1)}, u32[]{:S(2)}, u32[]{:S(2)}) collective-permute-start(bf16[128,512]{1,0:T(8,128)(2,1)S(1)} %attend.1.att_ref.refs_0_), channel_id=1, source_target_pairs={{0,16},{8,24},{16,0},{24,8},{1,17},{9,25},{17,1},{25,9},{2,18},{10... | collective-permute-start | bytes 393224 | tf_op jit(solution)/shard_map/ppermute | solution.py:48
  47.3 3.1 %collective-permute-start.22 = (bf16[128,512]{1,0:T(8,128)(2,1)S(1)}, bf16[128,512]{1,0:T(8,128)(2,1)S(1)}, u32[]{:S(2)}, u32[]{:S(2)}) collective-permute-start(bf16[128,512]{1,0:T(8,128)(2,1)S(1)} %attend.1.att_ref.refs_0_), channel_id=1, source_target_pairs={{0,8},{8,0},{16,24},{24,16},{1,9},{9,1},{17,25},{25,17},{2,10},{10... | collective-permute-start | bytes 393224 | tf_op jit(solution)/shard_map/ppermute | solution.py:48
  47.3 3.1 %collective-permute-start.23 = (bf16[128,512]{1,0:T(8,128)(2,1)S(1)}, bf16[128,512]{1,0:T(8,128)(2,1)S(1)}, u32[]{:S(2)}, u32[]{:S(2)}) collective-permute-start(bf16[128,512]{1,0:T(8,128)(2,1)S(1)} %collective-permute-done.21.refs_2_), channel_id=1, source_target_pairs={{0,8},{8,0},{16,24},{24,16},{1,9},{9,1},{17,25},{25,17},{2,10},{10... | collective-permute-start | bytes 393224 | tf_op jit(solution)/shard_map/ppermute | solution.py:48
  48.6 8.5 %collective-permute-start.19 = (bf16[1056,128]{1,0:T(8,128)(2,1)S(1)}, bf16[1056,128]{1,0:T(8,128)(2,1)S(1)}, u32[]{:S(2)}, u32[]{:S(2)}) collective-permute-start(bf16[1056,128]{1,0:T(8,128)(2,1)S(1)} %constant_dynamic-update-slice_fusion), channel_id=1, source_target_pairs={{0,16},{8,24},{16,0},{24,8},{1,17},{9,25},{17,1},{25,9},{2,18},{10... | collective-permute-start | bytes 811016 | tf_op jit(solution)/shard_map/ppermute | solution.py:48
  50.9 8.2 %collective-permute-start.24 = (bf16[512,128]{1,0:T(8,128)(2,1)S(1)}, bf16[512,128]{1,0:T(8,128)(2,1)S(1)}, u32[]{:S(2)}, u32[]{:S(2)}) collective-permute-start(bf16[512,128]{1,0:T(8,128)(2,1)S(1)} %bitcast.128), channel_id=1, source_target_pairs={{0,1},{1,0},{2,3},{3,2},{4,5},{5,4},{6,7},{7,6},{8,9},{9,8},{10,11... | collective-permute-start | bytes 393224 | tf_op jit(solution)/shard_map/ppermute | solution.py:48
  57.2 5.1 %collective-permute-start.20 = (bf16[544,128]{1,0:T(8,128)(2,1)S(1)}, bf16[544,128]{1,0:T(8,128)(2,1)S(1)}, u32[]{:S(2)}, u32[]{:S(2)}) collective-permute-start(bf16[544,128]{1,0:T(8,128)(2,1)S(1)} %constant_dynamic-update-slice_fusion.4), channel_id=1, source_target_pairs={{0,1},{1,0},{2,3},{3,2},{4,5},{5,4},{6,7},{7,6},{8,9},{9,8},{10,11... | collective-permute-start | bytes 417800 | tf_op jit(solution)/shard_map/ppermute | solution.py:48
  62.6 7.4 %collective-permute-start.26 = (bf16[288,128]{1,0:T(8,128)(2,1)S(1)}, bf16[288,128]{1,0:T(8,128)(2,1)S(1)}, u32[]{:S(2)}, u32[]{:S(2)}) collective-permute-start(bf16[288,128]{1,0:T(8,128)(2,1)S(1)} %constant_dynamic-update-slice_fusion.15), channel_id=1, source_target_pairs={{0,4},{1,5},{2,6},{3,7},{4,0},{5,1},{6,2},{7,3},{8,12},{9,13},{10,... | collective-permute-start | bytes 221192 | tf_op jit(solution)/shard_map/ppermute | solution.py:48
  65.5 6.3 %collective-permute-start.27 = (bf16[288,128]{1,0:T(8,128)(2,1)S(1)}, bf16[288,128]{1,0:T(8,128)(2,1)S(1)}, u32[]{:S(2)}, u32[]{:S(2)}) collective-permute-start(bf16[288,128]{1,0:T(8,128)(2,1)S(1)} %constant_dynamic-update-slice_fusion.21), channel_id=1, source_target_pairs={{0,6},{1,7},{2,4},{3,5},{4,2},{5,3},{6,0},{7,1},{8,14},{9,15},{10,... | collective-permute-start | bytes 221192 | tf_op jit(solution)/shard_map/ppermute | solution.py:48
  66.8 5.4 %collective-permute-start.25 = (bf16[288,128]{1,0:T(8,128)(2,1)S(1)}, bf16[288,128]{1,0:T(8,128)(2,1)S(1)}, u32[]{:S(2)}, u32[]{:S(2)}) collective-permute-start(bf16[288,128]{1,0:T(8,128)(2,1)S(1)} %constant_dynamic-update-slice_fusion.9), channel_id=1, source_target_pairs={{0,2},{1,3},{2,0},{3,1},{4,6},{5,7},{6,4},{7,5},{8,10},{9,11},{10,... | collective-permute-start | bytes 221192 | tf_op jit(solution)/shard_map/ppermute | solution.py:48
  72.2 4.6 %collective-permute-start.28 = (bf16[1,2,128,128]{3,2,1,0:T(8,128)(2,1)S(1)}, bf16[1,2,128,128]{3,2,1,0:T(8,128)(2,1)S(1)}, u32[]{:S(2)}, u32[]{:S(2)}) collective-permute-start(bf16[1,2,128,128]{3,2,1,0:T(8,128)(2,1)S(1)} %pad_maximum_fusion.2), channel_id=1, source_target_pairs={{0,2},{1,3},{2,0},{3,1},{4,6},{5,7},{6,4},{7,5},{8,10},{9,11},{10,... | collective-permute-start | bytes 196616 | tf_op jit(solution)/shard_map/ppermute | solution.py:48
  72.3 5.4 %collective-permute-start.29 = (bf16[1,2,128,128]{3,2,1,0:T(8,128)(2,1)S(1)}, bf16[1,2,128,128]{3,2,1,0:T(8,128)(2,1)S(1)}, u32[]{:S(2)}, u32[]{:S(2)}) collective-permute-start(bf16[1,2,128,128]{3,2,1,0:T(8,128)(2,1)S(1)} %pad_maximum_fusion.2), channel_id=1, source_target_pairs={{0,4},{1,5},{2,6},{3,7},{4,0},{5,1},{6,2},{7,3},{8,12},{9,13},{10,... | collective-permute-start | bytes 196616 | tf_op jit(solution)/shard_map/ppermute | solution.py:48
  75.5 6.1 %collective-permute-start.30 = (bf16[1,2,128,128]{3,2,1,0:T(8,128)(2,1)S(1)}, bf16[1,2,128,128]{3,2,1,0:T(8,128)(2,1)S(1)}, u32[]{:S(2)}, u32[]{:S(2)}) collective-permute-start(bf16[1,2,128,128]{3,2,1,0:T(8,128)(2,1)S(1)} %pad_maximum_fusion.2), channel_id=1, source_target_pairs={{0,6},{1,7},{2,4},{3,5},{4,2},{5,3},{6,0},{7,1},{8,14},{9,15},{10,... | collective-permute-start | bytes 196616 | tf_op jit(solution)/shard_map/ppermute | solution.py:48
  81.6 6.4 %collective-permute-start.31 = (bf16[4,2,128,128]{3,2,1,0:T(8,128)(2,1)S(1)}, bf16[4,2,128,128]{3,2,1,0:T(8,128)(2,1)S(1)}, u32[]{:S(2)}, u32[]{:S(2)}) collective-permute-start(bf16[4,2,128,128]{3,2,1,0:T(8,128)(2,1)S(1)} %pad_maximum_fusion), channel_id=1, source_target_pairs={{0,1},{1,0},{2,3},{3,2},{4,5},{5,4},{6,7},{7,6},{8,9},{9,8},{10,11... | collective-permute-start | bytes 786440 | tf_op jit(solution)/shard_map/ppermute | solution.py:48

commit v3 on v2

--- a/solution.py
+++ b/solution.py
@@ -74,17 +74,16 @@
     return counts
 
 
-def assembled(pieces, scratch, dsh):
+def assembled(refs, layout, scratch, dsh):
     me = lax.axis_index("ens")
-    for j, ref in enumerate(pieces):
+    for which, first, j in layout:
         start = pl.multiple_of((me ^ j) * dsh, dsh)
-        scratch[pl.ds(start, dsh), :] = ref[...]
+        scratch[pl.ds(start, dsh), :] = refs[which][first : first + dsh, :]
     return scratch[...]
 
 
-def weights_body(n_ens, dsh, n_ref, *refs):
-    q_refs, k_refs = refs[:n_ens], refs[n_ens : 2 * n_ens]
-    mask_ref, nb_ref, nm_ref, w_ref, scratch = refs[2 * n_ens :]
+def weights_body(q_layout, k_layout, dsh, n_ref, mask_ref, nb_ref, nm_ref, *refs):
+    pieces, (w_ref, scratch) = refs[:-2], refs[-2:]
     position = lax.axis_index("pix")
     n_pix = mask_ref.shape[0]
     counts = counts_of(nb_ref, nm_ref, position)
@@ -94,8 +93,8 @@
         lanes.append(jnp.where(mask_ref[pl.ds(row, 1), :] > 0, 1.0, 0.0) * counts[i])
     times = jnp.concatenate(lanes, axis=1)
     bias = jnp.where(times > 0, 0.0, -1e30)
-    queries = dot(n_ref[TILE : 2 * TILE, :], assembled(q_refs, scratch, dsh)).astype(BF16)
-    keys = dot(n_ref[...], assembled(k_refs, scratch, dsh)).astype(BF16)
+    queries = dot(n_ref[TILE : 2 * TILE, :], assembled(pieces, q_layout, scratch, dsh)).astype(BF16)
+    keys = dot(n_ref[...], assembled(pieces, k_layout, scratch, dsh)).astype(BF16)
     lane = lax.broadcasted_iota(jnp.int32, (TILE, LANES), 1)
     for h in range(HEADS):
         cols = slice(h // 2 * LANES, (h // 2 + 1) * LANES)
@@ -108,11 +107,10 @@
         w_ref[h] = (expos / total).astype(BF16)
 
 
-def attend_body(n_ens, dsh, n_ref, *refs):
-    v_refs = refs[:n_ens]
-    w_ref, nb_ref, nm_ref, att_ref, scratch = refs[n_ens:]
+def attend_body(layout, dsh, n_ref, w_ref, nb_ref, nm_ref, *refs):
+    pieces, (att_ref, scratch) = refs[:-2], refs[-2:]
     counts = counts_of(nb_ref, nm_ref, lax.axis_index("pix"))
-    values = dot(n_ref[...], assembled(v_refs, scratch, dsh)).astype(BF16)
+    values = dot(n_ref[...], assembled(pieces, layout, scratch, dsh)).astype(BF16)
     lane = lax.broadcasted_iota(jnp.int32, (TILE, LANES), 1)
     for g in range(HEADS // 2):
         cols = slice(g * LANES, (g + 1) * LANES)
@@ -126,10 +124,9 @@
         att_ref[:, cols] = jnp.where(lane < HD, halves[0], halves[1]).astype(BF16)
 
 
-def forecast_body(n_ens, dsh, x_ref, att_ref, read_ref, *refs):
-    o_refs = refs[:n_ens]
-    f_ref, scratch = refs[n_ens:]
-    hidden = x_ref[0].astype(F32) + dot(att_ref[...], assembled(o_refs, scratch, dsh), NT)
+def forecast_body(layout, dsh, x_ref, att_ref, read_ref, *refs):
+    pieces, (f_ref, wo_ref) = refs[:-2], refs[-2:]
+    hidden = x_ref[0].astype(F32) + dot(att_ref[...], assembled(pieces, layout, wo_ref, dsh), NT)
     f_ref[...] = dot(hidden.astype(BF16), read_ref[...]).astype(BF16)
 
 
@@ -138,10 +135,9 @@
     return mag + 2.0 * BREADTH * jnp.log1p(jnp.exp(mag * (-1.0 / BREADTH)))
 
 
-def backward_body(n_ens, dsh, factor, *refs):
-    f_refs, o_refs = refs[:n_ens], refs[n_ens : 2 * n_ens]
-    target_ref, pw_ref, mask_ref, read_ref, w_ref, nb_ref, nm_ref = refs[2 * n_ens : 2 * n_ens + 7]
-    gf_ref, con_ref, scratch = refs[2 * n_ens + 7 :]
+def backward_body(n_ens, factor, *refs):
+    f_refs = refs[:n_ens]
+    wo_ref, target_ref, pw_ref, mask_ref, read_ref, w_ref, nb_ref, nm_ref, gf_ref, con_ref = refs[n_ens:]
     position = lax.axis_index("pix")
     counts = counts_of(nb_ref, nm_ref, position)
     live = jnp.where(mask_ref[pl.ds(position, 1), :] > 0, 1.0, 0.0)
@@ -167,7 +163,7 @@
         con_ref[3 * TILE :, i * LANES : (i + 1) * LANES] = part
         loss = loss - part.astype(F32)
     grad_hidden = dot(gf_ref[:TILE, :], read_ref[...], NT).astype(BF16)
-    grad_att = dot(grad_hidden, assembled(o_refs, scratch, dsh)).astype(BF16)
+    grad_att = dot(grad_hidden, wo_ref[...]).astype(BF16)
     lane = lax.broadcasted_iota(jnp.int32, (TILE, LANES), 1)
     zero = jnp.zeros((), BF16)
     for g in range(HEADS // 2):
@@ -242,7 +238,20 @@
     for bit in bits:
         held = lax.optimization_barrier(pieces)
         pieces = held | {j ^ bit: xor_permute(piece, axis, bit) for j, piece in held.items()}
+    return pieces
+
+
+def in_order(pieces):
     return [pieces[j] for j in sorted(pieces)]
+
+
+def joined(arrays):
+    return arrays[0] if len(arrays) == 1 else jnp.concatenate(arrays)
+
+
+def both_cores(pieces):
+    held = lax.optimization_barrier(pieces)
+    return in_order(held | {j ^ 1: xor_permute(piece, "ens", 1) for j, piece in held.items()})
 
 
 def at(blocks, index):
@@ -276,12 +285,29 @@
     rows = sample_layer_feed.shape[1]
     assert rows == TILE and n_out == LANES
 
-    q_parts = gathered(w_query, "ens", ens_bits)
-    k_parts = gathered(w_key, "ens", ens_bits)
+    far = ens_bits[:-1]
+    w_out_t = w_out.T
+    qkv = jnp.concatenate([w_query, w_key, w_value])
+    qkv_far = gathered(qkv, "ens", far)
     up = lax.ppermute(sample_layer_feed, "pix", [(i, i + 1) for i in range(n_pix - 1)])
     down = lax.ppermute(sample_layer_feed, "pix", [(i + 1, i) for i in range(n_pix - 1)])
-    v_parts = gathered(w_value, "ens", ens_bits)
-    o_parts = gathered(w_out.T, "ens", ens_bits)
+    qkv_near = xor_permute(qkv, "ens", 1)
+    o_near = xor_permute(w_out_t, "ens", 1)
+    o_far = gathered(w_out_t, "ens", far)
+    up, down, qkv_near, o_near, qkv_far = lax.optimization_barrier((up, down, qkv_near, o_near, qkv_far))
+    shards = sorted(j for j in qkv_far if j)
+    qkv_far = joined([qkv_far[j] for j in shards])
+    qkv_cross = xor_permute(qkv_far, "ens", 1)
+
+    def shard_layout(width, first):
+        table = [(0, first, 0), (1, first, 1)]
+        for i, j in enumerate(shards):
+            table += [(2, i * width * dsh + first, j), (3, i * width * dsh + first, j ^ 1)]
+        return table
+
+    q_layout, k_layout, v_layout = (shard_layout(3, i * dsh) for i in range(3))
+    o_layout = shard_layout(1, 0)
+    qkv_parts = [("v", a) for a in (qkv, qkv_near, qkv_far, qkv_cross)]
 
     mask_rows = pix_mask.reshape(n_pix, TILE)
     half = ((d_model // 2, 3 * TILE), BF16)
@@ -293,52 +319,55 @@
         "normed",
         scratch=[pltpu.VMEM((d_model, 3 * TILE), BF16)],
     )
-    turned_sib = xor_permute(turned_send, "ens", 1)
 
     full = pltpu.VMEM((d_model, inner), BF16)
     (weights,) = call(
-        functools.partial(weights_body, n_ens, dsh),
+        functools.partial(weights_body, q_layout, k_layout, dsh),
         [((HEADS, TILE, 3 * TILE), BF16)],
-        [("v", normed)]
-        + [("v", a) for a in q_parts + k_parts]
-        + [("v", mask_rows), ("s", neighbours), ("s", neighbour_mask)],
-        2 * 10**9,
+        [("v", normed), ("v", mask_rows), ("s", neighbours), ("s", neighbour_mask)]
+        + qkv_parts,
+        10**9,
         "weights",
         scratch=[full],
     )
+    weights, o_far, turned_send = lax.optimization_barrier((weights, o_far, turned_send))
+    o_far = joined([o_far[j] for j in shards])
+    o_cross = xor_permute(o_far, "ens", 1)
+    turned_sib = xor_permute(turned_send, "ens", 1)
     (attended,) = call(
-        functools.partial(attend_body, n_ens, dsh),
+        functools.partial(attend_body, v_layout, dsh),
         [((TILE, inner), BF16)],
-        [("v", normed)]
-        + [("v", a) for a in v_parts]
-        + [("v", weights), ("s", neighbours), ("s", neighbour_mask)],
+        [("v", normed), ("v", weights), ("s", neighbours), ("s", neighbour_mask)]
+        + qkv_parts,
         10**9,
         "attend",
         scratch=[full],
     )
-    (forecast,) = call(
-        functools.partial(forecast_body, n_ens, dsh),
-        [((TILE, LANES), BF16)],
-        [("v", sample_layer_feed), ("v", attended), ("v", readout_matrix)] + [("v", a) for a in o_parts],
+    forecast, w_out_full = call(
+        functools.partial(forecast_body, o_layout, dsh),
+        [((TILE, LANES), BF16), ((d_model, inner), BF16)],
+        [("v", sample_layer_feed), ("v", attended), ("v", readout_matrix)]
+        + [("v", a) for a in (w_out_t, o_near, o_far, o_cross)],
         10**9,
         "forecast",
-        scratch=[full],
-    )
-    forecasts = gathered(forecast, "ens", ens_bits)
-    attended_all = gathered(attended, "ens", ens_bits)
+    )
+    forecasts = in_order(gathered(forecast, "ens", ens_bits))
+    forecast, attended = lax.optimization_barrier((forecast, attended))
+    attended_near = gathered(attended, "ens", far)
 
     factor = 1.0 / math.sqrt(n_ens * n_pix * TILE)
     grads, contrib = call(
-        functools.partial(backward_body, n_ens, dsh, factor),
+        functools.partial(backward_body, n_ens, factor),
         [((n_ens * TILE, LANES), BF16), ((3 * TILE + 16, inner), BF16)],
-        [("v", a) for a in forecasts + o_parts]
+        [("v", a) for a in forecasts + [w_out_full]]
         + [("v", target), ("v", pixel_weight.reshape(1, TILE)), ("v", mask_rows), ("v", readout_matrix)]
         + [("v", weights), ("s", neighbours), ("s", neighbour_mask)],
         10**9,
         "backward",
-        scratch=[full],
-    )
+    )
+    contrib, attended_near = lax.optimization_barrier((contrib, attended_near))
     contrib_sib = xor_permute(contrib, "ens", 1)
+    attended_all = both_cores(attended_near)
     blocks = n_ens // 2
     value_term, loss = call(
         functools.partial(value_body, blocks, dsh),
@@ -347,6 +376,7 @@
         10**9,
         "value_term",
     )
+    value_term, loss, grads = lax.optimization_barrier((value_term, loss, grads))
     (output_term,) = call(
         functools.partial(output_body, n_ens, dsh),
         [((dsh * inner // LANES, LANES), F32)],
@@ -356,15 +386,12 @@
         scratch=[pltpu.VMEM((n_ens * TILE, inner), BF16)],
     )
 
-    for bit in ens_bits[:-1]:
+    for bit in far[:-1]:
         upper = (e // bit) % 2
         halves = value_term.reshape(2, -1, LANES)
-        kept = at(halves, upper)
-        message = with_loss(at(halves, 1 - upper), loss)
-        got, other = split_loss(xor_permute(message, "ens", bit))
-        value_term = kept + got.astype(F32)
+        got, other = split_loss(xor_permute(with_loss(at(halves, 1 - upper), loss), "ens", bit))
+        value_term = at(halves, upper) + got.astype(F32)
         loss = loss + other
-    value_term = value_term.reshape(-1, LANES)
 
     n_bits = n_pix.bit_length() - 1
     groups = [[1]] + [[1 << b for b in range(s, min(s + 2, n_bits))] for s in range(1, n_bits, 2)]
@@ -379,34 +406,56 @@
     split = pieces_of(output_term, groups[0])
     got = exchanged([part_of(split, 1 - p % 2).astype(BF16)], groups[0])[0]
     output_term = part_of(split, p % 2) + got.astype(F32)
-    for group in groups:
+    upper, low = (e // far[-1]) % 2, p % 2
+    quarters = [pieces_of(h, groups[0]) for h in value_term.reshape(2, -1, LANES)]
+    quarters = jnp.stack([part_of(q, i) for q in quarters for i in range(2)])
+    pos = 2 * upper + low
+    received = []
+    for d in (2, 1, 3):
+        pairs = [
+            (i * n_pix + k, (i ^ (far[-1] * (d // 2))) * n_pix + (k ^ (d % 2)))
+            for i in range(n_ens)
+            for k in range(n_pix)
+        ]
+        message = with_loss(at(quarters, pos ^ d), loss)
+        received.append((d, split_loss(lax.ppermute(message, ("ens", "pix"), pairs))))
+    value_term = at(quarters, pos)
+    losses = {0: loss}
+    for d, (block, other) in received:
+        value_term = value_term + block.astype(F32)
+        losses[d] = other
+    losses = jnp.stack([losses[d] for d in range(4)])
+    loss = functools.reduce(jnp.add, [at(losses, pos ^ i) for i in range(4)])
+
+    for group in groups[1:]:
         size, pos = 1 << len(group), (p // group[0]) % (1 << len(group))
-        moving = [value_term] if group == groups[0] else [value_term, output_term]
-        split = [pieces_of(t, group) for t in moving]
+        split = [pieces_of(t, group) for t in (value_term, output_term)]
         messages = [
             with_loss(jnp.concatenate([part_of(s, pos ^ d) for s in split]), loss) for d in range(1, size)
         ]
         received = [split_loss(m) for m in exchanged(messages, group)]
         kept = [part_of(s, pos) for s in split]
         for block, _ in received:
-            block = block.astype(F32).reshape(len(kept), -1, LANES)
+            block = block.astype(F32).reshape(2, -1, LANES)
             kept = [k + block[i] for i, k in enumerate(kept)]
-        value_term = kept[0]
-        output_term = kept[1] if len(kept) > 1 else output_term
+        value_term, output_term = kept
         losses = jnp.stack([loss] + [other for _, other in received])
         loss = functools.reduce(jnp.add, [at(losses, pos ^ i) for i in range(size)])
     terms = [value_term, output_term]
     piece = jnp.stack(terms).astype(BF16)
     pieces = {0: piece}
-    for group in reversed(groups):
-        stack = jnp.stack([pieces[j] for j in sorted(pieces)])
+    pair = {1: xor_permute(piece, "pix", 1)}
+    for group in reversed(groups[1:]):
         keys = sorted(pieces)
-        new = dict(pieces)
-        for d in range(1, 1 << len(group)):
-            got = xor_permute(stack, "pix", d * group[0])
-            for i, j in enumerate(keys):
-                new[j ^ (d * group[0])] = got[i]
-        pieces = new
+        stack = jnp.stack([pieces[j] for j in keys])
+        new = {d: xor_permute(stack, "pix", d * group[0]) for d in range(1, 1 << len(group))}
+        for i, j in enumerate(keys):
+            pieces.update({j ^ (d * group[0]): got[i] for d, got in new.items()})
+    later = [j for j in sorted(pieces) if j]
+    for batch in (later[: len(later) // 3], later[len(later) // 3 :]):
+        got = xor_permute(jnp.stack([pieces[j] for j in batch]), "pix", 1)
+        pair.update({j ^ 1: got[i] for i, j in enumerate(batch)})
+    pieces.update(pair)
     scale = 1.0 / (n_ens * n_pix * TILE * n_out)
     grad_w_value, grad_w_out, loss = call(
         functools.partial(finish_body, n_pix, dsh, scale),

time: 89.4 us -> 85.4 us (0.955)
  waiting for transfers between devices: 42.9 us -> 38.9 us
  starting transfers between devices: 33.8 us -> 31.2 us
  local copies, waits for them, and re-layouts: 2.05 us -> 3.83 us
    ppermute x30 -> x24, waiting for transfers between devices: 41 us -> 26.3 us  [xor_permute(): return lax.ppermute(value, axis, [(i, i ^ mask) for i in range(size)])]
    ppermute x1, waiting for transfers between devices: 1.91 us -> 10 us  [per_device(): lax.ppermute(sample_layer_feed, 'pix', [(i, i + 1) for i in range(n_pix -...]
    ppermute x30 -> x24, starting transfers between devices: 28.6 us -> 21.6 us  [xor_permute(): return lax.ppermute(value, axis, [(i, i ^ mask) for i in range(size)])]
    ppermute x0 -> x3, starting transfers between devices: none -> 4.92 us  [per_device(): lax.ppermute(message, ('ens', 'pix'), pairs)]
    ppermute x0 -> x3, waiting for transfers between devices: none -> 2.63 us  [per_device(): lax.ppermute(message, ('ens', 'pix'), pairs)]
    unnamed x27 -> x30, local copies, waits for them, and re-layouts: 1.9 us -> 3.57 us
  transfers between devices with their start and end apart: 32 -> 29, of which waited for: 17 -> 16; matrix products, arithmetic and copies ran while one was open for 2% -> 1% of each run, Pallas kernels for 6% -> 9%
where the time goes in v3:
time: 85.4 us; the launch traced here: 85.2 us
  waiting for transfers between devices  38.9 us (46%)
  starting transfers between devices  31.2 us (37%)
  Pallas kernels  9.71 us (11%)
  local copies, waits for them, and re-layouts  3.83 us (4%)
  between operations  1.03 us (1%)
    ppermute x24, waiting for transfers between devices, xor_permute(): return lax.ppermute(value, axis, [(i, i ^ mask) for i in range(size)])  26.3 us
    ppermute x24, starting transfers between devices, xor_permute(): return lax.ppermute(value, axis, [(i, i ^ mask) for i in range(size)])  21.6 us
    ppermute x1, waiting for transfers between devices, per_device(): lax.ppermute(sample_layer_feed, 'pix', [(i, i + 1) for i in range(n_pix -...  10 us
    pallas_call x8, Pallas kernels, call(): pl.pallas_call(body, out_shape=[jax.ShapeDtypeStruct(s, d) for s, d in ou...  9.71 us
    ppermute x3, starting transfers between devices, per_device(): lax.ppermute(message, ('ens', 'pix'), pairs)  4.92 us
    unnamed x30, local copies, waits for them, and re-layouts  3.57 us
    ppermute x1, starting transfers between devices, per_device(): lax.ppermute(sample_layer_feed, 'pix', [(i, i + 1) for i in range(n_pix -...  3.43 us
    ppermute x3, waiting for transfers between devices, per_device(): lax.ppermute(message, ('ens', 'pix'), pairs)  2.63 us
  transfers between devices with their start and end apart: 29, of which 16 were waited for; matrix products, arithmetic and copies ran while one was open for 1% of the time, Pallas kernels for 9%

profile of v3, /device:TPU:0, one launch (start us, length us, event | category | flops | bytes accessed | tf_op | source)
XLA Modules:
  0.0 85.2 jit_solution(3241679521486107453)
XLA Ops:
  0.6 1.0 %constant_dynamic-update-slice_fusion.2 = bf16[768,512]{1,0:T(8,128)(2,1)S(1)} fusion(bf16[256,512]{1,0:T(8,128)(2,1)} %param.14), kind=kLoop, calls=%fused_computation.18 | loop fusion | bytes 524288
  1.7 0.0 copy-done.9
  1.7 0.0 copy-start.10
  1.7 0.9 %copy-done.10 = bf16[256,512]{1,0:T(8,128)(2,1)S(1)} copy-done((bf16[256,512]{1,0:T(8,128)(2,1)S(1)}, bf16[256,512]{1,0:T(8,128)(2,1)}, u32[]{:S(2)}) %copy-start.10) | copy-done | bytes 262168
  2.6 0.0 copy-start
  2.7 3.0 %collective-permute-start.4 = (bf16[768,512]{1,0:T(8,128)(2,1)S(1)}, bf16[768,512]{1,0:T(8,128)(2,1)S(1)}, u32[]{:S(2)}, u32[]{:S(2)}) collective-permute-start(bf16[768,512]{1,0:T(8,128)(2,1)S(1)} %constant_dynamic-update-slice_fusion.refs_0_), channel_id=1, source_target_pairs={{0,16},{8,24},{16,0},{24,8},{1,17},{9,25},{17,1},{25,9},{2,18},{10... | collective-permute-start | bytes 2359304 | tf_op jit(solution)/shard_map/ppermute | solution.py:48
  5.7 0.1 copy.15
  5.8 0.6 collective-permute-start.3
  6.4 3.4 %collective-permute-start = (bf16[1,128,1024]{2,1,0:T(8,128)(2,1)S(1)}, bf16[1,128,1024]{2,1,0:T(8,128)(2,1)S(1)}, u32[]{:S(2)}, u32[]{:S(2)}) collective-permute-start(bf16[1,128,1024]{2,1,0:T(8,128)(2,1)S(1)} %copy-done), channel_id=1, source_target_pairs={{0,1},{1,2},{2,3},{3,4},{4,5},{5,6},{6,7},{8,9},{9,10},{10,11},{11... | collective-permute-start | bytes 786440 | tf_op jit(solution)/shard_map/ppermute | solution.py:292
  9.8 1.3 %collective-permute-start.1 = (bf16[1,128,1024]{2,1,0:T(8,128)(2,1)S(1)}, bf16[1,128,1024]{2,1,0:T(8,128)(2,1)S(1)}, u32[]{:S(2)}, u32[]{:S(2)}) collective-permute-start(bf16[1,128,1024]{2,1,0:T(8,128)(2,1)S(1)} %copy-done), channel_id=1, source_target_pairs={{1,0},{2,1},{3,2},{4,3},{5,4},{6,5},{7,6},{9,8},{10,9},{11,10},{12... | collective-permute-start | bytes 786440 | tf_op jit(solution)/shard_map/ppermute | solution.py:293
  11.1 10.0 %collective-permute-done.up_ref = bf16[1,128,1024]{2,1,0:T(8,128)(2,1)S(1)} collective-permute-done((bf16[1,128,1024]{2,1,0:T(8,128)(2,1)S(1)}, bf16[1,128,1024]{2,1,0:T(8,128)(2,1)S(1)}, u32[]{:S(2)}, u32[]{:S(2)}) %collective-permute-start) | collective-permute-done | bytes 262176 | tf_op jit(solution)/shard_map/ppermute | solution.py:292
  21.2 2.0 %collective-permute-done.4.refs_2_ = bf16[768,512]{1,0:T(8,128)(2,1)S(1)} collective-permute-done((bf16[768,512]{1,0:T(8,128)(2,1)S(1)}, bf16[768,512]{1,0:T(8,128)(2,1)S(1)}, u32[]{:S(2)}, u32[]{:S(2)}) %collective-permute-start.4) | collective-permute-done | bytes 786464 | tf_op jit(solution)/shard_map/ppermute | solution.py:48
  23.2 1.7 %collective-permute-start.6 = (bf16[256,512]{1,0:T(8,128)(2,1)S(1)}, bf16[256,512]{1,0:T(8,128)(2,1)S(1)}, u32[]{:S(2)}, u32[]{:S(2)}) collective-permute-start(bf16[256,512]{1,0:T(8,128)(2,1)S(1)} %bitcast.126), channel_id=1, source_target_pairs={{0,16},{8,24},{16,0},{24,8},{1,17},{9,25},{17,1},{25,9},{2,18},{10... | collective-permute-start | bytes 786440 | tf_op jit(solution)/shard_map/ppermute | solution.py:48
  25.0 1.3 %normed.1 = (bf16[384,1024]{1,0:T(8,128)(2,1)S(1)}, bf16[512,384]{1,0:T(8,128)(2,1)S(1)}, bf16[512,384]{1,0:T(8,128)(2,1)}) custom-call(bf16[1,128,1024]{2,1,0:T(8,128)(2,1)S(1)} %copy-done, bf16[1,128,1024]{2,1,0:T(8,128)(2,1)S(1)} %collective-permute-done.up_ref, bf16[1,128,1024]{2,1,0:T(8,128)(2,1)S(1)} %collective-permute-done.1.down_ref, ...), custom_call_target="tpu_custom_call" | custom-call | flops 10000000 | bytes 1048576 | tf_op jit(solution)/shard_map/normed/pallas_call | solution.py:34
  26.3 0.6 copy-done.3
  27.0 0.0 copy-done.4
  27.0 2.2 %weights.1.w_ref.refs_9_ = bf16[8,128,384]{2,1,0:T(8,128)(2,1)S(1)} custom-call(bf16[384,1024]{1,0:T(8,128)(2,1)S(1)} %get-tuple-element.37.n_ref, s32[8,128]{1,0:T(8,128)S(1)} %bitcast.134, s32[1,9]{1,0:T(1,128)S(1)} %copy-done.3, s32[1,9]{1,0:T(1,128)S(1)} %copy-done.4, bf16[768,512]{1,0:T(8,128)(2,1)S(1)} %constant_dynamic-update-slice_fusion.refs_0_, ...), custom_call_target="tpu_custom_call" | custom-call | flops 1000000000 | bytes 1048576 | tf_op jit(solution)/shard_map/weights/pallas_call | solution.py:34
  29.2 2.7 %collective-permute-done.6.refs_2_ = bf16[256,512]{1,0:T(8,128)(2,1)S(1)} collective-permute-done((bf16[256,512]{1,0:T(8,128)(2,1)S(1)}, bf16[256,512]{1,0:T(8,128)(2,1)S(1)}, u32[]{:S(2)}, u32[]{:S(2)}) %collective-permute-start.6) | collective-permute-done | bytes 262176 | tf_op jit(solution)/shard_map/ppermute | solution.py:48
  31.9 1.5 %attend.1.att_ref.refs_0_ = bf16[128,512]{1,0:T(8,128)(2,1)S(1)} custom-call(bf16[384,1024]{1,0:T(8,128)(2,1)S(1)} %get-tuple-element.37.n_ref, bf16[8,128,384]{2,1,0:T(8,128)(2,1)S(1)} %weights.1.w_ref.refs_9_, s32[1,9]{1,0:T(1,128)S(1)} %copy-done.3, s32[1,9]{1,0:T(1,128)S(1)} %copy-done.4, bf16[768,512]{1,0:T(8,128)(2,1)S(1)} %constant_dynamic-update-slice_fusion.refs_0_, ...), custom_call_target="tpu_custom_call" | custom-call | flops 1000000000 | bytes 1048576 | tf_op jit(solution)/shard_map/attend/pallas_call | solution.py:34
  33.5 0.0 copy-start.7
  33.5 0.7 forecast.1
  34.2 1.8 %collective-permute-start.9 = (bf16[128,128]{1,0:T(8,128)(2,1)S(1)}, bf16[128,128]{1,0:T(8,128)(2,1)S(1)}, u32[]{:S(2)}, u32[]{:S(2)}) collective-permute-start(bf16[128,128]{1,0:T(8,128)(2,1)S(1)} %get-tuple-element.46.refs_0_), channel_id=1, source_target_pairs={{0,16},{8,24},{16,0},{24,8},{1,17},{9,25},{17,1},{25,9},{2,18},{10... | collective-permute-start | bytes 98312 | tf_op jit(solution)/shard_map/ppermute | solution.py:48
  36.0 0.3 collective-permute-start.12
  36.3 1.9 %collective-permute-done.9.refs_2_ = bf16[128,128]{1,0:T(8,128)(2,1)S(1)} collective-permute-done((bf16[128,128]{1,0:T(8,128)(2,1)S(1)}, bf16[128,128]{1,0:T(8,128)(2,1)S(1)}, u32[]{:S(2)}, u32[]{:S(2)}) %collective-permute-start.9) | collective-permute-done | bytes 32800 | tf_op jit(solution)/shard_map/ppermute | solution.py:48
  38.2 0.5 collective-permute-start.11
  38.7 0.7 collective-permute-done.10.refs_1_
  39.4 0.2 collective-permute-done.11.refs_3_
  39.6 0.7 copy-done.8
  40.2 1.6 %backward.1 = (bf16[512,128]{1,0:T(8,128)(2,1)S(1)}, bf16[400,512]{1,0:T(8,128)(2,1)S(1)}) custom-call(bf16[128,128]{1,0:T(8,128)(2,1)S(1)} %get-tuple-element.46.refs_0_, bf16[128,128]{1,0:T(8,128)(2,1)S(1)} %collective-permute-done.10.refs_1_, bf16[128,128]{1,0:T(8,128)(2,1)S(1)} %collective-permute-done.9.refs_2_, ...), custom_call_target="tpu_custom_call" | custom-call | flops 1000000000 | bytes 1048576 | tf_op jit(solution)/shard_map/backward/pallas_call | solution.py:34
  41.8 0.4 collective-permute-start.13
  42.2 0.2 collective-permute-start.7
  42.4 0.3 collective-permute-start.17
  42.7 0.2 collective-permute-start.18
  42.9 1.9 %collective-permute-done.7.sib_ref = bf16[512,384]{1,0:T(8,128)(2,1)S(1)} collective-permute-done((bf16[512,384]{1,0:T(8,128)(2,1)}, bf16[512,384]{1,0:T(8,128)(2,1)S(1)}, u32[]{:S(2)}, u32[]{:S(2)}) %collective-permute-start.7) | collective-permute-done | bytes 393248 | tf_op jit(solution)/shard_map/ppermute | solution.py:48
  44.8 0.7 value_term.1
  45.5 0.1 fusion.32
  45.6 0.1 pad_maximum_fusion
  45.7 0.0 copy-start.6
  45.7 0.1 fusion.3
  45.9 3.0 %collective-permute-start.16 = (bf16[544,128]{1,0:T(8,128)(2,1)S(1)}, bf16[544,128]{1,0:T(8,128)(2,1)S(1)}, u32[]{:S(2)}, u32[]{:S(2)}) collective-permute-start(bf16[544,128]{1,0:T(8,128)(2,1)S(1)} %constant_dynamic-update-slice_fusion.11), channel_id=1, source_target_pairs={{0,17},{1,16},{2,19},{3,18},{4,21},{5,20},{6,23},{7,22},{8,25},{9,... | collective-permute-start | bytes 417800 | tf_op jit(solution)/shard_map/ppermute | solution.py:421
  48.9 0.3 collective-permute-start.14
  49.2 0.4 output_term.1
  49.6 0.5 collective-permute-start.19
  50.1 1.6 %collective-permute-start.15 = (bf16[544,128]{1,0:T(8,128)(2,1)S(1)}, bf16[544,128]{1,0:T(8,128)(2,1)S(1)}, u32[]{:S(2)}, u32[]{:S(2)}) collective-permute-start(bf16[544,128]{1,0:T(8,128)(2,1)S(1)} %constant_dynamic-update-slice_fusion.7), channel_id=1, source_target_pairs={{0,1},{1,0},{2,3},{3,2},{4,5},{5,4},{6,7},{7,6},{8,9},{9,8},{10,11... | collective-permute-start | bytes 417800 | tf_op jit(solution)/shard_map/ppermute | solution.py:421
  51.8 4.4 %collective-permute-done.19 = bf16[512,128]{1,0:T(8,128)(2,1)S(1)} collective-permute-done((bf16[512,128]{1,0:T(8,128)(2,1)S(1)}, bf16[512,128]{1,0:T(8,128)(2,1)S(1)}, u32[]{:S(2)}, u32[]{:S(2)}) %collective-permute-start.19) | collective-permute-done | bytes 131104 | tf_op jit(solution)/shard_map/ppermute | solution.py:48
  56.2 2.6 %collective-permute-done.15 = bf16[544,128]{1,0:T(8,128)(2,1)S(1)} collective-permute-done((bf16[544,128]{1,0:T(8,128)(2,1)S(1)}, bf16[544,128]{1,0:T(8,128)(2,1)S(1)}, u32[]{:S(2)}, u32[]{:S(2)}) %collective-permute-start.15) | collective-permute-done | bytes 139296 | tf_op jit(solution)/shard_map/ppermute | solution.py:421
  58.9 0.1 fusion.1
  59.1 2.6 %collective-permute-start.21 = (bf16[288,128]{1,0:T(8,128)(2,1)S(1)}, bf16[288,128]{1,0:T(8,128)(2,1)S(1)}, u32[]{:S(2)}, u32[]{:S(2)}) collective-permute-start(bf16[288,128]{1,0:T(8,128)(2,1)S(1)} %constant_dynamic-update-slice_fusion.21), channel_id=1, source_target_pairs={{0,4},{1,5},{2,6},{3,7},{4,0},{5,1},{6,2},{7,3},{8,12},{9,13},{10,... | collective-permute-start | bytes 221192 | tf_op jit(solution)/shard_map/ppermute | solution.py:48
  61.8 1.3 %collective-permute-start.22 = (bf16[288,128]{1,0:T(8,128)(2,1)S(1)}, bf16[288,128]{1,0:T(8,128)(2,1)S(1)}, u32[]{:S(2)}, u32[]{:S(2)}) collective-permute-start(bf16[288,128]{1,0:T(8,128)(2,1)S(1)} %constant_dynamic-update-slice_fusion.27), channel_id=1, source_target_pairs={{0,6},{1,7},{2,4},{3,5},{4,2},{5,3},{6,0},{7,1},{8,14},{9,15},{10,... | collective-permute-start | bytes 221192 | tf_op jit(solution)/shard_map/ppermute | solution.py:48
  63.1 0.3 collective-permute-start.20
  63.4 3.5 %collective-permute-done.21 = bf16[288,128]{1,0:T(8,128)(2,1)S(1)} collective-permute-done((bf16[288,128]{1,0:T(8,128)(2,1)S(1)}, bf16[288,128]{1,0:T(8,128)(2,1)S(1)}, u32[]{:S(2)}, u32[]{:S(2)}) %collective-permute-start.21) | collective-permute-done | bytes 73760 | tf_op jit(solution)/shard_map/ppermute | solution.py:48
  67.0 1.2 %collective-permute-done.22 = bf16[288,128]{1,0:T(8,128)(2,1)S(1)} collective-permute-done((bf16[288,128]{1,0:T(8,128)(2,1)S(1)}, bf16[288,128]{1,0:T(8,128)(2,1)S(1)}, u32[]{:S(2)}, u32[]{:S(2)}) %collective-permute-start.22) | collective-permute-done | bytes 73760 | tf_op jit(solution)/shard_map/ppermute | solution.py:48
  68.2 0.3 collective-permute-done.20
  68.6 3.0 %collective-permute-start.26 = (bf16[1,2,128,128]{3,2,1,0:T(8,128)(2,1)S(1)}, bf16[1,2,128,128]{3,2,1,0:T(8,128)(2,1)S(1)}, u32[]{:S(2)}, u32[]{:S(2)}) collective-permute-start(bf16[1,2,128,128]{3,2,1,0:T(8,128)(2,1)S(1)} %pad_maximum_fusion.3), channel_id=1, source_target_pairs={{0,4},{1,5},{2,6},{3,7},{4,0},{5,1},{6,2},{7,3},{8,12},{9,13},{10,... | collective-permute-start | bytes 196616 | tf_op jit(solution)/shard_map/ppermute | solution.py:48
  71.6 0.5 collective-permute-start.27
  72.1 0.2 collective-permute-start.24
  72.4 1.9 %collective-permute-start.23 = (bf16[2,128,128]{2,1,0:T(8,128)(2,1)S(1)}, bf16[2,128,128]{2,1,0:T(8,128)(2,1)S(1)}, u32[]{:S(2)}, u32[]{:S(2)}) collective-permute-start(bf16[2,128,128]{2,1,0:T(8,128)(2,1)S(1)} %pad_maximum_fusion.2.refs_0_), channel_id=1, source_target_pairs={{0,1},{1,0},{2,3},{3,2},{4,5},{5,4},{6,7},{7,6},{8,9},{9,8},{10,11... | collective-permute-start | bytes 196616 | tf_op jit(solution)/shard_map/ppermute | solution.py:48
  74.3 1.0 %collective-permute-done.26 = bf16[1,2,128,128]{3,2,1,0:T(8,128)(2,1)S(1)} collective-permute-done((bf16[1,2,128,128]{3,2,1,0:T(8,128)(2,1)S(1)}, bf16[1,2,128,128]{3,2,1,0:T(8,128)(2,1)S(1)}, u32[]{:S(2)}, u32[]{:S(2)}) %collective-permute-start.26) | collective-permute-done | bytes 65568 | tf_op jit(solution)/shard_map/ppermute | solution.py:48
  75.3 2.4 %collective-permute-done.27 = bf16[1,2,128,128]{3,2,1,0:T(8,128)(2,1)S(1)} collective-permute-done((bf16[1,2,128,128]{3,2,1,0:T(8,128)(2,1)S(1)}, bf16[1,2,128,128]{3,2,1,0:T(8,128)(2,1)S(1)}, u32[]{:S(2)}, u32[]{:S(2)}) %collective-permute-start.27) | collective-permute-done | bytes 65568 | tf_op jit(solution)/shard_map/ppermute | solution.py:48
  77.8 1.9 %collective-permute-start.28 = (bf16[2,2,128,128]{3,2,1,0:T(8,128)(2,1)S(1)}, bf16[2,2,128,128]{3,2,1,0:T(8,128)(2,1)S(1)}, u32[]{:S(2)}, u32[]{:S(2)}) collective-permute-start(bf16[2,2,128,128]{3,2,1,0:T(8,128)(2,1)S(1)} %pad_maximum_fusion.1), channel_id=1, source_target_pairs={{0,1},{1,0},{2,3},{3,2},{4,5},{5,4},{6,7},{7,6},{8,9},{9,8},{10,11... | collective-permute-start | bytes 393224 | tf_op jit(solution)/shard_map/ppermute | solution.py:48
  79.6 0.3 collective-permute-start.25
  79.9 2.9 %collective-permute-done.28 = bf16[2,2,128,128]{3,2,1,0:T(8,128)(2,1)S(1)} collective-permute-done((bf16[2,2,128,128]{3,2,1,0:T(8,128)(2,1)S(1)}, bf16[2,2,128,128]{3,2,1,0:T(8,128)(2,1)S(1)}, u32[]{:S(2)}, u32[]{:S(2)}) %collective-permute-start.28) | collective-permute-done | bytes 131104 | tf_op jit(solution)/shard_map/ppermute | solution.py:48
  82.8 1.2 %collective-permute-done.25 = bf16[1,2,128,128]{3,2,1,0:T(8,128)(2,1)S(1)} collective-permute-done((bf16[1,2,128,128]{3,2,1,0:T(8,128)(2,1)S(1)}, bf16[1,2,128,128]{3,2,1,0:T(8,128)(2,1)S(1)}, u32[]{:S(2)}, u32[]{:S(2)}) %collective-permute-start.25) | collective-permute-done | bytes 65568 | tf_op jit(solution)/shard_map/ppermute | solution.py:48
  84.0 1.2 %finish.1 = (f32[256,512]{1,0:T(8,128)}, f32[512,256]{1,0:T(8,128)}, f32[1,1]{1,0:T(1,128)}) custom-call(bf16[2,128,128]{2,1,0:T(8,128)(2,1)S(1)} %pad_maximum_fusion.2.refs_0_, bf16[2,128,128]{2,1,0:T(8,128)(2,1)S(1)} %collective-permute-done.23.refs_1_, bf16[2,128,128]{2,1,0:T(8,128)(2,1)S(1)} %bitcast.131, bf16[2,128,128]{2,1,0:T(8,128)(2,1)S(1)} %bitcast.132, ...), custom_call_target="tpu_custom_call" | custom-call | flops 1000000 | bytes 1048576 | tf_op jit(solution)/shard_map/finish/pallas_call | solution.py:34
  (78 shorter events, 0.7 us)
Async XLA Ops:
  0.6 1.0 %copy-start.9 = (bf16[256,512]{1,0:T(8,128)(2,1)S(1)}, bf16[256,512]{1,0:T(8,128)(2,1)}, u32[]{:S(2)}) copy-start(bf16[256,512]{1,0:T(8,128)(2,1)} %param.15) | copy-start | bytes 786436
  1.7 1.0 %copy-start.10 = (bf16[256,512]{1,0:T(8,128)(2,1)S(1)}, bf16[256,512]{1,0:T(8,128)(2,1)}, u32[]{:S(2)}) copy-start(bf16[256,512]{1,0:T(8,128)(2,1)} %param.16) | copy-start | bytes 786436
  2.6 3.0 %copy-start.11 = (bf16[512,256]{1,0:T(8,128)(2,1)S(1)}, bf16[512,256]{1,0:T(8,128)(2,1)}, u32[]{:S(2)}) copy-start(bf16[512,256]{1,0:T(8,128)(2,1)} %param.17) | copy-start | bytes 786436
  2.6 3.7 %copy-start = (bf16[1,128,1024]{2,1,0:T(8,128)(2,1)S(1)}, bf16[1,128,1024]{2,1,0:T(8,128)(2,1)}, u32[]{:S(2)}) copy-start(bf16[1,128,1024]{2,1,0:T(8,128)(2,1)} %x_ref.3) | copy-start | bytes 786436
  2.7 20.5 %collective-permute-start.4 = (bf16[768,512]{1,0:T(8,128)(2,1)S(1)}, bf16[768,512]{1,0:T(8,128)(2,1)S(1)}, u32[]{:S(2)}, u32[]{:S(2)}) collective-permute-start(bf16[768,512]{1,0:T(8,128)(2,1)S(1)} %constant_dynamic-update-slice_fusion.refs_0_), channel_id=1, source_target_pairs={{0,16},{8,24},{16,0},{24,8},{1,17},{9,25},{17,1},{25,9},{2,18},{10... | collective-permute-start | bytes 2359304 | tf_op jit(solution)/shard_map/ppermute | solution.py:48
  5.7 17.5 %collective-permute-start.2 = (bf16[768,512]{1,0:T(8,128)(2,1)S(1)}, bf16[768,512]{1,0:T(8,128)(2,1)S(1)}, u32[]{:S(2)}, u32[]{:S(2)}) collective-permute-start(bf16[768,512]{1,0:T(8,128)(2,1)S(1)} %constant_dynamic-update-slice_fusion.refs_0_), channel_id=1, source_target_pairs={{0,8},{8,0},{16,24},{24,16},{1,9},{9,1},{17,25},{25,17},{2,10},{10... | collective-permute-start | bytes 2359304 | tf_op jit(solution)/shard_map/ppermute | solution.py:48
  5.7 19.3 %copy-start.1 = (f32[1024]{0:T(1024)S(1)}, f32[1024]{0:T(1024)}, u32[]{:S(2)}) copy-start(f32[1024]{0:T(1024)} %param.13) | copy-start | bytes 12292
  5.8 5.3 %collective-permute-start.3 = (bf16[256,512]{1,0:T(8,128)(2,1)S(1)}, bf16[256,512]{1,0:T(8,128)(2,1)S(1)}, u32[]{:S(2)}, u32[]{:S(2)}) collective-permute-start(bf16[256,512]{1,0:T(8,128)(2,1)S(1)} %bitcast.125), channel_id=1, source_target_pairs={{0,8},{8,0},{16,24},{24,16},{1,9},{9,1},{17,25},{25,17},{2,10},{10... | collective-permute-start | bytes 786440 | tf_op jit(solution)/shard_map/ppermute | solution.py:48
  6.4 14.8 %collective-permute-start = (bf16[1,128,1024]{2,1,0:T(8,128)(2,1)S(1)}, bf16[1,128,1024]{2,1,0:T(8,128)(2,1)S(1)}, u32[]{:S(2)}, u32[]{:S(2)}) collective-permute-start(bf16[1,128,1024]{2,1,0:T(8,128)(2,1)S(1)} %copy-done), channel_id=1, source_target_pairs={{0,1},{1,2},{2,3},{3,4},{4,5},{5,6},{6,7},{8,9},{9,10},{10,11},{11... | collective-permute-start | bytes 786440 | tf_op jit(solution)/shard_map/ppermute | solution.py:292
  9.8 11.3 %collective-permute-start.1 = (bf16[1,128,1024]{2,1,0:T(8,128)(2,1)S(1)}, bf16[1,128,1024]{2,1,0:T(8,128)(2,1)S(1)}, u32[]{:S(2)}, u32[]{:S(2)}) collective-permute-start(bf16[1,128,1024]{2,1,0:T(8,128)(2,1)S(1)} %copy-done), channel_id=1, source_target_pairs={{1,0},{2,1},{3,2},{4,3},{5,4},{6,5},{7,6},{9,8},{10,9},{11,10},{12... | collective-permute-start | bytes 786440 | tf_op jit(solution)/shard_map/ppermute | solution.py:293
  23.2 3.1 %collective-permute-start.5 = (bf16[768,512]{1,0:T(8,128)(2,1)S(1)}, bf16[768,512]{1,0:T(8,128)(2,1)S(1)}, u32[]{:S(2)}, u32[]{:S(2)}) collective-permute-start(bf16[768,512]{1,0:T(8,128)(2,1)S(1)} %collective-permute-done.4.refs_2_), channel_id=1, source_target_pairs={{0,8},{8,0},{16,24},{24,16},{1,9},{9,1},{17,25},{25,17},{2,10},{10... | collective-permute-start | bytes 2359304 | tf_op jit(solution)/shard_map/ppermute | solution.py:48
  23.2 8.7 %collective-permute-start.6 = (bf16[256,512]{1,0:T(8,128)(2,1)S(1)}, bf16[256,512]{1,0:T(8,128)(2,1)S(1)}, u32[]{:S(2)}, u32[]{:S(2)}) collective-permute-start(bf16[256,512]{1,0:T(8,128)(2,1)S(1)} %bitcast.126), channel_id=1, source_target_pairs={{0,16},{8,24},{16,0},{24,8},{1,17},{9,25},{17,1},{25,9},{2,18},{10... | collective-permute-start | bytes 786440 | tf_op jit(solution)/shard_map/ppermute | solution.py:48
  24.9 1.4 %copy-start.2 = (s32[1024]{0:T(1024)S(1)}, s32[1024]{0:T(1024)}, u32[]{:S(2)}) copy-start(s32[1024]{0:T(1024)} %param.21) | copy-start | bytes 12292
  26.3 0.7 copy-start.3
  26.3 0.7 copy-start.4
  31.9 1.6 %copy-start.5 = (bf16[1024,128]{1,0:T(8,128)(2,1)S(1)}, bf16[1024,128]{1,0:T(8,128)(2,1)}, u32[]{:S(2)}) copy-start(bf16[1024,128]{1,0:T(8,128)(2,1)} %read_ref.3) | copy-start | bytes 786436
  31.9 1.6 %collective-permute-start.8 = (bf16[256,512]{1,0:T(8,128)(2,1)S(1)}, bf16[256,512]{1,0:T(8,128)(2,1)S(1)}, u32[]{:S(2)}, u32[]{:S(2)}) collective-permute-start(bf16[256,512]{1,0:T(8,128)(2,1)S(1)} %collective-permute-done.6.refs_2_), channel_id=1, source_target_pairs={{0,8},{8,0},{16,24},{24,16},{1,9},{9,1},{17,25},{25,17},{2,10},{10... | collective-permute-start | bytes 786440 | tf_op jit(solution)/shard_map/ppermute | solution.py:48
  33.5 6.1 %copy-start.7 = (f32[128,128]{1,0:T(8,128)S(1)}, f32[128,128]{1,0:T(8,128)}, u32[]{:S(2)}) copy-start(f32[128,128]{1,0:T(8,128)} %refs_5_.1) | copy-start | bytes 196612
  34.2 4.0 %collective-permute-start.9 = (bf16[128,128]{1,0:T(8,128)(2,1)S(1)}, bf16[128,128]{1,0:T(8,128)(2,1)S(1)}, u32[]{:S(2)}, u32[]{:S(2)}) collective-permute-start(bf16[128,128]{1,0:T(8,128)(2,1)S(1)} %get-tuple-element.46.refs_0_), channel_id=1, source_target_pairs={{0,16},{8,24},{16,0},{24,8},{1,17},{9,25},{17,1},{25,9},{2,18},{10... | collective-permute-start | bytes 98312 | tf_op jit(solution)/shard_map/ppermute | solution.py:48
  36.0 5.8 %collective-permute-start.12 = (bf16[128,512]{1,0:T(8,128)(2,1)S(1)}, bf16[128,512]{1,0:T(8,128)(2,1)S(1)}, u32[]{:S(2)}, u32[]{:S(2)}) collective-permute-start(bf16[128,512]{1,0:T(8,128)(2,1)S(1)} %attend.1.att_ref.refs_0_), channel_id=1, source_target_pairs={{0,16},{8,24},{16,0},{24,8},{1,17},{9,25},{17,1},{25,9},{2,18},{10... | collective-permute-start | bytes 393224 | tf_op jit(solution)/shard_map/ppermute | solution.py:48
  38.2 1.2 %collective-permute-start.10 = (bf16[128,128]{1,0:T(8,128)(2,1)S(1)}, bf16[128,128]{1,0:T(8,128)(2,1)S(1)}, u32[]{:S(2)}, u32[]{:S(2)}) collective-permute-start(bf16[128,128]{1,0:T(8,128)(2,1)S(1)} %get-tuple-element.46.refs_0_), channel_id=1, source_target_pairs={{0,8},{8,0},{16,24},{24,16},{1,9},{9,1},{17,25},{25,17},{2,10},{10... | collective-permute-start | bytes 98312 | tf_op jit(solution)/shard_map/ppermute | solution.py:48
  38.2 1.4 %collective-permute-start.11 = (bf16[128,128]{1,0:T(8,128)(2,1)S(1)}, bf16[128,128]{1,0:T(8,128)(2,1)S(1)}, u32[]{:S(2)}, u32[]{:S(2)}) collective-permute-start(bf16[128,128]{1,0:T(8,128)(2,1)S(1)} %collective-permute-done.9.refs_2_), channel_id=1, source_target_pairs={{0,8},{8,0},{16,24},{24,16},{1,9},{9,1},{17,25},{25,17},{2,10},{10... | collective-permute-start | bytes 98312 | tf_op jit(solution)/shard_map/ppermute | solution.py:48
  39.6 0.7 copy-start.8
  41.8 3.0 %collective-permute-start.13 = (bf16[400,512]{1,0:T(8,128)(2,1)S(1)}, bf16[400,512]{1,0:T(8,128)(2,1)S(1)}, u32[]{:S(2)}, u32[]{:S(2)}) collective-permute-start(bf16[400,512]{1,0:T(8,128)(2,1)S(1)} %get-tuple-element.51.own_con), channel_id=1, source_target_pairs={{0,8},{8,0},{16,24},{24,16},{1,9},{9,1},{17,25},{25,17},{2,10},{10... | collective-permute-start | bytes 1228808 | tf_op jit(solution)/shard_map/ppermute | solution.py:48
  42.2 2.5 %collective-permute-start.7 = (bf16[512,384]{1,0:T(8,128)(2,1)}, bf16[512,384]{1,0:T(8,128)(2,1)S(1)}, u32[]{:S(2)}, u32[]{:S(2)}) collective-permute-start(bf16[512,384]{1,0:T(8,128)(2,1)} %get-tuple-element.41), channel_id=1, source_target_pairs={{0,8},{8,0},{16,24},{24,16},{1,9},{9,1},{17,25},{25,17},{2,10},{10... | collective-permute-start | bytes 1179656 | tf_op jit(solution)/shard_map/ppermute | solution.py:48
  42.4 6.8 %collective-permute-start.17 = (bf16[128,512]{1,0:T(8,128)(2,1)S(1)}, bf16[128,512]{1,0:T(8,128)(2,1)S(1)}, u32[]{:S(2)}, u32[]{:S(2)}) collective-permute-start(bf16[128,512]{1,0:T(8,128)(2,1)S(1)} %attend.1.att_ref.refs_0_), channel_id=1, source_target_pairs={{0,8},{8,0},{16,24},{24,16},{1,9},{9,1},{17,25},{25,17},{2,10},{10... | collective-permute-start | bytes 393224 | tf_op jit(solution)/shard_map/ppermute | solution.py:48
  42.7 6.4 %collective-permute-start.18 = (bf16[128,512]{1,0:T(8,128)(2,1)S(1)}, bf16[128,512]{1,0:T(8,128)(2,1)S(1)}, u32[]{:S(2)}, u32[]{:S(2)}) collective-permute-start(bf16[128,512]{1,0:T(8,128)(2,1)S(1)} %collective-permute-done.12.refs_2_), channel_id=1, source_target_pairs={{0,8},{8,0},{16,24},{24,16},{1,9},{9,1},{17,25},{25,17},{2,10},{10... | collective-permute-start | bytes 393224 | tf_op jit(solution)/shard_map/ppermute | solution.py:48
  45.7 3.4 %copy-start.6 = (bf16[1024,128]{1,0:T(8,128)(2,1)S(1)}, bf16[1024,128]{1,0:T(8,128)(2,1)}, u32[]{:S(2)}) copy-start(bf16[1024,128]{1,0:T(8,128)(2,1)} %read_ref.3) | copy-start | bytes 786436
  45.9 10.3 %collective-permute-start.16 = (bf16[544,128]{1,0:T(8,128)(2,1)S(1)}, bf16[544,128]{1,0:T(8,128)(2,1)S(1)}, u32[]{:S(2)}, u32[]{:S(2)}) collective-permute-start(bf16[544,128]{1,0:T(8,128)(2,1)S(1)} %constant_dynamic-update-slice_fusion.11), channel_id=1, source_target_pairs={{0,17},{1,16},{2,19},{3,18},{4,21},{5,20},{6,23},{7,22},{8,25},{9,... | collective-permute-start | bytes 417800 | tf_op jit(solution)/shard_map/ppermute | solution.py:421
  48.9 7.3 %collective-permute-start.14 = (bf16[544,128]{1,0:T(8,128)(2,1)S(1)}, bf16[544,128]{1,0:T(8,128)(2,1)S(1)}, u32[]{:S(2)}, u32[]{:S(2)}) collective-permute-start(bf16[544,128]{1,0:T(8,128)(2,1)S(1)} %constant_dynamic-update-slice_fusion.3), channel_id=1, source_target_pairs={{0,16},{1,17},{2,18},{3,19},{4,20},{5,21},{6,22},{7,23},{8,24},{9,... | collective-permute-start | bytes 417800 | tf_op jit(solution)/shard_map/ppermute | solution.py:421
  49.6 6.5 %collective-permute-start.19 = (bf16[512,128]{1,0:T(8,128)(2,1)S(1)}, bf16[512,128]{1,0:T(8,128)(2,1)S(1)}, u32[]{:S(2)}, u32[]{:S(2)}) collective-permute-start(bf16[512,128]{1,0:T(8,128)(2,1)S(1)} %bitcast.151), channel_id=1, source_target_pairs={{0,1},{1,0},{2,3},{3,2},{4,5},{5,4},{6,7},{7,6},{8,9},{9,8},{10,11... | collective-permute-start | bytes 393224 | tf_op jit(solution)/shard_map/ppermute | solution.py:48
  50.1 8.8 %collective-permute-start.15 = (bf16[544,128]{1,0:T(8,128)(2,1)S(1)}, bf16[544,128]{1,0:T(8,128)(2,1)S(1)}, u32[]{:S(2)}, u32[]{:S(2)}) collective-permute-start(bf16[544,128]{1,0:T(8,128)(2,1)S(1)} %constant_dynamic-update-slice_fusion.7), channel_id=1, source_target_pairs={{0,1},{1,0},{2,3},{3,2},{4,5},{5,4},{6,7},{7,6},{8,9},{9,8},{10,11... | collective-permute-start | bytes 417800 | tf_op jit(solution)/shard_map/ppermute | solution.py:421
  59.1 7.9 %collective-permute-start.21 = (bf16[288,128]{1,0:T(8,128)(2,1)S(1)}, bf16[288,128]{1,0:T(8,128)(2,1)S(1)}, u32[]{:S(2)}, u32[]{:S(2)}) collective-permute-start(bf16[288,128]{1,0:T(8,128)(2,1)S(1)} %constant_dynamic-update-slice_fusion.21), channel_id=1, source_target_pairs={{0,4},{1,5},{2,6},{3,7},{4,0},{5,1},{6,2},{7,3},{8,12},{9,13},{10,... | collective-permute-start | bytes 221192 | tf_op jit(solution)/shard_map/ppermute | solution.py:48
  61.8 6.4 %collective-permute-start.22 = (bf16[288,128]{1,0:T(8,128)(2,1)S(1)}, bf16[288,128]{1,0:T(8,128)(2,1)S(1)}, u32[]{:S(2)}, u32[]{:S(2)}) collective-permute-start(bf16[288,128]{1,0:T(8,128)(2,1)S(1)} %constant_dynamic-update-slice_fusion.27), channel_id=1, source_target_pairs={{0,6},{1,7},{2,4},{3,5},{4,2},{5,3},{6,0},{7,1},{8,14},{9,15},{10,... | collective-permute-start | bytes 221192 | tf_op jit(solution)/shard_map/ppermute | solution.py:48
  63.1 5.4 %collective-permute-start.20 = (bf16[288,128]{1,0:T(8,128)(2,1)S(1)}, bf16[288,128]{1,0:T(8,128)(2,1)S(1)}, u32[]{:S(2)}, u32[]{:S(2)}) collective-permute-start(bf16[288,128]{1,0:T(8,128)(2,1)S(1)} %constant_dynamic-update-slice_fusion.15), channel_id=1, source_target_pairs={{0,2},{1,3},{2,0},{3,1},{4,6},{5,7},{6,4},{7,5},{8,10},{9,11},{10,... | collective-permute-start | bytes 221192 | tf_op jit(solution)/shard_map/ppermute | solution.py:48
  68.6 6.7 %collective-permute-start.26 = (bf16[1,2,128,128]{3,2,1,0:T(8,128)(2,1)S(1)}, bf16[1,2,128,128]{3,2,1,0:T(8,128)(2,1)S(1)}, u32[]{:S(2)}, u32[]{:S(2)}) collective-permute-start(bf16[1,2,128,128]{3,2,1,0:T(8,128)(2,1)S(1)} %pad_maximum_fusion.3), channel_id=1, source_target_pairs={{0,4},{1,5},{2,6},{3,7},{4,0},{5,1},{6,2},{7,3},{8,12},{9,13},{10,... | collective-permute-start | bytes 196616 | tf_op jit(solution)/shard_map/ppermute | solution.py:48
  71.6 6.2 %collective-permute-start.27 = (bf16[1,2,128,128]{3,2,1,0:T(8,128)(2,1)S(1)}, bf16[1,2,128,128]{3,2,1,0:T(8,128)(2,1)S(1)}, u32[]{:S(2)}, u32[]{:S(2)}) collective-permute-start(bf16[1,2,128,128]{3,2,1,0:T(8,128)(2,1)S(1)} %pad_maximum_fusion.3), channel_id=1, source_target_pairs={{0,6},{1,7},{2,4},{3,5},{4,2},{5,3},{6,0},{7,1},{8,14},{9,15},{10,... | collective-permute-start | bytes 196616 | tf_op jit(solution)/shard_map/ppermute | solution.py:48
  72.1 7.5 %collective-permute-start.24 = (bf16[1,2,128,128]{3,2,1,0:T(8,128)(2,1)S(1)}, bf16[1,2,128,128]{3,2,1,0:T(8,128)(2,1)S(1)}, u32[]{:S(2)}, u32[]{:S(2)}) collective-permute-start(bf16[1,2,128,128]{3,2,1,0:T(8,128)(2,1)S(1)} %pad_maximum_fusion.3), channel_id=1, source_target_pairs={{0,2},{1,3},{2,0},{3,1},{4,6},{5,7},{6,4},{7,5},{8,10},{9,11},{10,... | collective-permute-start | bytes 196616 | tf_op jit(solution)/shard_map/ppermute | solution.py:48
  72.4 10.4 %collective-permute-start.23 = (bf16[2,128,128]{2,1,0:T(8,128)(2,1)S(1)}, bf16[2,128,128]{2,1,0:T(8,128)(2,1)S(1)}, u32[]{:S(2)}, u32[]{:S(2)}) collective-permute-start(bf16[2,128,128]{2,1,0:T(8,128)(2,1)S(1)} %pad_maximum_fusion.2.refs_0_), channel_id=1, source_target_pairs={{0,1},{1,0},{2,3},{3,2},{4,5},{5,4},{6,7},{7,6},{8,9},{9,8},{10,11... | collective-permute-start | bytes 196616 | tf_op jit(solution)/shard_map/ppermute | solution.py:48
  77.8 5.0 %collective-permute-start.28 = (bf16[2,2,128,128]{3,2,1,0:T(8,128)(2,1)S(1)}, bf16[2,2,128,128]{3,2,1,0:T(8,128)(2,1)S(1)}, u32[]{:S(2)}, u32[]{:S(2)}) collective-permute-start(bf16[2,2,128,128]{3,2,1,0:T(8,128)(2,1)S(1)} %pad_maximum_fusion.1), channel_id=1, source_target_pairs={{0,1},{1,0},{2,3},{3,2},{4,5},{5,4},{6,7},{7,6},{8,9},{9,8},{10,11... | collective-permute-start | bytes 393224 | tf_op jit(solution)/shard_map/ppermute | solution.py:48
  79.6 4.3 %collective-permute-start.25 = (bf16[1,2,128,128]{3,2,1,0:T(8,128)(2,1)S(1)}, bf16[1,2,128,128]{3,2,1,0:T(8,128)(2,1)S(1)}, u32[]{:S(2)}, u32[]{:S(2)}) collective-permute-start(bf16[1,2,128,128]{3,2,1,0:T(8,128)(2,1)S(1)} %collective-permute-done.24), channel_id=1, source_target_pairs={{0,1},{1,0},{2,3},{3,2},{4,5},{5,4},{6,7},{7,6},{8,9},{9,8},{10,11... | collective-permute-start | bytes 196616 | tf_op jit(solution)/shard_map/ppermute | solution.py:48

commit v4 on v3

--- a/solution.py
+++ b/solution.py
@@ -75,10 +75,11 @@
 
 
 def assembled(refs, layout, scratch, dsh):
-    me = lax.axis_index("ens")
-    for which, first, j in layout:
-        start = pl.multiple_of((me ^ j) * dsh, dsh)
-        scratch[pl.ds(start, dsh), :] = refs[which][first : first + dsh, :]
+    me, side = lax.axis_index("ens"), (lax.axis_index("pix") // 2) % 2
+    for which, first, rows, j, place in layout:
+        offset = place * rows if place < 2 else (side ^ (place - 2)) * rows
+        start = pl.multiple_of((me ^ j) * dsh + offset, rows)
+        scratch[pl.ds(start, rows), :] = refs[which][first : first + rows, :]
     return scratch[...]
 
 
@@ -286,28 +287,40 @@
     assert rows == TILE and n_out == LANES
 
     far = ens_bits[:-1]
-    w_out_t = w_out.T
-    qkv = jnp.concatenate([w_query, w_key, w_value])
-    qkv_far = gathered(qkv, "ens", far)
+    half, side = dsh // 2, (p // 2) % 2
+    w_vo = jnp.concatenate([w_value, w_out.T])
+
+    def half_of(w):
+        return jnp.where(side == 0, w[:half], w[half:])
+
+    qk_far = gathered(jnp.concatenate([w_query, half_of(w_key)]), "ens", far)
+    vo_far = gathered(w_vo, "ens", far)
     up = lax.ppermute(sample_layer_feed, "pix", [(i, i + 1) for i in range(n_pix - 1)])
     down = lax.ppermute(sample_layer_feed, "pix", [(i + 1, i) for i in range(n_pix - 1)])
-    qkv_near = xor_permute(qkv, "ens", 1)
-    o_near = xor_permute(w_out_t, "ens", 1)
-    o_far = gathered(w_out_t, "ens", far)
-    up, down, qkv_near, o_near, qkv_far = lax.optimization_barrier((up, down, qkv_near, o_near, qkv_far))
-    shards = sorted(j for j in qkv_far if j)
-    qkv_far = joined([qkv_far[j] for j in shards])
-    qkv_cross = xor_permute(qkv_far, "ens", 1)
-
-    def shard_layout(width, first):
-        table = [(0, first, 0), (1, first, 1)]
+    w_qk = jnp.concatenate([w_query, w_key])
+    qk_near = xor_permute(w_qk, "ens", 1)
+    shards = sorted(j for j in qk_far if j)
+    pieces = []
+    for j in shards:
+        whole = qk_far[j].shape[0] // half - 1
+        pieces += [(part, i // 2, j, i % 2) for i, part in enumerate(jnp.split(qk_far[j][: whole * half], max(whole, 1))) if whole]
+        for m in range(1):
+            part = qk_far[j][(whole + m) * half : (whole + m + 1) * half]
+            pieces.append((part, 2 - 1 + m, j, 2))
+            pieces.append((xor_permute(part, "pix", 2), 2 - 1 + m, j, 3))
+    parts = [piece[0] for piece in pieces]
+    up, down, qk_near, parts = lax.optimization_barrier((up, down, qk_near, parts))
+    parts += [xor_permute(part, "ens", 1) for part in parts]
+    qk_layout = [[(0, m * dsh, dsh, 0, 0), (1, m * dsh, dsh, 1, 0)] for m in (0, 1)]
+    for i, (_, m, j, place) in enumerate(pieces * 2):
+        qk_layout[m].append((2 + i, 0, half, j if i < len(pieces) else j ^ 1, place))
+
+    def layout(first):
+        table = [(0, first, dsh, 0, 0), (1, first, dsh, 1, 0)]
         for i, j in enumerate(shards):
-            table += [(2, i * width * dsh + first, j), (3, i * width * dsh + first, j ^ 1)]
+            row = 2 * i * dsh + first
+            table += [(2, row, dsh, j, 0), (3, row, dsh, j ^ 1, 0)]
         return table
-
-    q_layout, k_layout, v_layout = (shard_layout(3, i * dsh) for i in range(3))
-    o_layout = shard_layout(1, 0)
-    qkv_parts = [("v", a) for a in (qkv, qkv_near, qkv_far, qkv_cross)]
 
     mask_rows = pix_mask.reshape(n_pix, TILE)
     half = ((d_model // 2, 3 * TILE), BF16)
@@ -322,32 +335,33 @@
 
     full = pltpu.VMEM((d_model, inner), BF16)
     (weights,) = call(
-        functools.partial(weights_body, q_layout, k_layout, dsh),
+        functools.partial(weights_body, qk_layout[0], qk_layout[1], dsh),
         [((HEADS, TILE, 3 * TILE), BF16)],
         [("v", normed), ("v", mask_rows), ("s", neighbours), ("s", neighbour_mask)]
-        + qkv_parts,
+        + [("v", a) for a in [w_qk, qk_near] + parts],
         10**9,
         "weights",
         scratch=[full],
     )
-    weights, o_far, turned_send = lax.optimization_barrier((weights, o_far, turned_send))
-    o_far = joined([o_far[j] for j in shards])
-    o_cross = xor_permute(o_far, "ens", 1)
+    weights, vo_far, turned_send, w_vo = lax.optimization_barrier((weights, vo_far, turned_send, w_vo))
+    vo_near = xor_permute(w_vo, "ens", 1)
+    vo_far = joined([vo_far[j] for j in shards])
+    vo_cross = xor_permute(vo_far, "ens", 1)
     turned_sib = xor_permute(turned_send, "ens", 1)
     (attended,) = call(
-        functools.partial(attend_body, v_layout, dsh),
+        functools.partial(attend_body, layout(0), dsh),
         [((TILE, inner), BF16)],
         [("v", normed), ("v", weights), ("s", neighbours), ("s", neighbour_mask)]
-        + qkv_parts,
+        + [("v", a) for a in (w_vo, vo_near, vo_far, vo_cross)],
         10**9,
         "attend",
         scratch=[full],
     )
     forecast, w_out_full = call(
-        functools.partial(forecast_body, o_layout, dsh),
+        functools.partial(forecast_body, layout(dsh), dsh),
         [((TILE, LANES), BF16), ((d_model, inner), BF16)],
         [("v", sample_layer_feed), ("v", attended), ("v", readout_matrix)]
-        + [("v", a) for a in (w_out_t, o_near, o_far, o_cross)],
+        + [("v", a) for a in (w_vo, vo_near, vo_far, vo_cross)],
         10**9,
         "forecast",
     )
@@ -396,16 +410,34 @@
     n_bits = n_pix.bit_length() - 1
     groups = [[1]] + [[1 << b for b in range(s, min(s + 2, n_bits))] for s in range(1, n_bits, 2)]
 
-    def pieces_of(term, group):
+    def pieces_of(term, group, higher=None):
         size = 1 << len(group)
-        return term.reshape(n_pix // (group[0] * size), size, -1, LANES)
+        higher = n_pix // (group[0] * size) if higher is None else higher
+        return term.reshape(higher, size, -1, LANES)
 
     def exchanged(messages, group):
         return [xor_permute(m, "pix", (d + 1) * group[0]) for d, m in enumerate(messages)]
 
-    split = pieces_of(output_term, groups[0])
-    got = exchanged([part_of(split, 1 - p % 2).astype(BF16)], groups[0])[0]
-    output_term = part_of(split, p % 2) + got.astype(F32)
+    def sent(term, group, total=None, higher=None):
+        size, pos = 1 << len(group), (p // group[0]) % (1 << len(group))
+        split = pieces_of(term, group, higher)
+        messages = [part_of(split, pos ^ d).astype(BF16) for d in range(1, size)]
+        if total is not None:
+            messages = [with_loss(m, total) for m in messages]
+        return part_of(split, pos), exchanged(messages, group)
+
+    def added(kept, received):
+        return functools.reduce(jnp.add, [m.astype(F32) for m in received], kept)
+
+    def added_with_loss(kept, received, total, group):
+        size, pos = 1 << len(group), (p // group[0]) % (1 << len(group))
+        received = [split_loss(m) for m in received]
+        totals = jnp.stack([total] + [other for _, other in received])
+        total = functools.reduce(jnp.add, [at(totals, pos ^ i) for i in range(size)])
+        return added(kept, [m for m, _ in received]), total
+
+    for bit in [bit for group in groups[1:] for bit in group]:
+        output_term = added(*sent(output_term, [bit]))
     upper, low = (e // far[-1]) % 2, p % 2
     quarters = [pieces_of(h, groups[0]) for h in value_term.reshape(2, -1, LANES)]
     quarters = jnp.stack([part_of(q, i) for q in quarters for i in range(2)])
@@ -427,20 +459,11 @@
     losses = jnp.stack([losses[d] for d in range(4)])
     loss = functools.reduce(jnp.add, [at(losses, pos ^ i) for i in range(4)])
 
+    output_term = added(*sent(output_term, groups[0], higher=1))
     for group in groups[1:]:
-        size, pos = 1 << len(group), (p // group[0]) % (1 << len(group))
-        split = [pieces_of(t, group) for t in (value_term, output_term)]
-        messages = [
-            with_loss(jnp.concatenate([part_of(s, pos ^ d) for s in split]), loss) for d in range(1, size)
-        ]
-        received = [split_loss(m) for m in exchanged(messages, group)]
-        kept = [part_of(s, pos) for s in split]
-        for block, _ in received:
-            block = block.astype(F32).reshape(2, -1, LANES)
-            kept = [k + block[i] for i, k in enumerate(kept)]
-        value_term, output_term = kept
-        losses = jnp.stack([loss] + [other for _, other in received])
-        loss = functools.reduce(jnp.add, [at(losses, pos ^ i) for i in range(size)])
+        kept, received = sent(value_term, group, loss)
+        output_term, received = lax.optimization_barrier((output_term, received))
+        value_term, loss = added_with_loss(kept, received, loss, group)
     terms = [value_term, output_term]
     piece = jnp.stack(terms).astype(BF16)
     pieces = {0: piece}
@@ -452,9 +475,8 @@
         for i, j in enumerate(keys):
             pieces.update({j ^ (d * group[0]): got[i] for d, got in new.items()})
     later = [j for j in sorted(pieces) if j]
-    for batch in (later[: len(later) // 3], later[len(later) // 3 :]):
-        got = xor_permute(jnp.stack([pieces[j] for j in batch]), "pix", 1)
-        pair.update({j ^ 1: got[i] for i, j in enumerate(batch)})
+    got = xor_permute(jnp.stack([pieces[j] for j in later]), "pix", 1)
+    pair.update({j ^ 1: got[i] for i, j in enumerate(later)})
     pieces.update(pair)
     scale = 1.0 / (n_ens * n_pix * TILE * n_out)
     grad_w_value, grad_w_out, loss = call(

time: 85.4 us -> 80.6 us (0.944)
  waiting for transfers between devices: 38.9 us -> 32.8 us
  starting transfers between devices: 31.2 us -> 33.3 us
  local copies, waits for them, and re-layouts: 3.83 us -> 2.75 us
  other arithmetic: 0.45 us -> 1.51 us
    ppermute x1, waiting for transfers between devices: 10 us -> 4.17 us  [per_device(): lax.ppermute(sample_layer_feed, 'pix', [(i, i + 1) for i in range(n_pix -...]
    ppermute x24 -> x29, starting transfers between devices: 21.6 us -> 25 us  [xor_permute(): return lax.ppermute(value, axis, [(i, i ^ mask) for i in range(size)])]
    ppermute x3, starting transfers between devices: 4.92 us -> 3.55 us  [per_device(): lax.ppermute(message, ('ens', 'pix'), pairs)]
    unnamed x30 -> x28, local copies, waits for them, and re-layouts: 3.57 us -> 2.43 us
    select_n x0 -> x1, other arithmetic: none -> 1.02 us  [half_of(): return jnp.where(side == 0, w[:half], w[half:])]
    ppermute x24 -> x29, waiting for transfers between devices: 26.3 us -> 26.1 us  [xor_permute(): return lax.ppermute(value, axis, [(i, i ^ mask) for i in range(size)])]
  transfers between devices with their start and end apart: 29 -> 34, of which waited for: 16 -> 20; matrix products, arithmetic and copies ran while one was open for 1% -> 1% of each run, Pallas kernels for 9% -> 6%
where the time goes in v4:
time: 80.6 us; the launch traced here: 80.4 us
  starting transfers between devices  33.3 us (41%)
  waiting for transfers between devices  32.8 us (41%)
  Pallas kernels  8.9 us (11%)
  local copies, waits for them, and re-layouts  2.75 us (3%)
  other arithmetic  1.51 us (2%)
  between operations  1.14 us (1%)
    ppermute x29, waiting for transfers between devices, xor_permute(): return lax.ppermute(value, axis, [(i, i ^ mask) for i in range(size)])  26.1 us
    ppermute x29, starting transfers between devices, xor_permute(): return lax.ppermute(value, axis, [(i, i ^ mask) for i in range(size)])  25 us
    pallas_call x8, Pallas kernels, call(): pl.pallas_call(body, out_shape=[jax.ShapeDtypeStruct(s, d) for s, d in ou...  8.9 us
    ppermute x1, waiting for transfers between devices, per_device(): lax.ppermute(sample_layer_feed, 'pix', [(i, i + 1) for i in range(n_pix -...  4.17 us
    ppermute x3, starting transfers between devices, per_device(): lax.ppermute(message, ('ens', 'pix'), pairs)  3.55 us
    ppermute x1, starting transfers between devices, per_device(): lax.ppermute(sample_layer_feed, 'pix', [(i, i + 1) for i in range(n_pix -...  3.43 us
    ppermute x3, waiting for transfers between devices, per_device(): lax.ppermute(message, ('ens', 'pix'), pairs)  2.51 us
    unnamed x28, local copies, waits for them, and re-layouts  2.43 us
  transfers between devices with their start and end apart: 34, of which 20 were waited for; matrix products, arithmetic and copies ran while one was open for 1% of the time, Pallas kernels for 6%

profile of v4, /device:TPU:0, one launch (start us, length us, event | category | flops | bytes accessed | tf_op | source)
XLA Modules:
  0.0 80.4 jit_solution(7219556266770295443)
XLA Ops:
  0.7 1.0 %slice_select_fusion = bf16[128,512]{1,0:T(8,128)(2,1)S(1)} fusion(bf16[256,512]{1,0:T(8,128)(2,1)} %param.15, pred[]{:T(512)S(6)} %eq.12), kind=kLoop, calls=%fused_computation.20 | loop fusion | flops 65536 | bytes 393217 | tf_op jit(solution)/shard_map/jit(_where)/select_n | solution.py:294
  1.8 3.0 %collective-permute-start.3 = (bf16[384,512]{1,0:T(8,128)(2,1)S(1)}, bf16[384,512]{1,0:T(8,128)(2,1)S(1)}, u32[]{:S(2)}, u32[]{:S(2)}) collective-permute-start(bf16[384,512]{1,0:T(8,128)(2,1)S(1)} %pad_maximum_fusion.2), channel_id=1, source_target_pairs={{0,16},{8,24},{16,0},{24,8},{1,17},{9,25},{17,1},{25,9},{2,18},{10... | collective-permute-start | bytes 1179656 | tf_op jit(solution)/shard_map/ppermute | solution.py:48
  4.9 0.1 collective-permute-start.2
  4.9 0.8 %copy-done = bf16[1,128,1024]{2,1,0:T(8,128)(2,1)S(1)} copy-done((bf16[1,128,1024]{2,1,0:T(8,128)(2,1)S(1)}, bf16[1,128,1024]{2,1,0:T(8,128)(2,1)}, u32[]{:S(2)}) %copy-start) | copy-done | bytes 262168
  5.7 3.4 %collective-permute-start = (bf16[1,128,1024]{2,1,0:T(8,128)(2,1)S(1)}, bf16[1,128,1024]{2,1,0:T(8,128)(2,1)S(1)}, u32[]{:S(2)}, u32[]{:S(2)}) collective-permute-start(bf16[1,128,1024]{2,1,0:T(8,128)(2,1)S(1)} %copy-done), channel_id=1, source_target_pairs={{0,1},{1,2},{2,3},{3,4},{4,5},{5,6},{6,7},{8,9},{9,10},{10,11},{11... | collective-permute-start | bytes 786440 | tf_op jit(solution)/shard_map/ppermute | solution.py:298
  9.2 1.3 %collective-permute-start.1 = (bf16[1,128,1024]{2,1,0:T(8,128)(2,1)S(1)}, bf16[1,128,1024]{2,1,0:T(8,128)(2,1)S(1)}, u32[]{:S(2)}, u32[]{:S(2)}) collective-permute-start(bf16[1,128,1024]{2,1,0:T(8,128)(2,1)S(1)} %copy-done), channel_id=1, source_target_pairs={{1,0},{2,1},{3,2},{4,3},{5,4},{6,5},{7,6},{9,8},{10,9},{11,10},{12... | collective-permute-start | bytes 786440 | tf_op jit(solution)/shard_map/ppermute | solution.py:299
  10.5 0.1 copy.15
  10.7 0.9 %collective-permute-start.9 = (bf16[512,512]{1,0:T(8,128)(2,1)S(1)}, bf16[512,512]{1,0:T(8,128)(2,1)S(1)}, u32[]{:S(2)}, u32[]{:S(2)}) collective-permute-start(bf16[512,512]{1,0:T(8,128)(2,1)S(1)} %pad_maximum_fusion.1.refs_0_), channel_id=1, source_target_pairs={{0,16},{8,24},{16,0},{24,8},{1,17},{9,25},{17,1},{25,9},{2,18},{10... | collective-permute-start | bytes 1572872 | tf_op jit(solution)/shard_map/ppermute | solution.py:48
  11.6 3.1 %collective-permute-done.3 = bf16[384,512]{1,0:T(8,128)(2,1)S(1)} collective-permute-done((bf16[384,512]{1,0:T(8,128)(2,1)S(1)}, bf16[384,512]{1,0:T(8,128)(2,1)S(1)}, u32[]{:S(2)}, u32[]{:S(2)}) %collective-permute-start.3) | collective-permute-done | bytes 393248 | tf_op jit(solution)/shard_map/ppermute | solution.py:48
  14.7 1.1 %collective-permute-start.4 = (bf16[128,512]{1,0:T(8,128)(2,1)S(1)}, bf16[128,512]{1,0:T(8,128)(2,1)S(1)}, u32[]{:S(2)}, u32[]{:S(2)}) collective-permute-start(bf16[128,512]{1,0:T(8,128)(2,1)S(1)} %get-tuple-element.48.refs_4_), channel_id=1, source_target_pairs={{0,2},{1,3},{2,0},{3,1},{4,6},{5,7},{6,4},{7,5},{8,10},{9,11},{10,... | collective-permute-start | bytes 393224 | tf_op jit(solution)/shard_map/ppermute | solution.py:48
  15.8 4.2 %collective-permute-done.up_ref = bf16[1,128,1024]{2,1,0:T(8,128)(2,1)S(1)} collective-permute-done((bf16[1,128,1024]{2,1,0:T(8,128)(2,1)S(1)}, bf16[1,128,1024]{2,1,0:T(8,128)(2,1)S(1)}, u32[]{:S(2)}, u32[]{:S(2)}) %collective-permute-start) | collective-permute-done | bytes 262176 | tf_op jit(solution)/shard_map/ppermute | solution.py:298
  20.0 2.5 %collective-permute-done.4.refs_5_ = bf16[128,512]{1,0:T(8,128)(2,1)S(1)} collective-permute-done((bf16[128,512]{1,0:T(8,128)(2,1)S(1)}, bf16[128,512]{1,0:T(8,128)(2,1)S(1)}, u32[]{:S(2)}, u32[]{:S(2)}) %collective-permute-start.4) | collective-permute-done | bytes 131104 | tf_op jit(solution)/shard_map/ppermute | solution.py:48
  22.5 0.5 collective-permute-start.6
  23.0 0.5 collective-permute-start.8
  23.5 0.6 normed.1
  24.1 0.2 collective-permute-done.7.refs_8_
  24.4 0.2 collective-permute-done.8.refs_9_
  24.6 0.6 copy-done.2
  25.2 2.2 %weights.1.w_ref.refs_9_ = bf16[8,128,384]{2,1,0:T(8,128)(2,1)S(1)} custom-call(bf16[384,1024]{1,0:T(8,128)(2,1)S(1)} %get-tuple-element.44.n_ref, s32[8,128]{1,0:T(8,128)S(1)} %bitcast.136, s32[1,9]{1,0:T(1,128)S(1)} %copy-done.2, s32[1,9]{1,0:T(1,128)S(1)} %copy-done.3, bf16[512,512]{1,0:T(8,128)(2,1)S(1)} %constant_dynamic-update-slice_fusion.refs_0_, ...), custom_call_target="tpu_custom_call" | custom-call | flops 1000000000 | bytes 1048576 | tf_op jit(solution)/shard_map/weights/pallas_call | solution.py:34
  27.4 0.4 collective-permute-start.11
  27.8 0.2 collective-permute-start.12
  28.0 1.4 %collective-permute-done.11.refs_1_ = bf16[512,512]{1,0:T(8,128)(2,1)S(1)} collective-permute-done((bf16[512,512]{1,0:T(8,128)(2,1)S(1)}, bf16[512,512]{1,0:T(8,128)(2,1)S(1)}, u32[]{:S(2)}, u32[]{:S(2)}) %collective-permute-start.11) | collective-permute-done | bytes 524320 | tf_op jit(solution)/shard_map/ppermute | solution.py:48
  29.4 0.7 collective-permute-done.12.refs_3_
  30.2 1.5 %attend.1.att_ref.refs_0_ = bf16[128,512]{1,0:T(8,128)(2,1)S(1)} custom-call(bf16[384,1024]{1,0:T(8,128)(2,1)S(1)} %get-tuple-element.44.n_ref, bf16[8,128,384]{2,1,0:T(8,128)(2,1)S(1)} %weights.1.w_ref.refs_9_, s32[1,9]{1,0:T(1,128)S(1)} %copy-done.2, s32[1,9]{1,0:T(1,128)S(1)} %copy-done.3, bf16[512,512]{1,0:T(8,128)(2,1)S(1)} %pad_maximum_fusion.1.refs_0_, ...), custom_call_target="tpu_custom_call" | custom-call | flops 1000000000 | bytes 1048576 | tf_op jit(solution)/shard_map/attend/pallas_call | solution.py:34
  31.7 0.7 forecast.1
  32.4 1.1 %collective-permute-start.13 = (bf16[128,128]{1,0:T(8,128)(2,1)S(1)}, bf16[128,128]{1,0:T(8,128)(2,1)S(1)}, u32[]{:S(2)}, u32[]{:S(2)}) collective-permute-start(bf16[128,128]{1,0:T(8,128)(2,1)S(1)} %get-tuple-element.56.refs_0_), channel_id=1, source_target_pairs={{0,16},{8,24},{16,0},{24,8},{1,17},{9,25},{17,1},{25,9},{2,18},{10... | collective-permute-start | bytes 98312 | tf_op jit(solution)/shard_map/ppermute | solution.py:48
  33.5 1.0 %collective-permute-start.16 = (bf16[128,512]{1,0:T(8,128)(2,1)S(1)}, bf16[128,512]{1,0:T(8,128)(2,1)S(1)}, u32[]{:S(2)}, u32[]{:S(2)}) collective-permute-start(bf16[128,512]{1,0:T(8,128)(2,1)S(1)} %attend.1.att_ref.refs_0_), channel_id=1, source_target_pairs={{0,16},{8,24},{16,0},{24,8},{1,17},{9,25},{17,1},{25,9},{2,18},{10... | collective-permute-start | bytes 393224 | tf_op jit(solution)/shard_map/ppermute | solution.py:48
  34.5 2.2 %collective-permute-done.13.refs_2_ = bf16[128,128]{1,0:T(8,128)(2,1)S(1)} collective-permute-done((bf16[128,128]{1,0:T(8,128)(2,1)S(1)}, bf16[128,128]{1,0:T(8,128)(2,1)S(1)}, u32[]{:S(2)}, u32[]{:S(2)}) %collective-permute-start.13) | collective-permute-done | bytes 32800 | tf_op jit(solution)/shard_map/ppermute | solution.py:48
  36.7 0.5 collective-permute-start.15
  37.2 0.7 collective-permute-done.14.refs_1_
  37.9 0.2 collective-permute-done.15.refs_3_
  38.0 0.7 copy-done.7
  38.7 1.6 %backward.1 = (bf16[512,128]{1,0:T(8,128)(2,1)S(1)}, bf16[400,512]{1,0:T(8,128)(2,1)S(1)}) custom-call(bf16[128,128]{1,0:T(8,128)(2,1)S(1)} %get-tuple-element.56.refs_0_, bf16[128,128]{1,0:T(8,128)(2,1)S(1)} %collective-permute-done.14.refs_1_, bf16[128,128]{1,0:T(8,128)(2,1)S(1)} %collective-permute-done.13.refs_2_, ...), custom_call_target="tpu_custom_call" | custom-call | flops 1000000000 | bytes 1048576 | tf_op jit(solution)/shard_map/backward/pallas_call | solution.py:34
  40.3 0.4 collective-permute-start.17
  40.7 0.2 collective-permute-start.10
  40.9 0.4 collective-permute-start.21
  41.2 0.2 collective-permute-start.22
  41.4 1.3 %collective-permute-done.10.sib_ref = bf16[512,384]{1,0:T(8,128)(2,1)S(1)} collective-permute-done((bf16[512,384]{1,0:T(8,128)(2,1)S(1)}, bf16[512,384]{1,0:T(8,128)(2,1)S(1)}, u32[]{:S(2)}, u32[]{:S(2)}) %collective-permute-start.10) | collective-permute-done | bytes 393248 | tf_op jit(solution)/shard_map/ppermute | solution.py:48
  42.7 0.7 value_term.1
  43.4 0.4 output_term.1
  43.8 1.2 %collective-permute-start.23 = (bf16[512,128]{1,0:T(8,128)(2,1)S(1)}, bf16[512,128]{1,0:T(8,128)(2,1)S(1)}, u32[]{:S(2)}, u32[]{:S(2)}) collective-permute-start(bf16[512,128]{1,0:T(8,128)(2,1)S(1)} %bitcast.156), channel_id=1, source_target_pairs={{0,2},{1,3},{2,0},{3,1},{4,6},{5,7},{6,4},{7,5},{8,10},{9,11},{10,... | collective-permute-start | bytes 393224 | tf_op jit(solution)/shard_map/ppermute | solution.py:48
  45.5 1.1 %collective-permute-start.20 = (bf16[544,128]{1,0:T(8,128)(2,1)S(1)}, bf16[544,128]{1,0:T(8,128)(2,1)S(1)}, u32[]{:S(2)}, u32[]{:S(2)}) collective-permute-start(bf16[544,128]{1,0:T(8,128)(2,1)S(1)} %constant_dynamic-update-slice_fusion.10), channel_id=1, source_target_pairs={{0,17},{1,16},{2,19},{3,18},{4,21},{5,20},{6,23},{7,22},{8,25},{9,... | collective-permute-start | bytes 417800 | tf_op jit(solution)/shard_map/ppermute | solution.py:453
  46.6 1.3 %collective-permute-start.19 = (bf16[544,128]{1,0:T(8,128)(2,1)S(1)}, bf16[544,128]{1,0:T(8,128)(2,1)S(1)}, u32[]{:S(2)}, u32[]{:S(2)}) collective-permute-start(bf16[544,128]{1,0:T(8,128)(2,1)S(1)} %constant_dynamic-update-slice_fusion.6), channel_id=1, source_target_pairs={{0,1},{1,0},{2,3},{3,2},{4,5},{5,4},{6,7},{7,6},{8,9},{9,8},{10,11... | collective-permute-start | bytes 417800 | tf_op jit(solution)/shard_map/ppermute | solution.py:453
  47.9 1.1 %collective-permute-start.18 = (bf16[544,128]{1,0:T(8,128)(2,1)S(1)}, bf16[544,128]{1,0:T(8,128)(2,1)S(1)}, u32[]{:S(2)}, u32[]{:S(2)}) collective-permute-start(bf16[544,128]{1,0:T(8,128)(2,1)S(1)} %constant_dynamic-update-slice_fusion.2), channel_id=1, source_target_pairs={{0,16},{1,17},{2,18},{3,19},{4,20},{5,21},{6,22},{7,23},{8,24},{9,... | collective-permute-start | bytes 417800 | tf_op jit(solution)/shard_map/ppermute | solution.py:453
  49.0 0.6 collective-permute-done.23
  49.7 2.7 %collective-permute-start.24 = (bf16[256,128]{1,0:T(8,128)(2,1)S(1)}, bf16[256,128]{1,0:T(8,128)(2,1)S(1)}, u32[]{:S(2)}, u32[]{:S(2)}) collective-permute-start(bf16[256,128]{1,0:T(8,128)(2,1)S(1)} %fusion.8), channel_id=1, source_target_pairs={{0,4},{1,5},{2,6},{3,7},{4,0},{5,1},{6,2},{7,3},{8,12},{9,13},{10,... | collective-permute-start | bytes 196616 | tf_op jit(solution)/shard_map/ppermute | solution.py:48
  52.4 0.6 collective-permute-done.20
  53.0 1.3 %collective-permute-done.18 = bf16[544,128]{1,0:T(8,128)(2,1)S(1)} collective-permute-done((bf16[544,128]{1,0:T(8,128)(2,1)S(1)}, bf16[544,128]{1,0:T(8,128)(2,1)S(1)}, u32[]{:S(2)}, u32[]{:S(2)}) %collective-permute-start.18) | collective-permute-done | bytes 139296 | tf_op jit(solution)/shard_map/ppermute | solution.py:453
  54.3 0.6 collective-permute-done.19
  55.1 0.6 collective-permute-start.26
  55.7 2.6 %collective-permute-start.27 = (bf16[160,128]{1,0:T(8,128)(2,1)S(1)}, bf16[160,128]{1,0:T(8,128)(2,1)S(1)}, u32[]{:S(2)}, u32[]{:S(2)}) collective-permute-start(bf16[160,128]{1,0:T(8,128)(2,1)S(1)} %constant_dynamic-update-slice_fusion.19), channel_id=1, source_target_pairs={{0,4},{1,5},{2,6},{3,7},{4,0},{5,1},{6,2},{7,3},{8,12},{9,13},{10,... | collective-permute-start | bytes 122888 | tf_op jit(solution)/shard_map/ppermute | solution.py:48
  58.4 1.2 %collective-permute-start.25 = (bf16[128,128]{1,0:T(8,128)(2,1)S(1)}, bf16[128,128]{1,0:T(8,128)(2,1)S(1)}, u32[]{:S(2)}, u32[]{:S(2)}) collective-permute-start(bf16[128,128]{1,0:T(8,128)(2,1)S(1)} %fusion.12), channel_id=1, source_target_pairs={{0,1},{1,0},{2,3},{3,2},{4,5},{5,4},{6,7},{7,6},{8,9},{9,8},{10,11... | collective-permute-start | bytes 98312 | tf_op jit(solution)/shard_map/ppermute | solution.py:48
  59.6 1.0 %collective-permute-start.28 = (bf16[160,128]{1,0:T(8,128)(2,1)S(1)}, bf16[160,128]{1,0:T(8,128)(2,1)S(1)}, u32[]{:S(2)}, u32[]{:S(2)}) collective-permute-start(bf16[160,128]{1,0:T(8,128)(2,1)S(1)} %constant_dynamic-update-slice_fusion.24), channel_id=1, source_target_pairs={{0,6},{1,7},{2,4},{3,5},{4,2},{5,3},{6,0},{7,1},{8,14},{9,15},{10,... | collective-permute-start | bytes 122888 | tf_op jit(solution)/shard_map/ppermute | solution.py:48
  60.6 1.8 %collective-permute-done.25 = bf16[128,128]{1,0:T(8,128)(2,1)S(1)} collective-permute-done((bf16[128,128]{1,0:T(8,128)(2,1)S(1)}, bf16[128,128]{1,0:T(8,128)(2,1)S(1)}, u32[]{:S(2)}, u32[]{:S(2)}) %collective-permute-start.25) | collective-permute-done | bytes 32800 | tf_op jit(solution)/shard_map/ppermute | solution.py:48
  62.4 3.0 %collective-permute-done.28 = bf16[160,128]{1,0:T(8,128)(2,1)S(1)} collective-permute-done((bf16[160,128]{1,0:T(8,128)(2,1)S(1)}, bf16[160,128]{1,0:T(8,128)(2,1)S(1)}, u32[]{:S(2)}, u32[]{:S(2)}) %collective-permute-start.28) | collective-permute-done | bytes 40992 | tf_op jit(solution)/shard_map/ppermute | solution.py:48
  65.5 0.1 collective-permute-start.30
  65.5 1.0 %collective-permute-start.32 = (bf16[1,2,128,128]{3,2,1,0:T(8,128)(2,1)S(1)}, bf16[1,2,128,128]{3,2,1,0:T(8,128)(2,1)S(1)}, u32[]{:S(2)}, u32[]{:S(2)}) collective-permute-start(bf16[1,2,128,128]{3,2,1,0:T(8,128)(2,1)S(1)} %pad_maximum_fusion.5), channel_id=1, source_target_pairs={{0,6},{1,7},{2,4},{3,5},{4,2},{5,3},{6,0},{7,1},{8,14},{9,15},{10,... | collective-permute-start | bytes 196616 | tf_op jit(solution)/shard_map/ppermute | solution.py:48
  66.6 2.4 %collective-permute-start.31 = (bf16[1,2,128,128]{3,2,1,0:T(8,128)(2,1)S(1)}, bf16[1,2,128,128]{3,2,1,0:T(8,128)(2,1)S(1)}, u32[]{:S(2)}, u32[]{:S(2)}) collective-permute-start(bf16[1,2,128,128]{3,2,1,0:T(8,128)(2,1)S(1)} %pad_maximum_fusion.5), channel_id=1, source_target_pairs={{0,4},{1,5},{2,6},{3,7},{4,0},{5,1},{6,2},{7,3},{8,12},{9,13},{10,... | collective-permute-start | bytes 196616 | tf_op jit(solution)/shard_map/ppermute | solution.py:48
  69.0 0.9 %collective-permute-start.29 = (bf16[2,128,128]{2,1,0:T(8,128)(2,1)S(1)}, bf16[2,128,128]{2,1,0:T(8,128)(2,1)S(1)}, u32[]{:S(2)}, u32[]{:S(2)}) collective-permute-start(bf16[2,128,128]{2,1,0:T(8,128)(2,1)S(1)} %pad_maximum_fusion.4.refs_0_), channel_id=1, source_target_pairs={{0,1},{1,0},{2,3},{3,2},{4,5},{5,4},{6,7},{7,6},{8,9},{9,8},{10,11... | collective-permute-start | bytes 196616 | tf_op jit(solution)/shard_map/ppermute | solution.py:48
  70.0 1.8 %collective-permute-done.32 = bf16[1,2,128,128]{3,2,1,0:T(8,128)(2,1)S(1)} collective-permute-done((bf16[1,2,128,128]{3,2,1,0:T(8,128)(2,1)S(1)}, bf16[1,2,128,128]{3,2,1,0:T(8,128)(2,1)S(1)}, u32[]{:S(2)}, u32[]{:S(2)}) %collective-permute-start.32) | collective-permute-done | bytes 65568 | tf_op jit(solution)/shard_map/ppermute | solution.py:48
  71.8 1.6 %collective-permute-done.31 = bf16[1,2,128,128]{3,2,1,0:T(8,128)(2,1)S(1)} collective-permute-done((bf16[1,2,128,128]{3,2,1,0:T(8,128)(2,1)S(1)}, bf16[1,2,128,128]{3,2,1,0:T(8,128)(2,1)S(1)}, u32[]{:S(2)}, u32[]{:S(2)}) %collective-permute-start.31) | collective-permute-done | bytes 65568 | tf_op jit(solution)/shard_map/ppermute | solution.py:48
  73.4 0.9 %collective-permute-start.33 = (bf16[3,2,128,128]{3,2,1,0:T(8,128)(2,1)S(1)}, bf16[3,2,128,128]{3,2,1,0:T(8,128)(2,1)S(1)}, u32[]{:S(2)}, u32[]{:S(2)}) collective-permute-start(bf16[3,2,128,128]{3,2,1,0:T(8,128)(2,1)S(1)} %pad_maximum_fusion.3), channel_id=1, source_target_pairs={{0,1},{1,0},{2,3},{3,2},{4,5},{5,4},{6,7},{7,6},{8,9},{9,8},{10,11... | collective-permute-start | bytes 589832 | tf_op jit(solution)/shard_map/ppermute | solution.py:48
  74.3 4.8 %collective-permute-done.33 = bf16[3,2,128,128]{3,2,1,0:T(8,128)(2,1)S(1)} collective-permute-done((bf16[3,2,128,128]{3,2,1,0:T(8,128)(2,1)S(1)}, bf16[3,2,128,128]{3,2,1,0:T(8,128)(2,1)S(1)}, u32[]{:S(2)}, u32[]{:S(2)}) %collective-permute-start.33) | collective-permute-done | bytes 196640 | tf_op jit(solution)/shard_map/ppermute | solution.py:48
  79.2 1.2 %finish.1 = (f32[256,512]{1,0:T(8,128)}, f32[512,256]{1,0:T(8,128)}, f32[1,1]{1,0:T(1,128)}) custom-call(bf16[2,128,128]{2,1,0:T(8,128)(2,1)S(1)} %pad_maximum_fusion.4.refs_0_, bf16[2,128,128]{2,1,0:T(8,128)(2,1)S(1)} %collective-permute-done.29.refs_1_, bf16[2,128,128]{2,1,0:T(8,128)(2,1)S(1)} %bitcast.131, ...), custom_call_target="tpu_custom_call" | custom-call | flops 1000000 | bytes 1048576 | tf_op jit(solution)/shard_map/finish/pallas_call | solution.py:34
  (90 shorter events, 1.0 us)
Async XLA Ops:
  0.6 1.1 %copy-start.8 = (bf16[256,512]{1,0:T(8,128)(2,1)S(1)}, bf16[256,512]{1,0:T(8,128)(2,1)}, u32[]{:S(2)}) copy-start(bf16[256,512]{1,0:T(8,128)(2,1)} %param.14) | copy-start | bytes 786436
  1.7 3.0 %copy-start.9 = (bf16[256,512]{1,0:T(8,128)(2,1)S(1)}, bf16[256,512]{1,0:T(8,128)(2,1)}, u32[]{:S(2)}) copy-start(bf16[256,512]{1,0:T(8,128)(2,1)} %param.15) | copy-start | bytes 786436
  1.8 12.9 %collective-permute-start.3 = (bf16[384,512]{1,0:T(8,128)(2,1)S(1)}, bf16[384,512]{1,0:T(8,128)(2,1)S(1)}, u32[]{:S(2)}, u32[]{:S(2)}) collective-permute-start(bf16[384,512]{1,0:T(8,128)(2,1)S(1)} %pad_maximum_fusion.2), channel_id=1, source_target_pairs={{0,16},{8,24},{16,0},{24,8},{1,17},{9,25},{17,1},{25,9},{2,18},{10... | collective-permute-start | bytes 1179656 | tf_op jit(solution)/shard_map/ppermute | solution.py:48
  4.8 1.0 %copy-start = (bf16[1,128,1024]{2,1,0:T(8,128)(2,1)S(1)}, bf16[1,128,1024]{2,1,0:T(8,128)(2,1)}, u32[]{:S(2)}) copy-start(bf16[1,128,1024]{2,1,0:T(8,128)(2,1)} %x_ref.3) | copy-start | bytes 786436
  4.8 5.7 %copy-start.10 = (bf16[512,256]{1,0:T(8,128)(2,1)S(1)}, bf16[512,256]{1,0:T(8,128)(2,1)}, u32[]{:S(2)}) copy-start(bf16[512,256]{1,0:T(8,128)(2,1)} %param.17) | copy-start | bytes 786436
  4.8 5.8 %copy-start.11 = (bf16[256,512]{1,0:T(8,128)(2,1)S(1)}, bf16[256,512]{1,0:T(8,128)(2,1)}, u32[]{:S(2)}) copy-start(bf16[256,512]{1,0:T(8,128)(2,1)} %param.16) | copy-start | bytes 786436
  4.9 15.1 %collective-permute-start.2 = (bf16[512,512]{1,0:T(8,128)(2,1)S(1)}, bf16[512,512]{1,0:T(8,128)(2,1)S(1)}, u32[]{:S(2)}, u32[]{:S(2)}) collective-permute-start(bf16[512,512]{1,0:T(8,128)(2,1)S(1)} %constant_dynamic-update-slice_fusion.refs_0_), channel_id=1, source_target_pairs={{0,8},{8,0},{16,24},{24,16},{1,9},{9,1},{17,25},{25,17},{2,10},{10... | collective-permute-start | bytes 1572872 | tf_op jit(solution)/shard_map/ppermute | solution.py:48
  5.7 14.2 %collective-permute-start = (bf16[1,128,1024]{2,1,0:T(8,128)(2,1)S(1)}, bf16[1,128,1024]{2,1,0:T(8,128)(2,1)S(1)}, u32[]{:S(2)}, u32[]{:S(2)}) collective-permute-start(bf16[1,128,1024]{2,1,0:T(8,128)(2,1)S(1)} %copy-done), channel_id=1, source_target_pairs={{0,1},{1,2},{2,3},{3,4},{4,5},{5,6},{6,7},{8,9},{9,10},{10,11},{11... | collective-permute-start | bytes 786440 | tf_op jit(solution)/shard_map/ppermute | solution.py:298
  9.2 10.8 %collective-permute-start.1 = (bf16[1,128,1024]{2,1,0:T(8,128)(2,1)S(1)}, bf16[1,128,1024]{2,1,0:T(8,128)(2,1)S(1)}, u32[]{:S(2)}, u32[]{:S(2)}) collective-permute-start(bf16[1,128,1024]{2,1,0:T(8,128)(2,1)S(1)} %copy-done), channel_id=1, source_target_pairs={{1,0},{2,1},{3,2},{4,3},{5,4},{6,5},{7,6},{9,8},{10,9},{11,10},{12... | collective-permute-start | bytes 786440 | tf_op jit(solution)/shard_map/ppermute | solution.py:299
  10.7 16.7 %collective-permute-start.9 = (bf16[512,512]{1,0:T(8,128)(2,1)S(1)}, bf16[512,512]{1,0:T(8,128)(2,1)S(1)}, u32[]{:S(2)}, u32[]{:S(2)}) collective-permute-start(bf16[512,512]{1,0:T(8,128)(2,1)S(1)} %pad_maximum_fusion.1.refs_0_), channel_id=1, source_target_pairs={{0,16},{8,24},{16,0},{24,8},{1,17},{9,25},{17,1},{25,9},{2,18},{10... | collective-permute-start | bytes 1572872 | tf_op jit(solution)/shard_map/ppermute | solution.py:48
  14.7 8.8 %copy-start.1 = (f32[1024]{0:T(1024)S(1)}, f32[1024]{0:T(1024)}, u32[]{:S(2)}) copy-start(f32[1024]{0:T(1024)} %param.13) | copy-start | bytes 12292
  14.7 7.8 %collective-permute-start.4 = (bf16[128,512]{1,0:T(8,128)(2,1)S(1)}, bf16[128,512]{1,0:T(8,128)(2,1)S(1)}, u32[]{:S(2)}, u32[]{:S(2)}) collective-permute-start(bf16[128,512]{1,0:T(8,128)(2,1)S(1)} %get-tuple-element.48.refs_4_), channel_id=1, source_target_pairs={{0,2},{1,3},{2,0},{3,1},{4,6},{5,7},{6,4},{7,5},{8,10},{9,11},{10,... | collective-permute-start | bytes 393224 | tf_op jit(solution)/shard_map/ppermute | solution.py:48
  22.5 1.6 %collective-permute-start.5 = (bf16[128,512]{1,0:T(8,128)(2,1)S(1)}, bf16[128,512]{1,0:T(8,128)(2,1)S(1)}, u32[]{:S(2)}, u32[]{:S(2)}) collective-permute-start(bf16[128,512]{1,0:T(8,128)(2,1)S(1)} %get-tuple-element.46.refs_2_), channel_id=1, source_target_pairs={{0,8},{8,0},{16,24},{24,16},{1,9},{9,1},{17,25},{25,17},{2,10},{10... | collective-permute-start | bytes 393224 | tf_op jit(solution)/shard_map/ppermute | solution.py:48
  22.5 1.6 %collective-permute-start.6 = (bf16[128,512]{1,0:T(8,128)(2,1)S(1)}, bf16[128,512]{1,0:T(8,128)(2,1)S(1)}, u32[]{:S(2)}, u32[]{:S(2)}) collective-permute-start(bf16[128,512]{1,0:T(8,128)(2,1)S(1)} %get-tuple-element.47.refs_3_), channel_id=1, source_target_pairs={{0,8},{8,0},{16,24},{24,16},{1,9},{9,1},{17,25},{25,17},{2,10},{10... | collective-permute-start | bytes 393224 | tf_op jit(solution)/shard_map/ppermute | solution.py:48
  23.0 1.3 %collective-permute-start.7 = (bf16[128,512]{1,0:T(8,128)(2,1)S(1)}, bf16[128,512]{1,0:T(8,128)(2,1)S(1)}, u32[]{:S(2)}, u32[]{:S(2)}) collective-permute-start(bf16[128,512]{1,0:T(8,128)(2,1)S(1)} %get-tuple-element.48.refs_4_), channel_id=1, source_target_pairs={{0,8},{8,0},{16,24},{24,16},{1,9},{9,1},{17,25},{25,17},{2,10},{10... | collective-permute-start | bytes 393224 | tf_op jit(solution)/shard_map/ppermute | solution.py:48
  23.0 1.5 %collective-permute-start.8 = (bf16[128,512]{1,0:T(8,128)(2,1)S(1)}, bf16[128,512]{1,0:T(8,128)(2,1)S(1)}, u32[]{:S(2)}, u32[]{:S(2)}) collective-permute-start(bf16[128,512]{1,0:T(8,128)(2,1)S(1)} %collective-permute-done.4.refs_5_), channel_id=1, source_target_pairs={{0,8},{8,0},{16,24},{24,16},{1,9},{9,1},{17,25},{25,17},{2,10},{10... | collective-permute-start | bytes 393224 | tf_op jit(solution)/shard_map/ppermute | solution.py:48
  23.5 1.0 %copy-start.6 = (s32[1024]{0:T(1024)S(1)}, s32[1024]{0:T(1024)}, u32[]{:S(2)}) copy-start(s32[1024]{0:T(1024)} %param.21) | copy-start | bytes 12292
  24.5 0.7 copy-start.2
  24.5 0.7 copy-start.3
  27.4 4.3 %copy-start.4 = (bf16[1024,128]{1,0:T(8,128)(2,1)S(1)}, bf16[1024,128]{1,0:T(8,128)(2,1)}, u32[]{:S(2)}) copy-start(bf16[1024,128]{1,0:T(8,128)(2,1)} %read_ref.3) | copy-start | bytes 786436
  27.4 2.0 %collective-permute-start.11 = (bf16[512,512]{1,0:T(8,128)(2,1)S(1)}, bf16[512,512]{1,0:T(8,128)(2,1)S(1)}, u32[]{:S(2)}, u32[]{:S(2)}) collective-permute-start(bf16[512,512]{1,0:T(8,128)(2,1)S(1)} %pad_maximum_fusion.1.refs_0_), channel_id=1, source_target_pairs={{0,8},{8,0},{16,24},{24,16},{1,9},{9,1},{17,25},{25,17},{2,10},{10... | collective-permute-start | bytes 1572872 | tf_op jit(solution)/shard_map/ppermute | solution.py:48
  27.8 2.3 %collective-permute-start.12 = (bf16[512,512]{1,0:T(8,128)(2,1)S(1)}, bf16[512,512]{1,0:T(8,128)(2,1)S(1)}, u32[]{:S(2)}, u32[]{:S(2)}) collective-permute-start(bf16[512,512]{1,0:T(8,128)(2,1)S(1)} %collective-permute-done.9.refs_2_), channel_id=1, source_target_pairs={{0,8},{8,0},{16,24},{24,16},{1,9},{9,1},{17,25},{25,17},{2,10},{10... | collective-permute-start | bytes 1572872 | tf_op jit(solution)/shard_map/ppermute | solution.py:48
  31.7 6.3 %copy-start.5 = (f32[128,128]{1,0:T(8,128)S(1)}, f32[128,128]{1,0:T(8,128)}, u32[]{:S(2)}) copy-start(f32[128,128]{1,0:T(8,128)} %refs_5_.1) | copy-start | bytes 196612
  32.4 4.3 %collective-permute-start.13 = (bf16[128,128]{1,0:T(8,128)(2,1)S(1)}, bf16[128,128]{1,0:T(8,128)(2,1)S(1)}, u32[]{:S(2)}, u32[]{:S(2)}) collective-permute-start(bf16[128,128]{1,0:T(8,128)(2,1)S(1)} %get-tuple-element.56.refs_0_), channel_id=1, source_target_pairs={{0,16},{8,24},{16,0},{24,8},{1,17},{9,25},{17,1},{25,9},{2,18},{10... | collective-permute-start | bytes 98312 | tf_op jit(solution)/shard_map/ppermute | solution.py:48
  33.5 6.8 %collective-permute-start.16 = (bf16[128,512]{1,0:T(8,128)(2,1)S(1)}, bf16[128,512]{1,0:T(8,128)(2,1)S(1)}, u32[]{:S(2)}, u32[]{:S(2)}) collective-permute-start(bf16[128,512]{1,0:T(8,128)(2,1)S(1)} %attend.1.att_ref.refs_0_), channel_id=1, source_target_pairs={{0,16},{8,24},{16,0},{24,8},{1,17},{9,25},{17,1},{25,9},{2,18},{10... | collective-permute-start | bytes 393224 | tf_op jit(solution)/shard_map/ppermute | solution.py:48
  36.7 1.2 %collective-permute-start.14 = (bf16[128,128]{1,0:T(8,128)(2,1)S(1)}, bf16[128,128]{1,0:T(8,128)(2,1)S(1)}, u32[]{:S(2)}, u32[]{:S(2)}) collective-permute-start(bf16[128,128]{1,0:T(8,128)(2,1)S(1)} %get-tuple-element.56.refs_0_), channel_id=1, source_target_pairs={{0,8},{8,0},{16,24},{24,16},{1,9},{9,1},{17,25},{25,17},{2,10},{10... | collective-permute-start | bytes 98312 | tf_op jit(solution)/shard_map/ppermute | solution.py:48
  36.7 1.4 %collective-permute-start.15 = (bf16[128,128]{1,0:T(8,128)(2,1)S(1)}, bf16[128,128]{1,0:T(8,128)(2,1)S(1)}, u32[]{:S(2)}, u32[]{:S(2)}) collective-permute-start(bf16[128,128]{1,0:T(8,128)(2,1)S(1)} %collective-permute-done.13.refs_2_), channel_id=1, source_target_pairs={{0,8},{8,0},{16,24},{24,16},{1,9},{9,1},{17,25},{25,17},{2,10},{10... | collective-permute-start | bytes 98312 | tf_op jit(solution)/shard_map/ppermute | solution.py:48
  38.0 0.7 copy-start.7
  40.3 2.4 %collective-permute-start.17 = (bf16[400,512]{1,0:T(8,128)(2,1)S(1)}, bf16[400,512]{1,0:T(8,128)(2,1)S(1)}, u32[]{:S(2)}, u32[]{:S(2)}) collective-permute-start(bf16[400,512]{1,0:T(8,128)(2,1)S(1)} %get-tuple-element.61.own_con), channel_id=1, source_target_pairs={{0,8},{8,0},{16,24},{24,16},{1,9},{9,1},{17,25},{25,17},{2,10},{10... | collective-permute-start | bytes 1228808 | tf_op jit(solution)/shard_map/ppermute | solution.py:48
  40.7 2.0 %collective-permute-start.10 = (bf16[512,384]{1,0:T(8,128)(2,1)S(1)}, bf16[512,384]{1,0:T(8,128)(2,1)S(1)}, u32[]{:S(2)}, u32[]{:S(2)}) collective-permute-start(bf16[512,384]{1,0:T(8,128)(2,1)S(1)} %get-tuple-element.51), channel_id=1, source_target_pairs={{0,8},{8,0},{16,24},{24,16},{1,9},{9,1},{17,25},{25,17},{2,10},{10... | collective-permute-start | bytes 1179656 | tf_op jit(solution)/shard_map/ppermute | solution.py:48
  40.9 2.5 %collective-permute-start.21 = (bf16[128,512]{1,0:T(8,128)(2,1)S(1)}, bf16[128,512]{1,0:T(8,128)(2,1)S(1)}, u32[]{:S(2)}, u32[]{:S(2)}) collective-permute-start(bf16[128,512]{1,0:T(8,128)(2,1)S(1)} %attend.1.att_ref.refs_0_), channel_id=1, source_target_pairs={{0,8},{8,0},{16,24},{24,16},{1,9},{9,1},{17,25},{25,17},{2,10},{10... | collective-permute-start | bytes 393224 | tf_op jit(solution)/shard_map/ppermute | solution.py:48
  41.2 2.2 %collective-permute-start.22 = (bf16[128,512]{1,0:T(8,128)(2,1)S(1)}, bf16[128,512]{1,0:T(8,128)(2,1)S(1)}, u32[]{:S(2)}, u32[]{:S(2)}) collective-permute-start(bf16[128,512]{1,0:T(8,128)(2,1)S(1)} %collective-permute-done.16.refs_2_), channel_id=1, source_target_pairs={{0,8},{8,0},{16,24},{24,16},{1,9},{9,1},{17,25},{25,17},{2,10},{10... | collective-permute-start | bytes 393224 | tf_op jit(solution)/shard_map/ppermute | solution.py:48
  43.8 5.8 %collective-permute-start.23 = (bf16[512,128]{1,0:T(8,128)(2,1)S(1)}, bf16[512,128]{1,0:T(8,128)(2,1)S(1)}, u32[]{:S(2)}, u32[]{:S(2)}) collective-permute-start(bf16[512,128]{1,0:T(8,128)(2,1)S(1)} %bitcast.156), channel_id=1, source_target_pairs={{0,2},{1,3},{2,0},{3,1},{4,6},{5,7},{6,4},{7,5},{8,10},{9,11},{10,... | collective-permute-start | bytes 393224 | tf_op jit(solution)/shard_map/ppermute | solution.py:48
  45.5 7.5 %collective-permute-start.20 = (bf16[544,128]{1,0:T(8,128)(2,1)S(1)}, bf16[544,128]{1,0:T(8,128)(2,1)S(1)}, u32[]{:S(2)}, u32[]{:S(2)}) collective-permute-start(bf16[544,128]{1,0:T(8,128)(2,1)S(1)} %constant_dynamic-update-slice_fusion.10), channel_id=1, source_target_pairs={{0,17},{1,16},{2,19},{3,18},{4,21},{5,20},{6,23},{7,22},{8,25},{9,... | collective-permute-start | bytes 417800 | tf_op jit(solution)/shard_map/ppermute | solution.py:453
  46.6 8.4 %collective-permute-start.19 = (bf16[544,128]{1,0:T(8,128)(2,1)S(1)}, bf16[544,128]{1,0:T(8,128)(2,1)S(1)}, u32[]{:S(2)}, u32[]{:S(2)}) collective-permute-start(bf16[544,128]{1,0:T(8,128)(2,1)S(1)} %constant_dynamic-update-slice_fusion.6), channel_id=1, source_target_pairs={{0,1},{1,0},{2,3},{3,2},{4,5},{5,4},{6,7},{7,6},{8,9},{9,8},{10,11... | collective-permute-start | bytes 417800 | tf_op jit(solution)/shard_map/ppermute | solution.py:453
  47.9 6.4 %collective-permute-start.18 = (bf16[544,128]{1,0:T(8,128)(2,1)S(1)}, bf16[544,128]{1,0:T(8,128)(2,1)S(1)}, u32[]{:S(2)}, u32[]{:S(2)}) collective-permute-start(bf16[544,128]{1,0:T(8,128)(2,1)S(1)} %constant_dynamic-update-slice_fusion.2), channel_id=1, source_target_pairs={{0,16},{1,17},{2,18},{3,19},{4,20},{5,21},{6,22},{7,23},{8,24},{9,... | collective-permute-start | bytes 417800 | tf_op jit(solution)/shard_map/ppermute | solution.py:453
  49.7 8.6 %collective-permute-start.24 = (bf16[256,128]{1,0:T(8,128)(2,1)S(1)}, bf16[256,128]{1,0:T(8,128)(2,1)S(1)}, u32[]{:S(2)}, u32[]{:S(2)}) collective-permute-start(bf16[256,128]{1,0:T(8,128)(2,1)S(1)} %fusion.8), channel_id=1, source_target_pairs={{0,4},{1,5},{2,6},{3,7},{4,0},{5,1},{6,2},{7,3},{8,12},{9,13},{10,... | collective-permute-start | bytes 196616 | tf_op jit(solution)/shard_map/ppermute | solution.py:48
  55.1 7.2 %collective-permute-start.26 = (bf16[160,128]{1,0:T(8,128)(2,1)S(1)}, bf16[160,128]{1,0:T(8,128)(2,1)S(1)}, u32[]{:S(2)}, u32[]{:S(2)}) collective-permute-start(bf16[160,128]{1,0:T(8,128)(2,1)S(1)} %constant_dynamic-update-slice_fusion.14), channel_id=1, source_target_pairs={{0,2},{1,3},{2,0},{3,1},{4,6},{5,7},{6,4},{7,5},{8,10},{9,11},{10,... | collective-permute-start | bytes 122888 | tf_op jit(solution)/shard_map/ppermute | solution.py:48
  55.7 6.7 %collective-permute-start.27 = (bf16[160,128]{1,0:T(8,128)(2,1)S(1)}, bf16[160,128]{1,0:T(8,128)(2,1)S(1)}, u32[]{:S(2)}, u32[]{:S(2)}) collective-permute-start(bf16[160,128]{1,0:T(8,128)(2,1)S(1)} %constant_dynamic-update-slice_fusion.19), channel_id=1, source_target_pairs={{0,4},{1,5},{2,6},{3,7},{4,0},{5,1},{6,2},{7,3},{8,12},{9,13},{10,... | collective-permute-start | bytes 122888 | tf_op jit(solution)/shard_map/ppermute | solution.py:48
  58.4 4.0 %collective-permute-start.25 = (bf16[128,128]{1,0:T(8,128)(2,1)S(1)}, bf16[128,128]{1,0:T(8,128)(2,1)S(1)}, u32[]{:S(2)}, u32[]{:S(2)}) collective-permute-start(bf16[128,128]{1,0:T(8,128)(2,1)S(1)} %fusion.12), channel_id=1, source_target_pairs={{0,1},{1,0},{2,3},{3,2},{4,5},{5,4},{6,7},{7,6},{8,9},{9,8},{10,11... | collective-permute-start | bytes 98312 | tf_op jit(solution)/shard_map/ppermute | solution.py:48
  59.6 5.8 %collective-permute-start.28 = (bf16[160,128]{1,0:T(8,128)(2,1)S(1)}, bf16[160,128]{1,0:T(8,128)(2,1)S(1)}, u32[]{:S(2)}, u32[]{:S(2)}) collective-permute-start(bf16[160,128]{1,0:T(8,128)(2,1)S(1)} %constant_dynamic-update-slice_fusion.24), channel_id=1, source_target_pairs={{0,6},{1,7},{2,4},{3,5},{4,2},{5,3},{6,0},{7,1},{8,14},{9,15},{10,... | collective-permute-start | bytes 122888 | tf_op jit(solution)/shard_map/ppermute | solution.py:48
  65.5 4.5 %collective-permute-start.30 = (bf16[1,2,128,128]{3,2,1,0:T(8,128)(2,1)S(1)}, bf16[1,2,128,128]{3,2,1,0:T(8,128)(2,1)S(1)}, u32[]{:S(2)}, u32[]{:S(2)}) collective-permute-start(bf16[1,2,128,128]{3,2,1,0:T(8,128)(2,1)S(1)} %pad_maximum_fusion.5), channel_id=1, source_target_pairs={{0,2},{1,3},{2,0},{3,1},{4,6},{5,7},{6,4},{7,5},{8,10},{9,11},{10,... | collective-permute-start | bytes 196616 | tf_op jit(solution)/shard_map/ppermute | solution.py:48
  65.5 6.2 %collective-permute-start.32 = (bf16[1,2,128,128]{3,2,1,0:T(8,128)(2,1)S(1)}, bf16[1,2,128,128]{3,2,1,0:T(8,128)(2,1)S(1)}, u32[]{:S(2)}, u32[]{:S(2)}) collective-permute-start(bf16[1,2,128,128]{3,2,1,0:T(8,128)(2,1)S(1)} %pad_maximum_fusion.5), channel_id=1, source_target_pairs={{0,6},{1,7},{2,4},{3,5},{4,2},{5,3},{6,0},{7,1},{8,14},{9,15},{10,... | collective-permute-start | bytes 196616 | tf_op jit(solution)/shard_map/ppermute | solution.py:48
  66.6 6.8 %collective-permute-start.31 = (bf16[1,2,128,128]{3,2,1,0:T(8,128)(2,1)S(1)}, bf16[1,2,128,128]{3,2,1,0:T(8,128)(2,1)S(1)}, u32[]{:S(2)}, u32[]{:S(2)}) collective-permute-start(bf16[1,2,128,128]{3,2,1,0:T(8,128)(2,1)S(1)} %pad_maximum_fusion.5), channel_id=1, source_target_pairs={{0,4},{1,5},{2,6},{3,7},{4,0},{5,1},{6,2},{7,3},{8,12},{9,13},{10,... | collective-permute-start | bytes 196616 | tf_op jit(solution)/shard_map/ppermute | solution.py:48
  69.0 10.1 %collective-permute-start.29 = (bf16[2,128,128]{2,1,0:T(8,128)(2,1)S(1)}, bf16[2,128,128]{2,1,0:T(8,128)(2,1)S(1)}, u32[]{:S(2)}, u32[]{:S(2)}) collective-permute-start(bf16[2,128,128]{2,1,0:T(8,128)(2,1)S(1)} %pad_maximum_fusion.4.refs_0_), channel_id=1, source_target_pairs={{0,1},{1,0},{2,3},{3,2},{4,5},{5,4},{6,7},{7,6},{8,9},{9,8},{10,11... | collective-permute-start | bytes 196616 | tf_op jit(solution)/shard_map/ppermute | solution.py:48
  73.4 5.7 %collective-permute-start.33 = (bf16[3,2,128,128]{3,2,1,0:T(8,128)(2,1)S(1)}, bf16[3,2,128,128]{3,2,1,0:T(8,128)(2,1)S(1)}, u32[]{:S(2)}, u32[]{:S(2)}) collective-permute-start(bf16[3,2,128,128]{3,2,1,0:T(8,128)(2,1)S(1)} %pad_maximum_fusion.3), channel_id=1, source_target_pairs={{0,1},{1,0},{2,3},{3,2},{4,5},{5,4},{6,7},{7,6},{8,9},{9,8},{10,11... | collective-permute-start | bytes 589832 | tf_op jit(solution)/shard_map/ppermute | solution.py:48

commit v5 on v4

--- a/solution.py
+++ b/solution.py
@@ -38,7 +38,7 @@
         out_specs=[VMEM] * len(outs),
         scratch_shapes=list(scratch),
         compiler_params=pltpu.CompilerParams(vmem_limit_bytes=vmem * 2**20),
-        cost_estimate=pl.CostEstimate(flops=flops, bytes_accessed=2**20, transcendentals=0),
+        cost_estimate=pl.CostEstimate(flops=flops, bytes_accessed=flops // 1000, transcendentals=0),
         name=name,
     )(*[a for _, a in ins])
 
@@ -48,8 +48,12 @@
     return lax.ppermute(value, axis, [(i, i ^ mask) for i in range(size)])
 
 
-def normed_body(n_ens, dsh, x_ref, up_ref, down_ref, gain_ref, n_ref, keep_ref, send_ref, turned_ref):
+def normed_body(
+    n_ens, dsh, x_ref, up_ref, down_ref, gain_ref, pw_ref, mask_ref, n_ref, keep_ref, send_ref, lw_ref, turned_ref
+):
     core = lax.axis_index("ens") % 2
+    live = jnp.where(mask_ref[pl.ds(lax.axis_index("pix"), 1), :] > 0, 1.0, 0.0)
+    lw_ref[...] = jnp.broadcast_to(pw_ref[...] * live, (LANES, TILE)).T
     gain = gain_ref[...]
     for i, ref in enumerate((up_ref, x_ref, down_ref)):
         rows = ref[0].astype(F32)
@@ -138,11 +142,10 @@
 
 def backward_body(n_ens, factor, *refs):
     f_refs = refs[:n_ens]
-    wo_ref, target_ref, pw_ref, mask_ref, read_ref, w_ref, nb_ref, nm_ref, gf_ref, con_ref = refs[n_ens:]
+    wo_ref, target_ref, lw_ref, read_ref, w_ref, nb_ref, nm_ref, gf_ref, con_ref = refs[n_ens:]
     position = lax.axis_index("pix")
     counts = counts_of(nb_ref, nm_ref, position)
-    live = jnp.where(mask_ref[pl.ds(position, 1), :] > 0, 1.0, 0.0)
-    lw = jnp.broadcast_to(pw_ref[...] * live, (LANES, TILE)).T
+    lw = lw_ref[...]
     target = target_ref[...]
     fc = [ref[...].astype(F32) for ref in f_refs]
     sums = [jnp.zeros((TILE, LANES), F32) for _ in range(n_ens)]
@@ -287,6 +290,7 @@
     assert rows == TILE and n_out == LANES
 
     far = ens_bits[:-1]
+    mask_rows = pix_mask.reshape(n_pix, TILE)
     half, side = dsh // 2, (p // 2) % 2
     w_vo = jnp.concatenate([w_value, w_out.T])
 
@@ -299,21 +303,32 @@
     down = lax.ppermute(sample_layer_feed, "pix", [(i + 1, i) for i in range(n_pix - 1)])
     w_qk = jnp.concatenate([w_query, w_key])
     qk_near = xor_permute(w_qk, "ens", 1)
+    turned = ((d_model // 2, 3 * TILE), BF16)
+    normed, turned_keep, turned_send, lw = call(
+        functools.partial(normed_body, n_ens, dsh),
+        [((3 * TILE, d_model), BF16), turned, turned, ((TILE, LANES), F32)],
+        [("v", sample_layer_feed), ("v", up), ("v", down), ("v", gain.reshape(1, -1))]
+        + [("v", pixel_weight.reshape(1, TILE)), ("v", mask_rows)],
+        10**7,
+        "normed",
+        scratch=[pltpu.VMEM((d_model, 3 * TILE), BF16)],
+    )
+
     shards = sorted(j for j in qk_far if j)
-    pieces = []
-    for j in shards:
-        whole = qk_far[j].shape[0] // half - 1
-        pieces += [(part, i // 2, j, i % 2) for i, part in enumerate(jnp.split(qk_far[j][: whole * half], max(whole, 1))) if whole]
-        for m in range(1):
-            part = qk_far[j][(whole + m) * half : (whole + m + 1) * half]
-            pieces.append((part, 2 - 1 + m, j, 2))
-            pieces.append((xor_permute(part, "pix", 2), 2 - 1 + m, j, 3))
-    parts = [piece[0] for piece in pieces]
-    up, down, qk_near, parts = lax.optimization_barrier((up, down, qk_near, parts))
-    parts += [xor_permute(part, "ens", 1) for part in parts]
-    qk_layout = [[(0, m * dsh, dsh, 0, 0), (1, m * dsh, dsh, 1, 0)] for m in (0, 1)]
-    for i, (_, m, j, place) in enumerate(pieces * 2):
-        qk_layout[m].append((2 + i, 0, half, j if i < len(pieces) else j ^ 1, place))
+    qk_far = [qk_far[j] for j in shards]
+    k_far = joined([rows[dsh:] for rows in qk_far])
+    k_other = xor_permute(k_far, "pix", 2)
+    normed, qk_near, k_far, k_other, qk_far = lax.optimization_barrier((normed, qk_near, k_far, k_other, qk_far))
+    q_far = joined([rows[:dsh] for rows in qk_far])
+    q_cross = [xor_permute(part, "ens", 1) for part in jnp.split(q_far, 2 * len(shards))]
+    k_cross, k_other_cross = xor_permute(k_far, "ens", 1), xor_permute(k_other, "ens", 1)
+    parts = [q_far, k_far, k_other, k_cross, k_other_cross] + q_cross
+    q_layout, k_layout = ([(0, m * dsh, dsh, 0, 0), (1, m * dsh, dsh, 1, 0)] for m in (0, 1))
+    for i, j in enumerate(shards):
+        q_layout.append((2, i * dsh, dsh, j, 0))
+        q_layout += [(7 + 2 * i + m, 0, half, j ^ 1, m) for m in (0, 1)]
+        k_layout += [(3 + m, i * half, half, j, 2 + m) for m in (0, 1)]
+        k_layout += [(5 + m, i * half, half, j ^ 1, 2 + m) for m in (0, 1)]
 
     def layout(first):
         table = [(0, first, dsh, 0, 0), (1, first, dsh, 1, 0)]
@@ -322,24 +337,13 @@
             table += [(2, row, dsh, j, 0), (3, row, dsh, j ^ 1, 0)]
         return table
 
-    mask_rows = pix_mask.reshape(n_pix, TILE)
-    half = ((d_model // 2, 3 * TILE), BF16)
-    normed, turned_keep, turned_send = call(
-        functools.partial(normed_body, n_ens, dsh),
-        [((3 * TILE, d_model), BF16), half, half],
-        [("v", sample_layer_feed), ("v", up), ("v", down), ("v", gain.reshape(1, -1))],
-        10**7,
-        "normed",
-        scratch=[pltpu.VMEM((d_model, 3 * TILE), BF16)],
-    )
-
     full = pltpu.VMEM((d_model, inner), BF16)
     (weights,) = call(
-        functools.partial(weights_body, qk_layout[0], qk_layout[1], dsh),
+        functools.partial(weights_body, q_layout, k_layout, dsh),
         [((HEADS, TILE, 3 * TILE), BF16)],
         [("v", normed), ("v", mask_rows), ("s", neighbours), ("s", neighbour_mask)]
         + [("v", a) for a in [w_qk, qk_near] + parts],
-        10**9,
+        10**3,
         "weights",
         scratch=[full],
     )
@@ -367,6 +371,7 @@
     )
     forecasts = in_order(gathered(forecast, "ens", ens_bits))
     forecast, attended = lax.optimization_barrier((forecast, attended))
+    forecasts, turned_sib = lax.optimization_barrier((forecasts, turned_sib))
     attended_near = gathered(attended, "ens", far)
 
     factor = 1.0 / math.sqrt(n_ens * n_pix * TILE)
@@ -374,7 +379,7 @@
         functools.partial(backward_body, n_ens, factor),
         [((n_ens * TILE, LANES), BF16), ((3 * TILE + 16, inner), BF16)],
         [("v", a) for a in forecasts + [w_out_full]]
-        + [("v", target), ("v", pixel_weight.reshape(1, TILE)), ("v", mask_rows), ("v", readout_matrix)]
+        + [("v", target), ("v", lw), ("v", readout_matrix)]
         + [("v", weights), ("s", neighbours), ("s", neighbour_mask)],
         10**9,
         "backward",
@@ -429,15 +434,10 @@
     def added(kept, received):
         return functools.reduce(jnp.add, [m.astype(F32) for m in received], kept)
 
-    def added_with_loss(kept, received, total, group):
-        size, pos = 1 << len(group), (p // group[0]) % (1 << len(group))
-        received = [split_loss(m) for m in received]
-        totals = jnp.stack([total] + [other for _, other in received])
-        total = functools.reduce(jnp.add, [at(totals, pos ^ i) for i in range(size)])
-        return added(kept, [m for m, _ in received]), total
-
-    for bit in [bit for group in groups[1:] for bit in group]:
+    later = [bit for group in groups[1:] for bit in group]
+    for bit in later[:-1]:
         output_term = added(*sent(output_term, [bit]))
+    output_kept, output_got = sent(output_term, groups[0], higher=2)
     upper, low = (e // far[-1]) % 2, p % 2
     quarters = [pieces_of(h, groups[0]) for h in value_term.reshape(2, -1, LANES)]
     quarters = jnp.stack([part_of(q, i) for q in quarters for i in range(2)])
@@ -459,22 +459,35 @@
     losses = jnp.stack([losses[d] for d in range(4)])
     loss = functools.reduce(jnp.add, [at(losses, pos ^ i) for i in range(4)])
 
-    output_term = added(*sent(output_term, groups[0], higher=1))
     for group in groups[1:]:
-        kept, received = sent(value_term, group, loss)
-        output_term, received = lax.optimization_barrier((output_term, received))
-        value_term, loss = added_with_loss(kept, received, loss, group)
+        size, pos = 1 << len(group), (p // group[0]) % (1 << len(group))
+        split = pieces_of(value_term, group)
+        kept, messages = part_of(split, pos), {d: part_of(split, pos ^ d).astype(BF16) for d in range(1, size)}
+        top = size // 2
+        if group == groups[-1]:
+            split = pieces_of(added(output_kept, output_got), [later[-1]], 1)
+            own = (p // later[-1]) % 2
+            output_kept = part_of(split, own)
+            messages[top] = jnp.concatenate([messages[top], part_of(split, 1 - own).astype(BF16)])
+        received = {d: split_loss(xor_permute(with_loss(m, loss), "pix", d * group[0])) for d, m in messages.items()}
+        if group == groups[-1]:
+            both, other = received[top]
+            output_term = output_kept + both[-output_kept.shape[0] :].astype(F32)
+            received[top] = (both[: kept.shape[0]], other)
+        totals = jnp.stack([loss] + [received[d][1] for d in range(1, size)])
+        loss = functools.reduce(jnp.add, [at(totals, pos ^ i) for i in range(size)])
+        value_term = added(kept, [received[d][0] for d in range(1, size)])
     terms = [value_term, output_term]
     piece = jnp.stack(terms).astype(BF16)
-    pieces = {0: piece}
-    pair = {1: xor_permute(piece, "pix", 1)}
+    pieces, near = {0: piece}, groups[1][0]
+    pair = {1: xor_permute(piece, "pix", 1), near ^ 1: xor_permute(piece, "pix", near ^ 1)}
     for group in reversed(groups[1:]):
         keys = sorted(pieces)
         stack = jnp.stack([pieces[j] for j in keys])
         new = {d: xor_permute(stack, "pix", d * group[0]) for d in range(1, 1 << len(group))}
         for i, j in enumerate(keys):
             pieces.update({j ^ (d * group[0]): got[i] for d, got in new.items()})
-    later = [j for j in sorted(pieces) if j]
+    later = [j for j in sorted(pieces) if j not in (0, near)]
     got = xor_permute(jnp.stack([pieces[j] for j in later]), "pix", 1)
     pair.update({j ^ 1: got[i] for i, j in enumerate(later)})
     pieces.update(pair)

time: 80.6 us -> 78.3 us (0.971)
  starting transfers between devices: 33.3 us -> 32.2 us
    ppermute x29, waiting for transfers between devices: 26.1 us -> 22.6 us  [xor_permute(): return lax.ppermute(value, axis, [(i, i ^ mask) for i in range(size)])]
    ppermute x3, waiting for transfers between devices: 2.51 us -> 5.48 us  [per_device(): lax.ppermute(message, ('ens', 'pix'), pairs)]
    ppermute x29, starting transfers between devices: 25 us -> 23.9 us  [xor_permute(): return lax.ppermute(value, axis, [(i, i ^ mask) for i in range(size)])]
    unnamed x28 -> x29, local copies, waits for them, and re-layouts: 2.43 us -> 1.79 us
  transfers between devices with their start and end apart: 34 -> 34, of which waited for: 20 -> 20; matrix products, arithmetic and copies ran while one was open for 1% -> 1% of each run, Pallas kernels for 6% -> 9%
where the time goes in v5:
time: 78.3 us; the launch traced here: 78.1 us
  starting transfers between devices  32.2 us (41%)
  waiting for transfers between devices  32.2 us (41%)
  Pallas kernels  8.86 us (11%)
  local copies, waits for them, and re-layouts  2.12 us (3%)
  other arithmetic  1.51 us (2%)
  between operations  1.16 us (1%)
    ppermute x29, starting transfers between devices, xor_permute(): return lax.ppermute(value, axis, [(i, i ^ mask) for i in range(size)])  23.9 us
    ppermute x29, waiting for transfers between devices, xor_permute(): return lax.ppermute(value, axis, [(i, i ^ mask) for i in range(size)])  22.6 us
    pallas_call x8, Pallas kernels, call(): pl.pallas_call(body, out_shape=[jax.ShapeDtypeStruct(s, d) for s, d in ou...  8.86 us
    ppermute x3, waiting for transfers between devices, per_device(): lax.ppermute(message, ('ens', 'pix'), pairs)  5.48 us
    ppermute x1, waiting for transfers between devices, per_device(): lax.ppermute(sample_layer_feed, 'pix', [(i, i + 1) for i in range(n_pix -...  4.18 us
    ppermute x3, starting transfers between devices, per_device(): lax.ppermute(message, ('ens', 'pix'), pairs)  3.55 us
    ppermute x1, starting transfers between devices, per_device(): lax.ppermute(sample_layer_feed, 'pix', [(i, i + 1) for i in range(n_pix -...  3.43 us
    unnamed x29, local copies, waits for them, and re-layouts  1.79 us
  transfers between devices with their start and end apart: 34, of which 20 were waited for; matrix products, arithmetic and copies ran while one was open for 1% of the time, Pallas kernels for 9%

profile of v5, /device:TPU:0, one launch (start us, length us, event | category | flops | bytes accessed | tf_op | source)
XLA Modules:
  0.0 78.1 jit_solution(6055040307336121838)
XLA Ops:
  0.7 1.0 %slice_select_fusion = bf16[128,512]{1,0:T(8,128)(2,1)S(1)} fusion(bf16[256,512]{1,0:T(8,128)(2,1)} %param.15, pred[]{:T(512)S(6)} %eq.11), kind=kLoop, calls=%fused_computation.20 | loop fusion | flops 65536 | bytes 393217 | tf_op jit(solution)/shard_map/jit(_where)/select_n | solution.py:298
  1.8 3.0 %collective-permute-start.3 = (bf16[384,512]{1,0:T(8,128)(2,1)S(1)}, bf16[384,512]{1,0:T(8,128)(2,1)S(1)}, u32[]{:S(2)}, u32[]{:S(2)}) collective-permute-start(bf16[384,512]{1,0:T(8,128)(2,1)S(1)} %pad_maximum_fusion.2), channel_id=1, source_target_pairs={{0,16},{8,24},{16,0},{24,8},{1,17},{9,25},{17,1},{25,9},{2,18},{10... | collective-permute-start | bytes 1179656 | tf_op jit(solution)/shard_map/ppermute | solution.py:48
  4.9 0.1 collective-permute-start.2
  4.9 0.8 %copy-done = bf16[1,128,1024]{2,1,0:T(8,128)(2,1)S(1)} copy-done((bf16[1,128,1024]{2,1,0:T(8,128)(2,1)S(1)}, bf16[1,128,1024]{2,1,0:T(8,128)(2,1)}, u32[]{:S(2)}) %copy-start) | copy-done | bytes 262168
  5.7 3.4 %collective-permute-start = (bf16[1,128,1024]{2,1,0:T(8,128)(2,1)S(1)}, bf16[1,128,1024]{2,1,0:T(8,128)(2,1)S(1)}, u32[]{:S(2)}, u32[]{:S(2)}) collective-permute-start(bf16[1,128,1024]{2,1,0:T(8,128)(2,1)S(1)} %copy-done), channel_id=1, source_target_pairs={{0,1},{1,2},{2,3},{3,4},{4,5},{5,6},{6,7},{8,9},{9,10},{10,11},{11... | collective-permute-start | bytes 786440 | tf_op jit(solution)/shard_map/ppermute | solution.py:302
  9.2 1.3 %collective-permute-start.1 = (bf16[1,128,1024]{2,1,0:T(8,128)(2,1)S(1)}, bf16[1,128,1024]{2,1,0:T(8,128)(2,1)S(1)}, u32[]{:S(2)}, u32[]{:S(2)}) collective-permute-start(bf16[1,128,1024]{2,1,0:T(8,128)(2,1)S(1)} %copy-done), channel_id=1, source_target_pairs={{1,0},{2,1},{3,2},{4,3},{5,4},{6,5},{7,6},{9,8},{10,9},{11,10},{12... | collective-permute-start | bytes 786440 | tf_op jit(solution)/shard_map/ppermute | solution.py:303
  10.5 0.1 copy.20
  10.7 0.9 %collective-permute-start.9 = (bf16[512,512]{1,0:T(8,128)(2,1)S(1)}, bf16[512,512]{1,0:T(8,128)(2,1)S(1)}, u32[]{:S(2)}, u32[]{:S(2)}) collective-permute-start(bf16[512,512]{1,0:T(8,128)(2,1)S(1)} %pad_maximum_fusion.1.refs_0_), channel_id=1, source_target_pairs={{0,16},{8,24},{16,0},{24,8},{1,17},{9,25},{17,1},{25,9},{2,18},{10... | collective-permute-start | bytes 1572872 | tf_op jit(solution)/shard_map/ppermute | solution.py:48
  11.6 3.1 %collective-permute-done.3 = bf16[384,512]{1,0:T(8,128)(2,1)S(1)} collective-permute-done((bf16[384,512]{1,0:T(8,128)(2,1)S(1)}, bf16[384,512]{1,0:T(8,128)(2,1)S(1)}, u32[]{:S(2)}, u32[]{:S(2)}) %collective-permute-start.3) | collective-permute-done | bytes 393248 | tf_op jit(solution)/shard_map/ppermute | solution.py:48
  14.7 1.1 %collective-permute-start.4 = (bf16[128,512]{1,0:T(8,128)(2,1)S(1)}, bf16[128,512]{1,0:T(8,128)(2,1)S(1)}, u32[]{:S(2)}, u32[]{:S(2)}) collective-permute-start(bf16[128,512]{1,0:T(8,128)(2,1)S(1)} %slice.175.refs_3_), channel_id=1, source_target_pairs={{0,2},{1,3},{2,0},{3,1},{4,6},{5,7},{6,4},{7,5},{8,10},{9,11},{10,... | collective-permute-start | bytes 393224 | tf_op jit(solution)/shard_map/ppermute | solution.py:48
  15.8 4.2 %collective-permute-done.up_ref = bf16[1,128,1024]{2,1,0:T(8,128)(2,1)S(1)} collective-permute-done((bf16[1,128,1024]{2,1,0:T(8,128)(2,1)S(1)}, bf16[1,128,1024]{2,1,0:T(8,128)(2,1)S(1)}, u32[]{:S(2)}, u32[]{:S(2)}) %collective-permute-start) | collective-permute-done | bytes 262176 | tf_op jit(solution)/shard_map/ppermute | solution.py:302
  20.0 0.6 copy-done.5
  20.6 0.6 normed.1
  21.2 1.3 %collective-permute-done.4.refs_4_ = bf16[128,512]{1,0:T(8,128)(2,1)S(1)} collective-permute-done((bf16[128,512]{1,0:T(8,128)(2,1)S(1)}, bf16[128,512]{1,0:T(8,128)(2,1)S(1)}, u32[]{:S(2)}, u32[]{:S(2)}) %collective-permute-start.4) | collective-permute-done | bytes 131104 | tf_op jit(solution)/shard_map/ppermute | solution.py:48
  22.5 0.1 collective-permute-start.7
  22.6 0.5 collective-permute-start.8
  23.1 0.1 collective-permute-start.5
  23.2 0.4 collective-permute-start.6
  23.6 0.3 collective-permute-done.7.refs_7_
  23.9 0.2 collective-permute-done.8.refs_8_
  24.1 0.3 collective-permute-done.5.refs_5_
  24.5 0.2 collective-permute-done.6.refs_6_
  24.6 2.2 %weights.1.w_ref.refs_8_ = bf16[8,128,384]{2,1,0:T(8,128)(2,1)S(1)} custom-call(bf16[384,1024]{1,0:T(8,128)(2,1)S(1)} %get-tuple-element.43.n_ref, s32[8,128]{1,0:T(8,128)S(1)} %bitcast.133, s32[1,9]{1,0:T(1,128)S(1)} %copy-done.3, s32[1,9]{1,0:T(1,128)S(1)} %copy-done.4, bf16[512,512]{1,0:T(8,128)(2,1)S(1)} %constant_dynamic-update-slice_fusion.refs_0_, ...), custom_call_target="tpu_custom_call" | custom-call | flops 1000 | bytes 1 | tf_op jit(solution)/shard_map/weights/pallas_call | solution.py:34
  26.9 0.4 collective-permute-start.10
  27.3 0.2 collective-permute-start.11
  27.5 0.3 collective-permute-start.15
  27.8 1.1 %collective-permute-done.10.refs_1_ = bf16[512,512]{1,0:T(8,128)(2,1)S(1)} collective-permute-done((bf16[512,512]{1,0:T(8,128)(2,1)S(1)}, bf16[512,512]{1,0:T(8,128)(2,1)S(1)}, u32[]{:S(2)}, u32[]{:S(2)}) %collective-permute-start.10) | collective-permute-done | bytes 524320 | tf_op jit(solution)/shard_map/ppermute | solution.py:48
  28.9 0.7 collective-permute-done.11.refs_3_
  29.6 1.5 %attend.1.att_ref.refs_0_ = bf16[128,512]{1,0:T(8,128)(2,1)S(1)} custom-call(bf16[384,1024]{1,0:T(8,128)(2,1)S(1)} %get-tuple-element.43.n_ref, bf16[8,128,384]{2,1,0:T(8,128)(2,1)S(1)} %weights.1.w_ref.refs_8_, s32[1,9]{1,0:T(1,128)S(1)} %copy-done.3, s32[1,9]{1,0:T(1,128)S(1)} %copy-done.4, bf16[512,512]{1,0:T(8,128)(2,1)S(1)} %pad_maximum_fusion.1.refs_0_, ...), custom_call_target="tpu_custom_call" | custom-call | flops 1000000000 | bytes 1000000 | tf_op jit(solution)/shard_map/attend/pallas_call | solution.py:34
  31.2 0.7 forecast.1
  31.9 1.0 %collective-permute-start.12 = (bf16[128,128]{1,0:T(8,128)(2,1)S(1)}, bf16[128,128]{1,0:T(8,128)(2,1)S(1)}, u32[]{:S(2)}, u32[]{:S(2)}) collective-permute-start(bf16[128,128]{1,0:T(8,128)(2,1)S(1)} %get-tuple-element.57.refs_0_), channel_id=1, source_target_pairs={{0,16},{8,24},{16,0},{24,8},{1,17},{9,25},{17,1},{25,9},{2,18},{10... | collective-permute-start | bytes 98312 | tf_op jit(solution)/shard_map/ppermute | solution.py:48
  32.9 1.1 %collective-permute-start.16 = (bf16[128,512]{1,0:T(8,128)(2,1)S(1)}, bf16[128,512]{1,0:T(8,128)(2,1)S(1)}, u32[]{:S(2)}, u32[]{:S(2)}) collective-permute-start(bf16[128,512]{1,0:T(8,128)(2,1)S(1)} %attend.1.att_ref.refs_0_), channel_id=1, source_target_pairs={{0,16},{8,24},{16,0},{24,8},{1,17},{9,25},{17,1},{25,9},{2,18},{10... | collective-permute-start | bytes 393224 | tf_op jit(solution)/shard_map/ppermute | solution.py:48
  34.0 2.2 %collective-permute-done.12.refs_2_ = bf16[128,128]{1,0:T(8,128)(2,1)S(1)} collective-permute-done((bf16[128,128]{1,0:T(8,128)(2,1)S(1)}, bf16[128,128]{1,0:T(8,128)(2,1)S(1)}, u32[]{:S(2)}, u32[]{:S(2)}) %collective-permute-start.12) | collective-permute-done | bytes 32800 | tf_op jit(solution)/shard_map/ppermute | solution.py:48
  36.1 0.5 collective-permute-start.14
  36.7 0.7 collective-permute-done.13.refs_1_
  37.3 0.2 collective-permute-done.14.refs_3_
  37.5 1.5 %backward.1 = (bf16[512,128]{1,0:T(8,128)(2,1)S(1)}, bf16[400,512]{1,0:T(8,128)(2,1)S(1)}) custom-call(bf16[128,128]{1,0:T(8,128)(2,1)S(1)} %get-tuple-element.57.refs_0_, bf16[128,128]{1,0:T(8,128)(2,1)S(1)} %collective-permute-done.13.refs_1_, bf16[128,128]{1,0:T(8,128)(2,1)S(1)} %collective-permute-done.12.refs_2_, ...), custom_call_target="tpu_custom_call" | custom-call | flops 1000000000 | bytes 1000000 | tf_op jit(solution)/shard_map/backward/pallas_call | solution.py:34
  39.0 0.4 collective-permute-start.17
  39.4 0.2 collective-permute-start.22
  39.6 0.3 collective-permute-start.23
  40.0 0.9 %collective-permute-done.17.sib_con = bf16[400,512]{1,0:T(8,128)(2,1)S(1)} collective-permute-done((bf16[400,512]{1,0:T(8,128)(2,1)S(1)}, bf16[400,512]{1,0:T(8,128)(2,1)S(1)}, u32[]{:S(2)}, u32[]{:S(2)}) %collective-permute-start.17) | collective-permute-done | bytes 409632 | tf_op jit(solution)/shard_map/ppermute | solution.py:48
  40.8 0.7 value_term.1
  41.6 0.4 output_term.1
  42.0 2.5 %collective-permute-start.24 = (bf16[512,128]{1,0:T(8,128)(2,1)S(1)}, bf16[512,128]{1,0:T(8,128)(2,1)S(1)}, u32[]{:S(2)}, u32[]{:S(2)}) collective-permute-start(bf16[512,128]{1,0:T(8,128)(2,1)S(1)} %bitcast.153), channel_id=1, source_target_pairs={{0,2},{1,3},{2,0},{3,1},{4,6},{5,7},{6,4},{7,5},{8,10},{9,11},{10,... | collective-permute-start | bytes 393224 | tf_op jit(solution)/shard_map/ppermute | solution.py:48
  44.9 1.0 %collective-permute-start.18 = (bf16[544,128]{1,0:T(8,128)(2,1)S(1)}, bf16[544,128]{1,0:T(8,128)(2,1)S(1)}, u32[]{:S(2)}, u32[]{:S(2)}) collective-permute-start(bf16[544,128]{1,0:T(8,128)(2,1)S(1)} %constant_dynamic-update-slice_fusion.2), channel_id=1, source_target_pairs={{0,16},{1,17},{2,18},{3,19},{4,20},{5,21},{6,22},{7,23},{8,24},{9,... | collective-permute-start | bytes 417800 | tf_op jit(solution)/shard_map/ppermute | solution.py:453
  45.8 0.6 collective-permute-start.19
  46.5 2.0 %collective-permute-start.20 = (bf16[544,128]{1,0:T(8,128)(2,1)S(1)}, bf16[544,128]{1,0:T(8,128)(2,1)S(1)}, u32[]{:S(2)}, u32[]{:S(2)}) collective-permute-start(bf16[544,128]{1,0:T(8,128)(2,1)S(1)} %constant_dynamic-update-slice_fusion.10), channel_id=1, source_target_pairs={{0,17},{1,16},{2,19},{3,18},{4,21},{5,20},{6,23},{7,22},{8,25},{9,... | collective-permute-start | bytes 417800 | tf_op jit(solution)/shard_map/ppermute | solution.py:453
  48.5 0.8 %collective-permute-start.25 = (bf16[256,128]{1,0:T(8,128)(2,1)S(1)}, bf16[256,128]{1,0:T(8,128)(2,1)S(1)}, u32[]{:S(2)}, u32[]{:S(2)}) collective-permute-start(bf16[256,128]{1,0:T(8,128)(2,1)S(1)} %bitcast.154), channel_id=1, source_target_pairs={{0,1},{1,0},{2,3},{3,2},{4,5},{5,4},{6,7},{7,6},{8,9},{9,8},{10,11... | collective-permute-start | bytes 196616 | tf_op jit(solution)/shard_map/ppermute | solution.py:48
  49.4 4.3 %collective-permute-done.20 = bf16[544,128]{1,0:T(8,128)(2,1)S(1)} collective-permute-done((bf16[544,128]{1,0:T(8,128)(2,1)S(1)}, bf16[544,128]{1,0:T(8,128)(2,1)S(1)}, u32[]{:S(2)}, u32[]{:S(2)}) %collective-permute-start.20) | collective-permute-done | bytes 139296 | tf_op jit(solution)/shard_map/ppermute | solution.py:453
  53.7 1.1 %collective-permute-done.19 = bf16[544,128]{1,0:T(8,128)(2,1)S(1)} collective-permute-done((bf16[544,128]{1,0:T(8,128)(2,1)S(1)}, bf16[544,128]{1,0:T(8,128)(2,1)S(1)}, u32[]{:S(2)}, u32[]{:S(2)}) %collective-permute-start.19) | collective-permute-done | bytes 139296 | tf_op jit(solution)/shard_map/ppermute | solution.py:453
  55.1 0.5 collective-permute-done.25
  55.7 2.7 %collective-permute-start.26 = (bf16[288,128]{1,0:T(8,128)(2,1)S(1)}, bf16[288,128]{1,0:T(8,128)(2,1)S(1)}, u32[]{:S(2)}, u32[]{:S(2)}) collective-permute-start(bf16[288,128]{1,0:T(8,128)(2,1)S(1)} %constant_dynamic-update-slice_fusion.19), channel_id=1, source_target_pairs={{0,4},{1,5},{2,6},{3,7},{4,0},{5,1},{6,2},{7,3},{8,12},{9,13},{10,... | collective-permute-start | bytes 221192 | tf_op jit(solution)/shard_map/ppermute | solution.py:48
  58.4 0.8 %collective-permute-start.21 = (bf16[160,128]{1,0:T(8,128)(2,1)S(1)}, bf16[160,128]{1,0:T(8,128)(2,1)S(1)}, u32[]{:S(2)}, u32[]{:S(2)}) collective-permute-start(bf16[160,128]{1,0:T(8,128)(2,1)S(1)} %constant_dynamic-update-slice_fusion.14), channel_id=1, source_target_pairs={{0,2},{1,3},{2,0},{3,1},{4,6},{5,7},{6,4},{7,5},{8,10},{9,11},{10,... | collective-permute-start | bytes 122888 | tf_op jit(solution)/shard_map/ppermute | solution.py:48
  59.3 4.9 %collective-permute-done.27 = bf16[160,128]{1,0:T(8,128)(2,1)S(1)} collective-permute-done((bf16[160,128]{1,0:T(8,128)(2,1)S(1)}, bf16[160,128]{1,0:T(8,128)(2,1)S(1)}, u32[]{:S(2)}, u32[]{:S(2)}) %collective-permute-start.27) | collective-permute-done | bytes 40992 | tf_op jit(solution)/shard_map/ppermute | solution.py:48
  64.3 1.3 %collective-permute-start.31 = (bf16[1,2,128,128]{3,2,1,0:T(8,128)(2,1)S(1)}, bf16[1,2,128,128]{3,2,1,0:T(8,128)(2,1)S(1)}, u32[]{:S(2)}, u32[]{:S(2)}) collective-permute-start(bf16[1,2,128,128]{3,2,1,0:T(8,128)(2,1)S(1)} %pad_maximum_fusion.5), channel_id=1, source_target_pairs={{0,4},{1,5},{2,6},{3,7},{4,0},{5,1},{6,2},{7,3},{8,12},{9,13},{10,... | collective-permute-start | bytes 196616 | tf_op jit(solution)/shard_map/ppermute | solution.py:48
  65.6 0.9 %collective-permute-start.32 = (bf16[1,2,128,128]{3,2,1,0:T(8,128)(2,1)S(1)}, bf16[1,2,128,128]{3,2,1,0:T(8,128)(2,1)S(1)}, u32[]{:S(2)}, u32[]{:S(2)}) collective-permute-start(bf16[1,2,128,128]{3,2,1,0:T(8,128)(2,1)S(1)} %pad_maximum_fusion.5), channel_id=1, source_target_pairs={{0,6},{1,7},{2,4},{3,5},{4,2},{5,3},{6,0},{7,1},{8,14},{9,15},{10,... | collective-permute-start | bytes 196616 | tf_op jit(solution)/shard_map/ppermute | solution.py:48
  66.5 1.3 %collective-permute-start.29 = (bf16[1,2,128,128]{3,2,1,0:T(8,128)(2,1)S(1)}, bf16[1,2,128,128]{3,2,1,0:T(8,128)(2,1)S(1)}, u32[]{:S(2)}, u32[]{:S(2)}) collective-permute-start(bf16[1,2,128,128]{3,2,1,0:T(8,128)(2,1)S(1)} %pad_maximum_fusion.5), channel_id=1, source_target_pairs={{0,2},{1,3},{2,0},{3,1},{4,6},{5,7},{6,4},{7,5},{8,10},{9,11},{10,... | collective-permute-start | bytes 196616 | tf_op jit(solution)/shard_map/ppermute | solution.py:48
  67.9 0.3 collective-permute-start.28
  68.2 1.9 %collective-permute-start.30 = (bf16[2,128,128]{2,1,0:T(8,128)(2,1)S(1)}, bf16[2,128,128]{2,1,0:T(8,128)(2,1)S(1)}, u32[]{:S(2)}, u32[]{:S(2)}) collective-permute-start(bf16[2,128,128]{2,1,0:T(8,128)(2,1)S(1)} %pad_maximum_fusion.4.refs_0_), channel_id=1, source_target_pairs={{0,3},{1,2},{2,1},{3,0},{4,7},{5,6},{6,5},{7,4},{8,11},{9,10},{10,... | collective-permute-start | bytes 196616 | tf_op jit(solution)/shard_map/ppermute | solution.py:48
  70.1 0.4 collective-permute-done.31
  70.5 1.3 %collective-permute-done.32 = bf16[1,2,128,128]{3,2,1,0:T(8,128)(2,1)S(1)} collective-permute-done((bf16[1,2,128,128]{3,2,1,0:T(8,128)(2,1)S(1)}, bf16[1,2,128,128]{3,2,1,0:T(8,128)(2,1)S(1)}, u32[]{:S(2)}, u32[]{:S(2)}) %collective-permute-start.32) | collective-permute-done | bytes 65568 | tf_op jit(solution)/shard_map/ppermute | solution.py:48
  71.8 0.8 %collective-permute-start.33 = (bf16[2,2,128,128]{3,2,1,0:T(8,128)(2,1)S(1)}, bf16[2,2,128,128]{3,2,1,0:T(8,128)(2,1)S(1)}, u32[]{:S(2)}, u32[]{:S(2)}) collective-permute-start(bf16[2,2,128,128]{3,2,1,0:T(8,128)(2,1)S(1)} %pad_maximum_fusion.3), channel_id=1, source_target_pairs={{0,1},{1,0},{2,3},{3,2},{4,5},{5,4},{6,7},{7,6},{8,9},{9,8},{10,11... | collective-permute-start | bytes 393224 | tf_op jit(solution)/shard_map/ppermute | solution.py:48
  72.7 4.2 %collective-permute-done.33 = bf16[2,2,128,128]{3,2,1,0:T(8,128)(2,1)S(1)} collective-permute-done((bf16[2,2,128,128]{3,2,1,0:T(8,128)(2,1)S(1)}, bf16[2,2,128,128]{3,2,1,0:T(8,128)(2,1)S(1)}, u32[]{:S(2)}, u32[]{:S(2)}) %collective-permute-start.33) | collective-permute-done | bytes 131104 | tf_op jit(solution)/shard_map/ppermute | solution.py:48
  76.9 1.2 %finish.1 = (f32[256,512]{1,0:T(8,128)}, f32[512,256]{1,0:T(8,128)}, f32[1,1]{1,0:T(1,128)}) custom-call(bf16[2,128,128]{2,1,0:T(8,128)(2,1)S(1)} %pad_maximum_fusion.4.refs_0_, bf16[2,128,128]{2,1,0:T(8,128)(2,1)S(1)} %collective-permute-done.28.refs_1_, bf16[2,128,128]{2,1,0:T(8,128)(2,1)S(1)} %bitcast.131, ...), custom_call_target="tpu_custom_call" | custom-call | flops 1000000 | bytes 1000 | tf_op jit(solution)/shard_map/finish/pallas_call | solution.py:34
  (93 shorter events, 1.1 us)
Async XLA Ops:
  0.6 1.1 %copy-start.8 = (bf16[256,512]{1,0:T(8,128)(2,1)S(1)}, bf16[256,512]{1,0:T(8,128)(2,1)}, u32[]{:S(2)}) copy-start(bf16[256,512]{1,0:T(8,128)(2,1)} %param.14) | copy-start | bytes 786436
  1.7 3.0 %copy-start.9 = (bf16[256,512]{1,0:T(8,128)(2,1)S(1)}, bf16[256,512]{1,0:T(8,128)(2,1)}, u32[]{:S(2)}) copy-start(bf16[256,512]{1,0:T(8,128)(2,1)} %param.15) | copy-start | bytes 786436
  1.8 12.9 %collective-permute-start.3 = (bf16[384,512]{1,0:T(8,128)(2,1)S(1)}, bf16[384,512]{1,0:T(8,128)(2,1)S(1)}, u32[]{:S(2)}, u32[]{:S(2)}) collective-permute-start(bf16[384,512]{1,0:T(8,128)(2,1)S(1)} %pad_maximum_fusion.2), channel_id=1, source_target_pairs={{0,16},{8,24},{16,0},{24,8},{1,17},{9,25},{17,1},{25,9},{2,18},{10... | collective-permute-start | bytes 1179656 | tf_op jit(solution)/shard_map/ppermute | solution.py:48
  4.8 1.0 %copy-start = (bf16[1,128,1024]{2,1,0:T(8,128)(2,1)S(1)}, bf16[1,128,1024]{2,1,0:T(8,128)(2,1)}, u32[]{:S(2)}) copy-start(bf16[1,128,1024]{2,1,0:T(8,128)(2,1)} %x_ref.3) | copy-start | bytes 786436
  4.8 5.7 %copy-start.10 = (bf16[512,256]{1,0:T(8,128)(2,1)S(1)}, bf16[512,256]{1,0:T(8,128)(2,1)}, u32[]{:S(2)}) copy-start(bf16[512,256]{1,0:T(8,128)(2,1)} %param.17) | copy-start | bytes 786436
  4.8 5.8 %copy-start.11 = (bf16[256,512]{1,0:T(8,128)(2,1)S(1)}, bf16[256,512]{1,0:T(8,128)(2,1)}, u32[]{:S(2)}) copy-start(bf16[256,512]{1,0:T(8,128)(2,1)} %param.16) | copy-start | bytes 786436
  4.9 17.6 %collective-permute-start.2 = (bf16[512,512]{1,0:T(8,128)(2,1)S(1)}, bf16[512,512]{1,0:T(8,128)(2,1)S(1)}, u32[]{:S(2)}, u32[]{:S(2)}) collective-permute-start(bf16[512,512]{1,0:T(8,128)(2,1)S(1)} %constant_dynamic-update-slice_fusion.refs_0_), channel_id=1, source_target_pairs={{0,8},{8,0},{16,24},{24,16},{1,9},{9,1},{17,25},{25,17},{2,10},{10... | collective-permute-start | bytes 1572872 | tf_op jit(solution)/shard_map/ppermute | solution.py:48
  5.7 14.2 %collective-permute-start = (bf16[1,128,1024]{2,1,0:T(8,128)(2,1)S(1)}, bf16[1,128,1024]{2,1,0:T(8,128)(2,1)S(1)}, u32[]{:S(2)}, u32[]{:S(2)}) collective-permute-start(bf16[1,128,1024]{2,1,0:T(8,128)(2,1)S(1)} %copy-done), channel_id=1, source_target_pairs={{0,1},{1,2},{2,3},{3,4},{4,5},{5,6},{6,7},{8,9},{9,10},{10,11},{11... | collective-permute-start | bytes 786440 | tf_op jit(solution)/shard_map/ppermute | solution.py:302
  9.2 10.8 %collective-permute-start.1 = (bf16[1,128,1024]{2,1,0:T(8,128)(2,1)S(1)}, bf16[1,128,1024]{2,1,0:T(8,128)(2,1)S(1)}, u32[]{:S(2)}, u32[]{:S(2)}) collective-permute-start(bf16[1,128,1024]{2,1,0:T(8,128)(2,1)S(1)} %copy-done), channel_id=1, source_target_pairs={{1,0},{2,1},{3,2},{4,3},{5,4},{6,5},{7,6},{9,8},{10,9},{11,10},{12... | collective-permute-start | bytes 786440 | tf_op jit(solution)/shard_map/ppermute | solution.py:303
  10.7 16.2 %collective-permute-start.9 = (bf16[512,512]{1,0:T(8,128)(2,1)S(1)}, bf16[512,512]{1,0:T(8,128)(2,1)S(1)}, u32[]{:S(2)}, u32[]{:S(2)}) collective-permute-start(bf16[512,512]{1,0:T(8,128)(2,1)S(1)} %pad_maximum_fusion.1.refs_0_), channel_id=1, source_target_pairs={{0,16},{8,24},{16,0},{24,8},{1,17},{9,25},{17,1},{25,9},{2,18},{10... | collective-permute-start | bytes 1572872 | tf_op jit(solution)/shard_map/ppermute | solution.py:48
  14.7 5.3 %copy-start.2 = (f32[1024]{0:T(1024)S(1)}, f32[1024]{0:T(1024)}, u32[]{:S(2)}) copy-start(f32[1024]{0:T(1024)} %param.13) | copy-start | bytes 12292
  14.7 5.3 %copy-start.1 = (s32[1024]{0:T(1024)S(1)}, s32[1024]{0:T(1024)}, u32[]{:S(2)}) copy-start(s32[1024]{0:T(1024)} %param.21) | copy-start | bytes 12292
  14.7 7.8 %collective-permute-start.4 = (bf16[128,512]{1,0:T(8,128)(2,1)S(1)}, bf16[128,512]{1,0:T(8,128)(2,1)S(1)}, u32[]{:S(2)}, u32[]{:S(2)}) collective-permute-start(bf16[128,512]{1,0:T(8,128)(2,1)S(1)} %slice.175.refs_3_), channel_id=1, source_target_pairs={{0,2},{1,3},{2,0},{3,1},{4,6},{5,7},{6,4},{7,5},{8,10},{9,11},{10,... | collective-permute-start | bytes 393224 | tf_op jit(solution)/shard_map/ppermute | solution.py:48
  20.0 0.7 copy-start.5
  22.5 1.4 %collective-permute-start.7 = (bf16[128,512]{1,0:T(8,128)(2,1)S(1)}, bf16[128,512]{1,0:T(8,128)(2,1)S(1)}, u32[]{:S(2)}, u32[]{:S(2)}) collective-permute-start(bf16[128,512]{1,0:T(8,128)(2,1)S(1)} %get-tuple-element.91), channel_id=1, source_target_pairs={{0,8},{8,0},{16,24},{24,16},{1,9},{9,1},{17,25},{25,17},{2,10},{10... | collective-permute-start | bytes 393224 | tf_op jit(solution)/shard_map/ppermute | solution.py:48
  22.6 2.0 %copy-start.3 = (s32[1,9]{1,0:T(1,128)S(1)}, s32[1,9]{1,0:T(1,128)}, u32[]{:S(2)}) copy-start(s32[1,9]{1,0:T(1,128)} %refs_9_.1) | copy-start | bytes 112
  22.6 2.0 %copy-start.4 = (s32[1,9]{1,0:T(1,128)S(1)}, s32[1,9]{1,0:T(1,128)}, u32[]{:S(2)}) copy-start(s32[1,9]{1,0:T(1,128)} %refs_10_.1) | copy-start | bytes 112
  22.6 1.5 %collective-permute-start.8 = (bf16[128,512]{1,0:T(8,128)(2,1)S(1)}, bf16[128,512]{1,0:T(8,128)(2,1)S(1)}, u32[]{:S(2)}, u32[]{:S(2)}) collective-permute-start(bf16[128,512]{1,0:T(8,128)(2,1)S(1)} %get-tuple-element.90), channel_id=1, source_target_pairs={{0,8},{8,0},{16,24},{24,16},{1,9},{9,1},{17,25},{25,17},{2,10},{10... | collective-permute-start | bytes 393224 | tf_op jit(solution)/shard_map/ppermute | solution.py:48
  23.1 1.3 %collective-permute-start.5 = (bf16[128,512]{1,0:T(8,128)(2,1)S(1)}, bf16[128,512]{1,0:T(8,128)(2,1)S(1)}, u32[]{:S(2)}, u32[]{:S(2)}) collective-permute-start(bf16[128,512]{1,0:T(8,128)(2,1)S(1)} %slice.175.refs_3_), channel_id=1, source_target_pairs={{0,8},{8,0},{16,24},{24,16},{1,9},{9,1},{17,25},{25,17},{2,10},{10... | collective-permute-start | bytes 393224 | tf_op jit(solution)/shard_map/ppermute | solution.py:48
  23.2 1.4 %collective-permute-start.6 = (bf16[128,512]{1,0:T(8,128)(2,1)S(1)}, bf16[128,512]{1,0:T(8,128)(2,1)S(1)}, u32[]{:S(2)}, u32[]{:S(2)}) collective-permute-start(bf16[128,512]{1,0:T(8,128)(2,1)S(1)} %collective-permute-done.4.refs_4_), channel_id=1, source_target_pairs={{0,8},{8,0},{16,24},{24,16},{1,9},{9,1},{17,25},{25,17},{2,10},{10... | collective-permute-start | bytes 393224 | tf_op jit(solution)/shard_map/ppermute | solution.py:48
  26.9 4.3 %copy-start.6 = (bf16[1024,128]{1,0:T(8,128)(2,1)S(1)}, bf16[1024,128]{1,0:T(8,128)(2,1)}, u32[]{:S(2)}) copy-start(bf16[1024,128]{1,0:T(8,128)(2,1)} %read_ref.3) | copy-start | bytes 786436
  26.9 2.0 %collective-permute-start.10 = (bf16[512,512]{1,0:T(8,128)(2,1)S(1)}, bf16[512,512]{1,0:T(8,128)(2,1)S(1)}, u32[]{:S(2)}, u32[]{:S(2)}) collective-permute-start(bf16[512,512]{1,0:T(8,128)(2,1)S(1)} %pad_maximum_fusion.1.refs_0_), channel_id=1, source_target_pairs={{0,8},{8,0},{16,24},{24,16},{1,9},{9,1},{17,25},{25,17},{2,10},{10... | collective-permute-start | bytes 1572872 | tf_op jit(solution)/shard_map/ppermute | solution.py:48
  27.3 2.3 %collective-permute-start.11 = (bf16[512,512]{1,0:T(8,128)(2,1)S(1)}, bf16[512,512]{1,0:T(8,128)(2,1)S(1)}, u32[]{:S(2)}, u32[]{:S(2)}) collective-permute-start(bf16[512,512]{1,0:T(8,128)(2,1)S(1)} %collective-permute-done.9.refs_2_), channel_id=1, source_target_pairs={{0,8},{8,0},{16,24},{24,16},{1,9},{9,1},{17,25},{25,17},{2,10},{10... | collective-permute-start | bytes 1572872 | tf_op jit(solution)/shard_map/ppermute | solution.py:48
  27.5 9.2 %collective-permute-start.15 = (bf16[512,384]{1,0:T(8,128)(2,1)S(1)}, bf16[512,384]{1,0:T(8,128)(2,1)S(1)}, u32[]{:S(2)}, u32[]{:S(2)}) collective-permute-start(bf16[512,384]{1,0:T(8,128)(2,1)S(1)} %get-tuple-element.55), channel_id=1, source_target_pairs={{0,8},{8,0},{16,24},{24,16},{1,9},{9,1},{17,25},{25,17},{2,10},{10... | collective-permute-start | bytes 1179656 | tf_op jit(solution)/shard_map/ppermute | solution.py:48
  31.2 6.3 %copy-start.7 = (f32[128,128]{1,0:T(8,128)S(1)}, f32[128,128]{1,0:T(8,128)}, u32[]{:S(2)}) copy-start(f32[128,128]{1,0:T(8,128)} %refs_5_.1) | copy-start | bytes 196612
  31.9 4.3 %collective-permute-start.12 = (bf16[128,128]{1,0:T(8,128)(2,1)S(1)}, bf16[128,128]{1,0:T(8,128)(2,1)S(1)}, u32[]{:S(2)}, u32[]{:S(2)}) collective-permute-start(bf16[128,128]{1,0:T(8,128)(2,1)S(1)} %get-tuple-element.57.refs_0_), channel_id=1, source_target_pairs={{0,16},{8,24},{16,0},{24,8},{1,17},{9,25},{17,1},{25,9},{2,18},{10... | collective-permute-start | bytes 98312 | tf_op jit(solution)/shard_map/ppermute | solution.py:48
  32.9 6.1 %collective-permute-start.16 = (bf16[128,512]{1,0:T(8,128)(2,1)S(1)}, bf16[128,512]{1,0:T(8,128)(2,1)S(1)}, u32[]{:S(2)}, u32[]{:S(2)}) collective-permute-start(bf16[128,512]{1,0:T(8,128)(2,1)S(1)} %attend.1.att_ref.refs_0_), channel_id=1, source_target_pairs={{0,16},{8,24},{16,0},{24,8},{1,17},{9,25},{17,1},{25,9},{2,18},{10... | collective-permute-start | bytes 393224 | tf_op jit(solution)/shard_map/ppermute | solution.py:48
  36.1 1.2 %collective-permute-start.13 = (bf16[128,128]{1,0:T(8,128)(2,1)S(1)}, bf16[128,128]{1,0:T(8,128)(2,1)S(1)}, u32[]{:S(2)}, u32[]{:S(2)}) collective-permute-start(bf16[128,128]{1,0:T(8,128)(2,1)S(1)} %get-tuple-element.57.refs_0_), channel_id=1, source_target_pairs={{0,8},{8,0},{16,24},{24,16},{1,9},{9,1},{17,25},{25,17},{2,10},{10... | collective-permute-start | bytes 98312 | tf_op jit(solution)/shard_map/ppermute | solution.py:48
  36.1 1.4 %collective-permute-start.14 = (bf16[128,128]{1,0:T(8,128)(2,1)S(1)}, bf16[128,128]{1,0:T(8,128)(2,1)S(1)}, u32[]{:S(2)}, u32[]{:S(2)}) collective-permute-start(bf16[128,128]{1,0:T(8,128)(2,1)S(1)} %collective-permute-done.12.refs_2_), channel_id=1, source_target_pairs={{0,8},{8,0},{16,24},{24,16},{1,9},{9,1},{17,25},{25,17},{2,10},{10... | collective-permute-start | bytes 98312 | tf_op jit(solution)/shard_map/ppermute | solution.py:48
  39.0 1.8 %collective-permute-start.17 = (bf16[400,512]{1,0:T(8,128)(2,1)S(1)}, bf16[400,512]{1,0:T(8,128)(2,1)S(1)}, u32[]{:S(2)}, u32[]{:S(2)}) collective-permute-start(bf16[400,512]{1,0:T(8,128)(2,1)S(1)} %get-tuple-element.65.own_con), channel_id=1, source_target_pairs={{0,8},{8,0},{16,24},{24,16},{1,9},{9,1},{17,25},{25,17},{2,10},{10... | collective-permute-start | bytes 1228808 | tf_op jit(solution)/shard_map/ppermute | solution.py:48
  39.4 2.1 %collective-permute-start.22 = (bf16[128,512]{1,0:T(8,128)(2,1)S(1)}, bf16[128,512]{1,0:T(8,128)(2,1)S(1)}, u32[]{:S(2)}, u32[]{:S(2)}) collective-permute-start(bf16[128,512]{1,0:T(8,128)(2,1)S(1)} %attend.1.att_ref.refs_0_), channel_id=1, source_target_pairs={{0,8},{8,0},{16,24},{24,16},{1,9},{9,1},{17,25},{25,17},{2,10},{10... | collective-permute-start | bytes 393224 | tf_op jit(solution)/shard_map/ppermute | solution.py:48
  39.6 1.9 %collective-permute-start.23 = (bf16[128,512]{1,0:T(8,128)(2,1)S(1)}, bf16[128,512]{1,0:T(8,128)(2,1)S(1)}, u32[]{:S(2)}, u32[]{:S(2)}) collective-permute-start(bf16[128,512]{1,0:T(8,128)(2,1)S(1)} %collective-permute-done.16.refs_2_), channel_id=1, source_target_pairs={{0,8},{8,0},{16,24},{24,16},{1,9},{9,1},{17,25},{25,17},{2,10},{10... | collective-permute-start | bytes 393224 | tf_op jit(solution)/shard_map/ppermute | solution.py:48
  42.0 6.5 %collective-permute-start.24 = (bf16[512,128]{1,0:T(8,128)(2,1)S(1)}, bf16[512,128]{1,0:T(8,128)(2,1)S(1)}, u32[]{:S(2)}, u32[]{:S(2)}) collective-permute-start(bf16[512,128]{1,0:T(8,128)(2,1)S(1)} %bitcast.153), channel_id=1, source_target_pairs={{0,2},{1,3},{2,0},{3,1},{4,6},{5,7},{6,4},{7,5},{8,10},{9,11},{10,... | collective-permute-start | bytes 393224 | tf_op jit(solution)/shard_map/ppermute | solution.py:48
  44.9 8.9 %collective-permute-start.18 = (bf16[544,128]{1,0:T(8,128)(2,1)S(1)}, bf16[544,128]{1,0:T(8,128)(2,1)S(1)}, u32[]{:S(2)}, u32[]{:S(2)}) collective-permute-start(bf16[544,128]{1,0:T(8,128)(2,1)S(1)} %constant_dynamic-update-slice_fusion.2), channel_id=1, source_target_pairs={{0,16},{1,17},{2,18},{3,19},{4,20},{5,21},{6,22},{7,23},{8,24},{9,... | collective-permute-start | bytes 417800 | tf_op jit(solution)/shard_map/ppermute | solution.py:453
  45.8 9.0 %collective-permute-start.19 = (bf16[544,128]{1,0:T(8,128)(2,1)S(1)}, bf16[544,128]{1,0:T(8,128)(2,1)S(1)}, u32[]{:S(2)}, u32[]{:S(2)}) collective-permute-start(bf16[544,128]{1,0:T(8,128)(2,1)S(1)} %constant_dynamic-update-slice_fusion.6), channel_id=1, source_target_pairs={{0,1},{1,0},{2,3},{3,2},{4,5},{5,4},{6,7},{7,6},{8,9},{9,8},{10,11... | collective-permute-start | bytes 417800 | tf_op jit(solution)/shard_map/ppermute | solution.py:453
  46.5 7.2 %collective-permute-start.20 = (bf16[544,128]{1,0:T(8,128)(2,1)S(1)}, bf16[544,128]{1,0:T(8,128)(2,1)S(1)}, u32[]{:S(2)}, u32[]{:S(2)}) collective-permute-start(bf16[544,128]{1,0:T(8,128)(2,1)S(1)} %constant_dynamic-update-slice_fusion.10), channel_id=1, source_target_pairs={{0,17},{1,16},{2,19},{3,18},{4,21},{5,20},{6,23},{7,22},{8,25},{9,... | collective-permute-start | bytes 417800 | tf_op jit(solution)/shard_map/ppermute | solution.py:453
  48.5 7.0 %collective-permute-start.25 = (bf16[256,128]{1,0:T(8,128)(2,1)S(1)}, bf16[256,128]{1,0:T(8,128)(2,1)S(1)}, u32[]{:S(2)}, u32[]{:S(2)}) collective-permute-start(bf16[256,128]{1,0:T(8,128)(2,1)S(1)} %bitcast.154), channel_id=1, source_target_pairs={{0,1},{1,0},{2,3},{3,2},{4,5},{5,4},{6,7},{7,6},{8,9},{9,8},{10,11... | collective-permute-start | bytes 196616 | tf_op jit(solution)/shard_map/ppermute | solution.py:48
  55.7 8.5 %collective-permute-start.26 = (bf16[288,128]{1,0:T(8,128)(2,1)S(1)}, bf16[288,128]{1,0:T(8,128)(2,1)S(1)}, u32[]{:S(2)}, u32[]{:S(2)}) collective-permute-start(bf16[288,128]{1,0:T(8,128)(2,1)S(1)} %constant_dynamic-update-slice_fusion.19), channel_id=1, source_target_pairs={{0,4},{1,5},{2,6},{3,7},{4,0},{5,1},{6,2},{7,3},{8,12},{9,13},{10,... | collective-permute-start | bytes 221192 | tf_op jit(solution)/shard_map/ppermute | solution.py:48
  58.4 5.8 %collective-permute-start.27 = (bf16[160,128]{1,0:T(8,128)(2,1)S(1)}, bf16[160,128]{1,0:T(8,128)(2,1)S(1)}, u32[]{:S(2)}, u32[]{:S(2)}) collective-permute-start(bf16[160,128]{1,0:T(8,128)(2,1)S(1)} %constant_dynamic-update-slice_fusion.25), channel_id=1, source_target_pairs={{0,6},{1,7},{2,4},{3,5},{4,2},{5,3},{6,0},{7,1},{8,14},{9,15},{10,... | collective-permute-start | bytes 122888 | tf_op jit(solution)/shard_map/ppermute | solution.py:48
  58.4 5.8 %collective-permute-start.21 = (bf16[160,128]{1,0:T(8,128)(2,1)S(1)}, bf16[160,128]{1,0:T(8,128)(2,1)S(1)}, u32[]{:S(2)}, u32[]{:S(2)}) collective-permute-start(bf16[160,128]{1,0:T(8,128)(2,1)S(1)} %constant_dynamic-update-slice_fusion.14), channel_id=1, source_target_pairs={{0,2},{1,3},{2,0},{3,1},{4,6},{5,7},{6,4},{7,5},{8,10},{9,11},{10,... | collective-permute-start | bytes 122888 | tf_op jit(solution)/shard_map/ppermute | solution.py:48
  64.3 6.2 %collective-permute-start.31 = (bf16[1,2,128,128]{3,2,1,0:T(8,128)(2,1)S(1)}, bf16[1,2,128,128]{3,2,1,0:T(8,128)(2,1)S(1)}, u32[]{:S(2)}, u32[]{:S(2)}) collective-permute-start(bf16[1,2,128,128]{3,2,1,0:T(8,128)(2,1)S(1)} %pad_maximum_fusion.5), channel_id=1, source_target_pairs={{0,4},{1,5},{2,6},{3,7},{4,0},{5,1},{6,2},{7,3},{8,12},{9,13},{10,... | collective-permute-start | bytes 196616 | tf_op jit(solution)/shard_map/ppermute | solution.py:48
  65.6 6.2 %collective-permute-start.32 = (bf16[1,2,128,128]{3,2,1,0:T(8,128)(2,1)S(1)}, bf16[1,2,128,128]{3,2,1,0:T(8,128)(2,1)S(1)}, u32[]{:S(2)}, u32[]{:S(2)}) collective-permute-start(bf16[1,2,128,128]{3,2,1,0:T(8,128)(2,1)S(1)} %pad_maximum_fusion.5), channel_id=1, source_target_pairs={{0,6},{1,7},{2,4},{3,5},{4,2},{5,3},{6,0},{7,1},{8,14},{9,15},{10,... | collective-permute-start | bytes 196616 | tf_op jit(solution)/shard_map/ppermute | solution.py:48
  66.5 10.4 %collective-permute-start.29 = (bf16[1,2,128,128]{3,2,1,0:T(8,128)(2,1)S(1)}, bf16[1,2,128,128]{3,2,1,0:T(8,128)(2,1)S(1)}, u32[]{:S(2)}, u32[]{:S(2)}) collective-permute-start(bf16[1,2,128,128]{3,2,1,0:T(8,128)(2,1)S(1)} %pad_maximum_fusion.5), channel_id=1, source_target_pairs={{0,2},{1,3},{2,0},{3,1},{4,6},{5,7},{6,4},{7,5},{8,10},{9,11},{10,... | collective-permute-start | bytes 196616 | tf_op jit(solution)/shard_map/ppermute | solution.py:48
  67.9 9.0 %collective-permute-start.28 = (bf16[2,128,128]{2,1,0:T(8,128)(2,1)S(1)}, bf16[2,128,128]{2,1,0:T(8,128)(2,1)S(1)}, u32[]{:S(2)}, u32[]{:S(2)}) collective-permute-start(bf16[2,128,128]{2,1,0:T(8,128)(2,1)S(1)} %pad_maximum_fusion.4.refs_0_), channel_id=1, source_target_pairs={{0,1},{1,0},{2,3},{3,2},{4,5},{5,4},{6,7},{7,6},{8,9},{9,8},{10,11... | collective-permute-start | bytes 196616 | tf_op jit(solution)/shard_map/ppermute | solution.py:48
  68.2 8.7 %collective-permute-start.30 = (bf16[2,128,128]{2,1,0:T(8,128)(2,1)S(1)}, bf16[2,128,128]{2,1,0:T(8,128)(2,1)S(1)}, u32[]{:S(2)}, u32[]{:S(2)}) collective-permute-start(bf16[2,128,128]{2,1,0:T(8,128)(2,1)S(1)} %pad_maximum_fusion.4.refs_0_), channel_id=1, source_target_pairs={{0,3},{1,2},{2,1},{3,0},{4,7},{5,6},{6,5},{7,4},{8,11},{9,10},{10,... | collective-permute-start | bytes 196616 | tf_op jit(solution)/shard_map/ppermute | solution.py:48
  71.8 5.0 %collective-permute-start.33 = (bf16[2,2,128,128]{3,2,1,0:T(8,128)(2,1)S(1)}, bf16[2,2,128,128]{3,2,1,0:T(8,128)(2,1)S(1)}, u32[]{:S(2)}, u32[]{:S(2)}) collective-permute-start(bf16[2,2,128,128]{3,2,1,0:T(8,128)(2,1)S(1)} %pad_maximum_fusion.3), channel_id=1, source_target_pairs={{0,1},{1,0},{2,3},{3,2},{4,5},{5,4},{6,7},{7,6},{8,9},{9,8},{10,11... | collective-permute-start | bytes 393224 | tf_op jit(solution)/shard_map/ppermute | solution.py:48

commit v6 on v5

--- a/solution.py
+++ b/solution.py
@@ -223,9 +223,7 @@
 
 def in_parts(total):
     first = lax.reduce_precision(total, 8, 7)
-    second = lax.reduce_precision(total - first, 8, 7)
-    third = total - first - second
-    return [part.astype(BF16) for part in (first, second, third, jnp.zeros_like(total))]
+    return [first.astype(BF16), (total - first).astype(BF16)]
 
 
 def with_loss(block, total):
@@ -233,8 +231,8 @@
 
 
 def split_loss(message):
-    parts = message[-32:].astype(F32).reshape(4, 8, LANES)
-    return message[:-32], parts[0] + parts[1] + parts[2]
+    parts = message[-16:].astype(F32).reshape(2, 8, LANES)
+    return message[:-16], parts[0] + parts[1]
 
 
 def gathered(value, axis, bits):
@@ -331,10 +329,9 @@
         k_layout += [(5 + m, i * half, half, j ^ 1, 2 + m) for m in (0, 1)]
 
     def layout(first):
-        table = [(0, first, dsh, 0, 0), (1, first, dsh, 1, 0)]
+        table = [(0, first, dsh, 0, 0), (1, 0, dsh, 1, 0)]
         for i, j in enumerate(shards):
-            row = 2 * i * dsh + first
-            table += [(2, row, dsh, j, 0), (3, row, dsh, j ^ 1, 0)]
+            table += [(2, i * dsh, dsh, j, 0), (3, i * dsh, dsh, j ^ 1, 0)]
         return table
 
     full = pltpu.VMEM((d_model, inner), BF16)
@@ -348,15 +345,15 @@
         scratch=[full],
     )
     weights, vo_far, turned_send, w_vo = lax.optimization_barrier((weights, vo_far, turned_send, w_vo))
-    vo_near = xor_permute(w_vo, "ens", 1)
-    vo_far = joined([vo_far[j] for j in shards])
-    vo_cross = xor_permute(vo_far, "ens", 1)
+    vo_near = [xor_permute(w_vo[:dsh], "ens", 1), xor_permute(w_vo[dsh:], "ens", 1)]
+    vo_far = [joined([vo_far[j][m * dsh : (m + 1) * dsh] for j in shards]) for m in (0, 1)]
+    vo_cross = [xor_permute(part, "ens", 1) for part in vo_far]
     turned_sib = xor_permute(turned_send, "ens", 1)
     (attended,) = call(
         functools.partial(attend_body, layout(0), dsh),
         [((TILE, inner), BF16)],
         [("v", normed), ("v", weights), ("s", neighbours), ("s", neighbour_mask)]
-        + [("v", a) for a in (w_vo, vo_near, vo_far, vo_cross)],
+        + [("v", a) for a in (w_vo, vo_near[0], vo_far[0], vo_cross[0])],
         10**9,
         "attend",
         scratch=[full],
@@ -365,7 +362,7 @@
         functools.partial(forecast_body, layout(dsh), dsh),
         [((TILE, LANES), BF16), ((d_model, inner), BF16)],
         [("v", sample_layer_feed), ("v", attended), ("v", readout_matrix)]
-        + [("v", a) for a in (w_vo, vo_near, vo_far, vo_cross)],
+        + [("v", a) for a in (w_vo, vo_near[1], vo_far[1], vo_cross[1])],
         10**9,
         "forecast",
     )
@@ -435,9 +432,9 @@
         return functools.reduce(jnp.add, [m.astype(F32) for m in received], kept)
 
     later = [bit for group in groups[1:] for bit in group]
-    for bit in later[:-1]:
+    for bit in later[:-2]:
         output_term = added(*sent(output_term, [bit]))
-    output_kept, output_got = sent(output_term, groups[0], higher=2)
+    output_kept, output_got = sent(output_term, [later[-2]])
     upper, low = (e // far[-1]) % 2, p % 2
     quarters = [pieces_of(h, groups[0]) for h in value_term.reshape(2, -1, LANES)]
     quarters = jnp.stack([part_of(q, i) for q in quarters for i in range(2)])
@@ -459,24 +456,21 @@
     losses = jnp.stack([losses[d] for d in range(4)])
     loss = functools.reduce(jnp.add, [at(losses, pos ^ i) for i in range(4)])
 
+    value_term, output_got = lax.optimization_barrier((value_term, output_got))
+    output_kept, output_got = sent(added(output_kept, output_got), groups[0], higher=2)
     for group in groups[1:]:
         size, pos = 1 << len(group), (p // group[0]) % (1 << len(group))
         split = pieces_of(value_term, group)
-        kept, messages = part_of(split, pos), {d: part_of(split, pos ^ d).astype(BF16) for d in range(1, size)}
-        top = size // 2
+        messages = {d: with_loss(part_of(split, pos ^ d), loss) for d in range(1, size)}
+        received = {d: xor_permute(m, "pix", d * group[0]) for d, m in messages.items()}
         if group == groups[-1]:
-            split = pieces_of(added(output_kept, output_got), [later[-1]], 1)
-            own = (p // later[-1]) % 2
-            output_kept = part_of(split, own)
-            messages[top] = jnp.concatenate([messages[top], part_of(split, 1 - own).astype(BF16)])
-        received = {d: split_loss(xor_permute(with_loss(m, loss), "pix", d * group[0])) for d, m in messages.items()}
-        if group == groups[-1]:
-            both, other = received[top]
-            output_term = output_kept + both[-output_kept.shape[0] :].astype(F32)
-            received[top] = (both[: kept.shape[0]], other)
+            output_kept, output_got = sent(added(output_kept, output_got), [later[-1]], higher=1)
+            received, output_got = lax.optimization_barrier((received, output_got))
+        received = {d: split_loss(m) for d, m in received.items()}
         totals = jnp.stack([loss] + [received[d][1] for d in range(1, size)])
         loss = functools.reduce(jnp.add, [at(totals, pos ^ i) for i in range(size)])
-        value_term = added(kept, [received[d][0] for d in range(1, size)])
+        value_term = added(part_of(split, pos), [received[d][0] for d in range(1, size)])
+    output_term = added(output_kept, output_got)
     terms = [value_term, output_term]
     piece = jnp.stack(terms).astype(BF16)
     pieces, near = {0: piece}, groups[1][0]

time: 78.3 us -> 76.6 us (0.978)
  waiting for transfers between devices: 32.2 us -> 24.9 us
  starting transfers between devices: 32.2 us -> 37.8 us
    ppermute x29 -> x32, starting transfers between devices: 23.9 us -> 29.6 us  [xor_permute(): return lax.ppermute(value, axis, [(i, i ^ mask) for i in range(size)])]
    ppermute x29 -> x32, waiting for transfers between devices: 22.6 us -> 17.5 us  [xor_permute(): return lax.ppermute(value, axis, [(i, i ^ mask) for i in range(size)])]
    ppermute x3, waiting for transfers between devices: 5.48 us -> 3.16 us  [per_device(): lax.ppermute(message, ('ens', 'pix'), pairs)]
    unnamed x29 -> x26, local copies, waits for them, and re-layouts: 1.79 us -> 1.68 us
  transfers between devices with their start and end apart: 34 -> 37, of which waited for: 20 -> 19; matrix products, arithmetic and copies ran while one was open for 1% -> 1% of each run, Pallas kernels for 9% -> 10%
where the time goes in v6:
time: 76.6 us; the launch traced here: 76.4 us
  starting transfers between devices  37.8 us (49%)
  waiting for transfers between devices  24.9 us (33%)
  Pallas kernels  8.85 us (12%)
  local copies, waits for them, and re-layouts  2.14 us (3%)
  other arithmetic  1.46 us (2%)
  between operations  1.19 us (2%)
    ppermute x32, starting transfers between devices, xor_permute(): return lax.ppermute(value, axis, [(i, i ^ mask) for i in range(size)])  29.6 us
    ppermute x32, waiting for transfers between devices, xor_permute(): return lax.ppermute(value, axis, [(i, i ^ mask) for i in range(size)])  17.5 us
    pallas_call x8, Pallas kernels, call(): pl.pallas_call(body, out_shape=[jax.ShapeDtypeStruct(s, d) for s, d in ou...  8.85 us
    ppermute x1, waiting for transfers between devices, per_device(): lax.ppermute(sample_layer_feed, 'pix', [(i, i + 1) for i in range(n_pix -...  4.18 us
    ppermute x3, starting transfers between devices, per_device(): lax.ppermute(message, ('ens', 'pix'), pairs)  3.57 us
    ppermute x1, starting transfers between devices, per_device(): lax.ppermute(sample_layer_feed, 'pix', [(i, i + 1) for i in range(n_pix -...  3.43 us
    ppermute x3, waiting for transfers between devices, per_device(): lax.ppermute(message, ('ens', 'pix'), pairs)  3.16 us
    unnamed x26, local copies, waits for them, and re-layouts  1.68 us
  transfers between devices with their start and end apart: 37, of which 19 were waited for; matrix products, arithmetic and copies ran while one was open for 1% of the time, Pallas kernels for 10%

profile of v6, /device:TPU:0, one launch (start us, length us, event | category | flops | bytes accessed | tf_op | source)
XLA Modules:
  0.0 76.4 jit_solution(18282418799842372141)
XLA Ops:
  0.7 1.0 %slice_select_fusion = bf16[128,512]{1,0:T(8,128)(2,1)S(1)} fusion(bf16[256,512]{1,0:T(8,128)(2,1)} %param.15, pred[]{:T(512)S(6)} %eq.11), kind=kLoop, calls=%fused_computation.23 | loop fusion | flops 65536 | bytes 393217 | tf_op jit(solution)/shard_map/jit(_where)/select_n | solution.py:296
  1.8 3.0 %collective-permute-start.3 = (bf16[384,512]{1,0:T(8,128)(2,1)S(1)}, bf16[384,512]{1,0:T(8,128)(2,1)S(1)}, u32[]{:S(2)}, u32[]{:S(2)}) collective-permute-start(bf16[384,512]{1,0:T(8,128)(2,1)S(1)} %pad_maximum_fusion.2), channel_id=1, source_target_pairs={{0,16},{8,24},{16,0},{24,8},{1,17},{9,25},{17,1},{25,9},{2,18},{10... | collective-permute-start | bytes 1179656 | tf_op jit(solution)/shard_map/ppermute | solution.py:48
  4.9 0.8 %copy-done = bf16[1,128,1024]{2,1,0:T(8,128)(2,1)S(1)} copy-done((bf16[1,128,1024]{2,1,0:T(8,128)(2,1)S(1)}, bf16[1,128,1024]{2,1,0:T(8,128)(2,1)}, u32[]{:S(2)}) %copy-start) | copy-done | bytes 262168
  5.7 3.4 %collective-permute-start = (bf16[1,128,1024]{2,1,0:T(8,128)(2,1)S(1)}, bf16[1,128,1024]{2,1,0:T(8,128)(2,1)S(1)}, u32[]{:S(2)}, u32[]{:S(2)}) collective-permute-start(bf16[1,128,1024]{2,1,0:T(8,128)(2,1)S(1)} %copy-done), channel_id=1, source_target_pairs={{0,1},{1,2},{2,3},{3,4},{4,5},{5,6},{6,7},{8,9},{9,10},{10,11},{11... | collective-permute-start | bytes 786440 | tf_op jit(solution)/shard_map/ppermute | solution.py:300
  9.2 1.3 %collective-permute-start.1 = (bf16[1,128,1024]{2,1,0:T(8,128)(2,1)S(1)}, bf16[1,128,1024]{2,1,0:T(8,128)(2,1)S(1)}, u32[]{:S(2)}, u32[]{:S(2)}) collective-permute-start(bf16[1,128,1024]{2,1,0:T(8,128)(2,1)S(1)} %copy-done), channel_id=1, source_target_pairs={{1,0},{2,1},{3,2},{4,3},{5,4},{6,5},{7,6},{9,8},{10,9},{11,10},{12... | collective-permute-start | bytes 786440 | tf_op jit(solution)/shard_map/ppermute | solution.py:301
  10.5 0.1 copy.20
  10.7 0.9 %collective-permute-start.9 = (bf16[512,512]{1,0:T(8,128)(2,1)S(1)}, bf16[512,512]{1,0:T(8,128)(2,1)S(1)}, u32[]{:S(2)}, u32[]{:S(2)}) collective-permute-start(bf16[512,512]{1,0:T(8,128)(2,1)S(1)} %pad_maximum_fusion.1.refs_0_), channel_id=1, source_target_pairs={{0,16},{8,24},{16,0},{24,8},{1,17},{9,25},{17,1},{25,9},{2,18},{10... | collective-permute-start | bytes 1572872 | tf_op jit(solution)/shard_map/ppermute | solution.py:48
  11.6 3.1 %collective-permute-done.3 = bf16[384,512]{1,0:T(8,128)(2,1)S(1)} collective-permute-done((bf16[384,512]{1,0:T(8,128)(2,1)S(1)}, bf16[384,512]{1,0:T(8,128)(2,1)S(1)}, u32[]{:S(2)}, u32[]{:S(2)}) %collective-permute-start.3) | collective-permute-done | bytes 393248 | tf_op jit(solution)/shard_map/ppermute | solution.py:48
  14.7 1.1 %collective-permute-start.4 = (bf16[128,512]{1,0:T(8,128)(2,1)S(1)}, bf16[128,512]{1,0:T(8,128)(2,1)S(1)}, u32[]{:S(2)}, u32[]{:S(2)}) collective-permute-start(bf16[128,512]{1,0:T(8,128)(2,1)S(1)} %slice.154.refs_3_), channel_id=1, source_target_pairs={{0,2},{1,3},{2,0},{3,1},{4,6},{5,7},{6,4},{7,5},{8,10},{9,11},{10,... | collective-permute-start | bytes 393224 | tf_op jit(solution)/shard_map/ppermute | solution.py:48
  15.8 4.2 %collective-permute-done.up_ref = bf16[1,128,1024]{2,1,0:T(8,128)(2,1)S(1)} collective-permute-done((bf16[1,128,1024]{2,1,0:T(8,128)(2,1)S(1)}, bf16[1,128,1024]{2,1,0:T(8,128)(2,1)S(1)}, u32[]{:S(2)}, u32[]{:S(2)}) %collective-permute-start) | collective-permute-done | bytes 262176 | tf_op jit(solution)/shard_map/ppermute | solution.py:300
  20.0 0.6 copy-done.5
  20.6 0.6 normed.1
  21.2 1.3 %collective-permute-done.4.refs_4_ = bf16[128,512]{1,0:T(8,128)(2,1)S(1)} collective-permute-done((bf16[128,512]{1,0:T(8,128)(2,1)S(1)}, bf16[128,512]{1,0:T(8,128)(2,1)S(1)}, u32[]{:S(2)}, u32[]{:S(2)}) %collective-permute-start.4) | collective-permute-done | bytes 131104 | tf_op jit(solution)/shard_map/ppermute | solution.py:48
  22.6 0.5 collective-permute-start.8
  23.1 0.1 collective-permute-start.5
  23.2 0.4 collective-permute-start.6
  23.6 0.3 collective-permute-done.7.refs_7_
  23.9 0.2 collective-permute-done.8.refs_8_
  24.1 0.3 collective-permute-done.5.refs_5_
  24.5 0.2 collective-permute-done.6.refs_6_
  24.6 2.2 %weights.1.w_ref.refs_8_ = bf16[8,128,384]{2,1,0:T(8,128)(2,1)S(1)} custom-call(bf16[384,1024]{1,0:T(8,128)(2,1)S(1)} %get-tuple-element.49.n_ref, s32[8,128]{1,0:T(8,128)S(1)} %bitcast.96, s32[1,9]{1,0:T(1,128)S(1)} %copy-done.3, s32[1,9]{1,0:T(1,128)S(1)} %copy-done.4, bf16[512,512]{1,0:T(8,128)(2,1)S(1)} %constant_dynamic-update-slice_fusion.refs_0_, ...), custom_call_target="tpu_custom_call" | custom-call | flops 1000 | bytes 1 | tf_op jit(solution)/shard_map/weights/pallas_call | solution.py:34
  26.9 0.4 collective-permute-start.10
  27.4 0.2 collective-permute-start.11
  27.6 0.3 collective-permute-start.12
  27.9 0.2 collective-permute-start.13
  28.1 0.3 collective-permute-start.17
  28.4 0.1 collective-permute-done.10.refs_1_
  28.5 0.4 collective-permute-done.11.refs_3_
  29.0 1.5 %attend.1.att_ref.refs_0_ = bf16[128,512]{1,0:T(8,128)(2,1)S(1)} custom-call(bf16[384,1024]{1,0:T(8,128)(2,1)S(1)} %get-tuple-element.49.n_ref, bf16[8,128,384]{2,1,0:T(8,128)(2,1)S(1)} %weights.1.w_ref.refs_8_, s32[1,9]{1,0:T(1,128)S(1)} %copy-done.3, s32[1,9]{1,0:T(1,128)S(1)} %copy-done.4, bf16[512,512]{1,0:T(8,128)(2,1)S(1)} %pad_maximum_fusion.1.refs_0_, ...), custom_call_target="tpu_custom_call" | custom-call | flops 1000000000 | bytes 1000000 | tf_op jit(solution)/shard_map/attend/pallas_call | solution.py:34
  30.5 0.7 forecast.1
  31.2 1.1 %collective-permute-start.14 = (bf16[128,128]{1,0:T(8,128)(2,1)S(1)}, bf16[128,128]{1,0:T(8,128)(2,1)S(1)}, u32[]{:S(2)}, u32[]{:S(2)}) collective-permute-start(bf16[128,128]{1,0:T(8,128)(2,1)S(1)} %get-tuple-element.63.refs_0_), channel_id=1, source_target_pairs={{0,16},{8,24},{16,0},{24,8},{1,17},{9,25},{17,1},{25,9},{2,18},{10... | collective-permute-start | bytes 98312 | tf_op jit(solution)/shard_map/ppermute | solution.py:48
  32.3 1.0 %collective-permute-start.18 = (bf16[128,512]{1,0:T(8,128)(2,1)S(1)}, bf16[128,512]{1,0:T(8,128)(2,1)S(1)}, u32[]{:S(2)}, u32[]{:S(2)}) collective-permute-start(bf16[128,512]{1,0:T(8,128)(2,1)S(1)} %attend.1.att_ref.refs_0_), channel_id=1, source_target_pairs={{0,16},{8,24},{16,0},{24,8},{1,17},{9,25},{17,1},{25,9},{2,18},{10... | collective-permute-start | bytes 393224 | tf_op jit(solution)/shard_map/ppermute | solution.py:48
  33.3 2.2 %collective-permute-done.14.refs_2_ = bf16[128,128]{1,0:T(8,128)(2,1)S(1)} collective-permute-done((bf16[128,128]{1,0:T(8,128)(2,1)S(1)}, bf16[128,128]{1,0:T(8,128)(2,1)S(1)}, u32[]{:S(2)}, u32[]{:S(2)}) %collective-permute-start.14) | collective-permute-done | bytes 32800 | tf_op jit(solution)/shard_map/ppermute | solution.py:48
  35.5 0.5 collective-permute-start.16
  36.0 0.7 collective-permute-done.15.refs_1_
  36.7 0.2 collective-permute-done.16.refs_3_
  36.9 1.5 %backward.1 = (bf16[512,128]{1,0:T(8,128)(2,1)S(1)}, bf16[400,512]{1,0:T(8,128)(2,1)S(1)}) custom-call(bf16[128,128]{1,0:T(8,128)(2,1)S(1)} %get-tuple-element.63.refs_0_, bf16[128,128]{1,0:T(8,128)(2,1)S(1)} %collective-permute-done.15.refs_1_, bf16[128,128]{1,0:T(8,128)(2,1)S(1)} %collective-permute-done.14.refs_2_, ...), custom_call_target="tpu_custom_call" | custom-call | flops 1000000000 | bytes 1000000 | tf_op jit(solution)/shard_map/backward/pallas_call | solution.py:34
  38.4 0.4 collective-permute-start.19
  38.8 0.2 collective-permute-start.23
  39.1 0.3 collective-permute-start.24
  39.4 0.9 %collective-permute-done.19.sib_con = bf16[400,512]{1,0:T(8,128)(2,1)S(1)} collective-permute-done((bf16[400,512]{1,0:T(8,128)(2,1)S(1)}, bf16[400,512]{1,0:T(8,128)(2,1)S(1)}, u32[]{:S(2)}, u32[]{:S(2)}) %collective-permute-start.19) | collective-permute-done | bytes 409632 | tf_op jit(solution)/shard_map/ppermute | solution.py:48
  40.2 0.7 value_term.1
  41.3 1.0 %collective-permute-start.20 = (bf16[528,128]{1,0:T(8,128)(2,1)S(1)}, bf16[528,128]{1,0:T(8,128)(2,1)S(1)}, u32[]{:S(2)}, u32[]{:S(2)}) collective-permute-start(bf16[528,128]{1,0:T(8,128)(2,1)S(1)} %get-tuple-element.118), channel_id=1, source_target_pairs={{0,16},{1,17},{2,18},{3,19},{4,20},{5,21},{6,22},{7,23},{8,24},{9,... | collective-permute-start | bytes 405512 | tf_op jit(solution)/shard_map/ppermute | solution.py:450
  42.3 1.4 %collective-permute-start.21 = (bf16[528,128]{1,0:T(8,128)(2,1)S(1)}, bf16[528,128]{1,0:T(8,128)(2,1)S(1)}, u32[]{:S(2)}, u32[]{:S(2)}) collective-permute-start(bf16[528,128]{1,0:T(8,128)(2,1)S(1)} %get-tuple-element.116), channel_id=1, source_target_pairs={{0,1},{1,0},{2,3},{3,2},{4,5},{5,4},{6,7},{7,6},{8,9},{9,8},{10,11... | collective-permute-start | bytes 405512 | tf_op jit(solution)/shard_map/ppermute | solution.py:450
  43.8 1.1 %collective-permute-start.22 = (bf16[528,128]{1,0:T(8,128)(2,1)S(1)}, bf16[528,128]{1,0:T(8,128)(2,1)S(1)}, u32[]{:S(2)}, u32[]{:S(2)}) collective-permute-start(bf16[528,128]{1,0:T(8,128)(2,1)S(1)} %get-tuple-element.117), channel_id=1, source_target_pairs={{0,17},{1,16},{2,19},{3,18},{4,21},{5,20},{6,23},{7,22},{8,25},{9,... | collective-permute-start | bytes 405512 | tf_op jit(solution)/shard_map/ppermute | solution.py:450
  44.9 0.4 output_term.1
  45.3 2.5 %collective-permute-start.25 = (bf16[512,128]{1,0:T(8,128)(2,1)S(1)}, bf16[512,128]{1,0:T(8,128)(2,1)S(1)}, u32[]{:S(2)}, u32[]{:S(2)}) collective-permute-start(bf16[512,128]{1,0:T(8,128)(2,1)S(1)} %bitcast.117), channel_id=1, source_target_pairs={{0,2},{1,3},{2,0},{3,1},{4,6},{5,7},{6,4},{7,5},{8,10},{9,11},{10,... | collective-permute-start | bytes 393224 | tf_op jit(solution)/shard_map/ppermute | solution.py:48
  47.8 1.9 %collective-permute-done.21 = bf16[528,128]{1,0:T(8,128)(2,1)S(1)} collective-permute-done((bf16[528,128]{1,0:T(8,128)(2,1)S(1)}, bf16[528,128]{1,0:T(8,128)(2,1)S(1)}, u32[]{:S(2)}, u32[]{:S(2)}) %collective-permute-start.21) | collective-permute-done | bytes 135200 | tf_op jit(solution)/shard_map/ppermute | solution.py:450
  49.8 1.2 %collective-permute-done.22 = bf16[528,128]{1,0:T(8,128)(2,1)S(1)} collective-permute-done((bf16[528,128]{1,0:T(8,128)(2,1)S(1)}, bf16[528,128]{1,0:T(8,128)(2,1)S(1)}, u32[]{:S(2)}, u32[]{:S(2)}) %collective-permute-start.22) | collective-permute-done | bytes 135200 | tf_op jit(solution)/shard_map/ppermute | solution.py:450
  51.1 1.3 %collective-permute-start.29 = (bf16[256,128]{1,0:T(8,128)(2,1)S(1)}, bf16[256,128]{1,0:T(8,128)(2,1)S(1)}, u32[]{:S(2)}, u32[]{:S(2)}) collective-permute-start(bf16[256,128]{1,0:T(8,128)(2,1)S(1)} %bitcast.118), channel_id=1, source_target_pairs={{0,1},{1,0},{2,3},{3,2},{4,5},{5,4},{6,7},{7,6},{8,9},{9,8},{10,11... | collective-permute-start | bytes 196616 | tf_op jit(solution)/shard_map/ppermute | solution.py:48
  52.6 1.8 %collective-permute-start.26 = (bf16[144,128]{1,0:T(8,128)(2,1)S(1)}, bf16[144,128]{1,0:T(8,128)(2,1)S(1)}, u32[]{:S(2)}, u32[]{:S(2)}) collective-permute-start(bf16[144,128]{1,0:T(8,128)(2,1)S(1)} %get-tuple-element.115), channel_id=1, source_target_pairs={{0,2},{1,3},{2,0},{3,1},{4,6},{5,7},{6,4},{7,5},{8,10},{9,11},{10,... | collective-permute-start | bytes 110600 | tf_op jit(solution)/shard_map/ppermute | solution.py:48
  54.4 2.6 %collective-permute-start.27 = (bf16[144,128]{1,0:T(8,128)(2,1)S(1)}, bf16[144,128]{1,0:T(8,128)(2,1)S(1)}, u32[]{:S(2)}, u32[]{:S(2)}) collective-permute-start(bf16[144,128]{1,0:T(8,128)(2,1)S(1)} %get-tuple-element.114), channel_id=1, source_target_pairs={{0,4},{1,5},{2,6},{3,7},{4,0},{5,1},{6,2},{7,3},{8,12},{9,13},{10,... | collective-permute-start | bytes 110600 | tf_op jit(solution)/shard_map/ppermute | solution.py:48
  57.1 1.9 %collective-permute-start.30 = (bf16[128,128]{1,0:T(8,128)(2,1)S(1)}, bf16[128,128]{1,0:T(8,128)(2,1)S(1)}, u32[]{:S(2)}, u32[]{:S(2)}) collective-permute-start(bf16[128,128]{1,0:T(8,128)(2,1)S(1)} %fusion.12), channel_id=1, source_target_pairs={{0,4},{1,5},{2,6},{3,7},{4,0},{5,1},{6,2},{7,3},{8,12},{9,13},{10,... | collective-permute-start | bytes 98312 | tf_op jit(solution)/shard_map/ppermute | solution.py:48
  59.0 0.8 %collective-permute-done.27 = bf16[144,128]{1,0:T(8,128)(2,1)S(1)} collective-permute-done((bf16[144,128]{1,0:T(8,128)(2,1)S(1)}, bf16[144,128]{1,0:T(8,128)(2,1)S(1)}, u32[]{:S(2)}, u32[]{:S(2)}) %collective-permute-start.27) | collective-permute-done | bytes 36896 | tf_op jit(solution)/shard_map/ppermute | solution.py:48
  59.8 2.9 %collective-permute-done.28 = bf16[144,128]{1,0:T(8,128)(2,1)S(1)} collective-permute-done((bf16[144,128]{1,0:T(8,128)(2,1)S(1)}, bf16[144,128]{1,0:T(8,128)(2,1)S(1)}, u32[]{:S(2)}, u32[]{:S(2)}) %collective-permute-start.28) | collective-permute-done | bytes 36896 | tf_op jit(solution)/shard_map/ppermute | solution.py:48
  62.8 1.1 %collective-permute-start.34 = (bf16[1,2,128,128]{3,2,1,0:T(8,128)(2,1)S(1)}, bf16[1,2,128,128]{3,2,1,0:T(8,128)(2,1)S(1)}, u32[]{:S(2)}, u32[]{:S(2)}) collective-permute-start(bf16[1,2,128,128]{3,2,1,0:T(8,128)(2,1)S(1)} %pad_maximum_fusion.11), channel_id=1, source_target_pairs={{0,4},{1,5},{2,6},{3,7},{4,0},{5,1},{6,2},{7,3},{8,12},{9,13},{10,... | collective-permute-start | bytes 196616 | tf_op jit(solution)/shard_map/ppermute | solution.py:48
  64.0 2.2 %collective-permute-start.35 = (bf16[1,2,128,128]{3,2,1,0:T(8,128)(2,1)S(1)}, bf16[1,2,128,128]{3,2,1,0:T(8,128)(2,1)S(1)}, u32[]{:S(2)}, u32[]{:S(2)}) collective-permute-start(bf16[1,2,128,128]{3,2,1,0:T(8,128)(2,1)S(1)} %pad_maximum_fusion.11), channel_id=1, source_target_pairs={{0,6},{1,7},{2,4},{3,5},{4,2},{5,3},{6,0},{7,1},{8,14},{9,15},{10,... | collective-permute-start | bytes 196616 | tf_op jit(solution)/shard_map/ppermute | solution.py:48
  66.1 0.3 collective-permute-start.32
  66.5 2.0 %collective-permute-start.31 = (bf16[2,128,128]{2,1,0:T(8,128)(2,1)S(1)}, bf16[2,128,128]{2,1,0:T(8,128)(2,1)S(1)}, u32[]{:S(2)}, u32[]{:S(2)}) collective-permute-start(bf16[2,128,128]{2,1,0:T(8,128)(2,1)S(1)} %pad_maximum_fusion.10.refs_0_), channel_id=1, source_target_pairs={{0,1},{1,0},{2,3},{3,2},{4,5},{5,4},{6,7},{7,6},{8,9},{9,8},{10,11... | collective-permute-start | bytes 196616 | tf_op jit(solution)/shard_map/ppermute | solution.py:48
  68.4 1.3 %collective-permute-start.33 = (bf16[2,128,128]{2,1,0:T(8,128)(2,1)S(1)}, bf16[2,128,128]{2,1,0:T(8,128)(2,1)S(1)}, u32[]{:S(2)}, u32[]{:S(2)}) collective-permute-start(bf16[2,128,128]{2,1,0:T(8,128)(2,1)S(1)} %pad_maximum_fusion.10.refs_0_), channel_id=1, source_target_pairs={{0,3},{1,2},{2,1},{3,0},{4,7},{5,6},{6,5},{7,4},{8,11},{9,10},{10,... | collective-permute-start | bytes 196616 | tf_op jit(solution)/shard_map/ppermute | solution.py:48
  69.7 0.4 collective-permute-done.35
  70.1 1.4 %collective-permute-start.36 = (bf16[2,2,128,128]{3,2,1,0:T(8,128)(2,1)S(1)}, bf16[2,2,128,128]{3,2,1,0:T(8,128)(2,1)S(1)}, u32[]{:S(2)}, u32[]{:S(2)}) collective-permute-start(bf16[2,2,128,128]{3,2,1,0:T(8,128)(2,1)S(1)} %pad_maximum_fusion.9), channel_id=1, source_target_pairs={{0,1},{1,0},{2,3},{3,2},{4,5},{5,4},{6,7},{7,6},{8,9},{9,8},{10,11... | collective-permute-start | bytes 393224 | tf_op jit(solution)/shard_map/ppermute | solution.py:48
  71.6 3.6 %collective-permute-done.36 = bf16[2,2,128,128]{3,2,1,0:T(8,128)(2,1)S(1)} collective-permute-done((bf16[2,2,128,128]{3,2,1,0:T(8,128)(2,1)S(1)}, bf16[2,2,128,128]{3,2,1,0:T(8,128)(2,1)S(1)}, u32[]{:S(2)}, u32[]{:S(2)}) %collective-permute-start.36) | collective-permute-done | bytes 131104 | tf_op jit(solution)/shard_map/ppermute | solution.py:48
  75.2 1.2 %finish.1 = (f32[256,512]{1,0:T(8,128)}, f32[512,256]{1,0:T(8,128)}, f32[1,1]{1,0:T(1,128)}) custom-call(bf16[2,128,128]{2,1,0:T(8,128)(2,1)S(1)} %pad_maximum_fusion.10.refs_0_, bf16[2,128,128]{2,1,0:T(8,128)(2,1)S(1)} %collective-permute-done.31.refs_1_, bf16[2,128,128]{2,1,0:T(8,128)(2,1)S(1)} %bitcast.94, ...), custom_call_target="tpu_custom_call" | custom-call | flops 1000000 | bytes 1000 | tf_op jit(solution)/shard_map/finish/pallas_call | solution.py:34
  (91 shorter events, 1.2 us)
Async XLA Ops:
  0.6 1.1 %copy-start.8 = (bf16[256,512]{1,0:T(8,128)(2,1)S(1)}, bf16[256,512]{1,0:T(8,128)(2,1)}, u32[]{:S(2)}) copy-start(bf16[256,512]{1,0:T(8,128)(2,1)} %param.14) | copy-start | bytes 786436
  1.7 3.0 %copy-start.9 = (bf16[256,512]{1,0:T(8,128)(2,1)S(1)}, bf16[256,512]{1,0:T(8,128)(2,1)}, u32[]{:S(2)}) copy-start(bf16[256,512]{1,0:T(8,128)(2,1)} %param.15) | copy-start | bytes 786436
  1.8 12.9 %collective-permute-start.3 = (bf16[384,512]{1,0:T(8,128)(2,1)S(1)}, bf16[384,512]{1,0:T(8,128)(2,1)S(1)}, u32[]{:S(2)}, u32[]{:S(2)}) collective-permute-start(bf16[384,512]{1,0:T(8,128)(2,1)S(1)} %pad_maximum_fusion.2), channel_id=1, source_target_pairs={{0,16},{8,24},{16,0},{24,8},{1,17},{9,25},{17,1},{25,9},{2,18},{10... | collective-permute-start | bytes 1179656 | tf_op jit(solution)/shard_map/ppermute | solution.py:48
  4.8 1.0 %copy-start = (bf16[1,128,1024]{2,1,0:T(8,128)(2,1)S(1)}, bf16[1,128,1024]{2,1,0:T(8,128)(2,1)}, u32[]{:S(2)}) copy-start(bf16[1,128,1024]{2,1,0:T(8,128)(2,1)} %x_ref.3) | copy-start | bytes 786436
  4.8 5.7 %copy-start.10 = (bf16[512,256]{1,0:T(8,128)(2,1)S(1)}, bf16[512,256]{1,0:T(8,128)(2,1)}, u32[]{:S(2)}) copy-start(bf16[512,256]{1,0:T(8,128)(2,1)} %param.17) | copy-start | bytes 786436
  4.8 5.8 %copy-start.11 = (bf16[256,512]{1,0:T(8,128)(2,1)S(1)}, bf16[256,512]{1,0:T(8,128)(2,1)}, u32[]{:S(2)}) copy-start(bf16[256,512]{1,0:T(8,128)(2,1)} %param.16) | copy-start | bytes 786436
  4.9 17.6 %collective-permute-start.2 = (bf16[512,512]{1,0:T(8,128)(2,1)S(1)}, bf16[512,512]{1,0:T(8,128)(2,1)S(1)}, u32[]{:S(2)}, u32[]{:S(2)}) collective-permute-start(bf16[512,512]{1,0:T(8,128)(2,1)S(1)} %constant_dynamic-update-slice_fusion.refs_0_), channel_id=1, source_target_pairs={{0,8},{8,0},{16,24},{24,16},{1,9},{9,1},{17,25},{25,17},{2,10},{10... | collective-permute-start | bytes 1572872 | tf_op jit(solution)/shard_map/ppermute | solution.py:48
  5.7 14.2 %collective-permute-start = (bf16[1,128,1024]{2,1,0:T(8,128)(2,1)S(1)}, bf16[1,128,1024]{2,1,0:T(8,128)(2,1)S(1)}, u32[]{:S(2)}, u32[]{:S(2)}) collective-permute-start(bf16[1,128,1024]{2,1,0:T(8,128)(2,1)S(1)} %copy-done), channel_id=1, source_target_pairs={{0,1},{1,2},{2,3},{3,4},{4,5},{5,6},{6,7},{8,9},{9,10},{10,11},{11... | collective-permute-start | bytes 786440 | tf_op jit(solution)/shard_map/ppermute | solution.py:300
  9.2 10.8 %collective-permute-start.1 = (bf16[1,128,1024]{2,1,0:T(8,128)(2,1)S(1)}, bf16[1,128,1024]{2,1,0:T(8,128)(2,1)S(1)}, u32[]{:S(2)}, u32[]{:S(2)}) collective-permute-start(bf16[1,128,1024]{2,1,0:T(8,128)(2,1)S(1)} %copy-done), channel_id=1, source_target_pairs={{1,0},{2,1},{3,2},{4,3},{5,4},{6,5},{7,6},{9,8},{10,9},{11,10},{12... | collective-permute-start | bytes 786440 | tf_op jit(solution)/shard_map/ppermute | solution.py:301
  10.7 16.2 %collective-permute-start.9 = (bf16[512,512]{1,0:T(8,128)(2,1)S(1)}, bf16[512,512]{1,0:T(8,128)(2,1)S(1)}, u32[]{:S(2)}, u32[]{:S(2)}) collective-permute-start(bf16[512,512]{1,0:T(8,128)(2,1)S(1)} %pad_maximum_fusion.1.refs_0_), channel_id=1, source_target_pairs={{0,16},{8,24},{16,0},{24,8},{1,17},{9,25},{17,1},{25,9},{2,18},{10... | collective-permute-start | bytes 1572872 | tf_op jit(solution)/shard_map/ppermute | solution.py:48
  14.7 5.3 %copy-start.2 = (f32[1024]{0:T(1024)S(1)}, f32[1024]{0:T(1024)}, u32[]{:S(2)}) copy-start(f32[1024]{0:T(1024)} %param.13) | copy-start | bytes 12292
  14.7 5.3 %copy-start.1 = (s32[1024]{0:T(1024)S(1)}, s32[1024]{0:T(1024)}, u32[]{:S(2)}) copy-start(s32[1024]{0:T(1024)} %param.21) | copy-start | bytes 12292
  14.7 7.8 %collective-permute-start.4 = (bf16[128,512]{1,0:T(8,128)(2,1)S(1)}, bf16[128,512]{1,0:T(8,128)(2,1)S(1)}, u32[]{:S(2)}, u32[]{:S(2)}) collective-permute-start(bf16[128,512]{1,0:T(8,128)(2,1)S(1)} %slice.154.refs_3_), channel_id=1, source_target_pairs={{0,2},{1,3},{2,0},{3,1},{4,6},{5,7},{6,4},{7,5},{8,10},{9,11},{10,... | collective-permute-start | bytes 393224 | tf_op jit(solution)/shard_map/ppermute | solution.py:48
  20.0 0.7 copy-start.5
  22.5 1.4 %collective-permute-start.7 = (bf16[128,512]{1,0:T(8,128)(2,1)S(1)}, bf16[128,512]{1,0:T(8,128)(2,1)S(1)}, u32[]{:S(2)}, u32[]{:S(2)}) collective-permute-start(bf16[128,512]{1,0:T(8,128)(2,1)S(1)} %get-tuple-element.107), channel_id=1, source_target_pairs={{0,8},{8,0},{16,24},{24,16},{1,9},{9,1},{17,25},{25,17},{2,10},{10... | collective-permute-start | bytes 393224 | tf_op jit(solution)/shard_map/ppermute | solution.py:48
  22.6 2.0 %copy-start.3 = (s32[1,9]{1,0:T(1,128)S(1)}, s32[1,9]{1,0:T(1,128)}, u32[]{:S(2)}) copy-start(s32[1,9]{1,0:T(1,128)} %refs_9_.1) | copy-start | bytes 112
  22.6 2.0 %copy-start.4 = (s32[1,9]{1,0:T(1,128)S(1)}, s32[1,9]{1,0:T(1,128)}, u32[]{:S(2)}) copy-start(s32[1,9]{1,0:T(1,128)} %refs_10_.1) | copy-start | bytes 112
  22.6 1.5 %collective-permute-start.8 = (bf16[128,512]{1,0:T(8,128)(2,1)S(1)}, bf16[128,512]{1,0:T(8,128)(2,1)S(1)}, u32[]{:S(2)}, u32[]{:S(2)}) collective-permute-start(bf16[128,512]{1,0:T(8,128)(2,1)S(1)} %get-tuple-element.106), channel_id=1, source_target_pairs={{0,8},{8,0},{16,24},{24,16},{1,9},{9,1},{17,25},{25,17},{2,10},{10... | collective-permute-start | bytes 393224 | tf_op jit(solution)/shard_map/ppermute | solution.py:48
  23.1 1.3 %collective-permute-start.5 = (bf16[128,512]{1,0:T(8,128)(2,1)S(1)}, bf16[128,512]{1,0:T(8,128)(2,1)S(1)}, u32[]{:S(2)}, u32[]{:S(2)}) collective-permute-start(bf16[128,512]{1,0:T(8,128)(2,1)S(1)} %slice.154.refs_3_), channel_id=1, source_target_pairs={{0,8},{8,0},{16,24},{24,16},{1,9},{9,1},{17,25},{25,17},{2,10},{10... | collective-permute-start | bytes 393224 | tf_op jit(solution)/shard_map/ppermute | solution.py:48
  23.2 1.4 %collective-permute-start.6 = (bf16[128,512]{1,0:T(8,128)(2,1)S(1)}, bf16[128,512]{1,0:T(8,128)(2,1)S(1)}, u32[]{:S(2)}, u32[]{:S(2)}) collective-permute-start(bf16[128,512]{1,0:T(8,128)(2,1)S(1)} %collective-permute-done.4.refs_4_), channel_id=1, source_target_pairs={{0,8},{8,0},{16,24},{24,16},{1,9},{9,1},{17,25},{25,17},{2,10},{10... | collective-permute-start | bytes 393224 | tf_op jit(solution)/shard_map/ppermute | solution.py:48
  26.9 1.6 %collective-permute-start.10 = (bf16[256,512]{1,0:T(8,128)(2,1)S(1)}, bf16[256,512]{1,0:T(8,128)(2,1)S(1)}, u32[]{:S(2)}, u32[]{:S(2)}) collective-permute-start(bf16[256,512]{1,0:T(8,128)(2,1)S(1)} %get-tuple-element.105), channel_id=1, source_target_pairs={{0,8},{8,0},{16,24},{24,16},{1,9},{9,1},{17,25},{25,17},{2,10},{10... | collective-permute-start | bytes 786440 | tf_op jit(solution)/shard_map/ppermute | solution.py:48
  27.4 1.6 %collective-permute-start.11 = (bf16[256,512]{1,0:T(8,128)(2,1)S(1)}, bf16[256,512]{1,0:T(8,128)(2,1)S(1)}, u32[]{:S(2)}, u32[]{:S(2)}) collective-permute-start(bf16[256,512]{1,0:T(8,128)(2,1)S(1)} %get-tuple-element.103.refs_2_), channel_id=1, source_target_pairs={{0,8},{8,0},{16,24},{24,16},{1,9},{9,1},{17,25},{25,17},{2,10},{10... | collective-permute-start | bytes 786440 | tf_op jit(solution)/shard_map/ppermute | solution.py:48
  27.6 2.9 %collective-permute-start.12 = (bf16[256,512]{1,0:T(8,128)(2,1)S(1)}, bf16[256,512]{1,0:T(8,128)(2,1)S(1)}, u32[]{:S(2)}, u32[]{:S(2)}) collective-permute-start(bf16[256,512]{1,0:T(8,128)(2,1)S(1)} %get-tuple-element.104), channel_id=1, source_target_pairs={{0,8},{8,0},{16,24},{24,16},{1,9},{9,1},{17,25},{25,17},{2,10},{10... | collective-permute-start | bytes 786440 | tf_op jit(solution)/shard_map/ppermute | solution.py:48
  27.9 2.6 %copy-start.6 = (bf16[1024,128]{1,0:T(8,128)(2,1)S(1)}, bf16[1024,128]{1,0:T(8,128)(2,1)}, u32[]{:S(2)}) copy-start(bf16[1024,128]{1,0:T(8,128)(2,1)} %read_ref.3) | copy-start | bytes 786436
  27.9 2.6 %collective-permute-start.13 = (bf16[256,512]{1,0:T(8,128)(2,1)S(1)}, bf16[256,512]{1,0:T(8,128)(2,1)S(1)}, u32[]{:S(2)}, u32[]{:S(2)}) collective-permute-start(bf16[256,512]{1,0:T(8,128)(2,1)S(1)} %get-tuple-element.102.refs_2_), channel_id=1, source_target_pairs={{0,8},{8,0},{16,24},{24,16},{1,9},{9,1},{17,25},{25,17},{2,10},{10... | collective-permute-start | bytes 786440 | tf_op jit(solution)/shard_map/ppermute | solution.py:48
  28.1 8.8 %collective-permute-start.17 = (bf16[512,384]{1,0:T(8,128)(2,1)S(1)}, bf16[512,384]{1,0:T(8,128)(2,1)S(1)}, u32[]{:S(2)}, u32[]{:S(2)}) collective-permute-start(bf16[512,384]{1,0:T(8,128)(2,1)S(1)} %get-tuple-element.61), channel_id=1, source_target_pairs={{0,8},{8,0},{16,24},{24,16},{1,9},{9,1},{17,25},{25,17},{2,10},{10... | collective-permute-start | bytes 1179656 | tf_op jit(solution)/shard_map/ppermute | solution.py:48
  30.5 6.4 %copy-start.7 = (f32[128,128]{1,0:T(8,128)S(1)}, f32[128,128]{1,0:T(8,128)}, u32[]{:S(2)}) copy-start(f32[128,128]{1,0:T(8,128)} %refs_5_.1) | copy-start | bytes 196612
  31.2 4.3 %collective-permute-start.14 = (bf16[128,128]{1,0:T(8,128)(2,1)S(1)}, bf16[128,128]{1,0:T(8,128)(2,1)S(1)}, u32[]{:S(2)}, u32[]{:S(2)}) collective-permute-start(bf16[128,128]{1,0:T(8,128)(2,1)S(1)} %get-tuple-element.63.refs_0_), channel_id=1, source_target_pairs={{0,16},{8,24},{16,0},{24,8},{1,17},{9,25},{17,1},{25,9},{2,18},{10... | collective-permute-start | bytes 98312 | tf_op jit(solution)/shard_map/ppermute | solution.py:48
  32.3 6.1 %collective-permute-start.18 = (bf16[128,512]{1,0:T(8,128)(2,1)S(1)}, bf16[128,512]{1,0:T(8,128)(2,1)S(1)}, u32[]{:S(2)}, u32[]{:S(2)}) collective-permute-start(bf16[128,512]{1,0:T(8,128)(2,1)S(1)} %attend.1.att_ref.refs_0_), channel_id=1, source_target_pairs={{0,16},{8,24},{16,0},{24,8},{1,17},{9,25},{17,1},{25,9},{2,18},{10... | collective-permute-start | bytes 393224 | tf_op jit(solution)/shard_map/ppermute | solution.py:48
  35.5 1.2 %collective-permute-start.15 = (bf16[128,128]{1,0:T(8,128)(2,1)S(1)}, bf16[128,128]{1,0:T(8,128)(2,1)S(1)}, u32[]{:S(2)}, u32[]{:S(2)}) collective-permute-start(bf16[128,128]{1,0:T(8,128)(2,1)S(1)} %get-tuple-element.63.refs_0_), channel_id=1, source_target_pairs={{0,8},{8,0},{16,24},{24,16},{1,9},{9,1},{17,25},{25,17},{2,10},{10... | collective-permute-start | bytes 98312 | tf_op jit(solution)/shard_map/ppermute | solution.py:48
  35.5 1.4 %collective-permute-start.16 = (bf16[128,128]{1,0:T(8,128)(2,1)S(1)}, bf16[128,128]{1,0:T(8,128)(2,1)S(1)}, u32[]{:S(2)}, u32[]{:S(2)}) collective-permute-start(bf16[128,128]{1,0:T(8,128)(2,1)S(1)} %collective-permute-done.14.refs_2_), channel_id=1, source_target_pairs={{0,8},{8,0},{16,24},{24,16},{1,9},{9,1},{17,25},{25,17},{2,10},{10... | collective-permute-start | bytes 98312 | tf_op jit(solution)/shard_map/ppermute | solution.py:48
  38.4 1.8 %collective-permute-start.19 = (bf16[400,512]{1,0:T(8,128)(2,1)S(1)}, bf16[400,512]{1,0:T(8,128)(2,1)S(1)}, u32[]{:S(2)}, u32[]{:S(2)}) collective-permute-start(bf16[400,512]{1,0:T(8,128)(2,1)S(1)} %get-tuple-element.71.own_con), channel_id=1, source_target_pairs={{0,8},{8,0},{16,24},{24,16},{1,9},{9,1},{17,25},{25,17},{2,10},{10... | collective-permute-start | bytes 1228808 | tf_op jit(solution)/shard_map/ppermute | solution.py:48
  38.8 6.0 %collective-permute-start.23 = (bf16[128,512]{1,0:T(8,128)(2,1)S(1)}, bf16[128,512]{1,0:T(8,128)(2,1)S(1)}, u32[]{:S(2)}, u32[]{:S(2)}) collective-permute-start(bf16[128,512]{1,0:T(8,128)(2,1)S(1)} %attend.1.att_ref.refs_0_), channel_id=1, source_target_pairs={{0,8},{8,0},{16,24},{24,16},{1,9},{9,1},{17,25},{25,17},{2,10},{10... | collective-permute-start | bytes 393224 | tf_op jit(solution)/shard_map/ppermute | solution.py:48
  39.1 5.8 %collective-permute-start.24 = (bf16[128,512]{1,0:T(8,128)(2,1)S(1)}, bf16[128,512]{1,0:T(8,128)(2,1)S(1)}, u32[]{:S(2)}, u32[]{:S(2)}) collective-permute-start(bf16[128,512]{1,0:T(8,128)(2,1)S(1)} %collective-permute-done.18.refs_2_), channel_id=1, source_target_pairs={{0,8},{8,0},{16,24},{24,16},{1,9},{9,1},{17,25},{25,17},{2,10},{10... | collective-permute-start | bytes 393224 | tf_op jit(solution)/shard_map/ppermute | solution.py:48
  41.3 6.5 %collective-permute-start.20 = (bf16[528,128]{1,0:T(8,128)(2,1)S(1)}, bf16[528,128]{1,0:T(8,128)(2,1)S(1)}, u32[]{:S(2)}, u32[]{:S(2)}) collective-permute-start(bf16[528,128]{1,0:T(8,128)(2,1)S(1)} %get-tuple-element.118), channel_id=1, source_target_pairs={{0,16},{1,17},{2,18},{3,19},{4,20},{5,21},{6,22},{7,23},{8,24},{9,... | collective-permute-start | bytes 405512 | tf_op jit(solution)/shard_map/ppermute | solution.py:450
  42.3 7.4 %collective-permute-start.21 = (bf16[528,128]{1,0:T(8,128)(2,1)S(1)}, bf16[528,128]{1,0:T(8,128)(2,1)S(1)}, u32[]{:S(2)}, u32[]{:S(2)}) collective-permute-start(bf16[528,128]{1,0:T(8,128)(2,1)S(1)} %get-tuple-element.116), channel_id=1, source_target_pairs={{0,1},{1,0},{2,3},{3,2},{4,5},{5,4},{6,7},{7,6},{8,9},{9,8},{10,11... | collective-permute-start | bytes 405512 | tf_op jit(solution)/shard_map/ppermute | solution.py:450
  43.8 7.2 %collective-permute-start.22 = (bf16[528,128]{1,0:T(8,128)(2,1)S(1)}, bf16[528,128]{1,0:T(8,128)(2,1)S(1)}, u32[]{:S(2)}, u32[]{:S(2)}) collective-permute-start(bf16[528,128]{1,0:T(8,128)(2,1)S(1)} %get-tuple-element.117), channel_id=1, source_target_pairs={{0,17},{1,16},{2,19},{3,18},{4,21},{5,20},{6,23},{7,22},{8,25},{9,... | collective-permute-start | bytes 405512 | tf_op jit(solution)/shard_map/ppermute | solution.py:450
  45.3 5.7 %collective-permute-start.25 = (bf16[512,128]{1,0:T(8,128)(2,1)S(1)}, bf16[512,128]{1,0:T(8,128)(2,1)S(1)}, u32[]{:S(2)}, u32[]{:S(2)}) collective-permute-start(bf16[512,128]{1,0:T(8,128)(2,1)S(1)} %bitcast.117), channel_id=1, source_target_pairs={{0,2},{1,3},{2,0},{3,1},{4,6},{5,7},{6,4},{7,5},{8,10},{9,11},{10,... | collective-permute-start | bytes 393224 | tf_op jit(solution)/shard_map/ppermute | solution.py:48
  51.1 5.9 %collective-permute-start.29 = (bf16[256,128]{1,0:T(8,128)(2,1)S(1)}, bf16[256,128]{1,0:T(8,128)(2,1)S(1)}, u32[]{:S(2)}, u32[]{:S(2)}) collective-permute-start(bf16[256,128]{1,0:T(8,128)(2,1)S(1)} %bitcast.118), channel_id=1, source_target_pairs={{0,1},{1,0},{2,3},{3,2},{4,5},{5,4},{6,7},{7,6},{8,9},{9,8},{10,11... | collective-permute-start | bytes 196616 | tf_op jit(solution)/shard_map/ppermute | solution.py:48
  52.6 6.4 %collective-permute-start.26 = (bf16[144,128]{1,0:T(8,128)(2,1)S(1)}, bf16[144,128]{1,0:T(8,128)(2,1)S(1)}, u32[]{:S(2)}, u32[]{:S(2)}) collective-permute-start(bf16[144,128]{1,0:T(8,128)(2,1)S(1)} %get-tuple-element.115), channel_id=1, source_target_pairs={{0,2},{1,3},{2,0},{3,1},{4,6},{5,7},{6,4},{7,5},{8,10},{9,11},{10,... | collective-permute-start | bytes 110600 | tf_op jit(solution)/shard_map/ppermute | solution.py:48
  54.4 5.5 %collective-permute-start.27 = (bf16[144,128]{1,0:T(8,128)(2,1)S(1)}, bf16[144,128]{1,0:T(8,128)(2,1)S(1)}, u32[]{:S(2)}, u32[]{:S(2)}) collective-permute-start(bf16[144,128]{1,0:T(8,128)(2,1)S(1)} %get-tuple-element.114), channel_id=1, source_target_pairs={{0,4},{1,5},{2,6},{3,7},{4,0},{5,1},{6,2},{7,3},{8,12},{9,13},{10,... | collective-permute-start | bytes 110600 | tf_op jit(solution)/shard_map/ppermute | solution.py:48
  57.0 5.8 %collective-permute-start.28 = (bf16[144,128]{1,0:T(8,128)(2,1)S(1)}, bf16[144,128]{1,0:T(8,128)(2,1)S(1)}, u32[]{:S(2)}, u32[]{:S(2)}) collective-permute-start(bf16[144,128]{1,0:T(8,128)(2,1)S(1)} %get-tuple-element.113), channel_id=1, source_target_pairs={{0,6},{1,7},{2,4},{3,5},{4,2},{5,3},{6,0},{7,1},{8,14},{9,15},{10,... | collective-permute-start | bytes 110600 | tf_op jit(solution)/shard_map/ppermute | solution.py:48
  57.1 5.6 %collective-permute-start.30 = (bf16[128,128]{1,0:T(8,128)(2,1)S(1)}, bf16[128,128]{1,0:T(8,128)(2,1)S(1)}, u32[]{:S(2)}, u32[]{:S(2)}) collective-permute-start(bf16[128,128]{1,0:T(8,128)(2,1)S(1)} %fusion.12), channel_id=1, source_target_pairs={{0,4},{1,5},{2,6},{3,7},{4,0},{5,1},{6,2},{7,3},{8,12},{9,13},{10,... | collective-permute-start | bytes 98312 | tf_op jit(solution)/shard_map/ppermute | solution.py:48
  62.8 6.9 %collective-permute-start.34 = (bf16[1,2,128,128]{3,2,1,0:T(8,128)(2,1)S(1)}, bf16[1,2,128,128]{3,2,1,0:T(8,128)(2,1)S(1)}, u32[]{:S(2)}, u32[]{:S(2)}) collective-permute-start(bf16[1,2,128,128]{3,2,1,0:T(8,128)(2,1)S(1)} %pad_maximum_fusion.11), channel_id=1, source_target_pairs={{0,4},{1,5},{2,6},{3,7},{4,0},{5,1},{6,2},{7,3},{8,12},{9,13},{10,... | collective-permute-start | bytes 196616 | tf_op jit(solution)/shard_map/ppermute | solution.py:48
  64.0 6.1 %collective-permute-start.35 = (bf16[1,2,128,128]{3,2,1,0:T(8,128)(2,1)S(1)}, bf16[1,2,128,128]{3,2,1,0:T(8,128)(2,1)S(1)}, u32[]{:S(2)}, u32[]{:S(2)}) collective-permute-start(bf16[1,2,128,128]{3,2,1,0:T(8,128)(2,1)S(1)} %pad_maximum_fusion.11), channel_id=1, source_target_pairs={{0,6},{1,7},{2,4},{3,5},{4,2},{5,3},{6,0},{7,1},{8,14},{9,15},{10,... | collective-permute-start | bytes 196616 | tf_op jit(solution)/shard_map/ppermute | solution.py:48
  66.1 9.0 %collective-permute-start.32 = (bf16[1,2,128,128]{3,2,1,0:T(8,128)(2,1)S(1)}, bf16[1,2,128,128]{3,2,1,0:T(8,128)(2,1)S(1)}, u32[]{:S(2)}, u32[]{:S(2)}) collective-permute-start(bf16[1,2,128,128]{3,2,1,0:T(8,128)(2,1)S(1)} %pad_maximum_fusion.11), channel_id=1, source_target_pairs={{0,2},{1,3},{2,0},{3,1},{4,6},{5,7},{6,4},{7,5},{8,10},{9,11},{10,... | collective-permute-start | bytes 196616 | tf_op jit(solution)/shard_map/ppermute | solution.py:48
  66.5 8.7 %collective-permute-start.31 = (bf16[2,128,128]{2,1,0:T(8,128)(2,1)S(1)}, bf16[2,128,128]{2,1,0:T(8,128)(2,1)S(1)}, u32[]{:S(2)}, u32[]{:S(2)}) collective-permute-start(bf16[2,128,128]{2,1,0:T(8,128)(2,1)S(1)} %pad_maximum_fusion.10.refs_0_), channel_id=1, source_target_pairs={{0,1},{1,0},{2,3},{3,2},{4,5},{5,4},{6,7},{7,6},{8,9},{9,8},{10,11... | collective-permute-start | bytes 196616 | tf_op jit(solution)/shard_map/ppermute | solution.py:48
  68.4 6.7 %collective-permute-start.33 = (bf16[2,128,128]{2,1,0:T(8,128)(2,1)S(1)}, bf16[2,128,128]{2,1,0:T(8,128)(2,1)S(1)}, u32[]{:S(2)}, u32[]{:S(2)}) collective-permute-start(bf16[2,128,128]{2,1,0:T(8,128)(2,1)S(1)} %pad_maximum_fusion.10.refs_0_), channel_id=1, source_target_pairs={{0,3},{1,2},{2,1},{3,0},{4,7},{5,6},{6,5},{7,4},{8,11},{9,10},{10,... | collective-permute-start | bytes 196616 | tf_op jit(solution)/shard_map/ppermute | solution.py:48
  70.1 5.0 %collective-permute-start.36 = (bf16[2,2,128,128]{3,2,1,0:T(8,128)(2,1)S(1)}, bf16[2,2,128,128]{3,2,1,0:T(8,128)(2,1)S(1)}, u32[]{:S(2)}, u32[]{:S(2)}) collective-permute-start(bf16[2,2,128,128]{3,2,1,0:T(8,128)(2,1)S(1)} %pad_maximum_fusion.9), channel_id=1, source_target_pairs={{0,1},{1,0},{2,3},{3,2},{4,5},{5,4},{6,7},{7,6},{8,9},{9,8},{10,11... | collective-permute-start | bytes 393224 | tf_op jit(solution)/shard_map/ppermute | solution.py:48

commit v7 on v6

--- a/solution.py
+++ b/solution.py
@@ -180,19 +180,20 @@
             con_ref[rows, cols] = (both[rows] * counts[i]).astype(BF16)
 
 
-def value_body(blocks, dsh, keep_ref, sib_ref, own_con, sib_con, v_ref, loss_ref):
-    rows = 3 * TILE
-    term = dot(keep_ref[...], own_con[:rows, :]) + dot(sib_ref[...], sib_con[:rows, :])
+def value_body(blocks, dsh, rows, keep_ref, sib_ref, own_con, sib_con, v_ref, loss_ref):
+    keys = 3 * TILE
+    term = dot(keep_ref[...], own_con[:keys, :]) + dot(sib_ref[...], sib_con[:keys, :])
     parts = []
     for ref in (own_con, sib_con):
-        part = ref[rows:, :].astype(F32)
+        part = ref[keys:, :].astype(F32)
         parts.append(part[:, :LANES] + part[:, LANES : 2 * LANES] + part[:, 2 * LANES : 3 * LANES])
     loss_ref[...] = (parts[0] + parts[1])[:8]
     for b in range(blocks):
         for cb in range(term.shape[1] // LANES):
-            v_ref[b, cb * dsh : (cb + 1) * dsh, :] = term[
-                b * dsh : (b + 1) * dsh, cb * LANES : (cb + 1) * LANES
-            ]
+            for first in range(0, dsh, rows):
+                piece = (cb * dsh + first) // rows
+                part = term[b * dsh + first : b * dsh + first + rows, cb * LANES : (cb + 1) * LANES]
+                v_ref[b, piece % 2, piece // 2 * rows : (piece // 2 + 1) * rows, :] = part
 
 
 def output_body(n_ens, dsh, gf_ref, read_ref, *refs):
@@ -208,14 +209,16 @@
 
 
 def finish_body(n_pix, dsh, scale, *refs):
-    pieces = refs[:n_pix]
-    total_ref, gv_ref, go_ref, loss_ref, scratch = refs[n_pix:]
+    top = n_pix // 2
+    pieces = refs[:top]
+    total_ref, gv_ref, go_ref, loss_ref, scratch = refs[top:]
     loss_ref[...] = total_ref[:1, :1] * scale
     rows = scratch.shape[1] // n_pix
-    position = lax.axis_index("pix")
-    for j in range(n_pix):
-        start = pl.multiple_of((position ^ j) * rows, rows)
-        scratch[:, pl.ds(start, rows), :] = pieces[j][...].astype(F32)
+    position = lax.axis_index("pix") % top
+    for j, ref in enumerate(pieces):
+        for side in (0, 1):
+            start = pl.multiple_of(((position ^ j) + side * top) * rows, rows)
+            scratch[:, pl.ds(start, rows), :] = ref[:, side * rows : (side + 1) * rows, :].astype(F32)
     for cb in range(scratch.shape[1] // dsh):
         gv_ref[:, cb * LANES : (cb + 1) * LANES] = scratch[0, cb * dsh : (cb + 1) * dsh, :]
         go_ref[cb * LANES : (cb + 1) * LANES, :] = scratch[1, cb * dsh : (cb + 1) * dsh, :].T
@@ -386,8 +389,8 @@
     attended_all = both_cores(attended_near)
     blocks = n_ens // 2
     value_term, loss = call(
-        functools.partial(value_body, blocks, dsh),
-        [((blocks, dsh * inner // LANES, LANES), F32), ((8, LANES), F32)],
+        functools.partial(value_body, blocks, dsh, dsh * inner // (LANES * n_pix)),
+        [((blocks, 2, dsh * inner // (2 * LANES), LANES), F32), ((8, LANES), F32)],
         [("v", turned_keep), ("v", turned_sib), ("v", contrib), ("v", contrib_sib)],
         10**9,
         "value_term",
@@ -436,8 +439,7 @@
         output_term = added(*sent(output_term, [bit]))
     output_kept, output_got = sent(output_term, [later[-2]])
     upper, low = (e // far[-1]) % 2, p % 2
-    quarters = [pieces_of(h, groups[0]) for h in value_term.reshape(2, -1, LANES)]
-    quarters = jnp.stack([part_of(q, i) for q in quarters for i in range(2)])
+    quarters = value_term.reshape(4, -1, LANES)
     pos = 2 * upper + low
     received = []
     for d in (2, 1, 3):
@@ -458,38 +460,28 @@
 
     value_term, output_got = lax.optimization_barrier((value_term, output_got))
     output_kept, output_got = sent(added(output_kept, output_got), groups[0], higher=2)
-    for group in groups[1:]:
-        size, pos = 1 << len(group), (p // group[0]) % (1 << len(group))
-        split = pieces_of(value_term, group)
-        messages = {d: with_loss(part_of(split, pos ^ d), loss) for d in range(1, size)}
-        received = {d: xor_permute(m, "pix", d * group[0]) for d, m in messages.items()}
-        if group == groups[-1]:
-            output_kept, output_got = sent(added(output_kept, output_got), [later[-1]], higher=1)
-            received, output_got = lax.optimization_barrier((received, output_got))
-        received = {d: split_loss(m) for d, m in received.items()}
-        totals = jnp.stack([loss] + [received[d][1] for d in range(1, size)])
-        loss = functools.reduce(jnp.add, [at(totals, pos ^ i) for i in range(size)])
-        value_term = added(part_of(split, pos), [received[d][0] for d in range(1, size)])
+    for bit in later[:-1]:
+        kept, received = sent(value_term, [bit], loss)
+        block, other = split_loss(received[0])
+        value_term, loss = added(kept, [block]), loss + other
     output_term = added(output_kept, output_got)
-    terms = [value_term, output_term]
-    piece = jnp.stack(terms).astype(BF16)
-    pieces, near = {0: piece}, groups[1][0]
-    pair = {1: xor_permute(piece, "pix", 1), near ^ 1: xor_permute(piece, "pix", near ^ 1)}
-    for group in reversed(groups[1:]):
+    both = jnp.concatenate([value_term, output_term]).astype(BF16)
+    block, other = split_loss(xor_permute(with_loss(both, loss), "pix", later[-1]))
+    loss = loss + other
+    both = (both.astype(F32) + block.astype(F32)).astype(BF16)
+    pieces = {0: both.reshape(2, -1, LANES)}
+    rest = [1] + later[:-1]
+    for stage in reversed([rest[i : i + 2] for i in range(0, len(rest), 2)]):
         keys = sorted(pieces)
-        stack = jnp.stack([pieces[j] for j in keys])
-        new = {d: xor_permute(stack, "pix", d * group[0]) for d in range(1, 1 << len(group))}
-        for i, j in enumerate(keys):
-            pieces.update({j ^ (d * group[0]): got[i] for d, got in new.items()})
-    later = [j for j in sorted(pieces) if j not in (0, near)]
-    got = xor_permute(jnp.stack([pieces[j] for j in later]), "pix", 1)
-    pair.update({j ^ 1: got[i] for i, j in enumerate(later)})
-    pieces.update(pair)
+        stack = pieces[0][None] if len(keys) == 1 else jnp.stack([pieces[j] for j in keys])
+        for d in range(1, 1 << len(stage)):
+            got = xor_permute(stack, "pix", d * stage[0])
+            pieces.update({j ^ (d * stage[0]): got[i] for i, j in enumerate(keys)})
     scale = 1.0 / (n_ens * n_pix * TILE * n_out)
     grad_w_value, grad_w_out, loss = call(
         functools.partial(finish_body, n_pix, dsh, scale),
         [((dsh, inner), F32), ((inner, dsh), F32), ((1, 1), F32)],
-        [("v", pieces[j]) for j in range(n_pix)] + [("v", loss)],
+        [("v", pieces[j]) for j in sorted(pieces)] + [("v", loss)],
         10**6,
         "finish",
         scratch=[pltpu.VMEM((2, dsh * inner // LANES, LANES), F32)],

time: 76.6 us -> 74.1 us (0.967)
  starting transfers between devices: 37.8 us -> 31.2 us
  waiting for transfers between devices: 24.9 us -> 29.3 us
    ppermute x32 -> x27, starting transfers between devices: 29.6 us -> 22.9 us  [xor_permute(): return lax.ppermute(value, axis, [(i, i ^ mask) for i in range(size)])]
    ppermute x32 -> x27, waiting for transfers between devices: 17.5 us -> 22 us  [xor_permute(): return lax.ppermute(value, axis, [(i, i ^ mask) for i in range(size)])]
  transfers between devices with their start and end apart: 37 -> 32, of which waited for: 19 -> 20; matrix products, arithmetic and copies ran while one was open for 1% -> 1% of each run, Pallas kernels for 10% -> 10%
where the time goes in v7:
time: 74.1 us; the launch traced here: 73.9 us
  starting transfers between devices  31.2 us (42%)
  waiting for transfers between devices  29.3 us (40%)
  Pallas kernels  8.86 us (12%)
  local copies, waits for them, and re-layouts  1.99 us (3%)
  other arithmetic  1.39 us (2%)
  between operations  1.17 us (2%)
    ppermute x27, starting transfers between devices, xor_permute(): return lax.ppermute(value, axis, [(i, i ^ mask) for i in range(size)])  22.9 us
    ppermute x27, waiting for transfers between devices, xor_permute(): return lax.ppermute(value, axis, [(i, i ^ mask) for i in range(size)])  22 us
    pallas_call x8, Pallas kernels, call(): pl.pallas_call(body, out_shape=[jax.ShapeDtypeStruct(s, d) for s, d in ou...  8.86 us
    ppermute x1, waiting for transfers between devices, per_device(): lax.ppermute(sample_layer_feed, 'pix', [(i, i + 1) for i in range(n_pix -...  4.18 us
    ppermute x3, starting transfers between devices, per_device(): lax.ppermute(message, ('ens', 'pix'), pairs)  3.55 us
    ppermute x1, starting transfers between devices, per_device(): lax.ppermute(sample_layer_feed, 'pix', [(i, i + 1) for i in range(n_pix -...  3.43 us
    ppermute x3, waiting for transfers between devices, per_device(): lax.ppermute(message, ('ens', 'pix'), pairs)  3.15 us
    unnamed x26, local copies, waits for them, and re-layouts  1.68 us
  transfers between devices with their start and end apart: 32, of which 20 were waited for; matrix products, arithmetic and copies ran while one was open for 1% of the time, Pallas kernels for 10%

profile of v7, /device:TPU:0, one launch (start us, length us, event | category | flops | bytes accessed | tf_op | source)
XLA Modules:
  0.0 73.9 jit_solution(6312462652743793000)
XLA Ops:
  0.7 1.0 %slice_select_fusion = bf16[128,512]{1,0:T(8,128)(2,1)S(1)} fusion(bf16[256,512]{1,0:T(8,128)(2,1)} %param.15, pred[]{:T(512)S(6)} %eq.10), kind=kLoop, calls=%fused_computation.27 | loop fusion | flops 65536 | bytes 393217 | tf_op jit(solution)/shard_map/jit(_where)/select_n | solution.py:299
  1.8 3.0 %collective-permute-start.3 = (bf16[384,512]{1,0:T(8,128)(2,1)S(1)}, bf16[384,512]{1,0:T(8,128)(2,1)S(1)}, u32[]{:S(2)}, u32[]{:S(2)}) collective-permute-start(bf16[384,512]{1,0:T(8,128)(2,1)S(1)} %pad_maximum_fusion.1), channel_id=1, source_target_pairs={{0,16},{8,24},{16,0},{24,8},{1,17},{9,25},{17,1},{25,9},{2,18},{10... | collective-permute-start | bytes 1179656 | tf_op jit(solution)/shard_map/ppermute | solution.py:48
  4.9 0.1 collective-permute-start.2
  4.9 0.8 %copy-done = bf16[1,128,1024]{2,1,0:T(8,128)(2,1)S(1)} copy-done((bf16[1,128,1024]{2,1,0:T(8,128)(2,1)S(1)}, bf16[1,128,1024]{2,1,0:T(8,128)(2,1)}, u32[]{:S(2)}) %copy-start) | copy-done | bytes 262168
  5.7 3.4 %collective-permute-start = (bf16[1,128,1024]{2,1,0:T(8,128)(2,1)S(1)}, bf16[1,128,1024]{2,1,0:T(8,128)(2,1)S(1)}, u32[]{:S(2)}, u32[]{:S(2)}) collective-permute-start(bf16[1,128,1024]{2,1,0:T(8,128)(2,1)S(1)} %copy-done), channel_id=1, source_target_pairs={{0,1},{1,2},{2,3},{3,4},{4,5},{5,6},{6,7},{8,9},{9,10},{10,11},{11... | collective-permute-start | bytes 786440 | tf_op jit(solution)/shard_map/ppermute | solution.py:303
  9.2 1.3 %collective-permute-start.1 = (bf16[1,128,1024]{2,1,0:T(8,128)(2,1)S(1)}, bf16[1,128,1024]{2,1,0:T(8,128)(2,1)S(1)}, u32[]{:S(2)}, u32[]{:S(2)}) collective-permute-start(bf16[1,128,1024]{2,1,0:T(8,128)(2,1)S(1)} %copy-done), channel_id=1, source_target_pairs={{1,0},{2,1},{3,2},{4,3},{5,4},{6,5},{7,6},{9,8},{10,9},{11,10},{12... | collective-permute-start | bytes 786440 | tf_op jit(solution)/shard_map/ppermute | solution.py:304
  10.5 0.1 copy.17
  10.7 0.9 %collective-permute-start.9 = (bf16[512,512]{1,0:T(8,128)(2,1)S(1)}, bf16[512,512]{1,0:T(8,128)(2,1)S(1)}, u32[]{:S(2)}, u32[]{:S(2)}) collective-permute-start(bf16[512,512]{1,0:T(8,128)(2,1)S(1)} %pad_maximum_fusion.refs_0_), channel_id=1, source_target_pairs={{0,16},{8,24},{16,0},{24,8},{1,17},{9,25},{17,1},{25,9},{2,18},{10... | collective-permute-start | bytes 1572872 | tf_op jit(solution)/shard_map/ppermute | solution.py:48
  11.6 3.1 %collective-permute-done.3 = bf16[384,512]{1,0:T(8,128)(2,1)S(1)} collective-permute-done((bf16[384,512]{1,0:T(8,128)(2,1)S(1)}, bf16[384,512]{1,0:T(8,128)(2,1)S(1)}, u32[]{:S(2)}, u32[]{:S(2)}) %collective-permute-start.3) | collective-permute-done | bytes 393248 | tf_op jit(solution)/shard_map/ppermute | solution.py:48
  14.7 1.1 %collective-permute-start.4 = (bf16[128,512]{1,0:T(8,128)(2,1)S(1)}, bf16[128,512]{1,0:T(8,128)(2,1)S(1)}, u32[]{:S(2)}, u32[]{:S(2)}) collective-permute-start(bf16[128,512]{1,0:T(8,128)(2,1)S(1)} %slice.124.refs_3_), channel_id=1, source_target_pairs={{0,2},{1,3},{2,0},{3,1},{4,6},{5,7},{6,4},{7,5},{8,10},{9,11},{10,... | collective-permute-start | bytes 393224 | tf_op jit(solution)/shard_map/ppermute | solution.py:48
  15.8 4.2 %collective-permute-done.up_ref = bf16[1,128,1024]{2,1,0:T(8,128)(2,1)S(1)} collective-permute-done((bf16[1,128,1024]{2,1,0:T(8,128)(2,1)S(1)}, bf16[1,128,1024]{2,1,0:T(8,128)(2,1)S(1)}, u32[]{:S(2)}, u32[]{:S(2)}) %collective-permute-start) | collective-permute-done | bytes 262176 | tf_op jit(solution)/shard_map/ppermute | solution.py:303
  20.0 0.6 copy-done.5
  20.6 0.6 normed.1
  21.2 1.3 %collective-permute-done.4.refs_4_ = bf16[128,512]{1,0:T(8,128)(2,1)S(1)} collective-permute-done((bf16[128,512]{1,0:T(8,128)(2,1)S(1)}, bf16[128,512]{1,0:T(8,128)(2,1)S(1)}, u32[]{:S(2)}, u32[]{:S(2)}) %collective-permute-start.4) | collective-permute-done | bytes 131104 | tf_op jit(solution)/shard_map/ppermute | solution.py:48
  22.5 0.1 collective-permute-start.7
  22.6 0.5 collective-permute-start.8
  23.1 0.1 collective-permute-start.5
  23.2 0.4 collective-permute-start.6
  23.6 0.3 collective-permute-done.7.refs_7_
  23.9 0.2 collective-permute-done.8.refs_8_
  24.1 0.3 collective-permute-done.5.refs_5_
  24.4 0.2 collective-permute-done.6.refs_6_
  24.6 2.2 %weights.1.w_ref.refs_8_ = bf16[8,128,384]{2,1,0:T(8,128)(2,1)S(1)} custom-call(bf16[384,1024]{1,0:T(8,128)(2,1)S(1)} %get-tuple-element.45.n_ref, s32[8,128]{1,0:T(8,128)S(1)} %bitcast.65, s32[1,9]{1,0:T(1,128)S(1)} %copy-done.3, s32[1,9]{1,0:T(1,128)S(1)} %copy-done.4, bf16[512,512]{1,0:T(8,128)(2,1)S(1)} %constant_dynamic-update-slice_fusion.refs_0_, ...), custom_call_target="tpu_custom_call" | custom-call | flops 1000 | bytes 1 | tf_op jit(solution)/shard_map/weights/pallas_call | solution.py:34
  26.9 0.4 collective-permute-start.10
  27.4 0.3 collective-permute-start.11
  27.6 0.3 collective-permute-start.12
  27.9 0.2 collective-permute-start.13
  28.1 0.3 collective-permute-start.17
  28.4 0.1 collective-permute-done.10.refs_1_
  28.5 0.4 collective-permute-done.11.refs_3_
  29.0 1.5 %attend.1.att_ref.refs_0_ = bf16[128,512]{1,0:T(8,128)(2,1)S(1)} custom-call(bf16[384,1024]{1,0:T(8,128)(2,1)S(1)} %get-tuple-element.45.n_ref, bf16[8,128,384]{2,1,0:T(8,128)(2,1)S(1)} %weights.1.w_ref.refs_8_, s32[1,9]{1,0:T(1,128)S(1)} %copy-done.3, s32[1,9]{1,0:T(1,128)S(1)} %copy-done.4, bf16[512,512]{1,0:T(8,128)(2,1)S(1)} %pad_maximum_fusion.refs_0_, ...), custom_call_target="tpu_custom_call" | custom-call | flops 1000000000 | bytes 1000000 | tf_op jit(solution)/shard_map/attend/pallas_call | solution.py:34
  30.5 0.7 forecast.1
  31.2 1.0 %collective-permute-start.14 = (bf16[128,128]{1,0:T(8,128)(2,1)S(1)}, bf16[128,128]{1,0:T(8,128)(2,1)S(1)}, u32[]{:S(2)}, u32[]{:S(2)}) collective-permute-start(bf16[128,128]{1,0:T(8,128)(2,1)S(1)} %get-tuple-element.59.refs_0_), channel_id=1, source_target_pairs={{0,16},{8,24},{16,0},{24,8},{1,17},{9,25},{17,1},{25,9},{2,18},{10... | collective-permute-start | bytes 98312 | tf_op jit(solution)/shard_map/ppermute | solution.py:48
  32.3 1.0 %collective-permute-start.18 = (bf16[128,512]{1,0:T(8,128)(2,1)S(1)}, bf16[128,512]{1,0:T(8,128)(2,1)S(1)}, u32[]{:S(2)}, u32[]{:S(2)}) collective-permute-start(bf16[128,512]{1,0:T(8,128)(2,1)S(1)} %attend.1.att_ref.refs_0_), channel_id=1, source_target_pairs={{0,16},{8,24},{16,0},{24,8},{1,17},{9,25},{17,1},{25,9},{2,18},{10... | collective-permute-start | bytes 393224 | tf_op jit(solution)/shard_map/ppermute | solution.py:48
  33.3 2.2 %collective-permute-done.14.refs_2_ = bf16[128,128]{1,0:T(8,128)(2,1)S(1)} collective-permute-done((bf16[128,128]{1,0:T(8,128)(2,1)S(1)}, bf16[128,128]{1,0:T(8,128)(2,1)S(1)}, u32[]{:S(2)}, u32[]{:S(2)}) %collective-permute-start.14) | collective-permute-done | bytes 32800 | tf_op jit(solution)/shard_map/ppermute | solution.py:48
  35.5 0.5 collective-permute-start.16
  36.1 0.7 collective-permute-done.15.refs_1_
  36.8 0.2 collective-permute-done.16.refs_3_
  36.9 1.5 %backward.1 = (bf16[512,128]{1,0:T(8,128)(2,1)S(1)}, bf16[400,512]{1,0:T(8,128)(2,1)S(1)}) custom-call(bf16[128,128]{1,0:T(8,128)(2,1)S(1)} %get-tuple-element.59.refs_0_, bf16[128,128]{1,0:T(8,128)(2,1)S(1)} %collective-permute-done.15.refs_1_, bf16[128,128]{1,0:T(8,128)(2,1)S(1)} %collective-permute-done.14.refs_2_, ...), custom_call_target="tpu_custom_call" | custom-call | flops 1000000000 | bytes 1000000 | tf_op jit(solution)/shard_map/backward/pallas_call | solution.py:34
  38.4 0.4 collective-permute-start.19
  38.9 0.2 collective-permute-start.23
  39.0 0.3 collective-permute-start.24
  39.4 0.9 %collective-permute-done.19.sib_con = bf16[400,512]{1,0:T(8,128)(2,1)S(1)} collective-permute-done((bf16[400,512]{1,0:T(8,128)(2,1)S(1)}, bf16[400,512]{1,0:T(8,128)(2,1)S(1)}, u32[]{:S(2)}, u32[]{:S(2)}) %collective-permute-start.19) | collective-permute-done | bytes 409632 | tf_op jit(solution)/shard_map/ppermute | solution.py:48
  40.3 0.7 value_term.1
  41.0 0.1 fusion.3
  41.1 1.0 %collective-permute-start.20 = (bf16[528,128]{1,0:T(8,128)(2,1)S(1)}, bf16[528,128]{1,0:T(8,128)(2,1)S(1)}, u32[]{:S(2)}, u32[]{:S(2)}) collective-permute-start(bf16[528,128]{1,0:T(8,128)(2,1)S(1)} %get-tuple-element.98), channel_id=1, source_target_pairs={{0,16},{1,17},{2,18},{3,19},{4,20},{5,21},{6,22},{7,23},{8,24},{9,... | collective-permute-start | bytes 405512 | tf_op jit(solution)/shard_map/ppermute | solution.py:452
  42.1 1.4 %collective-permute-start.21 = (bf16[528,128]{1,0:T(8,128)(2,1)S(1)}, bf16[528,128]{1,0:T(8,128)(2,1)S(1)}, u32[]{:S(2)}, u32[]{:S(2)}) collective-permute-start(bf16[528,128]{1,0:T(8,128)(2,1)S(1)} %get-tuple-element.96), channel_id=1, source_target_pairs={{0,1},{1,0},{2,3},{3,2},{4,5},{5,4},{6,7},{7,6},{8,9},{9,8},{10,11... | collective-permute-start | bytes 405512 | tf_op jit(solution)/shard_map/ppermute | solution.py:452
  43.5 1.1 %collective-permute-start.22 = (bf16[528,128]{1,0:T(8,128)(2,1)S(1)}, bf16[528,128]{1,0:T(8,128)(2,1)S(1)}, u32[]{:S(2)}, u32[]{:S(2)}) collective-permute-start(bf16[528,128]{1,0:T(8,128)(2,1)S(1)} %get-tuple-element.97), channel_id=1, source_target_pairs={{0,17},{1,16},{2,19},{3,18},{4,21},{5,20},{6,23},{7,22},{8,25},{9,... | collective-permute-start | bytes 405512 | tf_op jit(solution)/shard_map/ppermute | solution.py:452
  44.6 0.4 output_term.1
  45.1 2.5 %collective-permute-start.25 = (bf16[512,128]{1,0:T(8,128)(2,1)S(1)}, bf16[512,128]{1,0:T(8,128)(2,1)S(1)}, u32[]{:S(2)}, u32[]{:S(2)}) collective-permute-start(bf16[512,128]{1,0:T(8,128)(2,1)S(1)} %bitcast.75), channel_id=1, source_target_pairs={{0,2},{1,3},{2,0},{3,1},{4,6},{5,7},{6,4},{7,5},{8,10},{9,11},{10,... | collective-permute-start | bytes 393224 | tf_op jit(solution)/shard_map/ppermute | solution.py:48
  47.6 1.9 %collective-permute-done.21 = bf16[528,128]{1,0:T(8,128)(2,1)S(1)} collective-permute-done((bf16[528,128]{1,0:T(8,128)(2,1)S(1)}, bf16[528,128]{1,0:T(8,128)(2,1)S(1)}, u32[]{:S(2)}, u32[]{:S(2)}) %collective-permute-start.21) | collective-permute-done | bytes 135200 | tf_op jit(solution)/shard_map/ppermute | solution.py:452
  49.5 1.2 %collective-permute-done.22 = bf16[528,128]{1,0:T(8,128)(2,1)S(1)} collective-permute-done((bf16[528,128]{1,0:T(8,128)(2,1)S(1)}, bf16[528,128]{1,0:T(8,128)(2,1)S(1)}, u32[]{:S(2)}, u32[]{:S(2)}) %collective-permute-start.22) | collective-permute-done | bytes 135200 | tf_op jit(solution)/shard_map/ppermute | solution.py:452
  50.8 0.1 fusion.1
  51.0 2.2 %collective-permute-start.26 = (bf16[272,128]{1,0:T(8,128)(2,1)S(1)}, bf16[272,128]{1,0:T(8,128)(2,1)S(1)}, u32[]{:S(2)}, u32[]{:S(2)}) collective-permute-start(bf16[272,128]{1,0:T(8,128)(2,1)S(1)} %pad_maximum_fusion.9), channel_id=1, source_target_pairs={{0,2},{1,3},{2,0},{3,1},{4,6},{5,7},{6,4},{7,5},{8,10},{9,11},{10,... | collective-permute-start | bytes 208904 | tf_op jit(solution)/shard_map/ppermute | solution.py:48
  53.3 0.9 %collective-permute-start.27 = (bf16[256,128]{1,0:T(8,128)(2,1)S(1)}, bf16[256,128]{1,0:T(8,128)(2,1)S(1)}, u32[]{:S(2)}, u32[]{:S(2)}) collective-permute-start(bf16[256,128]{1,0:T(8,128)(2,1)S(1)} %bitcast.76), channel_id=1, source_target_pairs={{0,1},{1,0},{2,3},{3,2},{4,5},{5,4},{6,7},{7,6},{8,9},{9,8},{10,11... | collective-permute-start | bytes 196616 | tf_op jit(solution)/shard_map/ppermute | solution.py:48
  54.2 3.5 %collective-permute-done.27 = bf16[256,128]{1,0:T(8,128)(2,1)S(1)} collective-permute-done((bf16[256,128]{1,0:T(8,128)(2,1)S(1)}, bf16[256,128]{1,0:T(8,128)(2,1)S(1)}, u32[]{:S(2)}, u32[]{:S(2)}) %collective-permute-start.27) | collective-permute-done | bytes 65568 | tf_op jit(solution)/shard_map/ppermute | solution.py:48
  57.8 2.7 %collective-permute-start.28 = (bf16[528,128]{1,0:T(8,128)(2,1)S(1)}, bf16[528,128]{1,0:T(8,128)(2,1)S(1)}, u32[]{:S(2)}, u32[]{:S(2)}) collective-permute-start(bf16[528,128]{1,0:T(8,128)(2,1)S(1)} %pad_maximum_fusion.8), channel_id=1, source_target_pairs={{0,4},{1,5},{2,6},{3,7},{4,0},{5,1},{6,2},{7,3},{8,12},{9,13},{10,... | collective-permute-start | bytes 405512 | tf_op jit(solution)/shard_map/ppermute | solution.py:48
  60.4 4.3 %collective-permute-done.28 = bf16[528,128]{1,0:T(8,128)(2,1)S(1)} collective-permute-done((bf16[528,128]{1,0:T(8,128)(2,1)S(1)}, bf16[528,128]{1,0:T(8,128)(2,1)S(1)}, u32[]{:S(2)}, u32[]{:S(2)}) %collective-permute-start.28) | collective-permute-done | bytes 135200 | tf_op jit(solution)/shard_map/ppermute | solution.py:48
  64.8 1.2 %collective-permute-start.29 = (bf16[1,2,256,128]{3,2,1,0:T(8,128)(2,1)S(1)}, bf16[1,2,256,128]{3,2,1,0:T(8,128)(2,1)S(1)}, u32[]{:S(2)}, u32[]{:S(2)}) collective-permute-start(bf16[1,2,256,128]{3,2,1,0:T(8,128)(2,1)S(1)} %bitcast.53), channel_id=1, source_target_pairs={{0,1},{1,0},{2,3},{3,2},{4,5},{5,4},{6,7},{7,6},{8,9},{9,8},{10,11... | collective-permute-start | bytes 393224 | tf_op jit(solution)/shard_map/ppermute | solution.py:48
  66.0 2.4 %collective-permute-start.31 = (bf16[1,2,256,128]{3,2,1,0:T(8,128)(2,1)S(1)}, bf16[1,2,256,128]{3,2,1,0:T(8,128)(2,1)S(1)}, u32[]{:S(2)}, u32[]{:S(2)}) collective-permute-start(bf16[1,2,256,128]{3,2,1,0:T(8,128)(2,1)S(1)} %bitcast.55), channel_id=1, source_target_pairs={{0,3},{1,2},{2,1},{3,0},{4,7},{5,6},{6,5},{7,4},{8,11},{9,10},{10,... | collective-permute-start | bytes 393224 | tf_op jit(solution)/shard_map/ppermute | solution.py:48
  68.3 2.3 %collective-permute-done.29 = bf16[1,2,256,128]{3,2,1,0:T(8,128)(2,1)S(1)} collective-permute-done((bf16[1,2,256,128]{3,2,1,0:T(8,128)(2,1)S(1)}, bf16[1,2,256,128]{3,2,1,0:T(8,128)(2,1)S(1)}, u32[]{:S(2)}, u32[]{:S(2)}) %collective-permute-start.29) | collective-permute-done | bytes 131104 | tf_op jit(solution)/shard_map/ppermute | solution.py:48
  70.7 0.3 collective-permute-done.30
  70.9 1.7 %collective-permute-done.31 = bf16[1,2,256,128]{3,2,1,0:T(8,128)(2,1)S(1)} collective-permute-done((bf16[1,2,256,128]{3,2,1,0:T(8,128)(2,1)S(1)}, bf16[1,2,256,128]{3,2,1,0:T(8,128)(2,1)S(1)}, u32[]{:S(2)}, u32[]{:S(2)}) %collective-permute-start.31) | collective-permute-done | bytes 131104 | tf_op jit(solution)/shard_map/ppermute | solution.py:48
  72.7 1.2 %finish.1 = (f32[256,512]{1,0:T(8,128)}, f32[512,256]{1,0:T(8,128)}, f32[1,1]{1,0:T(1,128)}) custom-call(bf16[2,256,128]{2,1,0:T(8,128)(2,1)S(1)} %bitcast.56, bf16[2,256,128]{2,1,0:T(8,128)(2,1)S(1)} %bitcast.61, bf16[2,256,128]{2,1,0:T(8,128)(2,1)S(1)} %bitcast.62, bf16[2,256,128]{2,1,0:T(8,128)(2,1)S(1)} %bitcast.63, f32[8,128]{1,0:T(8,128)S(1)} %fusion.10.refs_4_), custom_call_target="tpu_custom_call" | custom-call | flops 1000000 | bytes 1000 | tf_op jit(solution)/shard_map/finish/pallas_call | solution.py:34
  (73 shorter events, 0.7 us)
Async XLA Ops:
  0.6 1.1 %copy-start.8 = (bf16[256,512]{1,0:T(8,128)(2,1)S(1)}, bf16[256,512]{1,0:T(8,128)(2,1)}, u32[]{:S(2)}) copy-start(bf16[256,512]{1,0:T(8,128)(2,1)} %param.14) | copy-start | bytes 786436
  1.7 3.0 %copy-start.9 = (bf16[256,512]{1,0:T(8,128)(2,1)S(1)}, bf16[256,512]{1,0:T(8,128)(2,1)}, u32[]{:S(2)}) copy-start(bf16[256,512]{1,0:T(8,128)(2,1)} %param.15) | copy-start | bytes 786436
  1.8 12.9 %collective-permute-start.3 = (bf16[384,512]{1,0:T(8,128)(2,1)S(1)}, bf16[384,512]{1,0:T(8,128)(2,1)S(1)}, u32[]{:S(2)}, u32[]{:S(2)}) collective-permute-start(bf16[384,512]{1,0:T(8,128)(2,1)S(1)} %pad_maximum_fusion.1), channel_id=1, source_target_pairs={{0,16},{8,24},{16,0},{24,8},{1,17},{9,25},{17,1},{25,9},{2,18},{10... | collective-permute-start | bytes 1179656 | tf_op jit(solution)/shard_map/ppermute | solution.py:48
  4.8 1.0 %copy-start = (bf16[1,128,1024]{2,1,0:T(8,128)(2,1)S(1)}, bf16[1,128,1024]{2,1,0:T(8,128)(2,1)}, u32[]{:S(2)}) copy-start(bf16[1,128,1024]{2,1,0:T(8,128)(2,1)} %x_ref.3) | copy-start | bytes 786436
  4.8 5.7 %copy-start.10 = (bf16[512,256]{1,0:T(8,128)(2,1)S(1)}, bf16[512,256]{1,0:T(8,128)(2,1)}, u32[]{:S(2)}) copy-start(bf16[512,256]{1,0:T(8,128)(2,1)} %param.17) | copy-start | bytes 786436
  4.8 5.8 %copy-start.11 = (bf16[256,512]{1,0:T(8,128)(2,1)S(1)}, bf16[256,512]{1,0:T(8,128)(2,1)}, u32[]{:S(2)}) copy-start(bf16[256,512]{1,0:T(8,128)(2,1)} %param.16) | copy-start | bytes 786436
  4.9 17.6 %collective-permute-start.2 = (bf16[512,512]{1,0:T(8,128)(2,1)S(1)}, bf16[512,512]{1,0:T(8,128)(2,1)S(1)}, u32[]{:S(2)}, u32[]{:S(2)}) collective-permute-start(bf16[512,512]{1,0:T(8,128)(2,1)S(1)} %constant_dynamic-update-slice_fusion.refs_0_), channel_id=1, source_target_pairs={{0,8},{8,0},{16,24},{24,16},{1,9},{9,1},{17,25},{25,17},{2,10},{10... | collective-permute-start | bytes 1572872 | tf_op jit(solution)/shard_map/ppermute | solution.py:48
  5.7 14.2 %collective-permute-start = (bf16[1,128,1024]{2,1,0:T(8,128)(2,1)S(1)}, bf16[1,128,1024]{2,1,0:T(8,128)(2,1)S(1)}, u32[]{:S(2)}, u32[]{:S(2)}) collective-permute-start(bf16[1,128,1024]{2,1,0:T(8,128)(2,1)S(1)} %copy-done), channel_id=1, source_target_pairs={{0,1},{1,2},{2,3},{3,4},{4,5},{5,6},{6,7},{8,9},{9,10},{10,11},{11... | collective-permute-start | bytes 786440 | tf_op jit(solution)/shard_map/ppermute | solution.py:303
  9.2 10.8 %collective-permute-start.1 = (bf16[1,128,1024]{2,1,0:T(8,128)(2,1)S(1)}, bf16[1,128,1024]{2,1,0:T(8,128)(2,1)S(1)}, u32[]{:S(2)}, u32[]{:S(2)}) collective-permute-start(bf16[1,128,1024]{2,1,0:T(8,128)(2,1)S(1)} %copy-done), channel_id=1, source_target_pairs={{1,0},{2,1},{3,2},{4,3},{5,4},{6,5},{7,6},{9,8},{10,9},{11,10},{12... | collective-permute-start | bytes 786440 | tf_op jit(solution)/shard_map/ppermute | solution.py:304
  10.7 16.2 %collective-permute-start.9 = (bf16[512,512]{1,0:T(8,128)(2,1)S(1)}, bf16[512,512]{1,0:T(8,128)(2,1)S(1)}, u32[]{:S(2)}, u32[]{:S(2)}) collective-permute-start(bf16[512,512]{1,0:T(8,128)(2,1)S(1)} %pad_maximum_fusion.refs_0_), channel_id=1, source_target_pairs={{0,16},{8,24},{16,0},{24,8},{1,17},{9,25},{17,1},{25,9},{2,18},{10... | collective-permute-start | bytes 1572872 | tf_op jit(solution)/shard_map/ppermute | solution.py:48
  14.7 5.3 %copy-start.2 = (f32[1024]{0:T(1024)S(1)}, f32[1024]{0:T(1024)}, u32[]{:S(2)}) copy-start(f32[1024]{0:T(1024)} %param.13) | copy-start | bytes 12292
  14.7 5.3 %copy-start.1 = (s32[1024]{0:T(1024)S(1)}, s32[1024]{0:T(1024)}, u32[]{:S(2)}) copy-start(s32[1024]{0:T(1024)} %param.21) | copy-start | bytes 12292
  14.7 7.8 %collective-permute-start.4 = (bf16[128,512]{1,0:T(8,128)(2,1)S(1)}, bf16[128,512]{1,0:T(8,128)(2,1)S(1)}, u32[]{:S(2)}, u32[]{:S(2)}) collective-permute-start(bf16[128,512]{1,0:T(8,128)(2,1)S(1)} %slice.124.refs_3_), channel_id=1, source_target_pairs={{0,2},{1,3},{2,0},{3,1},{4,6},{5,7},{6,4},{7,5},{8,10},{9,11},{10,... | collective-permute-start | bytes 393224 | tf_op jit(solution)/shard_map/ppermute | solution.py:48
  20.0 0.7 copy-start.5
  22.5 1.4 %collective-permute-start.7 = (bf16[128,512]{1,0:T(8,128)(2,1)S(1)}, bf16[128,512]{1,0:T(8,128)(2,1)S(1)}, u32[]{:S(2)}, u32[]{:S(2)}) collective-permute-start(bf16[128,512]{1,0:T(8,128)(2,1)S(1)} %get-tuple-element.95), channel_id=1, source_target_pairs={{0,8},{8,0},{16,24},{24,16},{1,9},{9,1},{17,25},{25,17},{2,10},{10... | collective-permute-start | bytes 393224 | tf_op jit(solution)/shard_map/ppermute | solution.py:48
  22.6 2.0 %copy-start.3 = (s32[1,9]{1,0:T(1,128)S(1)}, s32[1,9]{1,0:T(1,128)}, u32[]{:S(2)}) copy-start(s32[1,9]{1,0:T(1,128)} %refs_9_.1) | copy-start | bytes 112
  22.6 2.0 %copy-start.4 = (s32[1,9]{1,0:T(1,128)S(1)}, s32[1,9]{1,0:T(1,128)}, u32[]{:S(2)}) copy-start(s32[1,9]{1,0:T(1,128)} %refs_10_.1) | copy-start | bytes 112
  22.6 1.5 %collective-permute-start.8 = (bf16[128,512]{1,0:T(8,128)(2,1)S(1)}, bf16[128,512]{1,0:T(8,128)(2,1)S(1)}, u32[]{:S(2)}, u32[]{:S(2)}) collective-permute-start(bf16[128,512]{1,0:T(8,128)(2,1)S(1)} %get-tuple-element.94), channel_id=1, source_target_pairs={{0,8},{8,0},{16,24},{24,16},{1,9},{9,1},{17,25},{25,17},{2,10},{10... | collective-permute-start | bytes 393224 | tf_op jit(solution)/shard_map/ppermute | solution.py:48
  23.1 1.3 %collective-permute-start.5 = (bf16[128,512]{1,0:T(8,128)(2,1)S(1)}, bf16[128,512]{1,0:T(8,128)(2,1)S(1)}, u32[]{:S(2)}, u32[]{:S(2)}) collective-permute-start(bf16[128,512]{1,0:T(8,128)(2,1)S(1)} %slice.124.refs_3_), channel_id=1, source_target_pairs={{0,8},{8,0},{16,24},{24,16},{1,9},{9,1},{17,25},{25,17},{2,10},{10... | collective-permute-start | bytes 393224 | tf_op jit(solution)/shard_map/ppermute | solution.py:48
  23.2 1.4 %collective-permute-start.6 = (bf16[128,512]{1,0:T(8,128)(2,1)S(1)}, bf16[128,512]{1,0:T(8,128)(2,1)S(1)}, u32[]{:S(2)}, u32[]{:S(2)}) collective-permute-start(bf16[128,512]{1,0:T(8,128)(2,1)S(1)} %collective-permute-done.4.refs_4_), channel_id=1, source_target_pairs={{0,8},{8,0},{16,24},{24,16},{1,9},{9,1},{17,25},{25,17},{2,10},{10... | collective-permute-start | bytes 393224 | tf_op jit(solution)/shard_map/ppermute | solution.py:48
  26.9 1.6 %collective-permute-start.10 = (bf16[256,512]{1,0:T(8,128)(2,1)S(1)}, bf16[256,512]{1,0:T(8,128)(2,1)S(1)}, u32[]{:S(2)}, u32[]{:S(2)}) collective-permute-start(bf16[256,512]{1,0:T(8,128)(2,1)S(1)} %get-tuple-element.93), channel_id=1, source_target_pairs={{0,8},{8,0},{16,24},{24,16},{1,9},{9,1},{17,25},{25,17},{2,10},{10... | collective-permute-start | bytes 786440 | tf_op jit(solution)/shard_map/ppermute | solution.py:48
  27.4 1.6 %collective-permute-start.11 = (bf16[256,512]{1,0:T(8,128)(2,1)S(1)}, bf16[256,512]{1,0:T(8,128)(2,1)S(1)}, u32[]{:S(2)}, u32[]{:S(2)}) collective-permute-start(bf16[256,512]{1,0:T(8,128)(2,1)S(1)} %get-tuple-element.91.refs_2_), channel_id=1, source_target_pairs={{0,8},{8,0},{16,24},{24,16},{1,9},{9,1},{17,25},{25,17},{2,10},{10... | collective-permute-start | bytes 786440 | tf_op jit(solution)/shard_map/ppermute | solution.py:48
  27.6 2.9 %collective-permute-start.12 = (bf16[256,512]{1,0:T(8,128)(2,1)S(1)}, bf16[256,512]{1,0:T(8,128)(2,1)S(1)}, u32[]{:S(2)}, u32[]{:S(2)}) collective-permute-start(bf16[256,512]{1,0:T(8,128)(2,1)S(1)} %get-tuple-element.92), channel_id=1, source_target_pairs={{0,8},{8,0},{16,24},{24,16},{1,9},{9,1},{17,25},{25,17},{2,10},{10... | collective-permute-start | bytes 786440 | tf_op jit(solution)/shard_map/ppermute | solution.py:48
  27.9 2.6 %copy-start.6 = (bf16[1024,128]{1,0:T(8,128)(2,1)S(1)}, bf16[1024,128]{1,0:T(8,128)(2,1)}, u32[]{:S(2)}) copy-start(bf16[1024,128]{1,0:T(8,128)(2,1)} %read_ref.3) | copy-start | bytes 786436
  27.9 2.6 %collective-permute-start.13 = (bf16[256,512]{1,0:T(8,128)(2,1)S(1)}, bf16[256,512]{1,0:T(8,128)(2,1)S(1)}, u32[]{:S(2)}, u32[]{:S(2)}) collective-permute-start(bf16[256,512]{1,0:T(8,128)(2,1)S(1)} %get-tuple-element.90.refs_2_), channel_id=1, source_target_pairs={{0,8},{8,0},{16,24},{24,16},{1,9},{9,1},{17,25},{25,17},{2,10},{10... | collective-permute-start | bytes 786440 | tf_op jit(solution)/shard_map/ppermute | solution.py:48
  28.1 8.8 %collective-permute-start.17 = (bf16[512,384]{1,0:T(8,128)(2,1)S(1)}, bf16[512,384]{1,0:T(8,128)(2,1)S(1)}, u32[]{:S(2)}, u32[]{:S(2)}) collective-permute-start(bf16[512,384]{1,0:T(8,128)(2,1)S(1)} %get-tuple-element.57), channel_id=1, source_target_pairs={{0,8},{8,0},{16,24},{24,16},{1,9},{9,1},{17,25},{25,17},{2,10},{10... | collective-permute-start | bytes 1179656 | tf_op jit(solution)/shard_map/ppermute | solution.py:48
  30.5 6.4 %copy-start.7 = (f32[128,128]{1,0:T(8,128)S(1)}, f32[128,128]{1,0:T(8,128)}, u32[]{:S(2)}) copy-start(f32[128,128]{1,0:T(8,128)} %refs_5_.1) | copy-start | bytes 196612
  31.2 4.3 %collective-permute-start.14 = (bf16[128,128]{1,0:T(8,128)(2,1)S(1)}, bf16[128,128]{1,0:T(8,128)(2,1)S(1)}, u32[]{:S(2)}, u32[]{:S(2)}) collective-permute-start(bf16[128,128]{1,0:T(8,128)(2,1)S(1)} %get-tuple-element.59.refs_0_), channel_id=1, source_target_pairs={{0,16},{8,24},{16,0},{24,8},{1,17},{9,25},{17,1},{25,9},{2,18},{10... | collective-permute-start | bytes 98312 | tf_op jit(solution)/shard_map/ppermute | solution.py:48
  32.3 6.2 %collective-permute-start.18 = (bf16[128,512]{1,0:T(8,128)(2,1)S(1)}, bf16[128,512]{1,0:T(8,128)(2,1)S(1)}, u32[]{:S(2)}, u32[]{:S(2)}) collective-permute-start(bf16[128,512]{1,0:T(8,128)(2,1)S(1)} %attend.1.att_ref.refs_0_), channel_id=1, source_target_pairs={{0,16},{8,24},{16,0},{24,8},{1,17},{9,25},{17,1},{25,9},{2,18},{10... | collective-permute-start | bytes 393224 | tf_op jit(solution)/shard_map/ppermute | solution.py:48
  35.5 1.2 %collective-permute-start.15 = (bf16[128,128]{1,0:T(8,128)(2,1)S(1)}, bf16[128,128]{1,0:T(8,128)(2,1)S(1)}, u32[]{:S(2)}, u32[]{:S(2)}) collective-permute-start(bf16[128,128]{1,0:T(8,128)(2,1)S(1)} %get-tuple-element.59.refs_0_), channel_id=1, source_target_pairs={{0,8},{8,0},{16,24},{24,16},{1,9},{9,1},{17,25},{25,17},{2,10},{10... | collective-permute-start | bytes 98312 | tf_op jit(solution)/shard_map/ppermute | solution.py:48
  35.5 1.4 %collective-permute-start.16 = (bf16[128,128]{1,0:T(8,128)(2,1)S(1)}, bf16[128,128]{1,0:T(8,128)(2,1)S(1)}, u32[]{:S(2)}, u32[]{:S(2)}) collective-permute-start(bf16[128,128]{1,0:T(8,128)(2,1)S(1)} %collective-permute-done.14.refs_2_), channel_id=1, source_target_pairs={{0,8},{8,0},{16,24},{24,16},{1,9},{9,1},{17,25},{25,17},{2,10},{10... | collective-permute-start | bytes 98312 | tf_op jit(solution)/shard_map/ppermute | solution.py:48
  38.4 1.8 %collective-permute-start.19 = (bf16[400,512]{1,0:T(8,128)(2,1)S(1)}, bf16[400,512]{1,0:T(8,128)(2,1)S(1)}, u32[]{:S(2)}, u32[]{:S(2)}) collective-permute-start(bf16[400,512]{1,0:T(8,128)(2,1)S(1)} %get-tuple-element.67.own_con), channel_id=1, source_target_pairs={{0,8},{8,0},{16,24},{24,16},{1,9},{9,1},{17,25},{25,17},{2,10},{10... | collective-permute-start | bytes 1228808 | tf_op jit(solution)/shard_map/ppermute | solution.py:48
  38.9 5.8 %collective-permute-start.23 = (bf16[128,512]{1,0:T(8,128)(2,1)S(1)}, bf16[128,512]{1,0:T(8,128)(2,1)S(1)}, u32[]{:S(2)}, u32[]{:S(2)}) collective-permute-start(bf16[128,512]{1,0:T(8,128)(2,1)S(1)} %attend.1.att_ref.refs_0_), channel_id=1, source_target_pairs={{0,8},{8,0},{16,24},{24,16},{1,9},{9,1},{17,25},{25,17},{2,10},{10... | collective-permute-start | bytes 393224 | tf_op jit(solution)/shard_map/ppermute | solution.py:48
  39.0 5.6 %collective-permute-start.24 = (bf16[128,512]{1,0:T(8,128)(2,1)S(1)}, bf16[128,512]{1,0:T(8,128)(2,1)S(1)}, u32[]{:S(2)}, u32[]{:S(2)}) collective-permute-start(bf16[128,512]{1,0:T(8,128)(2,1)S(1)} %collective-permute-done.18.refs_2_), channel_id=1, source_target_pairs={{0,8},{8,0},{16,24},{24,16},{1,9},{9,1},{17,25},{25,17},{2,10},{10... | collective-permute-start | bytes 393224 | tf_op jit(solution)/shard_map/ppermute | solution.py:48
  41.1 6.5 %collective-permute-start.20 = (bf16[528,128]{1,0:T(8,128)(2,1)S(1)}, bf16[528,128]{1,0:T(8,128)(2,1)S(1)}, u32[]{:S(2)}, u32[]{:S(2)}) collective-permute-start(bf16[528,128]{1,0:T(8,128)(2,1)S(1)} %get-tuple-element.98), channel_id=1, source_target_pairs={{0,16},{1,17},{2,18},{3,19},{4,20},{5,21},{6,22},{7,23},{8,24},{9,... | collective-permute-start | bytes 405512 | tf_op jit(solution)/shard_map/ppermute | solution.py:452
  42.1 7.4 %collective-permute-start.21 = (bf16[528,128]{1,0:T(8,128)(2,1)S(1)}, bf16[528,128]{1,0:T(8,128)(2,1)S(1)}, u32[]{:S(2)}, u32[]{:S(2)}) collective-permute-start(bf16[528,128]{1,0:T(8,128)(2,1)S(1)} %get-tuple-element.96), channel_id=1, source_target_pairs={{0,1},{1,0},{2,3},{3,2},{4,5},{5,4},{6,7},{7,6},{8,9},{9,8},{10,11... | collective-permute-start | bytes 405512 | tf_op jit(solution)/shard_map/ppermute | solution.py:452
  43.5 7.2 %collective-permute-start.22 = (bf16[528,128]{1,0:T(8,128)(2,1)S(1)}, bf16[528,128]{1,0:T(8,128)(2,1)S(1)}, u32[]{:S(2)}, u32[]{:S(2)}) collective-permute-start(bf16[528,128]{1,0:T(8,128)(2,1)S(1)} %get-tuple-element.97), channel_id=1, source_target_pairs={{0,17},{1,16},{2,19},{3,18},{4,21},{5,20},{6,23},{7,22},{8,25},{9,... | collective-permute-start | bytes 405512 | tf_op jit(solution)/shard_map/ppermute | solution.py:452
  45.1 5.7 %collective-permute-start.25 = (bf16[512,128]{1,0:T(8,128)(2,1)S(1)}, bf16[512,128]{1,0:T(8,128)(2,1)S(1)}, u32[]{:S(2)}, u32[]{:S(2)}) collective-permute-start(bf16[512,128]{1,0:T(8,128)(2,1)S(1)} %bitcast.75), channel_id=1, source_target_pairs={{0,2},{1,3},{2,0},{3,1},{4,6},{5,7},{6,4},{7,5},{8,10},{9,11},{10,... | collective-permute-start | bytes 393224 | tf_op jit(solution)/shard_map/ppermute | solution.py:48
  51.0 6.7 %collective-permute-start.26 = (bf16[272,128]{1,0:T(8,128)(2,1)S(1)}, bf16[272,128]{1,0:T(8,128)(2,1)S(1)}, u32[]{:S(2)}, u32[]{:S(2)}) collective-permute-start(bf16[272,128]{1,0:T(8,128)(2,1)S(1)} %pad_maximum_fusion.9), channel_id=1, source_target_pairs={{0,2},{1,3},{2,0},{3,1},{4,6},{5,7},{6,4},{7,5},{8,10},{9,11},{10,... | collective-permute-start | bytes 208904 | tf_op jit(solution)/shard_map/ppermute | solution.py:48
  53.3 4.3 %collective-permute-start.27 = (bf16[256,128]{1,0:T(8,128)(2,1)S(1)}, bf16[256,128]{1,0:T(8,128)(2,1)S(1)}, u32[]{:S(2)}, u32[]{:S(2)}) collective-permute-start(bf16[256,128]{1,0:T(8,128)(2,1)S(1)} %bitcast.76), channel_id=1, source_target_pairs={{0,1},{1,0},{2,3},{3,2},{4,5},{5,4},{6,7},{7,6},{8,9},{9,8},{10,11... | collective-permute-start | bytes 196616 | tf_op jit(solution)/shard_map/ppermute | solution.py:48
  57.8 7.0 %collective-permute-start.28 = (bf16[528,128]{1,0:T(8,128)(2,1)S(1)}, bf16[528,128]{1,0:T(8,128)(2,1)S(1)}, u32[]{:S(2)}, u32[]{:S(2)}) collective-permute-start(bf16[528,128]{1,0:T(8,128)(2,1)S(1)} %pad_maximum_fusion.8), channel_id=1, source_target_pairs={{0,4},{1,5},{2,6},{3,7},{4,0},{5,1},{6,2},{7,3},{8,12},{9,13},{10,... | collective-permute-start | bytes 405512 | tf_op jit(solution)/shard_map/ppermute | solution.py:48
  64.8 5.9 %collective-permute-start.29 = (bf16[1,2,256,128]{3,2,1,0:T(8,128)(2,1)S(1)}, bf16[1,2,256,128]{3,2,1,0:T(8,128)(2,1)S(1)}, u32[]{:S(2)}, u32[]{:S(2)}) collective-permute-start(bf16[1,2,256,128]{3,2,1,0:T(8,128)(2,1)S(1)} %bitcast.53), channel_id=1, source_target_pairs={{0,1},{1,0},{2,3},{3,2},{4,5},{5,4},{6,7},{7,6},{8,9},{9,8},{10,11... | collective-permute-start | bytes 393224 | tf_op jit(solution)/shard_map/ppermute | solution.py:48
  66.0 5.0 %collective-permute-start.30 = (bf16[1,2,256,128]{3,2,1,0:T(8,128)(2,1)S(1)}, bf16[1,2,256,128]{3,2,1,0:T(8,128)(2,1)S(1)}, u32[]{:S(2)}, u32[]{:S(2)}) collective-permute-start(bf16[1,2,256,128]{3,2,1,0:T(8,128)(2,1)S(1)} %bitcast.54), channel_id=1, source_target_pairs={{0,2},{1,3},{2,0},{3,1},{4,6},{5,7},{6,4},{7,5},{8,10},{9,11},{10,... | collective-permute-start | bytes 393224 | tf_op jit(solution)/shard_map/ppermute | solution.py:48
  66.0 6.7 %collective-permute-start.31 = (bf16[1,2,256,128]{3,2,1,0:T(8,128)(2,1)S(1)}, bf16[1,2,256,128]{3,2,1,0:T(8,128)(2,1)S(1)}, u32[]{:S(2)}, u32[]{:S(2)}) collective-permute-start(bf16[1,2,256,128]{3,2,1,0:T(8,128)(2,1)S(1)} %bitcast.55), channel_id=1, source_target_pairs={{0,3},{1,2},{2,1},{3,0},{4,7},{5,6},{6,5},{7,4},{8,11},{9,10},{10,... | collective-permute-start | bytes 393224 | tf_op jit(solution)/shard_map/ppermute | solution.py:48

commit v8 on v7

--- a/solution.py
+++ b/solution.py
@@ -48,11 +48,31 @@
     return lax.ppermute(value, axis, [(i, i ^ mask) for i in range(size)])
 
 
+def counts_of(nb_ref, nm_ref, position):
+    counts = []
+    for d in (-1, 0, 1):
+        total = jnp.int32(0)
+        for s in range(NB):
+            hit = (nb_ref[0, s] == position + d) & (nm_ref[0, s] > 0)
+            total = total + jnp.where(hit, 1, 0)
+        counts.append(total.astype(F32))
+    return counts
+
+
 def normed_body(
-    n_ens, dsh, x_ref, up_ref, down_ref, gain_ref, pw_ref, mask_ref, n_ref, keep_ref, send_ref, lw_ref, turned_ref
+    n_ens, dsh, x_ref, up_ref, down_ref, gain_ref, pw_ref, mask_ref, nb_ref, nm_ref, *refs
 ):
-    core = lax.axis_index("ens") % 2
-    live = jnp.where(mask_ref[pl.ds(lax.axis_index("pix"), 1), :] > 0, 1.0, 0.0)
+    n_ref, keep_ref, send_ref, lw_ref, rows_ref, turned_ref = refs
+    core, position = lax.axis_index("ens") % 2, lax.axis_index("pix")
+    counts = counts_of(nb_ref, nm_ref, position)
+    for i, d in enumerate((-1, 0, 1)):
+        row = jnp.clip(position + d, 0, mask_ref.shape[0] - 1)
+        named = jnp.full((1, TILE), counts[i], F32)
+        cols = slice(i * TILE, (i + 1) * TILE)
+        rows_ref[0:1, cols] = jnp.where(mask_ref[pl.ds(row, 1), :] > 0, named, 0.0)
+        rows_ref[1:2, cols] = named
+    rows_ref[2:, :] = jnp.zeros((6, 3 * TILE), F32)
+    live = jnp.where(mask_ref[pl.ds(position, 1), :] > 0, 1.0, 0.0)
     lw_ref[...] = jnp.broadcast_to(pw_ref[...] * live, (LANES, TILE)).T
     gain = gain_ref[...]
     for i, ref in enumerate((up_ref, x_ref, down_ref)):
@@ -67,17 +87,6 @@
         send_ref[b * dsh : (b + 1) * dsh, :] = turned_ref[pl.ds(theirs, dsh), :]
 
 
-def counts_of(nb_ref, nm_ref, position):
-    counts = []
-    for d in (-1, 0, 1):
-        total = jnp.int32(0)
-        for s in range(NB):
-            hit = (nb_ref[0, s] == position + d) & (nm_ref[0, s] > 0)
-            total = total + jnp.where(hit, 1, 0)
-        counts.append(total.astype(F32))
-    return counts
-
-
 def assembled(refs, layout, scratch, dsh):
     me, side = lax.axis_index("ens"), (lax.axis_index("pix") // 2) % 2
     for which, first, rows, j, place in layout:
@@ -87,46 +96,37 @@
     return scratch[...]
 
 
-def weights_body(q_layout, k_layout, dsh, n_ref, mask_ref, nb_ref, nm_ref, *refs):
+def weights_body(q_layout, k_layout, dsh, n_ref, rows_ref, *refs):
     pieces, (w_ref, scratch) = refs[:-2], refs[-2:]
-    position = lax.axis_index("pix")
-    n_pix = mask_ref.shape[0]
-    counts = counts_of(nb_ref, nm_ref, position)
-    lanes = []
-    for i, d in enumerate((-1, 0, 1)):
-        row = jnp.clip(position + d, 0, n_pix - 1)
-        lanes.append(jnp.where(mask_ref[pl.ds(row, 1), :] > 0, 1.0, 0.0) * counts[i])
-    times = jnp.concatenate(lanes, axis=1)
+    times = rows_ref[0:1, :]
     bias = jnp.where(times > 0, 0.0, -1e30)
     queries = dot(n_ref[TILE : 2 * TILE, :], assembled(pieces, q_layout, scratch, dsh)).astype(BF16)
     keys = dot(n_ref[...], assembled(pieces, k_layout, scratch, dsh)).astype(BF16)
     lane = lax.broadcasted_iota(jnp.int32, (TILE, LANES), 1)
-    for h in range(HEADS):
-        cols = slice(h // 2 * LANES, (h // 2 + 1) * LANES)
-        own = (lane < HD) if h % 2 == 0 else (lane >= HD)
-        query = jnp.where(own, queries[:, cols], jnp.zeros((), BF16))
-        scores = dot(query, keys[:, cols], NT) * HD ** (-0.5) + bias
+    zero = jnp.zeros((), BF16)
+    for g in range(HEADS // 2):
+        cols = slice(g * LANES, (g + 1) * LANES)
+        pair = queries[:, cols]
+        pair = jnp.concatenate([jnp.where(lane < HD, pair, zero), jnp.where(lane < HD, zero, pair)], axis=0)
+        scores = dot(pair, keys[:, cols], NT) * HD ** (-0.5) + bias
         top = jnp.max(scores, axis=-1, keepdims=True)
         expos = jnp.exp(scores - top)
         total = jnp.sum(expos * times, axis=-1, keepdims=True)
-        w_ref[h] = (expos / total).astype(BF16)
-
-
-def attend_body(layout, dsh, n_ref, w_ref, nb_ref, nm_ref, *refs):
+        w_ref[2 * g : 2 * g + 2] = (expos / total).astype(BF16).reshape(2, TILE, 3 * TILE)
+
+
+def attend_body(layout, dsh, n_ref, w_ref, rows_ref, *refs):
     pieces, (att_ref, scratch) = refs[:-2], refs[-2:]
-    counts = counts_of(nb_ref, nm_ref, lax.axis_index("pix"))
     values = dot(n_ref[...], assembled(pieces, layout, scratch, dsh)).astype(BF16)
     lane = lax.broadcasted_iota(jnp.int32, (TILE, LANES), 1)
     for g in range(HEADS // 2):
         cols = slice(g * LANES, (g + 1) * LANES)
-        halves = []
-        for h in (2 * g, 2 * g + 1):
-            total = jnp.zeros((TILE, LANES), F32)
-            for i in range(3):
-                rows = slice(i * TILE, (i + 1) * TILE)
-                total = total + counts[i] * dot(w_ref[h, :, rows], values[rows, cols])
-            halves.append(total)
-        att_ref[:, cols] = jnp.where(lane < HD, halves[0], halves[1]).astype(BF16)
+        pair = w_ref[2 * g : 2 * g + 2].reshape(2 * TILE, 3 * TILE)
+        total = jnp.zeros((2 * TILE, LANES), F32)
+        for i in range(3):
+            rows = slice(i * TILE, (i + 1) * TILE)
+            total = total + rows_ref[1:2, rows] * dot(pair[:, rows], values[rows, cols])
+        att_ref[:, cols] = jnp.where(lane < HD, total[:TILE], total[TILE:]).astype(BF16)
 
 
 def forecast_body(layout, dsh, x_ref, att_ref, read_ref, *refs):
@@ -142,9 +142,7 @@
 
 def backward_body(n_ens, factor, *refs):
     f_refs = refs[:n_ens]
-    wo_ref, target_ref, lw_ref, read_ref, w_ref, nb_ref, nm_ref, gf_ref, con_ref = refs[n_ens:]
-    position = lax.axis_index("pix")
-    counts = counts_of(nb_ref, nm_ref, position)
+    wo_ref, target_ref, lw_ref, read_ref, w_ref, rows_ref, gf_ref, con_ref = refs[n_ens:]
     lw = lw_ref[...]
     target = target_ref[...]
     fc = [ref[...].astype(F32) for ref in f_refs]
@@ -173,11 +171,11 @@
     for g in range(HEADS // 2):
         cols = slice(g * LANES, (g + 1) * LANES)
         pair = grad_att[:, cols]
-        both = dot(w_ref[2 * g], jnp.where(lane < HD, pair, zero), TN)
-        both = both + dot(w_ref[2 * g + 1], jnp.where(lane < HD, zero, pair), TN)
+        pair = jnp.concatenate([jnp.where(lane < HD, pair, zero), jnp.where(lane < HD, zero, pair)], axis=0)
+        both = dot(w_ref[2 * g : 2 * g + 2].reshape(2 * TILE, 3 * TILE), pair, TN)
         for i in range(3):
             rows = slice(i * TILE, (i + 1) * TILE)
-            con_ref[rows, cols] = (both[rows] * counts[i]).astype(BF16)
+            con_ref[rows, cols] = (both[rows] * rows_ref[1:2, rows]).astype(BF16)
 
 
 def value_body(blocks, dsh, rows, keep_ref, sib_ref, own_con, sib_con, v_ref, loss_ref):
@@ -305,11 +303,11 @@
     w_qk = jnp.concatenate([w_query, w_key])
     qk_near = xor_permute(w_qk, "ens", 1)
     turned = ((d_model // 2, 3 * TILE), BF16)
-    normed, turned_keep, turned_send, lw = call(
+    normed, turned_keep, turned_send, lw, key_rows = call(
         functools.partial(normed_body, n_ens, dsh),
-        [((3 * TILE, d_model), BF16), turned, turned, ((TILE, LANES), F32)],
+        [((3 * TILE, d_model), BF16), turned, turned, ((TILE, LANES), F32), ((8, 3 * TILE), F32)],
         [("v", sample_layer_feed), ("v", up), ("v", down), ("v", gain.reshape(1, -1))]
-        + [("v", pixel_weight.reshape(1, TILE)), ("v", mask_rows)],
+        + [("v", pixel_weight.reshape(1, TILE)), ("v", mask_rows), ("s", neighbours), ("s", neighbour_mask)],
         10**7,
         "normed",
         scratch=[pltpu.VMEM((d_model, 3 * TILE), BF16)],
@@ -341,7 +339,7 @@
     (weights,) = call(
         functools.partial(weights_body, q_layout, k_layout, dsh),
         [((HEADS, TILE, 3 * TILE), BF16)],
-        [("v", normed), ("v", mask_rows), ("s", neighbours), ("s", neighbour_mask)]
+        [("v", normed), ("v", key_rows)]
         + [("v", a) for a in [w_qk, qk_near] + parts],
         10**3,
         "weights",
@@ -355,7 +353,7 @@
     (attended,) = call(
         functools.partial(attend_body, layout(0), dsh),
         [((TILE, inner), BF16)],
-        [("v", normed), ("v", weights), ("s", neighbours), ("s", neighbour_mask)]
+        [("v", normed), ("v", weights), ("v", key_rows)]
         + [("v", a) for a in (w_vo, vo_near[0], vo_far[0], vo_cross[0])],
         10**9,
         "attend",
@@ -380,7 +378,7 @@
         [((n_ens * TILE, LANES), BF16), ((3 * TILE + 16, inner), BF16)],
         [("v", a) for a in forecasts + [w_out_full]]
         + [("v", target), ("v", lw), ("v", readout_matrix)]
-        + [("v", weights), ("s", neighbours), ("s", neighbour_mask)],
+        + [("v", weights), ("v", key_rows)],
         10**9,
         "backward",
     )

time: 74.1 us -> 72.9 us (0.984)
  Pallas kernels: 8.86 us -> 7.67 us
    pallas_call x8, Pallas kernels: 8.86 us -> 7.67 us  [call(): pl.pallas_call(body, out_shape=[jax.ShapeDtypeStruct(s, d) for s, d in ou...]
  transfers between devices with their start and end apart: 32 -> 32, of which waited for: 20 -> 21; matrix products, arithmetic and copies ran while one was open for 1% -> 1% of each run, Pallas kernels for 10% -> 9%
where the time goes in v8:
time: 72.9 us; the launch traced here: 72.7 us
  starting transfers between devices  31.6 us (43%)
  waiting for transfers between devices  28.9 us (40%)
  Pallas kernels  7.67 us (11%)
  local copies, waits for them, and re-layouts  1.99 us (3%)
  other arithmetic  1.39 us (2%)
  between operations  1.16 us (2%)
    ppermute x27, starting transfers between devices, xor_permute(): return lax.ppermute(value, axis, [(i, i ^ mask) for i in range(size)])  23.3 us
    ppermute x27, waiting for transfers between devices, xor_permute(): return lax.ppermute(value, axis, [(i, i ^ mask) for i in range(size)])  21.6 us
    pallas_call x8, Pallas kernels, call(): pl.pallas_call(body, out_shape=[jax.ShapeDtypeStruct(s, d) for s, d in ou...  7.67 us
    ppermute x1, waiting for transfers between devices, per_device(): lax.ppermute(sample_layer_feed, 'pix', [(i, i + 1) for i in range(n_pix -...  4.18 us
    ppermute x3, starting transfers between devices, per_device(): lax.ppermute(message, ('ens', 'pix'), pairs)  3.55 us
    ppermute x1, starting transfers between devices, per_device(): lax.ppermute(sample_layer_feed, 'pix', [(i, i + 1) for i in range(n_pix -...  3.43 us
    ppermute x3, waiting for transfers between devices, per_device(): lax.ppermute(message, ('ens', 'pix'), pairs)  3.11 us
    unnamed x26, local copies, waits for them, and re-layouts  1.68 us
  transfers between devices with their start and end apart: 32, of which 21 were waited for; matrix products, arithmetic and copies ran while one was open for 1% of the time, Pallas kernels for 9%

profile of v8, /device:TPU:0, one launch (start us, length us, event | category | flops | bytes accessed | tf_op | source)
XLA Modules:
  0.0 72.7 jit_solution(11018799069707854309)
XLA Ops:
  0.7 1.0 %slice_select_fusion = bf16[128,512]{1,0:T(8,128)(2,1)S(1)} fusion(bf16[256,512]{1,0:T(8,128)(2,1)} %param.15, pred[]{:T(512)S(6)} %eq.10), kind=kLoop, calls=%fused_computation.27 | loop fusion | flops 65536 | bytes 393217 | tf_op jit(solution)/shard_map/jit(_where)/select_n | solution.py:297
  1.8 3.0 %collective-permute-start.3 = (bf16[384,512]{1,0:T(8,128)(2,1)S(1)}, bf16[384,512]{1,0:T(8,128)(2,1)S(1)}, u32[]{:S(2)}, u32[]{:S(2)}) collective-permute-start(bf16[384,512]{1,0:T(8,128)(2,1)S(1)} %pad_maximum_fusion.1), channel_id=1, source_target_pairs={{0,16},{8,24},{16,0},{24,8},{1,17},{9,25},{17,1},{25,9},{2,18},{10... | collective-permute-start | bytes 1179656 | tf_op jit(solution)/shard_map/ppermute | solution.py:48
  4.9 0.1 collective-permute-start.2
  4.9 0.8 %copy-done = bf16[1,128,1024]{2,1,0:T(8,128)(2,1)S(1)} copy-done((bf16[1,128,1024]{2,1,0:T(8,128)(2,1)S(1)}, bf16[1,128,1024]{2,1,0:T(8,128)(2,1)}, u32[]{:S(2)}) %copy-start) | copy-done | bytes 262168
  5.7 3.4 %collective-permute-start = (bf16[1,128,1024]{2,1,0:T(8,128)(2,1)S(1)}, bf16[1,128,1024]{2,1,0:T(8,128)(2,1)S(1)}, u32[]{:S(2)}, u32[]{:S(2)}) collective-permute-start(bf16[1,128,1024]{2,1,0:T(8,128)(2,1)S(1)} %copy-done), channel_id=1, source_target_pairs={{0,1},{1,2},{2,3},{3,4},{4,5},{5,6},{6,7},{8,9},{9,10},{10,11},{11... | collective-permute-start | bytes 786440 | tf_op jit(solution)/shard_map/ppermute | solution.py:301
  9.2 1.3 %collective-permute-start.1 = (bf16[1,128,1024]{2,1,0:T(8,128)(2,1)S(1)}, bf16[1,128,1024]{2,1,0:T(8,128)(2,1)S(1)}, u32[]{:S(2)}, u32[]{:S(2)}) collective-permute-start(bf16[1,128,1024]{2,1,0:T(8,128)(2,1)S(1)} %copy-done), channel_id=1, source_target_pairs={{1,0},{2,1},{3,2},{4,3},{5,4},{6,5},{7,6},{9,8},{10,9},{11,10},{12... | collective-permute-start | bytes 786440 | tf_op jit(solution)/shard_map/ppermute | solution.py:302
  10.5 0.1 copy.17
  10.7 0.9 %collective-permute-start.9 = (bf16[512,512]{1,0:T(8,128)(2,1)S(1)}, bf16[512,512]{1,0:T(8,128)(2,1)S(1)}, u32[]{:S(2)}, u32[]{:S(2)}) collective-permute-start(bf16[512,512]{1,0:T(8,128)(2,1)S(1)} %pad_maximum_fusion.refs_0_), channel_id=1, source_target_pairs={{0,16},{8,24},{16,0},{24,8},{1,17},{9,25},{17,1},{25,9},{2,18},{10... | collective-permute-start | bytes 1572872 | tf_op jit(solution)/shard_map/ppermute | solution.py:48
  11.6 3.1 %collective-permute-done.3 = bf16[384,512]{1,0:T(8,128)(2,1)S(1)} collective-permute-done((bf16[384,512]{1,0:T(8,128)(2,1)S(1)}, bf16[384,512]{1,0:T(8,128)(2,1)S(1)}, u32[]{:S(2)}, u32[]{:S(2)}) %collective-permute-start.3) | collective-permute-done | bytes 393248 | tf_op jit(solution)/shard_map/ppermute | solution.py:48
  14.7 1.1 %collective-permute-start.4 = (bf16[128,512]{1,0:T(8,128)(2,1)S(1)}, bf16[128,512]{1,0:T(8,128)(2,1)S(1)}, u32[]{:S(2)}, u32[]{:S(2)}) collective-permute-start(bf16[128,512]{1,0:T(8,128)(2,1)S(1)} %slice.124.refs_3_), channel_id=1, source_target_pairs={{0,2},{1,3},{2,0},{3,1},{4,6},{5,7},{6,4},{7,5},{8,10},{9,11},{10,... | collective-permute-start | bytes 393224 | tf_op jit(solution)/shard_map/ppermute | solution.py:48
  15.8 4.2 %collective-permute-done.up_ref = bf16[1,128,1024]{2,1,0:T(8,128)(2,1)S(1)} collective-permute-done((bf16[1,128,1024]{2,1,0:T(8,128)(2,1)S(1)}, bf16[1,128,1024]{2,1,0:T(8,128)(2,1)S(1)}, u32[]{:S(2)}, u32[]{:S(2)}) %collective-permute-start) | collective-permute-done | bytes 262176 | tf_op jit(solution)/shard_map/ppermute | solution.py:301
  20.0 0.6 copy-done.3
  20.7 1.1 %normed.1 = (bf16[384,1024]{1,0:T(8,128)(2,1)S(1)}, bf16[512,384]{1,0:T(8,128)(2,1)S(1)}, bf16[512,384]{1,0:T(8,128)(2,1)S(1)}, f32[128,128]{1,0:T(8,128)S(1)}, f32[8,384]{1,0:T(8,128)S(1)}) custom-call(bf16[1,128,1024]{2,1,0:T(8,128)(2,1)S(1)} %copy-done, bf16[1,128,1024]{2,1,0:T(8,128)(2,1)S(1)} %collective-permute-done.up_ref, ...), custom_call_target="tpu_custom_call" | custom-call | flops 10000000 | bytes 10000 | tf_op jit(solution)/shard_map/normed/pallas_call | solution.py:34
  21.8 0.7 collective-permute-done.4.refs_4_
  22.5 0.1 collective-permute-start.7
  22.6 0.5 collective-permute-start.8
  23.1 0.1 collective-permute-start.5
  23.2 0.4 collective-permute-start.6
  23.6 0.3 collective-permute-done.7.refs_7_
  23.9 0.2 collective-permute-done.8.refs_8_
  24.1 0.3 collective-permute-done.5.refs_5_
  24.4 0.2 collective-permute-done.6.refs_6_
  24.6 1.6 %weights.1.w_ref.refs_8_ = bf16[8,128,384]{2,1,0:T(8,128)(2,1)S(1)} custom-call(bf16[384,1024]{1,0:T(8,128)(2,1)S(1)} %get-tuple-element.46.n_ref, f32[8,384]{1,0:T(8,128)S(1)} %get-tuple-element.47.rows_ref.refs_9_, bf16[512,512]{1,0:T(8,128)(2,1)S(1)} %constant_dynamic-update-slice_fusion.refs_0_, bf16[512,512]{1,0:T(8,128)(2,1)S(1)} %collective-permute-done.2.refs_1_, ...), custom_call_target="tpu_custom_call" | custom-call | flops 1000 | bytes 1 | tf_op jit(solution)/shard_map/weights/pallas_call | solution.py:34
  26.3 0.4 collective-permute-start.10
  26.7 0.3 collective-permute-start.11
  27.0 0.3 collective-permute-start.12
  27.3 0.2 collective-permute-start.13
  27.5 0.3 collective-permute-start.17
  27.8 0.1 collective-permute-done.10.refs_1_
  27.9 0.4 collective-permute-done.11.refs_3_
  28.3 0.9 %attend.1.att_ref.refs_0_ = bf16[128,512]{1,0:T(8,128)(2,1)S(1)} custom-call(bf16[384,1024]{1,0:T(8,128)(2,1)S(1)} %get-tuple-element.46.n_ref, bf16[8,128,384]{2,1,0:T(8,128)(2,1)S(1)} %weights.1.w_ref.refs_8_, f32[8,384]{1,0:T(8,128)S(1)} %get-tuple-element.47.rows_ref.refs_9_, bf16[512,512]{1,0:T(8,128)(2,1)S(1)} %pad_maximum_fusion.refs_0_, ...), custom_call_target="tpu_custom_call" | custom-call | flops 1000000000 | bytes 1000000 | tf_op jit(solution)/shard_map/attend/pallas_call | solution.py:34
  29.3 0.7 forecast.1
  30.0 1.0 %collective-permute-start.14 = (bf16[128,128]{1,0:T(8,128)(2,1)S(1)}, bf16[128,128]{1,0:T(8,128)(2,1)S(1)}, u32[]{:S(2)}, u32[]{:S(2)}) collective-permute-start(bf16[128,128]{1,0:T(8,128)(2,1)S(1)} %get-tuple-element.61.refs_0_), channel_id=1, source_target_pairs={{0,16},{8,24},{16,0},{24,8},{1,17},{9,25},{17,1},{25,9},{2,18},{10... | collective-permute-start | bytes 98312 | tf_op jit(solution)/shard_map/ppermute | solution.py:48
  31.1 1.0 %collective-permute-start.18 = (bf16[128,512]{1,0:T(8,128)(2,1)S(1)}, bf16[128,512]{1,0:T(8,128)(2,1)S(1)}, u32[]{:S(2)}, u32[]{:S(2)}) collective-permute-start(bf16[128,512]{1,0:T(8,128)(2,1)S(1)} %attend.1.att_ref.refs_0_), channel_id=1, source_target_pairs={{0,16},{8,24},{16,0},{24,8},{1,17},{9,25},{17,1},{25,9},{2,18},{10... | collective-permute-start | bytes 393224 | tf_op jit(solution)/shard_map/ppermute | solution.py:48
  32.1 2.2 %collective-permute-done.14.refs_2_ = bf16[128,128]{1,0:T(8,128)(2,1)S(1)} collective-permute-done((bf16[128,128]{1,0:T(8,128)(2,1)S(1)}, bf16[128,128]{1,0:T(8,128)(2,1)S(1)}, u32[]{:S(2)}, u32[]{:S(2)}) %collective-permute-start.14) | collective-permute-done | bytes 32800 | tf_op jit(solution)/shard_map/ppermute | solution.py:48
  34.3 0.5 collective-permute-start.16
  34.8 0.7 collective-permute-done.15.refs_1_
  35.5 0.2 collective-permute-done.16.refs_3_
  35.7 1.0 %backward.1 = (bf16[512,128]{1,0:T(8,128)(2,1)S(1)}, bf16[400,512]{1,0:T(8,128)(2,1)S(1)}) custom-call(bf16[128,128]{1,0:T(8,128)(2,1)S(1)} %get-tuple-element.61.refs_0_, bf16[128,128]{1,0:T(8,128)(2,1)S(1)} %collective-permute-done.15.refs_1_, bf16[128,128]{1,0:T(8,128)(2,1)S(1)} %collective-permute-done.14.refs_2_, ...), custom_call_target="tpu_custom_call" | custom-call | flops 1000000000 | bytes 1000000 | tf_op jit(solution)/shard_map/backward/pallas_call | solution.py:34
  36.7 0.1 collective-permute-done.18.refs_2_
  36.8 0.3 collective-permute-start.19
  37.1 0.2 collective-permute-start.23
  37.3 0.3 collective-permute-start.24
  37.6 0.9 %collective-permute-done.19.sib_con = bf16[400,512]{1,0:T(8,128)(2,1)S(1)} collective-permute-done((bf16[400,512]{1,0:T(8,128)(2,1)S(1)}, bf16[400,512]{1,0:T(8,128)(2,1)S(1)}, u32[]{:S(2)}, u32[]{:S(2)}) %collective-permute-start.19) | collective-permute-done | bytes 409632 | tf_op jit(solution)/shard_map/ppermute | solution.py:48
  38.5 0.7 value_term.1
  39.4 1.0 %collective-permute-start.20 = (bf16[528,128]{1,0:T(8,128)(2,1)S(1)}, bf16[528,128]{1,0:T(8,128)(2,1)S(1)}, u32[]{:S(2)}, u32[]{:S(2)}) collective-permute-start(bf16[528,128]{1,0:T(8,128)(2,1)S(1)} %get-tuple-element.100), channel_id=1, source_target_pairs={{0,16},{1,17},{2,18},{3,19},{4,20},{5,21},{6,22},{7,23},{8,24},{9,... | collective-permute-start | bytes 405512 | tf_op jit(solution)/shard_map/ppermute | solution.py:450
  40.4 2.0 %collective-permute-start.21 = (bf16[528,128]{1,0:T(8,128)(2,1)S(1)}, bf16[528,128]{1,0:T(8,128)(2,1)S(1)}, u32[]{:S(2)}, u32[]{:S(2)}) collective-permute-start(bf16[528,128]{1,0:T(8,128)(2,1)S(1)} %get-tuple-element.98), channel_id=1, source_target_pairs={{0,1},{1,0},{2,3},{3,2},{4,5},{5,4},{6,7},{7,6},{8,9},{9,8},{10,11... | collective-permute-start | bytes 405512 | tf_op jit(solution)/shard_map/ppermute | solution.py:450
  42.4 0.5 collective-permute-start.22
  42.9 0.4 output_term.1
  43.4 3.0 %collective-permute-start.25 = (bf16[512,128]{1,0:T(8,128)(2,1)S(1)}, bf16[512,128]{1,0:T(8,128)(2,1)S(1)}, u32[]{:S(2)}, u32[]{:S(2)}) collective-permute-start(bf16[512,128]{1,0:T(8,128)(2,1)S(1)} %bitcast.74), channel_id=1, source_target_pairs={{0,2},{1,3},{2,0},{3,1},{4,6},{5,7},{6,4},{7,5},{8,10},{9,11},{10,... | collective-permute-start | bytes 393224 | tf_op jit(solution)/shard_map/ppermute | solution.py:48
  46.5 1.9 %collective-permute-done.21 = bf16[528,128]{1,0:T(8,128)(2,1)S(1)} collective-permute-done((bf16[528,128]{1,0:T(8,128)(2,1)S(1)}, bf16[528,128]{1,0:T(8,128)(2,1)S(1)}, u32[]{:S(2)}, u32[]{:S(2)}) %collective-permute-start.21) | collective-permute-done | bytes 135200 | tf_op jit(solution)/shard_map/ppermute | solution.py:450
  48.3 1.2 %collective-permute-done.22 = bf16[528,128]{1,0:T(8,128)(2,1)S(1)} collective-permute-done((bf16[528,128]{1,0:T(8,128)(2,1)S(1)}, bf16[528,128]{1,0:T(8,128)(2,1)S(1)}, u32[]{:S(2)}, u32[]{:S(2)}) %collective-permute-start.22) | collective-permute-done | bytes 135200 | tf_op jit(solution)/shard_map/ppermute | solution.py:450
  49.6 0.1 fusion.1
  49.8 2.3 %collective-permute-start.26 = (bf16[272,128]{1,0:T(8,128)(2,1)S(1)}, bf16[272,128]{1,0:T(8,128)(2,1)S(1)}, u32[]{:S(2)}, u32[]{:S(2)}) collective-permute-start(bf16[272,128]{1,0:T(8,128)(2,1)S(1)} %pad_maximum_fusion.9), channel_id=1, source_target_pairs={{0,2},{1,3},{2,0},{3,1},{4,6},{5,7},{6,4},{7,5},{8,10},{9,11},{10,... | collective-permute-start | bytes 208904 | tf_op jit(solution)/shard_map/ppermute | solution.py:48
  52.1 0.8 %collective-permute-start.27 = (bf16[256,128]{1,0:T(8,128)(2,1)S(1)}, bf16[256,128]{1,0:T(8,128)(2,1)S(1)}, u32[]{:S(2)}, u32[]{:S(2)}) collective-permute-start(bf16[256,128]{1,0:T(8,128)(2,1)S(1)} %bitcast.75), channel_id=1, source_target_pairs={{0,1},{1,0},{2,3},{3,2},{4,5},{5,4},{6,7},{7,6},{8,9},{9,8},{10,11... | collective-permute-start | bytes 196616 | tf_op jit(solution)/shard_map/ppermute | solution.py:48
  53.0 3.5 %collective-permute-done.27 = bf16[256,128]{1,0:T(8,128)(2,1)S(1)} collective-permute-done((bf16[256,128]{1,0:T(8,128)(2,1)S(1)}, bf16[256,128]{1,0:T(8,128)(2,1)S(1)}, u32[]{:S(2)}, u32[]{:S(2)}) %collective-permute-start.27) | collective-permute-done | bytes 65568 | tf_op jit(solution)/shard_map/ppermute | solution.py:48
  56.6 2.6 %collective-permute-start.28 = (bf16[528,128]{1,0:T(8,128)(2,1)S(1)}, bf16[528,128]{1,0:T(8,128)(2,1)S(1)}, u32[]{:S(2)}, u32[]{:S(2)}) collective-permute-start(bf16[528,128]{1,0:T(8,128)(2,1)S(1)} %pad_maximum_fusion.8), channel_id=1, source_target_pairs={{0,4},{1,5},{2,6},{3,7},{4,0},{5,1},{6,2},{7,3},{8,12},{9,13},{10,... | collective-permute-start | bytes 405512 | tf_op jit(solution)/shard_map/ppermute | solution.py:48
  59.2 4.3 %collective-permute-done.28 = bf16[528,128]{1,0:T(8,128)(2,1)S(1)} collective-permute-done((bf16[528,128]{1,0:T(8,128)(2,1)S(1)}, bf16[528,128]{1,0:T(8,128)(2,1)S(1)}, u32[]{:S(2)}, u32[]{:S(2)}) %collective-permute-start.28) | collective-permute-done | bytes 135200 | tf_op jit(solution)/shard_map/ppermute | solution.py:48
  63.6 1.1 %collective-permute-start.29 = (bf16[1,2,256,128]{3,2,1,0:T(8,128)(2,1)S(1)}, bf16[1,2,256,128]{3,2,1,0:T(8,128)(2,1)S(1)}, u32[]{:S(2)}, u32[]{:S(2)}) collective-permute-start(bf16[1,2,256,128]{3,2,1,0:T(8,128)(2,1)S(1)} %bitcast.53), channel_id=1, source_target_pairs={{0,1},{1,0},{2,3},{3,2},{4,5},{5,4},{6,7},{7,6},{8,9},{9,8},{10,11... | collective-permute-start | bytes 393224 | tf_op jit(solution)/shard_map/ppermute | solution.py:48
  64.7 2.4 %collective-permute-start.31 = (bf16[1,2,256,128]{3,2,1,0:T(8,128)(2,1)S(1)}, bf16[1,2,256,128]{3,2,1,0:T(8,128)(2,1)S(1)}, u32[]{:S(2)}, u32[]{:S(2)}) collective-permute-start(bf16[1,2,256,128]{3,2,1,0:T(8,128)(2,1)S(1)} %bitcast.55), channel_id=1, source_target_pairs={{0,3},{1,2},{2,1},{3,0},{4,7},{5,6},{6,5},{7,4},{8,11},{9,10},{10,... | collective-permute-start | bytes 393224 | tf_op jit(solution)/shard_map/ppermute | solution.py:48
  67.2 1.5 %collective-permute-done.29 = bf16[1,2,256,128]{3,2,1,0:T(8,128)(2,1)S(1)} collective-permute-done((bf16[1,2,256,128]{3,2,1,0:T(8,128)(2,1)S(1)}, bf16[1,2,256,128]{3,2,1,0:T(8,128)(2,1)S(1)}, u32[]{:S(2)}, u32[]{:S(2)}) %collective-permute-start.29) | collective-permute-done | bytes 131104 | tf_op jit(solution)/shard_map/ppermute | solution.py:48
  68.6 1.0 %collective-permute-done.30 = bf16[1,2,256,128]{3,2,1,0:T(8,128)(2,1)S(1)} collective-permute-done((bf16[1,2,256,128]{3,2,1,0:T(8,128)(2,1)S(1)}, bf16[1,2,256,128]{3,2,1,0:T(8,128)(2,1)S(1)}, u32[]{:S(2)}, u32[]{:S(2)}) %collective-permute-start.30) | collective-permute-done | bytes 131104 | tf_op jit(solution)/shard_map/ppermute | solution.py:48
  69.7 1.8 %collective-permute-done.31 = bf16[1,2,256,128]{3,2,1,0:T(8,128)(2,1)S(1)} collective-permute-done((bf16[1,2,256,128]{3,2,1,0:T(8,128)(2,1)S(1)}, bf16[1,2,256,128]{3,2,1,0:T(8,128)(2,1)S(1)}, u32[]{:S(2)}, u32[]{:S(2)}) %collective-permute-start.31) | collective-permute-done | bytes 131104 | tf_op jit(solution)/shard_map/ppermute | solution.py:48
  71.5 1.2 %finish.1 = (f32[256,512]{1,0:T(8,128)}, f32[512,256]{1,0:T(8,128)}, f32[1,1]{1,0:T(1,128)}) custom-call(bf16[2,256,128]{2,1,0:T(8,128)(2,1)S(1)} %bitcast.56, bf16[2,256,128]{2,1,0:T(8,128)(2,1)S(1)} %bitcast.61, bf16[2,256,128]{2,1,0:T(8,128)(2,1)S(1)} %bitcast.62, bf16[2,256,128]{2,1,0:T(8,128)(2,1)S(1)} %bitcast.63, f32[8,128]{1,0:T(8,128)S(1)} %fusion.10.refs_4_), custom_call_target="tpu_custom_call" | custom-call | flops 1000000 | bytes 1000 | tf_op jit(solution)/shard_map/finish/pallas_call | solution.py:34
  (73 shorter events, 0.7 us)
Async XLA Ops:
  0.6 1.1 %copy-start.8 = (bf16[256,512]{1,0:T(8,128)(2,1)S(1)}, bf16[256,512]{1,0:T(8,128)(2,1)}, u32[]{:S(2)}) copy-start(bf16[256,512]{1,0:T(8,128)(2,1)} %param.14) | copy-start | bytes 786436
  1.7 3.0 %copy-start.9 = (bf16[256,512]{1,0:T(8,128)(2,1)S(1)}, bf16[256,512]{1,0:T(8,128)(2,1)}, u32[]{:S(2)}) copy-start(bf16[256,512]{1,0:T(8,128)(2,1)} %param.15) | copy-start | bytes 786436
  1.8 12.9 %collective-permute-start.3 = (bf16[384,512]{1,0:T(8,128)(2,1)S(1)}, bf16[384,512]{1,0:T(8,128)(2,1)S(1)}, u32[]{:S(2)}, u32[]{:S(2)}) collective-permute-start(bf16[384,512]{1,0:T(8,128)(2,1)S(1)} %pad_maximum_fusion.1), channel_id=1, source_target_pairs={{0,16},{8,24},{16,0},{24,8},{1,17},{9,25},{17,1},{25,9},{2,18},{10... | collective-permute-start | bytes 1179656 | tf_op jit(solution)/shard_map/ppermute | solution.py:48
  4.8 1.0 %copy-start = (bf16[1,128,1024]{2,1,0:T(8,128)(2,1)S(1)}, bf16[1,128,1024]{2,1,0:T(8,128)(2,1)}, u32[]{:S(2)}) copy-start(bf16[1,128,1024]{2,1,0:T(8,128)(2,1)} %x_ref.3) | copy-start | bytes 786436
  4.8 5.7 %copy-start.10 = (bf16[512,256]{1,0:T(8,128)(2,1)S(1)}, bf16[512,256]{1,0:T(8,128)(2,1)}, u32[]{:S(2)}) copy-start(bf16[512,256]{1,0:T(8,128)(2,1)} %param.17) | copy-start | bytes 786436
  4.8 5.8 %copy-start.11 = (bf16[256,512]{1,0:T(8,128)(2,1)S(1)}, bf16[256,512]{1,0:T(8,128)(2,1)}, u32[]{:S(2)}) copy-start(bf16[256,512]{1,0:T(8,128)(2,1)} %param.16) | copy-start | bytes 786436
  4.9 17.6 %collective-permute-start.2 = (bf16[512,512]{1,0:T(8,128)(2,1)S(1)}, bf16[512,512]{1,0:T(8,128)(2,1)S(1)}, u32[]{:S(2)}, u32[]{:S(2)}) collective-permute-start(bf16[512,512]{1,0:T(8,128)(2,1)S(1)} %constant_dynamic-update-slice_fusion.refs_0_), channel_id=1, source_target_pairs={{0,8},{8,0},{16,24},{24,16},{1,9},{9,1},{17,25},{25,17},{2,10},{10... | collective-permute-start | bytes 1572872 | tf_op jit(solution)/shard_map/ppermute | solution.py:48
  5.7 14.2 %collective-permute-start = (bf16[1,128,1024]{2,1,0:T(8,128)(2,1)S(1)}, bf16[1,128,1024]{2,1,0:T(8,128)(2,1)S(1)}, u32[]{:S(2)}, u32[]{:S(2)}) collective-permute-start(bf16[1,128,1024]{2,1,0:T(8,128)(2,1)S(1)} %copy-done), channel_id=1, source_target_pairs={{0,1},{1,2},{2,3},{3,4},{4,5},{5,6},{6,7},{8,9},{9,10},{10,11},{11... | collective-permute-start | bytes 786440 | tf_op jit(solution)/shard_map/ppermute | solution.py:301
  9.2 10.8 %collective-permute-start.1 = (bf16[1,128,1024]{2,1,0:T(8,128)(2,1)S(1)}, bf16[1,128,1024]{2,1,0:T(8,128)(2,1)S(1)}, u32[]{:S(2)}, u32[]{:S(2)}) collective-permute-start(bf16[1,128,1024]{2,1,0:T(8,128)(2,1)S(1)} %copy-done), channel_id=1, source_target_pairs={{1,0},{2,1},{3,2},{4,3},{5,4},{6,5},{7,6},{9,8},{10,9},{11,10},{12... | collective-permute-start | bytes 786440 | tf_op jit(solution)/shard_map/ppermute | solution.py:302
  10.7 15.6 %collective-permute-start.9 = (bf16[512,512]{1,0:T(8,128)(2,1)S(1)}, bf16[512,512]{1,0:T(8,128)(2,1)S(1)}, u32[]{:S(2)}, u32[]{:S(2)}) collective-permute-start(bf16[512,512]{1,0:T(8,128)(2,1)S(1)} %pad_maximum_fusion.refs_0_), channel_id=1, source_target_pairs={{0,16},{8,24},{16,0},{24,8},{1,17},{9,25},{17,1},{25,9},{2,18},{10... | collective-permute-start | bytes 1572872 | tf_op jit(solution)/shard_map/ppermute | solution.py:48
  14.7 5.3 %copy-start.2 = (s32[1024]{0:T(1024)S(1)}, s32[1024]{0:T(1024)}, u32[]{:S(2)}) copy-start(s32[1024]{0:T(1024)} %param.21) | copy-start | bytes 12292
  14.7 5.3 %copy-start.1 = (f32[1024]{0:T(1024)S(1)}, f32[1024]{0:T(1024)}, u32[]{:S(2)}) copy-start(f32[1024]{0:T(1024)} %param.13) | copy-start | bytes 12292
  14.7 7.8 %collective-permute-start.4 = (bf16[128,512]{1,0:T(8,128)(2,1)S(1)}, bf16[128,512]{1,0:T(8,128)(2,1)S(1)}, u32[]{:S(2)}, u32[]{:S(2)}) collective-permute-start(bf16[128,512]{1,0:T(8,128)(2,1)S(1)} %slice.124.refs_3_), channel_id=1, source_target_pairs={{0,2},{1,3},{2,0},{3,1},{4,6},{5,7},{6,4},{7,5},{8,10},{9,11},{10,... | collective-permute-start | bytes 393224 | tf_op jit(solution)/shard_map/ppermute | solution.py:48
  20.0 0.7 copy-start.3
  20.0 0.7 copy-start.4
  20.0 0.7 copy-start.5
  22.5 1.4 %collective-permute-start.7 = (bf16[128,512]{1,0:T(8,128)(2,1)S(1)}, bf16[128,512]{1,0:T(8,128)(2,1)S(1)}, u32[]{:S(2)}, u32[]{:S(2)}) collective-permute-start(bf16[128,512]{1,0:T(8,128)(2,1)S(1)} %get-tuple-element.97), channel_id=1, source_target_pairs={{0,8},{8,0},{16,24},{24,16},{1,9},{9,1},{17,25},{25,17},{2,10},{10... | collective-permute-start | bytes 393224 | tf_op jit(solution)/shard_map/ppermute | solution.py:48
  22.6 1.5 %collective-permute-start.8 = (bf16[128,512]{1,0:T(8,128)(2,1)S(1)}, bf16[128,512]{1,0:T(8,128)(2,1)S(1)}, u32[]{:S(2)}, u32[]{:S(2)}) collective-permute-start(bf16[128,512]{1,0:T(8,128)(2,1)S(1)} %get-tuple-element.96), channel_id=1, source_target_pairs={{0,8},{8,0},{16,24},{24,16},{1,9},{9,1},{17,25},{25,17},{2,10},{10... | collective-permute-start | bytes 393224 | tf_op jit(solution)/shard_map/ppermute | solution.py:48
  23.1 1.3 %collective-permute-start.5 = (bf16[128,512]{1,0:T(8,128)(2,1)S(1)}, bf16[128,512]{1,0:T(8,128)(2,1)S(1)}, u32[]{:S(2)}, u32[]{:S(2)}) collective-permute-start(bf16[128,512]{1,0:T(8,128)(2,1)S(1)} %slice.124.refs_3_), channel_id=1, source_target_pairs={{0,8},{8,0},{16,24},{24,16},{1,9},{9,1},{17,25},{25,17},{2,10},{10... | collective-permute-start | bytes 393224 | tf_op jit(solution)/shard_map/ppermute | solution.py:48
  23.2 1.5 %collective-permute-start.6 = (bf16[128,512]{1,0:T(8,128)(2,1)S(1)}, bf16[128,512]{1,0:T(8,128)(2,1)S(1)}, u32[]{:S(2)}, u32[]{:S(2)}) collective-permute-start(bf16[128,512]{1,0:T(8,128)(2,1)S(1)} %collective-permute-done.4.refs_4_), channel_id=1, source_target_pairs={{0,8},{8,0},{16,24},{24,16},{1,9},{9,1},{17,25},{25,17},{2,10},{10... | collective-permute-start | bytes 393224 | tf_op jit(solution)/shard_map/ppermute | solution.py:48
  26.3 1.6 %collective-permute-start.10 = (bf16[256,512]{1,0:T(8,128)(2,1)S(1)}, bf16[256,512]{1,0:T(8,128)(2,1)S(1)}, u32[]{:S(2)}, u32[]{:S(2)}) collective-permute-start(bf16[256,512]{1,0:T(8,128)(2,1)S(1)} %get-tuple-element.95), channel_id=1, source_target_pairs={{0,8},{8,0},{16,24},{24,16},{1,9},{9,1},{17,25},{25,17},{2,10},{10... | collective-permute-start | bytes 786440 | tf_op jit(solution)/shard_map/ppermute | solution.py:48
  26.7 1.6 %collective-permute-start.11 = (bf16[256,512]{1,0:T(8,128)(2,1)S(1)}, bf16[256,512]{1,0:T(8,128)(2,1)S(1)}, u32[]{:S(2)}, u32[]{:S(2)}) collective-permute-start(bf16[256,512]{1,0:T(8,128)(2,1)S(1)} %get-tuple-element.93.refs_2_), channel_id=1, source_target_pairs={{0,8},{8,0},{16,24},{24,16},{1,9},{9,1},{17,25},{25,17},{2,10},{10... | collective-permute-start | bytes 786440 | tf_op jit(solution)/shard_map/ppermute | solution.py:48
  27.0 2.3 %collective-permute-start.12 = (bf16[256,512]{1,0:T(8,128)(2,1)S(1)}, bf16[256,512]{1,0:T(8,128)(2,1)S(1)}, u32[]{:S(2)}, u32[]{:S(2)}) collective-permute-start(bf16[256,512]{1,0:T(8,128)(2,1)S(1)} %get-tuple-element.94), channel_id=1, source_target_pairs={{0,8},{8,0},{16,24},{24,16},{1,9},{9,1},{17,25},{25,17},{2,10},{10... | collective-permute-start | bytes 786440 | tf_op jit(solution)/shard_map/ppermute | solution.py:48
  27.3 2.0 %copy-start.6 = (bf16[1024,128]{1,0:T(8,128)(2,1)S(1)}, bf16[1024,128]{1,0:T(8,128)(2,1)}, u32[]{:S(2)}) copy-start(bf16[1024,128]{1,0:T(8,128)(2,1)} %read_ref.3) | copy-start | bytes 786436
  27.3 2.0 %collective-permute-start.13 = (bf16[256,512]{1,0:T(8,128)(2,1)S(1)}, bf16[256,512]{1,0:T(8,128)(2,1)S(1)}, u32[]{:S(2)}, u32[]{:S(2)}) collective-permute-start(bf16[256,512]{1,0:T(8,128)(2,1)S(1)} %get-tuple-element.92.refs_2_), channel_id=1, source_target_pairs={{0,8},{8,0},{16,24},{24,16},{1,9},{9,1},{17,25},{25,17},{2,10},{10... | collective-permute-start | bytes 786440 | tf_op jit(solution)/shard_map/ppermute | solution.py:48
  27.5 8.2 %collective-permute-start.17 = (bf16[512,384]{1,0:T(8,128)(2,1)S(1)}, bf16[512,384]{1,0:T(8,128)(2,1)S(1)}, u32[]{:S(2)}, u32[]{:S(2)}) collective-permute-start(bf16[512,384]{1,0:T(8,128)(2,1)S(1)} %get-tuple-element.59), channel_id=1, source_target_pairs={{0,8},{8,0},{16,24},{24,16},{1,9},{9,1},{17,25},{25,17},{2,10},{10... | collective-permute-start | bytes 1179656 | tf_op jit(solution)/shard_map/ppermute | solution.py:48
  29.3 6.4 %copy-start.7 = (f32[128,128]{1,0:T(8,128)S(1)}, f32[128,128]{1,0:T(8,128)}, u32[]{:S(2)}) copy-start(f32[128,128]{1,0:T(8,128)} %refs_5_.1) | copy-start | bytes 196612
  30.0 4.3 %collective-permute-start.14 = (bf16[128,128]{1,0:T(8,128)(2,1)S(1)}, bf16[128,128]{1,0:T(8,128)(2,1)S(1)}, u32[]{:S(2)}, u32[]{:S(2)}) collective-permute-start(bf16[128,128]{1,0:T(8,128)(2,1)S(1)} %get-tuple-element.61.refs_0_), channel_id=1, source_target_pairs={{0,16},{8,24},{16,0},{24,8},{1,17},{9,25},{17,1},{25,9},{2,18},{10... | collective-permute-start | bytes 98312 | tf_op jit(solution)/shard_map/ppermute | solution.py:48
  31.1 5.7 %collective-permute-start.18 = (bf16[128,512]{1,0:T(8,128)(2,1)S(1)}, bf16[128,512]{1,0:T(8,128)(2,1)S(1)}, u32[]{:S(2)}, u32[]{:S(2)}) collective-permute-start(bf16[128,512]{1,0:T(8,128)(2,1)S(1)} %attend.1.att_ref.refs_0_), channel_id=1, source_target_pairs={{0,16},{8,24},{16,0},{24,8},{1,17},{9,25},{17,1},{25,9},{2,18},{10... | collective-permute-start | bytes 393224 | tf_op jit(solution)/shard_map/ppermute | solution.py:48
  34.3 1.2 %collective-permute-start.15 = (bf16[128,128]{1,0:T(8,128)(2,1)S(1)}, bf16[128,128]{1,0:T(8,128)(2,1)S(1)}, u32[]{:S(2)}, u32[]{:S(2)}) collective-permute-start(bf16[128,128]{1,0:T(8,128)(2,1)S(1)} %get-tuple-element.61.refs_0_), channel_id=1, source_target_pairs={{0,8},{8,0},{16,24},{24,16},{1,9},{9,1},{17,25},{25,17},{2,10},{10... | collective-permute-start | bytes 98312 | tf_op jit(solution)/shard_map/ppermute | solution.py:48
  34.3 1.4 %collective-permute-start.16 = (bf16[128,128]{1,0:T(8,128)(2,1)S(1)}, bf16[128,128]{1,0:T(8,128)(2,1)S(1)}, u32[]{:S(2)}, u32[]{:S(2)}) collective-permute-start(bf16[128,128]{1,0:T(8,128)(2,1)S(1)} %collective-permute-done.14.refs_2_), channel_id=1, source_target_pairs={{0,8},{8,0},{16,24},{24,16},{1,9},{9,1},{17,25},{25,17},{2,10},{10... | collective-permute-start | bytes 98312 | tf_op jit(solution)/shard_map/ppermute | solution.py:48
  36.8 1.7 %collective-permute-start.19 = (bf16[400,512]{1,0:T(8,128)(2,1)S(1)}, bf16[400,512]{1,0:T(8,128)(2,1)S(1)}, u32[]{:S(2)}, u32[]{:S(2)}) collective-permute-start(bf16[400,512]{1,0:T(8,128)(2,1)S(1)} %get-tuple-element.69.own_con), channel_id=1, source_target_pairs={{0,8},{8,0},{16,24},{24,16},{1,9},{9,1},{17,25},{25,17},{2,10},{10... | collective-permute-start | bytes 1228808 | tf_op jit(solution)/shard_map/ppermute | solution.py:48
  37.1 5.8 %collective-permute-start.23 = (bf16[128,512]{1,0:T(8,128)(2,1)S(1)}, bf16[128,512]{1,0:T(8,128)(2,1)S(1)}, u32[]{:S(2)}, u32[]{:S(2)}) collective-permute-start(bf16[128,512]{1,0:T(8,128)(2,1)S(1)} %attend.1.att_ref.refs_0_), channel_id=1, source_target_pairs={{0,8},{8,0},{16,24},{24,16},{1,9},{9,1},{17,25},{25,17},{2,10},{10... | collective-permute-start | bytes 393224 | tf_op jit(solution)/shard_map/ppermute | solution.py:48
  37.3 5.6 %collective-permute-start.24 = (bf16[128,512]{1,0:T(8,128)(2,1)S(1)}, bf16[128,512]{1,0:T(8,128)(2,1)S(1)}, u32[]{:S(2)}, u32[]{:S(2)}) collective-permute-start(bf16[128,512]{1,0:T(8,128)(2,1)S(1)} %collective-permute-done.18.refs_2_), channel_id=1, source_target_pairs={{0,8},{8,0},{16,24},{24,16},{1,9},{9,1},{17,25},{25,17},{2,10},{10... | collective-permute-start | bytes 393224 | tf_op jit(solution)/shard_map/ppermute | solution.py:48
  39.4 7.1 %collective-permute-start.20 = (bf16[528,128]{1,0:T(8,128)(2,1)S(1)}, bf16[528,128]{1,0:T(8,128)(2,1)S(1)}, u32[]{:S(2)}, u32[]{:S(2)}) collective-permute-start(bf16[528,128]{1,0:T(8,128)(2,1)S(1)} %get-tuple-element.100), channel_id=1, source_target_pairs={{0,16},{1,17},{2,18},{3,19},{4,20},{5,21},{6,22},{7,23},{8,24},{9,... | collective-permute-start | bytes 405512 | tf_op jit(solution)/shard_map/ppermute | solution.py:450
  40.4 7.9 %collective-permute-start.21 = (bf16[528,128]{1,0:T(8,128)(2,1)S(1)}, bf16[528,128]{1,0:T(8,128)(2,1)S(1)}, u32[]{:S(2)}, u32[]{:S(2)}) collective-permute-start(bf16[528,128]{1,0:T(8,128)(2,1)S(1)} %get-tuple-element.98), channel_id=1, source_target_pairs={{0,1},{1,0},{2,3},{3,2},{4,5},{5,4},{6,7},{7,6},{8,9},{9,8},{10,11... | collective-permute-start | bytes 405512 | tf_op jit(solution)/shard_map/ppermute | solution.py:450
  42.4 7.1 %collective-permute-start.22 = (bf16[528,128]{1,0:T(8,128)(2,1)S(1)}, bf16[528,128]{1,0:T(8,128)(2,1)S(1)}, u32[]{:S(2)}, u32[]{:S(2)}) collective-permute-start(bf16[528,128]{1,0:T(8,128)(2,1)S(1)} %get-tuple-element.99), channel_id=1, source_target_pairs={{0,17},{1,16},{2,19},{3,18},{4,21},{5,20},{6,23},{7,22},{8,25},{9,... | collective-permute-start | bytes 405512 | tf_op jit(solution)/shard_map/ppermute | solution.py:450
  43.4 6.2 %collective-permute-start.25 = (bf16[512,128]{1,0:T(8,128)(2,1)S(1)}, bf16[512,128]{1,0:T(8,128)(2,1)S(1)}, u32[]{:S(2)}, u32[]{:S(2)}) collective-permute-start(bf16[512,128]{1,0:T(8,128)(2,1)S(1)} %bitcast.74), channel_id=1, source_target_pairs={{0,2},{1,3},{2,0},{3,1},{4,6},{5,7},{6,4},{7,5},{8,10},{9,11},{10,... | collective-permute-start | bytes 393224 | tf_op jit(solution)/shard_map/ppermute | solution.py:48
  49.8 6.7 %collective-permute-start.26 = (bf16[272,128]{1,0:T(8,128)(2,1)S(1)}, bf16[272,128]{1,0:T(8,128)(2,1)S(1)}, u32[]{:S(2)}, u32[]{:S(2)}) collective-permute-start(bf16[272,128]{1,0:T(8,128)(2,1)S(1)} %pad_maximum_fusion.9), channel_id=1, source_target_pairs={{0,2},{1,3},{2,0},{3,1},{4,6},{5,7},{6,4},{7,5},{8,10},{9,11},{10,... | collective-permute-start | bytes 208904 | tf_op jit(solution)/shard_map/ppermute | solution.py:48
  52.1 4.3 %collective-permute-start.27 = (bf16[256,128]{1,0:T(8,128)(2,1)S(1)}, bf16[256,128]{1,0:T(8,128)(2,1)S(1)}, u32[]{:S(2)}, u32[]{:S(2)}) collective-permute-start(bf16[256,128]{1,0:T(8,128)(2,1)S(1)} %bitcast.75), channel_id=1, source_target_pairs={{0,1},{1,0},{2,3},{3,2},{4,5},{5,4},{6,7},{7,6},{8,9},{9,8},{10,11... | collective-permute-start | bytes 196616 | tf_op jit(solution)/shard_map/ppermute | solution.py:48
  56.6 7.0 %collective-permute-start.28 = (bf16[528,128]{1,0:T(8,128)(2,1)S(1)}, bf16[528,128]{1,0:T(8,128)(2,1)S(1)}, u32[]{:S(2)}, u32[]{:S(2)}) collective-permute-start(bf16[528,128]{1,0:T(8,128)(2,1)S(1)} %pad_maximum_fusion.8), channel_id=1, source_target_pairs={{0,4},{1,5},{2,6},{3,7},{4,0},{5,1},{6,2},{7,3},{8,12},{9,13},{10,... | collective-permute-start | bytes 405512 | tf_op jit(solution)/shard_map/ppermute | solution.py:48
  63.6 5.0 %collective-permute-start.29 = (bf16[1,2,256,128]{3,2,1,0:T(8,128)(2,1)S(1)}, bf16[1,2,256,128]{3,2,1,0:T(8,128)(2,1)S(1)}, u32[]{:S(2)}, u32[]{:S(2)}) collective-permute-start(bf16[1,2,256,128]{3,2,1,0:T(8,128)(2,1)S(1)} %bitcast.53), channel_id=1, source_target_pairs={{0,1},{1,0},{2,3},{3,2},{4,5},{5,4},{6,7},{7,6},{8,9},{9,8},{10,11... | collective-permute-start | bytes 393224 | tf_op jit(solution)/shard_map/ppermute | solution.py:48
  64.7 5.0 %collective-permute-start.30 = (bf16[1,2,256,128]{3,2,1,0:T(8,128)(2,1)S(1)}, bf16[1,2,256,128]{3,2,1,0:T(8,128)(2,1)S(1)}, u32[]{:S(2)}, u32[]{:S(2)}) collective-permute-start(bf16[1,2,256,128]{3,2,1,0:T(8,128)(2,1)S(1)} %bitcast.54), channel_id=1, source_target_pairs={{0,2},{1,3},{2,0},{3,1},{4,6},{5,7},{6,4},{7,5},{8,10},{9,11},{10,... | collective-permute-start | bytes 393224 | tf_op jit(solution)/shard_map/ppermute | solution.py:48
  64.7 6.8 %collective-permute-start.31 = (bf16[1,2,256,128]{3,2,1,0:T(8,128)(2,1)S(1)}, bf16[1,2,256,128]{3,2,1,0:T(8,128)(2,1)S(1)}, u32[]{:S(2)}, u32[]{:S(2)}) collective-permute-start(bf16[1,2,256,128]{3,2,1,0:T(8,128)(2,1)S(1)} %bitcast.55), channel_id=1, source_target_pairs={{0,3},{1,2},{2,1},{3,0},{4,7},{5,6},{6,5},{7,4},{8,11},{9,10},{10,... | collective-permute-start | bytes 393224 | tf_op jit(solution)/shard_map/ppermute | solution.py:48

commit v9 on v8

--- a/solution.py
+++ b/solution.py
@@ -178,9 +178,13 @@
             con_ref[rows, cols] = (both[rows] * rows_ref[1:2, rows]).astype(BF16)
 
 
-def value_body(blocks, dsh, rows, keep_ref, sib_ref, own_con, sib_con, v_ref, loss_ref):
+def own_value_body(keep_ref, own_con, term_ref):
+    term_ref[...] = dot(keep_ref[...], own_con[: 3 * TILE, :])
+
+
+def value_body(blocks, dsh, rows, own_term, sib_ref, own_con, sib_con, v_ref, loss_ref):
     keys = 3 * TILE
-    term = dot(keep_ref[...], own_con[:keys, :]) + dot(sib_ref[...], sib_con[:keys, :])
+    term = own_term[...] + dot(sib_ref[...], sib_con[:keys, :])
     parts = []
     for ref in (own_con, sib_con):
         part = ref[keys:, :].astype(F32)
@@ -386,10 +390,17 @@
     contrib_sib = xor_permute(contrib, "ens", 1)
     attended_all = both_cores(attended_near)
     blocks = n_ens // 2
+    (own_term,) = call(
+        own_value_body,
+        [((d_model // 2, inner), F32)],
+        [("v", turned_keep), ("v", contrib)],
+        10**3,
+        "own_value",
+    )
     value_term, loss = call(
         functools.partial(value_body, blocks, dsh, dsh * inner // (LANES * n_pix)),
         [((blocks, 2, dsh * inner // (2 * LANES), LANES), F32), ((8, LANES), F32)],
-        [("v", turned_keep), ("v", turned_sib), ("v", contrib), ("v", contrib_sib)],
+        [("v", own_term), ("v", turned_sib), ("v", contrib), ("v", contrib_sib)],
         10**9,
         "value_term",
     )

time: 72.9 us -> 72.7 us (level)
    pallas_call x8 -> x9, Pallas kernels: 7.67 us -> 7.83 us  [call(): pl.pallas_call(body, out_shape=[jax.ShapeDtypeStruct(s, d) for s, d in ou...]
where the time goes in v9:
time: 72.7 us; the launch traced here: 72.5 us
  starting transfers between devices  31.6 us (43%)
  waiting for transfers between devices  28.5 us (39%)
  Pallas kernels  7.83 us (11%)
  local copies, waits for them, and re-layouts  1.99 us (3%)
  other arithmetic  1.38 us (2%)
  between operations  1.17 us (2%)
    ppermute x27, starting transfers between devices, xor_permute(): return lax.ppermute(value, axis, [(i, i ^ mask) for i in range(size)])  23.3 us
    ppermute x27, waiting for transfers between devices, xor_permute(): return lax.ppermute(value, axis, [(i, i ^ mask) for i in range(size)])  21.2 us
    pallas_call x9, Pallas kernels, call(): pl.pallas_call(body, out_shape=[jax.ShapeDtypeStruct(s, d) for s, d in ou...  7.83 us
    ppermute x1, waiting for transfers between devices, per_device(): lax.ppermute(sample_layer_feed, 'pix', [(i, i + 1) for i in range(n_pix -...  4.18 us
    ppermute x3, starting transfers between devices, per_device(): lax.ppermute(message, ('ens', 'pix'), pairs)  3.55 us
    ppermute x1, starting transfers between devices, per_device(): lax.ppermute(sample_layer_feed, 'pix', [(i, i + 1) for i in range(n_pix -...  3.43 us
    ppermute x3, waiting for transfers between devices, per_device(): lax.ppermute(message, ('ens', 'pix'), pairs)  3.11 us
    unnamed x26, local copies, waits for them, and re-layouts  1.68 us
  transfers between devices with their start and end apart: 32, of which 21 were waited for; matrix products, arithmetic and copies ran while one was open for 1% of the time, Pallas kernels for 9%

profile of v9, /device:TPU:0, one launch (start us, length us, event | category | flops | bytes accessed | tf_op | source)
XLA Modules:
  0.0 72.5 jit_solution(4240638284367514271)
XLA Ops:
  0.7 1.0 %slice_select_fusion = bf16[128,512]{1,0:T(8,128)(2,1)S(1)} fusion(bf16[256,512]{1,0:T(8,128)(2,1)} %param.15, pred[]{:T(512)S(6)} %eq.10), kind=kLoop, calls=%fused_computation.27 | loop fusion | flops 65536 | bytes 393217 | tf_op jit(solution)/shard_map/jit(_where)/select_n | solution.py:301
  1.8 3.0 %collective-permute-start.3 = (bf16[384,512]{1,0:T(8,128)(2,1)S(1)}, bf16[384,512]{1,0:T(8,128)(2,1)S(1)}, u32[]{:S(2)}, u32[]{:S(2)}) collective-permute-start(bf16[384,512]{1,0:T(8,128)(2,1)S(1)} %pad_maximum_fusion.1), channel_id=1, source_target_pairs={{0,16},{8,24},{16,0},{24,8},{1,17},{9,25},{17,1},{25,9},{2,18},{10... | collective-permute-start | bytes 1179656 | tf_op jit(solution)/shard_map/ppermute | solution.py:48
  4.9 0.1 collective-permute-start.2
  4.9 0.8 %copy-done = bf16[1,128,1024]{2,1,0:T(8,128)(2,1)S(1)} copy-done((bf16[1,128,1024]{2,1,0:T(8,128)(2,1)S(1)}, bf16[1,128,1024]{2,1,0:T(8,128)(2,1)}, u32[]{:S(2)}) %copy-start) | copy-done | bytes 262168
  5.7 3.4 %collective-permute-start = (bf16[1,128,1024]{2,1,0:T(8,128)(2,1)S(1)}, bf16[1,128,1024]{2,1,0:T(8,128)(2,1)S(1)}, u32[]{:S(2)}, u32[]{:S(2)}) collective-permute-start(bf16[1,128,1024]{2,1,0:T(8,128)(2,1)S(1)} %copy-done), channel_id=1, source_target_pairs={{0,1},{1,2},{2,3},{3,4},{4,5},{5,6},{6,7},{8,9},{9,10},{10,11},{11... | collective-permute-start | bytes 786440 | tf_op jit(solution)/shard_map/ppermute | solution.py:305
  9.2 1.3 %collective-permute-start.1 = (bf16[1,128,1024]{2,1,0:T(8,128)(2,1)S(1)}, bf16[1,128,1024]{2,1,0:T(8,128)(2,1)S(1)}, u32[]{:S(2)}, u32[]{:S(2)}) collective-permute-start(bf16[1,128,1024]{2,1,0:T(8,128)(2,1)S(1)} %copy-done), channel_id=1, source_target_pairs={{1,0},{2,1},{3,2},{4,3},{5,4},{6,5},{7,6},{9,8},{10,9},{11,10},{12... | collective-permute-start | bytes 786440 | tf_op jit(solution)/shard_map/ppermute | solution.py:306
  10.5 0.1 copy.17
  10.7 0.9 %collective-permute-start.9 = (bf16[512,512]{1,0:T(8,128)(2,1)S(1)}, bf16[512,512]{1,0:T(8,128)(2,1)S(1)}, u32[]{:S(2)}, u32[]{:S(2)}) collective-permute-start(bf16[512,512]{1,0:T(8,128)(2,1)S(1)} %pad_maximum_fusion.refs_0_), channel_id=1, source_target_pairs={{0,16},{8,24},{16,0},{24,8},{1,17},{9,25},{17,1},{25,9},{2,18},{10... | collective-permute-start | bytes 1572872 | tf_op jit(solution)/shard_map/ppermute | solution.py:48
  11.6 3.1 %collective-permute-done.3 = bf16[384,512]{1,0:T(8,128)(2,1)S(1)} collective-permute-done((bf16[384,512]{1,0:T(8,128)(2,1)S(1)}, bf16[384,512]{1,0:T(8,128)(2,1)S(1)}, u32[]{:S(2)}, u32[]{:S(2)}) %collective-permute-start.3) | collective-permute-done | bytes 393248 | tf_op jit(solution)/shard_map/ppermute | solution.py:48
  14.7 1.1 %collective-permute-start.4 = (bf16[128,512]{1,0:T(8,128)(2,1)S(1)}, bf16[128,512]{1,0:T(8,128)(2,1)S(1)}, u32[]{:S(2)}, u32[]{:S(2)}) collective-permute-start(bf16[128,512]{1,0:T(8,128)(2,1)S(1)} %slice.124.refs_3_), channel_id=1, source_target_pairs={{0,2},{1,3},{2,0},{3,1},{4,6},{5,7},{6,4},{7,5},{8,10},{9,11},{10,... | collective-permute-start | bytes 393224 | tf_op jit(solution)/shard_map/ppermute | solution.py:48
  15.8 4.2 %collective-permute-done.up_ref = bf16[1,128,1024]{2,1,0:T(8,128)(2,1)S(1)} collective-permute-done((bf16[1,128,1024]{2,1,0:T(8,128)(2,1)S(1)}, bf16[1,128,1024]{2,1,0:T(8,128)(2,1)S(1)}, u32[]{:S(2)}, u32[]{:S(2)}) %collective-permute-start) | collective-permute-done | bytes 262176 | tf_op jit(solution)/shard_map/ppermute | solution.py:305
  20.0 0.6 copy-done.3
  20.7 1.1 %normed.1 = (bf16[384,1024]{1,0:T(8,128)(2,1)S(1)}, bf16[512,384]{1,0:T(8,128)(2,1)S(1)}, bf16[512,384]{1,0:T(8,128)(2,1)S(1)}, f32[128,128]{1,0:T(8,128)S(1)}, f32[8,384]{1,0:T(8,128)S(1)}) custom-call(bf16[1,128,1024]{2,1,0:T(8,128)(2,1)S(1)} %copy-done, bf16[1,128,1024]{2,1,0:T(8,128)(2,1)S(1)} %collective-permute-done.up_ref, ...), custom_call_target="tpu_custom_call" | custom-call | flops 10000000 | bytes 10000 | tf_op jit(solution)/shard_map/normed/pallas_call | solution.py:34
  21.8 0.7 collective-permute-done.4.refs_4_
  22.5 0.1 collective-permute-start.7
  22.6 0.5 collective-permute-start.8
  23.1 0.1 collective-permute-start.5
  23.2 0.4 collective-permute-start.6
  23.6 0.3 collective-permute-done.7.refs_7_
  23.9 0.2 collective-permute-done.8.refs_8_
  24.1 0.3 collective-permute-done.5.refs_5_
  24.4 0.2 collective-permute-done.6.refs_6_
  24.6 1.6 %weights.1.w_ref.refs_8_ = bf16[8,128,384]{2,1,0:T(8,128)(2,1)S(1)} custom-call(bf16[384,1024]{1,0:T(8,128)(2,1)S(1)} %get-tuple-element.46.n_ref, f32[8,384]{1,0:T(8,128)S(1)} %get-tuple-element.47.rows_ref.refs_9_, bf16[512,512]{1,0:T(8,128)(2,1)S(1)} %constant_dynamic-update-slice_fusion.refs_0_, bf16[512,512]{1,0:T(8,128)(2,1)S(1)} %collective-permute-done.2.refs_1_, ...), custom_call_target="tpu_custom_call" | custom-call | flops 1000 | bytes 1 | tf_op jit(solution)/shard_map/weights/pallas_call | solution.py:34
  26.3 0.4 collective-permute-start.10
  26.7 0.3 collective-permute-start.11
  27.0 0.3 collective-permute-start.12
  27.3 0.2 collective-permute-start.13
  27.5 0.3 collective-permute-start.17
  27.8 0.1 collective-permute-done.10.refs_1_
  27.9 0.4 collective-permute-done.11.refs_3_
  28.3 0.9 %attend.1.att_ref.refs_0_ = bf16[128,512]{1,0:T(8,128)(2,1)S(1)} custom-call(bf16[384,1024]{1,0:T(8,128)(2,1)S(1)} %get-tuple-element.46.n_ref, bf16[8,128,384]{2,1,0:T(8,128)(2,1)S(1)} %weights.1.w_ref.refs_8_, f32[8,384]{1,0:T(8,128)S(1)} %get-tuple-element.47.rows_ref.refs_9_, bf16[512,512]{1,0:T(8,128)(2,1)S(1)} %pad_maximum_fusion.refs_0_, ...), custom_call_target="tpu_custom_call" | custom-call | flops 1000000000 | bytes 1000000 | tf_op jit(solution)/shard_map/attend/pallas_call | solution.py:34
  29.3 0.7 forecast.1
  30.0 1.0 %collective-permute-start.14 = (bf16[128,128]{1,0:T(8,128)(2,1)S(1)}, bf16[128,128]{1,0:T(8,128)(2,1)S(1)}, u32[]{:S(2)}, u32[]{:S(2)}) collective-permute-start(bf16[128,128]{1,0:T(8,128)(2,1)S(1)} %get-tuple-element.60.refs_0_), channel_id=1, source_target_pairs={{0,16},{8,24},{16,0},{24,8},{1,17},{9,25},{17,1},{25,9},{2,18},{10... | collective-permute-start | bytes 98312 | tf_op jit(solution)/shard_map/ppermute | solution.py:48
  31.1 1.0 %collective-permute-start.18 = (bf16[128,512]{1,0:T(8,128)(2,1)S(1)}, bf16[128,512]{1,0:T(8,128)(2,1)S(1)}, u32[]{:S(2)}, u32[]{:S(2)}) collective-permute-start(bf16[128,512]{1,0:T(8,128)(2,1)S(1)} %attend.1.att_ref.refs_0_), channel_id=1, source_target_pairs={{0,16},{8,24},{16,0},{24,8},{1,17},{9,25},{17,1},{25,9},{2,18},{10... | collective-permute-start | bytes 393224 | tf_op jit(solution)/shard_map/ppermute | solution.py:48
  32.1 2.2 %collective-permute-done.14.refs_2_ = bf16[128,128]{1,0:T(8,128)(2,1)S(1)} collective-permute-done((bf16[128,128]{1,0:T(8,128)(2,1)S(1)}, bf16[128,128]{1,0:T(8,128)(2,1)S(1)}, u32[]{:S(2)}, u32[]{:S(2)}) %collective-permute-start.14) | collective-permute-done | bytes 32800 | tf_op jit(solution)/shard_map/ppermute | solution.py:48
  34.3 0.5 collective-permute-start.16
  34.8 0.7 collective-permute-done.15.refs_1_
  35.5 0.2 collective-permute-done.16.refs_3_
  35.7 1.0 %backward.1 = (bf16[512,128]{1,0:T(8,128)(2,1)S(1)}, bf16[400,512]{1,0:T(8,128)(2,1)S(1)}) custom-call(bf16[128,128]{1,0:T(8,128)(2,1)S(1)} %get-tuple-element.60.refs_0_, bf16[128,128]{1,0:T(8,128)(2,1)S(1)} %collective-permute-done.15.refs_1_, bf16[128,128]{1,0:T(8,128)(2,1)S(1)} %collective-permute-done.14.refs_2_, ...), custom_call_target="tpu_custom_call" | custom-call | flops 1000000000 | bytes 1000000 | tf_op jit(solution)/shard_map/backward/pallas_call | solution.py:34
  36.7 0.1 collective-permute-done.18.refs_2_
  36.8 0.3 collective-permute-start.19
  37.1 0.2 collective-permute-start.23
  37.3 0.3 collective-permute-start.24
  37.6 0.4 own_value.1.own_term
  38.1 0.5 collective-permute-done.19.sib_con
  38.5 0.4 value_term.1
  39.1 1.0 %collective-permute-start.20 = (bf16[528,128]{1,0:T(8,128)(2,1)S(1)}, bf16[528,128]{1,0:T(8,128)(2,1)S(1)}, u32[]{:S(2)}, u32[]{:S(2)}) collective-permute-start(bf16[528,128]{1,0:T(8,128)(2,1)S(1)} %get-tuple-element.100), channel_id=1, source_target_pairs={{0,16},{1,17},{2,18},{3,19},{4,20},{5,21},{6,22},{7,23},{8,24},{9,... | collective-permute-start | bytes 405512 | tf_op jit(solution)/shard_map/ppermute | solution.py:461
  40.2 2.0 %collective-permute-start.21 = (bf16[528,128]{1,0:T(8,128)(2,1)S(1)}, bf16[528,128]{1,0:T(8,128)(2,1)S(1)}, u32[]{:S(2)}, u32[]{:S(2)}) collective-permute-start(bf16[528,128]{1,0:T(8,128)(2,1)S(1)} %get-tuple-element.98), channel_id=1, source_target_pairs={{0,1},{1,0},{2,3},{3,2},{4,5},{5,4},{6,7},{7,6},{8,9},{9,8},{10,11... | collective-permute-start | bytes 405512 | tf_op jit(solution)/shard_map/ppermute | solution.py:461
  42.2 0.5 collective-permute-start.22
  42.7 0.4 output_term.1
  43.1 3.0 %collective-permute-start.25 = (bf16[512,128]{1,0:T(8,128)(2,1)S(1)}, bf16[512,128]{1,0:T(8,128)(2,1)S(1)}, u32[]{:S(2)}, u32[]{:S(2)}) collective-permute-start(bf16[512,128]{1,0:T(8,128)(2,1)S(1)} %bitcast.74), channel_id=1, source_target_pairs={{0,2},{1,3},{2,0},{3,1},{4,6},{5,7},{6,4},{7,5},{8,10},{9,11},{10,... | collective-permute-start | bytes 393224 | tf_op jit(solution)/shard_map/ppermute | solution.py:48
  46.2 1.9 %collective-permute-done.21 = bf16[528,128]{1,0:T(8,128)(2,1)S(1)} collective-permute-done((bf16[528,128]{1,0:T(8,128)(2,1)S(1)}, bf16[528,128]{1,0:T(8,128)(2,1)S(1)}, u32[]{:S(2)}, u32[]{:S(2)}) %collective-permute-start.21) | collective-permute-done | bytes 135200 | tf_op jit(solution)/shard_map/ppermute | solution.py:461
  48.1 1.2 %collective-permute-done.22 = bf16[528,128]{1,0:T(8,128)(2,1)S(1)} collective-permute-done((bf16[528,128]{1,0:T(8,128)(2,1)S(1)}, bf16[528,128]{1,0:T(8,128)(2,1)S(1)}, u32[]{:S(2)}, u32[]{:S(2)}) %collective-permute-start.22) | collective-permute-done | bytes 135200 | tf_op jit(solution)/shard_map/ppermute | solution.py:461
  49.6 2.3 %collective-permute-start.26 = (bf16[272,128]{1,0:T(8,128)(2,1)S(1)}, bf16[272,128]{1,0:T(8,128)(2,1)S(1)}, u32[]{:S(2)}, u32[]{:S(2)}) collective-permute-start(bf16[272,128]{1,0:T(8,128)(2,1)S(1)} %pad_maximum_fusion.9), channel_id=1, source_target_pairs={{0,2},{1,3},{2,0},{3,1},{4,6},{5,7},{6,4},{7,5},{8,10},{9,11},{10,... | collective-permute-start | bytes 208904 | tf_op jit(solution)/shard_map/ppermute | solution.py:48
  51.9 0.8 %collective-permute-start.27 = (bf16[256,128]{1,0:T(8,128)(2,1)S(1)}, bf16[256,128]{1,0:T(8,128)(2,1)S(1)}, u32[]{:S(2)}, u32[]{:S(2)}) collective-permute-start(bf16[256,128]{1,0:T(8,128)(2,1)S(1)} %bitcast.75), channel_id=1, source_target_pairs={{0,1},{1,0},{2,3},{3,2},{4,5},{5,4},{6,7},{7,6},{8,9},{9,8},{10,11... | collective-permute-start | bytes 196616 | tf_op jit(solution)/shard_map/ppermute | solution.py:48
  52.7 3.5 %collective-permute-done.27 = bf16[256,128]{1,0:T(8,128)(2,1)S(1)} collective-permute-done((bf16[256,128]{1,0:T(8,128)(2,1)S(1)}, bf16[256,128]{1,0:T(8,128)(2,1)S(1)}, u32[]{:S(2)}, u32[]{:S(2)}) %collective-permute-start.27) | collective-permute-done | bytes 65568 | tf_op jit(solution)/shard_map/ppermute | solution.py:48
  56.3 2.6 %collective-permute-start.28 = (bf16[528,128]{1,0:T(8,128)(2,1)S(1)}, bf16[528,128]{1,0:T(8,128)(2,1)S(1)}, u32[]{:S(2)}, u32[]{:S(2)}) collective-permute-start(bf16[528,128]{1,0:T(8,128)(2,1)S(1)} %pad_maximum_fusion.8), channel_id=1, source_target_pairs={{0,4},{1,5},{2,6},{3,7},{4,0},{5,1},{6,2},{7,3},{8,12},{9,13},{10,... | collective-permute-start | bytes 405512 | tf_op jit(solution)/shard_map/ppermute | solution.py:48
  59.0 4.3 %collective-permute-done.28 = bf16[528,128]{1,0:T(8,128)(2,1)S(1)} collective-permute-done((bf16[528,128]{1,0:T(8,128)(2,1)S(1)}, bf16[528,128]{1,0:T(8,128)(2,1)S(1)}, u32[]{:S(2)}, u32[]{:S(2)}) %collective-permute-start.28) | collective-permute-done | bytes 135200 | tf_op jit(solution)/shard_map/ppermute | solution.py:48
  63.3 1.1 %collective-permute-start.29 = (bf16[1,2,256,128]{3,2,1,0:T(8,128)(2,1)S(1)}, bf16[1,2,256,128]{3,2,1,0:T(8,128)(2,1)S(1)}, u32[]{:S(2)}, u32[]{:S(2)}) collective-permute-start(bf16[1,2,256,128]{3,2,1,0:T(8,128)(2,1)S(1)} %bitcast.53), channel_id=1, source_target_pairs={{0,1},{1,0},{2,3},{3,2},{4,5},{5,4},{6,7},{7,6},{8,9},{9,8},{10,11... | collective-permute-start | bytes 393224 | tf_op jit(solution)/shard_map/ppermute | solution.py:48
  64.5 2.4 %collective-permute-start.31 = (bf16[1,2,256,128]{3,2,1,0:T(8,128)(2,1)S(1)}, bf16[1,2,256,128]{3,2,1,0:T(8,128)(2,1)S(1)}, u32[]{:S(2)}, u32[]{:S(2)}) collective-permute-start(bf16[1,2,256,128]{3,2,1,0:T(8,128)(2,1)S(1)} %bitcast.55), channel_id=1, source_target_pairs={{0,3},{1,2},{2,1},{3,0},{4,7},{5,6},{6,5},{7,4},{8,11},{9,10},{10,... | collective-permute-start | bytes 393224 | tf_op jit(solution)/shard_map/ppermute | solution.py:48
  66.9 1.5 %collective-permute-done.29 = bf16[1,2,256,128]{3,2,1,0:T(8,128)(2,1)S(1)} collective-permute-done((bf16[1,2,256,128]{3,2,1,0:T(8,128)(2,1)S(1)}, bf16[1,2,256,128]{3,2,1,0:T(8,128)(2,1)S(1)}, u32[]{:S(2)}, u32[]{:S(2)}) %collective-permute-start.29) | collective-permute-done | bytes 131104 | tf_op jit(solution)/shard_map/ppermute | solution.py:48
  68.4 1.0 %collective-permute-done.30 = bf16[1,2,256,128]{3,2,1,0:T(8,128)(2,1)S(1)} collective-permute-done((bf16[1,2,256,128]{3,2,1,0:T(8,128)(2,1)S(1)}, bf16[1,2,256,128]{3,2,1,0:T(8,128)(2,1)S(1)}, u32[]{:S(2)}, u32[]{:S(2)}) %collective-permute-start.30) | collective-permute-done | bytes 131104 | tf_op jit(solution)/shard_map/ppermute | solution.py:48
  69.4 1.8 %collective-permute-done.31 = bf16[1,2,256,128]{3,2,1,0:T(8,128)(2,1)S(1)} collective-permute-done((bf16[1,2,256,128]{3,2,1,0:T(8,128)(2,1)S(1)}, bf16[1,2,256,128]{3,2,1,0:T(8,128)(2,1)S(1)}, u32[]{:S(2)}, u32[]{:S(2)}) %collective-permute-start.31) | collective-permute-done | bytes 131104 | tf_op jit(solution)/shard_map/ppermute | solution.py:48
  71.2 1.2 %finish.1 = (f32[256,512]{1,0:T(8,128)}, f32[512,256]{1,0:T(8,128)}, f32[1,1]{1,0:T(1,128)}) custom-call(bf16[2,256,128]{2,1,0:T(8,128)(2,1)S(1)} %bitcast.56, bf16[2,256,128]{2,1,0:T(8,128)(2,1)S(1)} %bitcast.61, bf16[2,256,128]{2,1,0:T(8,128)(2,1)S(1)} %bitcast.62, bf16[2,256,128]{2,1,0:T(8,128)(2,1)S(1)} %bitcast.63, f32[8,128]{1,0:T(8,128)S(1)} %fusion.10.refs_4_), custom_call_target="tpu_custom_call" | custom-call | flops 1000000 | bytes 1000 | tf_op jit(solution)/shard_map/finish/pallas_call | solution.py:34
  (74 shorter events, 0.8 us)
Async XLA Ops:
  0.6 1.1 %copy-start.8 = (bf16[256,512]{1,0:T(8,128)(2,1)S(1)}, bf16[256,512]{1,0:T(8,128)(2,1)}, u32[]{:S(2)}) copy-start(bf16[256,512]{1,0:T(8,128)(2,1)} %param.14) | copy-start | bytes 786436
  1.7 3.0 %copy-start.9 = (bf16[256,512]{1,0:T(8,128)(2,1)S(1)}, bf16[256,512]{1,0:T(8,128)(2,1)}, u32[]{:S(2)}) copy-start(bf16[256,512]{1,0:T(8,128)(2,1)} %param.15) | copy-start | bytes 786436
  1.8 12.9 %collective-permute-start.3 = (bf16[384,512]{1,0:T(8,128)(2,1)S(1)}, bf16[384,512]{1,0:T(8,128)(2,1)S(1)}, u32[]{:S(2)}, u32[]{:S(2)}) collective-permute-start(bf16[384,512]{1,0:T(8,128)(2,1)S(1)} %pad_maximum_fusion.1), channel_id=1, source_target_pairs={{0,16},{8,24},{16,0},{24,8},{1,17},{9,25},{17,1},{25,9},{2,18},{10... | collective-permute-start | bytes 1179656 | tf_op jit(solution)/shard_map/ppermute | solution.py:48
  4.8 1.0 %copy-start = (bf16[1,128,1024]{2,1,0:T(8,128)(2,1)S(1)}, bf16[1,128,1024]{2,1,0:T(8,128)(2,1)}, u32[]{:S(2)}) copy-start(bf16[1,128,1024]{2,1,0:T(8,128)(2,1)} %x_ref.3) | copy-start | bytes 786436
  4.8 5.7 %copy-start.10 = (bf16[512,256]{1,0:T(8,128)(2,1)S(1)}, bf16[512,256]{1,0:T(8,128)(2,1)}, u32[]{:S(2)}) copy-start(bf16[512,256]{1,0:T(8,128)(2,1)} %param.17) | copy-start | bytes 786436
  4.8 5.8 %copy-start.11 = (bf16[256,512]{1,0:T(8,128)(2,1)S(1)}, bf16[256,512]{1,0:T(8,128)(2,1)}, u32[]{:S(2)}) copy-start(bf16[256,512]{1,0:T(8,128)(2,1)} %param.16) | copy-start | bytes 786436
  4.9 17.6 %collective-permute-start.2 = (bf16[512,512]{1,0:T(8,128)(2,1)S(1)}, bf16[512,512]{1,0:T(8,128)(2,1)S(1)}, u32[]{:S(2)}, u32[]{:S(2)}) collective-permute-start(bf16[512,512]{1,0:T(8,128)(2,1)S(1)} %constant_dynamic-update-slice_fusion.refs_0_), channel_id=1, source_target_pairs={{0,8},{8,0},{16,24},{24,16},{1,9},{9,1},{17,25},{25,17},{2,10},{10... | collective-permute-start | bytes 1572872 | tf_op jit(solution)/shard_map/ppermute | solution.py:48
  5.7 14.2 %collective-permute-start = (bf16[1,128,1024]{2,1,0:T(8,128)(2,1)S(1)}, bf16[1,128,1024]{2,1,0:T(8,128)(2,1)S(1)}, u32[]{:S(2)}, u32[]{:S(2)}) collective-permute-start(bf16[1,128,1024]{2,1,0:T(8,128)(2,1)S(1)} %copy-done), channel_id=1, source_target_pairs={{0,1},{1,2},{2,3},{3,4},{4,5},{5,6},{6,7},{8,9},{9,10},{10,11},{11... | collective-permute-start | bytes 786440 | tf_op jit(solution)/shard_map/ppermute | solution.py:305
  9.2 10.8 %collective-permute-start.1 = (bf16[1,128,1024]{2,1,0:T(8,128)(2,1)S(1)}, bf16[1,128,1024]{2,1,0:T(8,128)(2,1)S(1)}, u32[]{:S(2)}, u32[]{:S(2)}) collective-permute-start(bf16[1,128,1024]{2,1,0:T(8,128)(2,1)S(1)} %copy-done), channel_id=1, source_target_pairs={{1,0},{2,1},{3,2},{4,3},{5,4},{6,5},{7,6},{9,8},{10,9},{11,10},{12... | collective-permute-start | bytes 786440 | tf_op jit(solution)/shard_map/ppermute | solution.py:306
  10.7 15.6 %collective-permute-start.9 = (bf16[512,512]{1,0:T(8,128)(2,1)S(1)}, bf16[512,512]{1,0:T(8,128)(2,1)S(1)}, u32[]{:S(2)}, u32[]{:S(2)}) collective-permute-start(bf16[512,512]{1,0:T(8,128)(2,1)S(1)} %pad_maximum_fusion.refs_0_), channel_id=1, source_target_pairs={{0,16},{8,24},{16,0},{24,8},{1,17},{9,25},{17,1},{25,9},{2,18},{10... | collective-permute-start | bytes 1572872 | tf_op jit(solution)/shard_map/ppermute | solution.py:48
  14.7 5.3 %copy-start.2 = (s32[1024]{0:T(1024)S(1)}, s32[1024]{0:T(1024)}, u32[]{:S(2)}) copy-start(s32[1024]{0:T(1024)} %param.21) | copy-start | bytes 12292
  14.7 5.3 %copy-start.1 = (f32[1024]{0:T(1024)S(1)}, f32[1024]{0:T(1024)}, u32[]{:S(2)}) copy-start(f32[1024]{0:T(1024)} %param.13) | copy-start | bytes 12292
  14.7 7.8 %collective-permute-start.4 = (bf16[128,512]{1,0:T(8,128)(2,1)S(1)}, bf16[128,512]{1,0:T(8,128)(2,1)S(1)}, u32[]{:S(2)}, u32[]{:S(2)}) collective-permute-start(bf16[128,512]{1,0:T(8,128)(2,1)S(1)} %slice.124.refs_3_), channel_id=1, source_target_pairs={{0,2},{1,3},{2,0},{3,1},{4,6},{5,7},{6,4},{7,5},{8,10},{9,11},{10,... | collective-permute-start | bytes 393224 | tf_op jit(solution)/shard_map/ppermute | solution.py:48
  20.0 0.7 copy-start.3
  20.0 0.7 copy-start.4
  20.0 0.7 copy-start.5
  22.5 1.4 %collective-permute-start.7 = (bf16[128,512]{1,0:T(8,128)(2,1)S(1)}, bf16[128,512]{1,0:T(8,128)(2,1)S(1)}, u32[]{:S(2)}, u32[]{:S(2)}) collective-permute-start(bf16[128,512]{1,0:T(8,128)(2,1)S(1)} %get-tuple-element.97), channel_id=1, source_target_pairs={{0,8},{8,0},{16,24},{24,16},{1,9},{9,1},{17,25},{25,17},{2,10},{10... | collective-permute-start | bytes 393224 | tf_op jit(solution)/shard_map/ppermute | solution.py:48
  22.6 1.5 %collective-permute-start.8 = (bf16[128,512]{1,0:T(8,128)(2,1)S(1)}, bf16[128,512]{1,0:T(8,128)(2,1)S(1)}, u32[]{:S(2)}, u32[]{:S(2)}) collective-permute-start(bf16[128,512]{1,0:T(8,128)(2,1)S(1)} %get-tuple-element.96), channel_id=1, source_target_pairs={{0,8},{8,0},{16,24},{24,16},{1,9},{9,1},{17,25},{25,17},{2,10},{10... | collective-permute-start | bytes 393224 | tf_op jit(solution)/shard_map/ppermute | solution.py:48
  23.1 1.3 %collective-permute-start.5 = (bf16[128,512]{1,0:T(8,128)(2,1)S(1)}, bf16[128,512]{1,0:T(8,128)(2,1)S(1)}, u32[]{:S(2)}, u32[]{:S(2)}) collective-permute-start(bf16[128,512]{1,0:T(8,128)(2,1)S(1)} %slice.124.refs_3_), channel_id=1, source_target_pairs={{0,8},{8,0},{16,24},{24,16},{1,9},{9,1},{17,25},{25,17},{2,10},{10... | collective-permute-start | bytes 393224 | tf_op jit(solution)/shard_map/ppermute | solution.py:48
  23.2 1.5 %collective-permute-start.6 = (bf16[128,512]{1,0:T(8,128)(2,1)S(1)}, bf16[128,512]{1,0:T(8,128)(2,1)S(1)}, u32[]{:S(2)}, u32[]{:S(2)}) collective-permute-start(bf16[128,512]{1,0:T(8,128)(2,1)S(1)} %collective-permute-done.4.refs_4_), channel_id=1, source_target_pairs={{0,8},{8,0},{16,24},{24,16},{1,9},{9,1},{17,25},{25,17},{2,10},{10... | collective-permute-start | bytes 393224 | tf_op jit(solution)/shard_map/ppermute | solution.py:48
  26.3 1.6 %collective-permute-start.10 = (bf16[256,512]{1,0:T(8,128)(2,1)S(1)}, bf16[256,512]{1,0:T(8,128)(2,1)S(1)}, u32[]{:S(2)}, u32[]{:S(2)}) collective-permute-start(bf16[256,512]{1,0:T(8,128)(2,1)S(1)} %get-tuple-element.95), channel_id=1, source_target_pairs={{0,8},{8,0},{16,24},{24,16},{1,9},{9,1},{17,25},{25,17},{2,10},{10... | collective-permute-start | bytes 786440 | tf_op jit(solution)/shard_map/ppermute | solution.py:48
  26.7 1.6 %collective-permute-start.11 = (bf16[256,512]{1,0:T(8,128)(2,1)S(1)}, bf16[256,512]{1,0:T(8,128)(2,1)S(1)}, u32[]{:S(2)}, u32[]{:S(2)}) collective-permute-start(bf16[256,512]{1,0:T(8,128)(2,1)S(1)} %get-tuple-element.93.refs_2_), channel_id=1, source_target_pairs={{0,8},{8,0},{16,24},{24,16},{1,9},{9,1},{17,25},{25,17},{2,10},{10... | collective-permute-start | bytes 786440 | tf_op jit(solution)/shard_map/ppermute | solution.py:48
  27.0 2.3 %collective-permute-start.12 = (bf16[256,512]{1,0:T(8,128)(2,1)S(1)}, bf16[256,512]{1,0:T(8,128)(2,1)S(1)}, u32[]{:S(2)}, u32[]{:S(2)}) collective-permute-start(bf16[256,512]{1,0:T(8,128)(2,1)S(1)} %get-tuple-element.94), channel_id=1, source_target_pairs={{0,8},{8,0},{16,24},{24,16},{1,9},{9,1},{17,25},{25,17},{2,10},{10... | collective-permute-start | bytes 786440 | tf_op jit(solution)/shard_map/ppermute | solution.py:48
  27.3 2.0 %copy-start.6 = (bf16[1024,128]{1,0:T(8,128)(2,1)S(1)}, bf16[1024,128]{1,0:T(8,128)(2,1)}, u32[]{:S(2)}) copy-start(bf16[1024,128]{1,0:T(8,128)(2,1)} %read_ref.3) | copy-start | bytes 786436
  27.3 2.0 %collective-permute-start.13 = (bf16[256,512]{1,0:T(8,128)(2,1)S(1)}, bf16[256,512]{1,0:T(8,128)(2,1)S(1)}, u32[]{:S(2)}, u32[]{:S(2)}) collective-permute-start(bf16[256,512]{1,0:T(8,128)(2,1)S(1)} %get-tuple-element.92.refs_2_), channel_id=1, source_target_pairs={{0,8},{8,0},{16,24},{24,16},{1,9},{9,1},{17,25},{25,17},{2,10},{10... | collective-permute-start | bytes 786440 | tf_op jit(solution)/shard_map/ppermute | solution.py:48
  27.5 8.2 %collective-permute-start.17 = (bf16[512,384]{1,0:T(8,128)(2,1)S(1)}, bf16[512,384]{1,0:T(8,128)(2,1)S(1)}, u32[]{:S(2)}, u32[]{:S(2)}) collective-permute-start(bf16[512,384]{1,0:T(8,128)(2,1)S(1)} %get-tuple-element.59), channel_id=1, source_target_pairs={{0,8},{8,0},{16,24},{24,16},{1,9},{9,1},{17,25},{25,17},{2,10},{10... | collective-permute-start | bytes 1179656 | tf_op jit(solution)/shard_map/ppermute | solution.py:48
  29.3 6.4 %copy-start.7 = (f32[128,128]{1,0:T(8,128)S(1)}, f32[128,128]{1,0:T(8,128)}, u32[]{:S(2)}) copy-start(f32[128,128]{1,0:T(8,128)} %refs_5_.1) | copy-start | bytes 196612
  30.0 4.3 %collective-permute-start.14 = (bf16[128,128]{1,0:T(8,128)(2,1)S(1)}, bf16[128,128]{1,0:T(8,128)(2,1)S(1)}, u32[]{:S(2)}, u32[]{:S(2)}) collective-permute-start(bf16[128,128]{1,0:T(8,128)(2,1)S(1)} %get-tuple-element.60.refs_0_), channel_id=1, source_target_pairs={{0,16},{8,24},{16,0},{24,8},{1,17},{9,25},{17,1},{25,9},{2,18},{10... | collective-permute-start | bytes 98312 | tf_op jit(solution)/shard_map/ppermute | solution.py:48
  31.1 5.7 %collective-permute-start.18 = (bf16[128,512]{1,0:T(8,128)(2,1)S(1)}, bf16[128,512]{1,0:T(8,128)(2,1)S(1)}, u32[]{:S(2)}, u32[]{:S(2)}) collective-permute-start(bf16[128,512]{1,0:T(8,128)(2,1)S(1)} %attend.1.att_ref.refs_0_), channel_id=1, source_target_pairs={{0,16},{8,24},{16,0},{24,8},{1,17},{9,25},{17,1},{25,9},{2,18},{10... | collective-permute-start | bytes 393224 | tf_op jit(solution)/shard_map/ppermute | solution.py:48
  34.3 1.2 %collective-permute-start.15 = (bf16[128,128]{1,0:T(8,128)(2,1)S(1)}, bf16[128,128]{1,0:T(8,128)(2,1)S(1)}, u32[]{:S(2)}, u32[]{:S(2)}) collective-permute-start(bf16[128,128]{1,0:T(8,128)(2,1)S(1)} %get-tuple-element.60.refs_0_), channel_id=1, source_target_pairs={{0,8},{8,0},{16,24},{24,16},{1,9},{9,1},{17,25},{25,17},{2,10},{10... | collective-permute-start | bytes 98312 | tf_op jit(solution)/shard_map/ppermute | solution.py:48
  34.3 1.4 %collective-permute-start.16 = (bf16[128,128]{1,0:T(8,128)(2,1)S(1)}, bf16[128,128]{1,0:T(8,128)(2,1)S(1)}, u32[]{:S(2)}, u32[]{:S(2)}) collective-permute-start(bf16[128,128]{1,0:T(8,128)(2,1)S(1)} %collective-permute-done.14.refs_2_), channel_id=1, source_target_pairs={{0,8},{8,0},{16,24},{24,16},{1,9},{9,1},{17,25},{25,17},{2,10},{10... | collective-permute-start | bytes 98312 | tf_op jit(solution)/shard_map/ppermute | solution.py:48
  36.8 1.7 %collective-permute-start.19 = (bf16[400,512]{1,0:T(8,128)(2,1)S(1)}, bf16[400,512]{1,0:T(8,128)(2,1)S(1)}, u32[]{:S(2)}, u32[]{:S(2)}) collective-permute-start(bf16[400,512]{1,0:T(8,128)(2,1)S(1)} %get-tuple-element.68.own_con), channel_id=1, source_target_pairs={{0,8},{8,0},{16,24},{24,16},{1,9},{9,1},{17,25},{25,17},{2,10},{10... | collective-permute-start | bytes 1228808 | tf_op jit(solution)/shard_map/ppermute | solution.py:48
  37.1 5.5 %collective-permute-start.23 = (bf16[128,512]{1,0:T(8,128)(2,1)S(1)}, bf16[128,512]{1,0:T(8,128)(2,1)S(1)}, u32[]{:S(2)}, u32[]{:S(2)}) collective-permute-start(bf16[128,512]{1,0:T(8,128)(2,1)S(1)} %attend.1.att_ref.refs_0_), channel_id=1, source_target_pairs={{0,8},{8,0},{16,24},{24,16},{1,9},{9,1},{17,25},{25,17},{2,10},{10... | collective-permute-start | bytes 393224 | tf_op jit(solution)/shard_map/ppermute | solution.py:48
  37.3 5.4 %collective-permute-start.24 = (bf16[128,512]{1,0:T(8,128)(2,1)S(1)}, bf16[128,512]{1,0:T(8,128)(2,1)S(1)}, u32[]{:S(2)}, u32[]{:S(2)}) collective-permute-start(bf16[128,512]{1,0:T(8,128)(2,1)S(1)} %collective-permute-done.18.refs_2_), channel_id=1, source_target_pairs={{0,8},{8,0},{16,24},{24,16},{1,9},{9,1},{17,25},{25,17},{2,10},{10... | collective-permute-start | bytes 393224 | tf_op jit(solution)/shard_map/ppermute | solution.py:48
  39.1 7.1 %collective-permute-start.20 = (bf16[528,128]{1,0:T(8,128)(2,1)S(1)}, bf16[528,128]{1,0:T(8,128)(2,1)S(1)}, u32[]{:S(2)}, u32[]{:S(2)}) collective-permute-start(bf16[528,128]{1,0:T(8,128)(2,1)S(1)} %get-tuple-element.100), channel_id=1, source_target_pairs={{0,16},{1,17},{2,18},{3,19},{4,20},{5,21},{6,22},{7,23},{8,24},{9,... | collective-permute-start | bytes 405512 | tf_op jit(solution)/shard_map/ppermute | solution.py:461
  40.2 7.9 %collective-permute-start.21 = (bf16[528,128]{1,0:T(8,128)(2,1)S(1)}, bf16[528,128]{1,0:T(8,128)(2,1)S(1)}, u32[]{:S(2)}, u32[]{:S(2)}) collective-permute-start(bf16[528,128]{1,0:T(8,128)(2,1)S(1)} %get-tuple-element.98), channel_id=1, source_target_pairs={{0,1},{1,0},{2,3},{3,2},{4,5},{5,4},{6,7},{7,6},{8,9},{9,8},{10,11... | collective-permute-start | bytes 405512 | tf_op jit(solution)/shard_map/ppermute | solution.py:461
  42.2 7.1 %collective-permute-start.22 = (bf16[528,128]{1,0:T(8,128)(2,1)S(1)}, bf16[528,128]{1,0:T(8,128)(2,1)S(1)}, u32[]{:S(2)}, u32[]{:S(2)}) collective-permute-start(bf16[528,128]{1,0:T(8,128)(2,1)S(1)} %get-tuple-element.99), channel_id=1, source_target_pairs={{0,17},{1,16},{2,19},{3,18},{4,21},{5,20},{6,23},{7,22},{8,25},{9,... | collective-permute-start | bytes 405512 | tf_op jit(solution)/shard_map/ppermute | solution.py:461
  43.1 6.2 %collective-permute-start.25 = (bf16[512,128]{1,0:T(8,128)(2,1)S(1)}, bf16[512,128]{1,0:T(8,128)(2,1)S(1)}, u32[]{:S(2)}, u32[]{:S(2)}) collective-permute-start(bf16[512,128]{1,0:T(8,128)(2,1)S(1)} %bitcast.74), channel_id=1, source_target_pairs={{0,2},{1,3},{2,0},{3,1},{4,6},{5,7},{6,4},{7,5},{8,10},{9,11},{10,... | collective-permute-start | bytes 393224 | tf_op jit(solution)/shard_map/ppermute | solution.py:48
  49.6 6.7 %collective-permute-start.26 = (bf16[272,128]{1,0:T(8,128)(2,1)S(1)}, bf16[272,128]{1,0:T(8,128)(2,1)S(1)}, u32[]{:S(2)}, u32[]{:S(2)}) collective-permute-start(bf16[272,128]{1,0:T(8,128)(2,1)S(1)} %pad_maximum_fusion.9), channel_id=1, source_target_pairs={{0,2},{1,3},{2,0},{3,1},{4,6},{5,7},{6,4},{7,5},{8,10},{9,11},{10,... | collective-permute-start | bytes 208904 | tf_op jit(solution)/shard_map/ppermute | solution.py:48
  51.9 4.3 %collective-permute-start.27 = (bf16[256,128]{1,0:T(8,128)(2,1)S(1)}, bf16[256,128]{1,0:T(8,128)(2,1)S(1)}, u32[]{:S(2)}, u32[]{:S(2)}) collective-permute-start(bf16[256,128]{1,0:T(8,128)(2,1)S(1)} %bitcast.75), channel_id=1, source_target_pairs={{0,1},{1,0},{2,3},{3,2},{4,5},{5,4},{6,7},{7,6},{8,9},{9,8},{10,11... | collective-permute-start | bytes 196616 | tf_op jit(solution)/shard_map/ppermute | solution.py:48
  56.3 7.0 %collective-permute-start.28 = (bf16[528,128]{1,0:T(8,128)(2,1)S(1)}, bf16[528,128]{1,0:T(8,128)(2,1)S(1)}, u32[]{:S(2)}, u32[]{:S(2)}) collective-permute-start(bf16[528,128]{1,0:T(8,128)(2,1)S(1)} %pad_maximum_fusion.8), channel_id=1, source_target_pairs={{0,4},{1,5},{2,6},{3,7},{4,0},{5,1},{6,2},{7,3},{8,12},{9,13},{10,... | collective-permute-start | bytes 405512 | tf_op jit(solution)/shard_map/ppermute | solution.py:48
  63.3 5.0 %collective-permute-start.29 = (bf16[1,2,256,128]{3,2,1,0:T(8,128)(2,1)S(1)}, bf16[1,2,256,128]{3,2,1,0:T(8,128)(2,1)S(1)}, u32[]{:S(2)}, u32[]{:S(2)}) collective-permute-start(bf16[1,2,256,128]{3,2,1,0:T(8,128)(2,1)S(1)} %bitcast.53), channel_id=1, source_target_pairs={{0,1},{1,0},{2,3},{3,2},{4,5},{5,4},{6,7},{7,6},{8,9},{9,8},{10,11... | collective-permute-start | bytes 393224 | tf_op jit(solution)/shard_map/ppermute | solution.py:48
  64.5 5.0 %collective-permute-start.30 = (bf16[1,2,256,128]{3,2,1,0:T(8,128)(2,1)S(1)}, bf16[1,2,256,128]{3,2,1,0:T(8,128)(2,1)S(1)}, u32[]{:S(2)}, u32[]{:S(2)}) collective-permute-start(bf16[1,2,256,128]{3,2,1,0:T(8,128)(2,1)S(1)} %bitcast.54), channel_id=1, source_target_pairs={{0,2},{1,3},{2,0},{3,1},{4,6},{5,7},{6,4},{7,5},{8,10},{9,11},{10,... | collective-permute-start | bytes 393224 | tf_op jit(solution)/shard_map/ppermute | solution.py:48
  64.5 6.8 %collective-permute-start.31 = (bf16[1,2,256,128]{3,2,1,0:T(8,128)(2,1)S(1)}, bf16[1,2,256,128]{3,2,1,0:T(8,128)(2,1)S(1)}, u32[]{:S(2)}, u32[]{:S(2)}) collective-permute-start(bf16[1,2,256,128]{3,2,1,0:T(8,128)(2,1)S(1)} %bitcast.55), channel_id=1, source_target_pairs={{0,3},{1,2},{2,1},{3,0},{4,7},{5,6},{6,5},{7,4},{8,11},{9,10},{10,... | collective-permute-start | bytes 393224 | tf_op jit(solution)/shard_map/ppermute | solution.py:48

commit v10 on v9

--- a/solution.py
+++ b/solution.py
@@ -142,19 +142,15 @@
 
 def backward_body(n_ens, factor, *refs):
     f_refs = refs[:n_ens]
-    wo_ref, target_ref, lw_ref, read_ref, w_ref, rows_ref, gf_ref, con_ref = refs[n_ens:]
+    wo_ref, target_ref, lw_ref, read_ref, w_ref, rows_ref, con_ref = refs[n_ens:]
     lw = lw_ref[...]
     target = target_ref[...]
     fc = [ref[...].astype(F32) for ref in f_refs]
-    sums = [jnp.zeros((TILE, LANES), F32) for _ in range(n_ens)]
-    for i in range(n_ens):
-        for j in range(i + 1, n_ens):
-            t = jnp.tanh((fc[i] - fc[j]) / (2.0 * BREADTH))
-            sums[i] = sums[i] + t
-            sums[j] = sums[j] - t
-    for i in range(n_ens):
-        t = jnp.tanh((fc[i] - target) / (2.0 * BREADTH))
-        gf_ref[i * TILE : (i + 1) * TILE, :] = (lw * (t - sums[i] / (n_ens - 1)) * factor).astype(BF16)
+    tangents = jnp.zeros((TILE, LANES), F32)
+    for j in range(1, n_ens):
+        tangents = tangents + jnp.tanh((fc[0] - fc[j]) / (2.0 * BREADTH))
+    own = jnp.tanh((fc[0] - target) / (2.0 * BREADTH)) - tangents / (n_ens - 1)
+    own = (lw * own * factor).astype(BF16)
     others = jnp.zeros((TILE, LANES), F32)
     for j in range(1, n_ens):
         others = others + sabs(fc[0] - fc[j])
@@ -164,7 +160,7 @@
         part = loss.astype(BF16)
         con_ref[3 * TILE :, i * LANES : (i + 1) * LANES] = part
         loss = loss - part.astype(F32)
-    grad_hidden = dot(gf_ref[:TILE, :], read_ref[...], NT).astype(BF16)
+    grad_hidden = dot(own, read_ref[...], NT).astype(BF16)
     grad_att = dot(grad_hidden, wo_ref[...]).astype(BF16)
     lane = lax.broadcasted_iota(jnp.int32, (TILE, LANES), 1)
     zero = jnp.zeros((), BF16)
@@ -198,9 +194,20 @@
                 v_ref[b, piece % 2, piece // 2 * rows : (piece // 2 + 1) * rows, :] = part
 
 
-def output_body(n_ens, dsh, gf_ref, read_ref, *refs):
-    att_refs = refs[:n_ens]
-    o_ref, scratch = refs[n_ens:]
+def output_body(n_ens, dsh, factor, target_ref, lw_ref, read_ref, *refs):
+    f_refs, att_refs = refs[:n_ens], refs[n_ens : 2 * n_ens]
+    o_ref, scratch, gf_ref = refs[2 * n_ens :]
+    lw, target = lw_ref[...], target_ref[...]
+    fc = [ref[...].astype(F32) for ref in f_refs]
+    sums = [jnp.zeros((TILE, LANES), F32) for _ in range(n_ens)]
+    for i in range(n_ens):
+        for j in range(i + 1, n_ens):
+            t = jnp.tanh((fc[i] - fc[j]) / (2.0 * BREADTH))
+            sums[i] = sums[i] + t
+            sums[j] = sums[j] - t
+    for i in range(n_ens):
+        t = jnp.tanh((fc[i] - target) / (2.0 * BREADTH))
+        gf_ref[i * TILE : (i + 1) * TILE, :] = (lw * (t - sums[i] / (n_ens - 1)) * factor).astype(BF16)
     start = pl.multiple_of(lax.axis_index("ens") * dsh, dsh)
     for j in range(n_ens):
         scratch[j * TILE : (j + 1) * TILE, :] = att_refs[j][...]
@@ -377,9 +384,9 @@
     attended_near = gathered(attended, "ens", far)
 
     factor = 1.0 / math.sqrt(n_ens * n_pix * TILE)
-    grads, contrib = call(
+    (contrib,) = call(
         functools.partial(backward_body, n_ens, factor),
-        [((n_ens * TILE, LANES), BF16), ((3 * TILE + 16, inner), BF16)],
+        [((3 * TILE + 16, inner), BF16)],
         [("v", a) for a in forecasts + [w_out_full]]
         + [("v", target), ("v", lw), ("v", readout_matrix)]
         + [("v", weights), ("v", key_rows)],
@@ -404,14 +411,14 @@
         10**9,
         "value_term",
     )
-    value_term, loss, grads = lax.optimization_barrier((value_term, loss, grads))
+    value_term, loss, lw = lax.optimization_barrier((value_term, loss, lw))
     (output_term,) = call(
-        functools.partial(output_body, n_ens, dsh),
+        functools.partial(output_body, n_ens, dsh, factor),
         [((dsh * inner // LANES, LANES), F32)],
-        [("v", grads), ("v", readout_matrix)] + [("v", a) for a in attended_all],
+        [("v", target), ("v", lw), ("v", readout_matrix)] + [("v", a) for a in forecasts + attended_all],
         10**9,
         "output_term",
-        scratch=[pltpu.VMEM((n_ens * TILE, inner), BF16)],
+        scratch=[pltpu.VMEM((n_ens * TILE, inner), BF16), pltpu.VMEM((n_ens * TILE, LANES), BF16)],
     )
 
     for bit in far[:-1]:

time: 72.7 us -> 72.6 us (level)
  waiting for transfers between devices: 28.5 us -> 26.4 us
  starting transfers between devices: 31.6 us -> 32.6 us
  other arithmetic: 1.38 us -> 2.34 us
    ppermute x27, waiting for transfers between devices: 21.2 us -> 19.8 us  [xor_permute(): return lax.ppermute(value, axis, [(i, i ^ mask) for i in range(size)])]
    ppermute x27, starting transfers between devices: 23.3 us -> 24.4 us  [xor_permute(): return lax.ppermute(value, axis, [(i, i ^ mask) for i in range(size)])]
    concatenate x1, other arithmetic: 0.04 us -> 0.99 us  [per_device(): w_vo = jnp.concatenate([w_value, w_out.T])]
    unnamed x26 -> x24, local copies, waits for them, and re-layouts: 1.68 us -> 1.68 us
  transfers between devices with their start and end apart: 32 -> 32, of which waited for: 21 -> 21; matrix products, arithmetic and copies ran while one was open for 1% -> 2% of each run, Pallas kernels for 9% -> 9%
where the time goes in v10:
time: 72.6 us; the launch traced here: 72.4 us
  starting transfers between devices  32.6 us (45%)
  waiting for transfers between devices  26.4 us (36%)
  Pallas kernels  7.81 us (11%)
  other arithmetic  2.34 us (3%)
  local copies, waits for them, and re-layouts  1.99 us (3%)
  between operations  1.15 us (2%)
    ppermute x27, starting transfers between devices, xor_permute(): return lax.ppermute(value, axis, [(i, i ^ mask) for i in range(size)])  24.4 us
    ppermute x27, waiting for transfers between devices, xor_permute(): return lax.ppermute(value, axis, [(i, i ^ mask) for i in range(size)])  19.8 us
    pallas_call x9, Pallas kernels, call(): pl.pallas_call(body, out_shape=[jax.ShapeDtypeStruct(s, d) for s, d in ou...  7.81 us
    ppermute x1, waiting for transfers between devices, per_device(): lax.ppermute(sample_layer_feed, 'pix', [(i, i + 1) for i in range(n_pix -...  3.73 us
    ppermute x3, starting transfers between devices, per_device(): lax.ppermute(message, ('ens', 'pix'), pairs)  3.55 us
    ppermute x1, starting transfers between devices, per_device(): lax.ppermute(sample_layer_feed, 'pix', [(i, i + 1) for i in range(n_pix -...  3.43 us
    ppermute x3, waiting for transfers between devices, per_device(): lax.ppermute(message, ('ens', 'pix'), pairs)  2.94 us
    unnamed x24, local copies, waits for them, and re-layouts  1.68 us
  transfers between devices with their start and end apart: 32, of which 21 were waited for; matrix products, arithmetic and copies ran while one was open for 2% of the time, Pallas kernels for 9%

profile of v10, /device:TPU:0, one launch (start us, length us, event | category | flops | bytes accessed | tf_op | source)
XLA Modules:
  0.0 72.4 jit_solution(9366449363381013336)
XLA Ops:
  0.7 1.0 %slice_select_fusion = bf16[128,512]{1,0:T(8,128)(2,1)S(1)} fusion(bf16[256,512]{1,0:T(8,128)(2,1)} %param.15, pred[]{:T(512)S(6)} %eq.10), kind=kLoop, calls=%fused_computation.27 | loop fusion | flops 65536 | bytes 393217 | tf_op jit(solution)/shard_map/jit(_where)/select_n | solution.py:308
  1.8 3.0 %collective-permute-start.3 = (bf16[384,512]{1,0:T(8,128)(2,1)S(1)}, bf16[384,512]{1,0:T(8,128)(2,1)S(1)}, u32[]{:S(2)}, u32[]{:S(2)}) collective-permute-start(bf16[384,512]{1,0:T(8,128)(2,1)S(1)} %pad_maximum_fusion.1), channel_id=1, source_target_pairs={{0,16},{8,24},{16,0},{24,8},{1,17},{9,25},{17,1},{25,9},{2,18},{10... | collective-permute-start | bytes 1179656 | tf_op jit(solution)/shard_map/ppermute | solution.py:48
  4.8 0.1 collective-permute-start.2
  4.9 0.8 %copy-done = bf16[1,128,1024]{2,1,0:T(8,128)(2,1)S(1)} copy-done((bf16[1,128,1024]{2,1,0:T(8,128)(2,1)S(1)}, bf16[1,128,1024]{2,1,0:T(8,128)(2,1)}, u32[]{:S(2)}) %copy-start) | copy-done | bytes 262168
  5.7 3.4 %collective-permute-start = (bf16[1,128,1024]{2,1,0:T(8,128)(2,1)S(1)}, bf16[1,128,1024]{2,1,0:T(8,128)(2,1)S(1)}, u32[]{:S(2)}, u32[]{:S(2)}) collective-permute-start(bf16[1,128,1024]{2,1,0:T(8,128)(2,1)S(1)} %copy-done), channel_id=1, source_target_pairs={{0,1},{1,2},{2,3},{3,4},{4,5},{5,6},{6,7},{8,9},{9,10},{10,11},{11... | collective-permute-start | bytes 786440 | tf_op jit(solution)/shard_map/ppermute | solution.py:312
  9.2 1.3 %collective-permute-start.1 = (bf16[1,128,1024]{2,1,0:T(8,128)(2,1)S(1)}, bf16[1,128,1024]{2,1,0:T(8,128)(2,1)S(1)}, u32[]{:S(2)}, u32[]{:S(2)}) collective-permute-start(bf16[1,128,1024]{2,1,0:T(8,128)(2,1)S(1)} %copy-done), channel_id=1, source_target_pairs={{1,0},{2,1},{3,2},{4,3},{5,4},{6,5},{7,6},{9,8},{10,9},{11,10},{12... | collective-permute-start | bytes 786440 | tf_op jit(solution)/shard_map/ppermute | solution.py:313
  10.5 0.1 copy.17
  10.6 1.0 %pad_maximum_fusion.refs_0_ = bf16[512,512]{1,0:T(8,128)(2,1)S(1)} fusion(bf16[256,512]{1,0:T(8,128)(2,1)S(1)} %bitcast.68, bf16[256,512]{1,0:T(8,128)(2,1)} %param.16), kind=kLoop, calls=%fused_computation | loop fusion | flops 1048576 | bytes 1048576 | tf_op jit(solution)/shard_map/concatenate | solution.py:305
  11.6 0.9 %collective-permute-start.9 = (bf16[512,512]{1,0:T(8,128)(2,1)S(1)}, bf16[512,512]{1,0:T(8,128)(2,1)S(1)}, u32[]{:S(2)}, u32[]{:S(2)}) collective-permute-start(bf16[512,512]{1,0:T(8,128)(2,1)S(1)} %pad_maximum_fusion.refs_0_), channel_id=1, source_target_pairs={{0,16},{8,24},{16,0},{24,8},{1,17},{9,25},{17,1},{25,9},{2,18},{10... | collective-permute-start | bytes 1572872 | tf_op jit(solution)/shard_map/ppermute | solution.py:48
  12.5 1.5 %collective-permute-done.3 = bf16[384,512]{1,0:T(8,128)(2,1)S(1)} collective-permute-done((bf16[384,512]{1,0:T(8,128)(2,1)S(1)}, bf16[384,512]{1,0:T(8,128)(2,1)S(1)}, u32[]{:S(2)}, u32[]{:S(2)}) %collective-permute-start.3) | collective-permute-done | bytes 393248 | tf_op jit(solution)/shard_map/ppermute | solution.py:48
  14.0 2.2 %collective-permute-start.4 = (bf16[128,512]{1,0:T(8,128)(2,1)S(1)}, bf16[128,512]{1,0:T(8,128)(2,1)S(1)}, u32[]{:S(2)}, u32[]{:S(2)}) collective-permute-start(bf16[128,512]{1,0:T(8,128)(2,1)S(1)} %slice.124.refs_3_), channel_id=1, source_target_pairs={{0,2},{1,3},{2,0},{3,1},{4,6},{5,7},{6,4},{7,5},{8,10},{9,11},{10,... | collective-permute-start | bytes 393224 | tf_op jit(solution)/shard_map/ppermute | solution.py:48
  16.2 3.7 %collective-permute-done.up_ref = bf16[1,128,1024]{2,1,0:T(8,128)(2,1)S(1)} collective-permute-done((bf16[1,128,1024]{2,1,0:T(8,128)(2,1)S(1)}, bf16[1,128,1024]{2,1,0:T(8,128)(2,1)S(1)}, u32[]{:S(2)}, u32[]{:S(2)}) %collective-permute-start) | collective-permute-done | bytes 262176 | tf_op jit(solution)/shard_map/ppermute | solution.py:312
  20.0 0.6 copy-done.3
  20.6 1.1 %normed.1 = (bf16[384,1024]{1,0:T(8,128)(2,1)S(1)}, bf16[512,384]{1,0:T(8,128)(2,1)S(1)}, bf16[512,384]{1,0:T(8,128)(2,1)S(1)}, f32[128,128]{1,0:T(8,128)S(1)}, f32[8,384]{1,0:T(8,128)S(1)}) custom-call(bf16[1,128,1024]{2,1,0:T(8,128)(2,1)S(1)} %copy-done, bf16[1,128,1024]{2,1,0:T(8,128)(2,1)S(1)} %collective-permute-done.up_ref, ...), custom_call_target="tpu_custom_call" | custom-call | flops 10000000 | bytes 10000 | tf_op jit(solution)/shard_map/normed/pallas_call | solution.py:34
  21.8 0.7 collective-permute-done.4.refs_4_
  22.6 0.5 collective-permute-start.8
  23.1 0.1 collective-permute-start.5
  23.2 0.4 collective-permute-start.6
  23.6 0.3 collective-permute-done.7.refs_7_
  23.9 0.2 collective-permute-done.8.refs_8_
  24.1 0.3 collective-permute-done.5.refs_5_
  24.4 0.2 collective-permute-done.6.refs_6_
  24.6 1.6 %weights.1.w_ref.refs_8_ = bf16[8,128,384]{2,1,0:T(8,128)(2,1)S(1)} custom-call(bf16[384,1024]{1,0:T(8,128)(2,1)S(1)} %get-tuple-element.44.n_ref, f32[8,384]{1,0:T(8,128)S(1)} %get-tuple-element.45.rows_ref.refs_9_, bf16[512,512]{1,0:T(8,128)(2,1)S(1)} %constant_dynamic-update-slice_fusion.refs_0_, bf16[512,512]{1,0:T(8,128)(2,1)S(1)} %collective-permute-done.2.refs_1_, ...), custom_call_target="tpu_custom_call" | custom-call | flops 1000 | bytes 1 | tf_op jit(solution)/shard_map/weights/pallas_call | solution.py:34
  26.3 0.4 collective-permute-start.10
  26.7 0.3 collective-permute-start.11
  27.0 0.3 collective-permute-start.12
  27.3 0.2 collective-permute-start.13
  27.5 0.3 collective-permute-start.17
  27.8 0.1 collective-permute-done.10.refs_1_
  27.9 0.4 collective-permute-done.11.refs_3_
  28.3 0.9 %attend.1.att_ref.refs_4_ = bf16[128,512]{1,0:T(8,128)(2,1)S(1)} custom-call(bf16[384,1024]{1,0:T(8,128)(2,1)S(1)} %get-tuple-element.44.n_ref, bf16[8,128,384]{2,1,0:T(8,128)(2,1)S(1)} %weights.1.w_ref.refs_8_, f32[8,384]{1,0:T(8,128)S(1)} %get-tuple-element.45.rows_ref.refs_9_, bf16[512,512]{1,0:T(8,128)(2,1)S(1)} %pad_maximum_fusion.refs_0_, ...), custom_call_target="tpu_custom_call" | custom-call | flops 1000000000 | bytes 1000000 | tf_op jit(solution)/shard_map/attend/pallas_call | solution.py:34
  29.3 0.7 forecast.1
  30.0 1.1 %collective-permute-start.14 = (bf16[128,128]{1,0:T(8,128)(2,1)S(1)}, bf16[128,128]{1,0:T(8,128)(2,1)S(1)}, u32[]{:S(2)}, u32[]{:S(2)}) collective-permute-start(bf16[128,128]{1,0:T(8,128)(2,1)S(1)} %get-tuple-element.58.refs_0_), channel_id=1, source_target_pairs={{0,16},{8,24},{16,0},{24,8},{1,17},{9,25},{17,1},{25,9},{2,18},{10... | collective-permute-start | bytes 98312 | tf_op jit(solution)/shard_map/ppermute | solution.py:48
  31.1 1.0 %collective-permute-start.18 = (bf16[128,512]{1,0:T(8,128)(2,1)S(1)}, bf16[128,512]{1,0:T(8,128)(2,1)S(1)}, u32[]{:S(2)}, u32[]{:S(2)}) collective-permute-start(bf16[128,512]{1,0:T(8,128)(2,1)S(1)} %attend.1.att_ref.refs_4_), channel_id=1, source_target_pairs={{0,16},{8,24},{16,0},{24,8},{1,17},{9,25},{17,1},{25,9},{2,18},{10... | collective-permute-start | bytes 393224 | tf_op jit(solution)/shard_map/ppermute | solution.py:48
  32.1 2.2 %collective-permute-done.14.refs_2_ = bf16[128,128]{1,0:T(8,128)(2,1)S(1)} collective-permute-done((bf16[128,128]{1,0:T(8,128)(2,1)S(1)}, bf16[128,128]{1,0:T(8,128)(2,1)S(1)}, u32[]{:S(2)}, u32[]{:S(2)}) %collective-permute-start.14) | collective-permute-done | bytes 32800 | tf_op jit(solution)/shard_map/ppermute | solution.py:48
  34.3 0.5 collective-permute-start.16
  34.8 0.7 collective-permute-done.15.refs_1_
  35.5 0.2 collective-permute-done.16.refs_3_
  35.7 0.9 %backward.1.own_con = bf16[400,512]{1,0:T(8,128)(2,1)S(1)} custom-call(bf16[128,128]{1,0:T(8,128)(2,1)S(1)} %get-tuple-element.58.refs_0_, bf16[128,128]{1,0:T(8,128)(2,1)S(1)} %collective-permute-done.15.refs_1_, bf16[128,128]{1,0:T(8,128)(2,1)S(1)} %collective-permute-done.14.refs_2_, bf16[128,128]{1,0:T(8,128)(2,1)S(1)} %collective-permute-done.16.refs_3_, ...), custom_call_target="tpu_custom_call" | custom-call | flops 1000000000 | bytes 1000000 | tf_op jit(solution)/shard_map/backward/pallas_call | solution.py:34
  36.6 0.2 collective-permute-done.18.refs_6_
  36.8 0.2 collective-permute-start.19
  37.0 0.3 collective-permute-start.23
  37.3 0.2 collective-permute-start.24
  37.5 0.4 own_value.1.own_term
  37.9 0.6 collective-permute-done.19.sib_con
  38.5 0.4 value_term.1
  39.1 1.1 %collective-permute-start.20 = (bf16[528,128]{1,0:T(8,128)(2,1)S(1)}, bf16[528,128]{1,0:T(8,128)(2,1)S(1)}, u32[]{:S(2)}, u32[]{:S(2)}) collective-permute-start(bf16[528,128]{1,0:T(8,128)(2,1)S(1)} %get-tuple-element.96), channel_id=1, source_target_pairs={{0,16},{1,17},{2,18},{3,19},{4,20},{5,21},{6,22},{7,23},{8,24},{9,... | collective-permute-start | bytes 405512 | tf_op jit(solution)/shard_map/ppermute | solution.py:468
  40.2 2.0 %collective-permute-start.21 = (bf16[528,128]{1,0:T(8,128)(2,1)S(1)}, bf16[528,128]{1,0:T(8,128)(2,1)S(1)}, u32[]{:S(2)}, u32[]{:S(2)}) collective-permute-start(bf16[528,128]{1,0:T(8,128)(2,1)S(1)} %get-tuple-element.94), channel_id=1, source_target_pairs={{0,1},{1,0},{2,3},{3,2},{4,5},{5,4},{6,7},{7,6},{8,9},{9,8},{10,11... | collective-permute-start | bytes 405512 | tf_op jit(solution)/shard_map/ppermute | solution.py:468
  42.2 0.5 collective-permute-start.22
  42.6 0.5 output_term.1
  43.2 3.0 %collective-permute-start.25 = (bf16[512,128]{1,0:T(8,128)(2,1)S(1)}, bf16[512,128]{1,0:T(8,128)(2,1)S(1)}, u32[]{:S(2)}, u32[]{:S(2)}) collective-permute-start(bf16[512,128]{1,0:T(8,128)(2,1)S(1)} %bitcast.74), channel_id=1, source_target_pairs={{0,2},{1,3},{2,0},{3,1},{4,6},{5,7},{6,4},{7,5},{8,10},{9,11},{10,... | collective-permute-start | bytes 393224 | tf_op jit(solution)/shard_map/ppermute | solution.py:48
  46.3 1.7 %collective-permute-done.21 = bf16[528,128]{1,0:T(8,128)(2,1)S(1)} collective-permute-done((bf16[528,128]{1,0:T(8,128)(2,1)S(1)}, bf16[528,128]{1,0:T(8,128)(2,1)S(1)}, u32[]{:S(2)}, u32[]{:S(2)}) %collective-permute-start.21) | collective-permute-done | bytes 135200 | tf_op jit(solution)/shard_map/ppermute | solution.py:468
  48.0 1.2 %collective-permute-done.22 = bf16[528,128]{1,0:T(8,128)(2,1)S(1)} collective-permute-done((bf16[528,128]{1,0:T(8,128)(2,1)S(1)}, bf16[528,128]{1,0:T(8,128)(2,1)S(1)}, u32[]{:S(2)}, u32[]{:S(2)}) %collective-permute-start.22) | collective-permute-done | bytes 135200 | tf_op jit(solution)/shard_map/ppermute | solution.py:468
  49.5 2.3 %collective-permute-start.26 = (bf16[272,128]{1,0:T(8,128)(2,1)S(1)}, bf16[272,128]{1,0:T(8,128)(2,1)S(1)}, u32[]{:S(2)}, u32[]{:S(2)}) collective-permute-start(bf16[272,128]{1,0:T(8,128)(2,1)S(1)} %pad_maximum_fusion.9), channel_id=1, source_target_pairs={{0,2},{1,3},{2,0},{3,1},{4,6},{5,7},{6,4},{7,5},{8,10},{9,11},{10,... | collective-permute-start | bytes 208904 | tf_op jit(solution)/shard_map/ppermute | solution.py:48
  51.8 0.8 %collective-permute-start.27 = (bf16[256,128]{1,0:T(8,128)(2,1)S(1)}, bf16[256,128]{1,0:T(8,128)(2,1)S(1)}, u32[]{:S(2)}, u32[]{:S(2)}) collective-permute-start(bf16[256,128]{1,0:T(8,128)(2,1)S(1)} %bitcast.75), channel_id=1, source_target_pairs={{0,1},{1,0},{2,3},{3,2},{4,5},{5,4},{6,7},{7,6},{8,9},{9,8},{10,11... | collective-permute-start | bytes 196616 | tf_op jit(solution)/shard_map/ppermute | solution.py:48
  52.6 3.5 %collective-permute-done.27 = bf16[256,128]{1,0:T(8,128)(2,1)S(1)} collective-permute-done((bf16[256,128]{1,0:T(8,128)(2,1)S(1)}, bf16[256,128]{1,0:T(8,128)(2,1)S(1)}, u32[]{:S(2)}, u32[]{:S(2)}) %collective-permute-start.27) | collective-permute-done | bytes 65568 | tf_op jit(solution)/shard_map/ppermute | solution.py:48
  56.2 2.6 %collective-permute-start.28 = (bf16[528,128]{1,0:T(8,128)(2,1)S(1)}, bf16[528,128]{1,0:T(8,128)(2,1)S(1)}, u32[]{:S(2)}, u32[]{:S(2)}) collective-permute-start(bf16[528,128]{1,0:T(8,128)(2,1)S(1)} %pad_maximum_fusion.8), channel_id=1, source_target_pairs={{0,4},{1,5},{2,6},{3,7},{4,0},{5,1},{6,2},{7,3},{8,12},{9,13},{10,... | collective-permute-start | bytes 405512 | tf_op jit(solution)/shard_map/ppermute | solution.py:48
  58.9 4.3 %collective-permute-done.28 = bf16[528,128]{1,0:T(8,128)(2,1)S(1)} collective-permute-done((bf16[528,128]{1,0:T(8,128)(2,1)S(1)}, bf16[528,128]{1,0:T(8,128)(2,1)S(1)}, u32[]{:S(2)}, u32[]{:S(2)}) %collective-permute-start.28) | collective-permute-done | bytes 135200 | tf_op jit(solution)/shard_map/ppermute | solution.py:48
  63.2 1.0 %collective-permute-start.29 = (bf16[1,2,256,128]{3,2,1,0:T(8,128)(2,1)S(1)}, bf16[1,2,256,128]{3,2,1,0:T(8,128)(2,1)S(1)}, u32[]{:S(2)}, u32[]{:S(2)}) collective-permute-start(bf16[1,2,256,128]{3,2,1,0:T(8,128)(2,1)S(1)} %bitcast.53), channel_id=1, source_target_pairs={{0,1},{1,0},{2,3},{3,2},{4,5},{5,4},{6,7},{7,6},{8,9},{9,8},{10,11... | collective-permute-start | bytes 393224 | tf_op jit(solution)/shard_map/ppermute | solution.py:48
  64.3 2.5 %collective-permute-start.31 = (bf16[1,2,256,128]{3,2,1,0:T(8,128)(2,1)S(1)}, bf16[1,2,256,128]{3,2,1,0:T(8,128)(2,1)S(1)}, u32[]{:S(2)}, u32[]{:S(2)}) collective-permute-start(bf16[1,2,256,128]{3,2,1,0:T(8,128)(2,1)S(1)} %bitcast.55), channel_id=1, source_target_pairs={{0,3},{1,2},{2,1},{3,0},{4,7},{5,6},{6,5},{7,4},{8,11},{9,10},{10,... | collective-permute-start | bytes 393224 | tf_op jit(solution)/shard_map/ppermute | solution.py:48
  66.8 1.5 %collective-permute-done.29 = bf16[1,2,256,128]{3,2,1,0:T(8,128)(2,1)S(1)} collective-permute-done((bf16[1,2,256,128]{3,2,1,0:T(8,128)(2,1)S(1)}, bf16[1,2,256,128]{3,2,1,0:T(8,128)(2,1)S(1)}, u32[]{:S(2)}, u32[]{:S(2)}) %collective-permute-start.29) | collective-permute-done | bytes 131104 | tf_op jit(solution)/shard_map/ppermute | solution.py:48
  68.3 1.0 %collective-permute-done.30 = bf16[1,2,256,128]{3,2,1,0:T(8,128)(2,1)S(1)} collective-permute-done((bf16[1,2,256,128]{3,2,1,0:T(8,128)(2,1)S(1)}, bf16[1,2,256,128]{3,2,1,0:T(8,128)(2,1)S(1)}, u32[]{:S(2)}, u32[]{:S(2)}) %collective-permute-start.30) | collective-permute-done | bytes 131104 | tf_op jit(solution)/shard_map/ppermute | solution.py:48
  69.2 1.9 %collective-permute-done.31 = bf16[1,2,256,128]{3,2,1,0:T(8,128)(2,1)S(1)} collective-permute-done((bf16[1,2,256,128]{3,2,1,0:T(8,128)(2,1)S(1)}, bf16[1,2,256,128]{3,2,1,0:T(8,128)(2,1)S(1)}, u32[]{:S(2)}, u32[]{:S(2)}) %collective-permute-start.31) | collective-permute-done | bytes 131104 | tf_op jit(solution)/shard_map/ppermute | solution.py:48
  71.2 1.2 %finish.1 = (f32[256,512]{1,0:T(8,128)}, f32[512,256]{1,0:T(8,128)}, f32[1,1]{1,0:T(1,128)}) custom-call(bf16[2,256,128]{2,1,0:T(8,128)(2,1)S(1)} %bitcast.56, bf16[2,256,128]{2,1,0:T(8,128)(2,1)S(1)} %bitcast.61, bf16[2,256,128]{2,1,0:T(8,128)(2,1)S(1)} %bitcast.62, bf16[2,256,128]{2,1,0:T(8,128)(2,1)S(1)} %bitcast.63, f32[8,128]{1,0:T(8,128)S(1)} %fusion.10.refs_4_), custom_call_target="tpu_custom_call" | custom-call | flops 1000000 | bytes 1000 | tf_op jit(solution)/shard_map/finish/pallas_call | solution.py:34
  (72 shorter events, 0.8 us)
Async XLA Ops:
  0.6 1.1 %copy-start.8 = (bf16[256,512]{1,0:T(8,128)(2,1)S(1)}, bf16[256,512]{1,0:T(8,128)(2,1)}, u32[]{:S(2)}) copy-start(bf16[256,512]{1,0:T(8,128)(2,1)} %param.14) | copy-start | bytes 786436
  1.7 3.0 %copy-start.9 = (bf16[256,512]{1,0:T(8,128)(2,1)S(1)}, bf16[256,512]{1,0:T(8,128)(2,1)}, u32[]{:S(2)}) copy-start(bf16[256,512]{1,0:T(8,128)(2,1)} %param.15) | copy-start | bytes 786436
  1.8 12.2 %collective-permute-start.3 = (bf16[384,512]{1,0:T(8,128)(2,1)S(1)}, bf16[384,512]{1,0:T(8,128)(2,1)S(1)}, u32[]{:S(2)}, u32[]{:S(2)}) collective-permute-start(bf16[384,512]{1,0:T(8,128)(2,1)S(1)} %pad_maximum_fusion.1), channel_id=1, source_target_pairs={{0,16},{8,24},{16,0},{24,8},{1,17},{9,25},{17,1},{25,9},{2,18},{10... | collective-permute-start | bytes 1179656 | tf_op jit(solution)/shard_map/ppermute | solution.py:48
  4.8 1.0 %copy-start = (bf16[1,128,1024]{2,1,0:T(8,128)(2,1)S(1)}, bf16[1,128,1024]{2,1,0:T(8,128)(2,1)}, u32[]{:S(2)}) copy-start(bf16[1,128,1024]{2,1,0:T(8,128)(2,1)} %x_ref.3) | copy-start | bytes 786436
  4.8 5.7 %copy-start.10 = (bf16[512,256]{1,0:T(8,128)(2,1)S(1)}, bf16[512,256]{1,0:T(8,128)(2,1)}, u32[]{:S(2)}) copy-start(bf16[512,256]{1,0:T(8,128)(2,1)} %param.17) | copy-start | bytes 786436
  4.8 17.6 %collective-permute-start.2 = (bf16[512,512]{1,0:T(8,128)(2,1)S(1)}, bf16[512,512]{1,0:T(8,128)(2,1)S(1)}, u32[]{:S(2)}, u32[]{:S(2)}) collective-permute-start(bf16[512,512]{1,0:T(8,128)(2,1)S(1)} %constant_dynamic-update-slice_fusion.refs_0_), channel_id=1, source_target_pairs={{0,8},{8,0},{16,24},{24,16},{1,9},{9,1},{17,25},{25,17},{2,10},{10... | collective-permute-start | bytes 1572872 | tf_op jit(solution)/shard_map/ppermute | solution.py:48
  5.7 14.2 %collective-permute-start = (bf16[1,128,1024]{2,1,0:T(8,128)(2,1)S(1)}, bf16[1,128,1024]{2,1,0:T(8,128)(2,1)S(1)}, u32[]{:S(2)}, u32[]{:S(2)}) collective-permute-start(bf16[1,128,1024]{2,1,0:T(8,128)(2,1)S(1)} %copy-done), channel_id=1, source_target_pairs={{0,1},{1,2},{2,3},{3,4},{4,5},{5,6},{6,7},{8,9},{9,10},{10,11},{11... | collective-permute-start | bytes 786440 | tf_op jit(solution)/shard_map/ppermute | solution.py:312
  9.2 10.8 %collective-permute-start.1 = (bf16[1,128,1024]{2,1,0:T(8,128)(2,1)S(1)}, bf16[1,128,1024]{2,1,0:T(8,128)(2,1)S(1)}, u32[]{:S(2)}, u32[]{:S(2)}) collective-permute-start(bf16[1,128,1024]{2,1,0:T(8,128)(2,1)S(1)} %copy-done), channel_id=1, source_target_pairs={{1,0},{2,1},{3,2},{4,3},{5,4},{6,5},{7,6},{9,8},{10,9},{11,10},{12... | collective-permute-start | bytes 786440 | tf_op jit(solution)/shard_map/ppermute | solution.py:313
  11.6 14.6 %collective-permute-start.9 = (bf16[512,512]{1,0:T(8,128)(2,1)S(1)}, bf16[512,512]{1,0:T(8,128)(2,1)S(1)}, u32[]{:S(2)}, u32[]{:S(2)}) collective-permute-start(bf16[512,512]{1,0:T(8,128)(2,1)S(1)} %pad_maximum_fusion.refs_0_), channel_id=1, source_target_pairs={{0,16},{8,24},{16,0},{24,8},{1,17},{9,25},{17,1},{25,9},{2,18},{10... | collective-permute-start | bytes 1572872 | tf_op jit(solution)/shard_map/ppermute | solution.py:48
  14.0 6.0 %copy-start.2 = (s32[1024]{0:T(1024)S(1)}, s32[1024]{0:T(1024)}, u32[]{:S(2)}) copy-start(s32[1024]{0:T(1024)} %param.21) | copy-start | bytes 12292
  14.0 6.0 %copy-start.1 = (f32[1024]{0:T(1024)S(1)}, f32[1024]{0:T(1024)}, u32[]{:S(2)}) copy-start(f32[1024]{0:T(1024)} %param.13) | copy-start | bytes 12292
  14.0 8.5 %collective-permute-start.4 = (bf16[128,512]{1,0:T(8,128)(2,1)S(1)}, bf16[128,512]{1,0:T(8,128)(2,1)S(1)}, u32[]{:S(2)}, u32[]{:S(2)}) collective-permute-start(bf16[128,512]{1,0:T(8,128)(2,1)S(1)} %slice.124.refs_3_), channel_id=1, source_target_pairs={{0,2},{1,3},{2,0},{3,1},{4,6},{5,7},{6,4},{7,5},{8,10},{9,11},{10,... | collective-permute-start | bytes 393224 | tf_op jit(solution)/shard_map/ppermute | solution.py:48
  20.0 0.7 copy-start.3
  20.0 0.7 copy-start.4
  20.0 0.7 copy-start.5
  22.5 1.4 %collective-permute-start.7 = (bf16[128,512]{1,0:T(8,128)(2,1)S(1)}, bf16[128,512]{1,0:T(8,128)(2,1)S(1)}, u32[]{:S(2)}, u32[]{:S(2)}) collective-permute-start(bf16[128,512]{1,0:T(8,128)(2,1)S(1)} %get-tuple-element.93), channel_id=1, source_target_pairs={{0,8},{8,0},{16,24},{24,16},{1,9},{9,1},{17,25},{25,17},{2,10},{10... | collective-permute-start | bytes 393224 | tf_op jit(solution)/shard_map/ppermute | solution.py:48
  22.6 1.5 %collective-permute-start.8 = (bf16[128,512]{1,0:T(8,128)(2,1)S(1)}, bf16[128,512]{1,0:T(8,128)(2,1)S(1)}, u32[]{:S(2)}, u32[]{:S(2)}) collective-permute-start(bf16[128,512]{1,0:T(8,128)(2,1)S(1)} %get-tuple-element.92), channel_id=1, source_target_pairs={{0,8},{8,0},{16,24},{24,16},{1,9},{9,1},{17,25},{25,17},{2,10},{10... | collective-permute-start | bytes 393224 | tf_op jit(solution)/shard_map/ppermute | solution.py:48
  23.1 1.3 %collective-permute-start.5 = (bf16[128,512]{1,0:T(8,128)(2,1)S(1)}, bf16[128,512]{1,0:T(8,128)(2,1)S(1)}, u32[]{:S(2)}, u32[]{:S(2)}) collective-permute-start(bf16[128,512]{1,0:T(8,128)(2,1)S(1)} %slice.124.refs_3_), channel_id=1, source_target_pairs={{0,8},{8,0},{16,24},{24,16},{1,9},{9,1},{17,25},{25,17},{2,10},{10... | collective-permute-start | bytes 393224 | tf_op jit(solution)/shard_map/ppermute | solution.py:48
  23.2 1.5 %collective-permute-start.6 = (bf16[128,512]{1,0:T(8,128)(2,1)S(1)}, bf16[128,512]{1,0:T(8,128)(2,1)S(1)}, u32[]{:S(2)}, u32[]{:S(2)}) collective-permute-start(bf16[128,512]{1,0:T(8,128)(2,1)S(1)} %collective-permute-done.4.refs_4_), channel_id=1, source_target_pairs={{0,8},{8,0},{16,24},{24,16},{1,9},{9,1},{17,25},{25,17},{2,10},{10... | collective-permute-start | bytes 393224 | tf_op jit(solution)/shard_map/ppermute | solution.py:48
  26.3 1.6 %collective-permute-start.10 = (bf16[256,512]{1,0:T(8,128)(2,1)S(1)}, bf16[256,512]{1,0:T(8,128)(2,1)S(1)}, u32[]{:S(2)}, u32[]{:S(2)}) collective-permute-start(bf16[256,512]{1,0:T(8,128)(2,1)S(1)} %get-tuple-element.91), channel_id=1, source_target_pairs={{0,8},{8,0},{16,24},{24,16},{1,9},{9,1},{17,25},{25,17},{2,10},{10... | collective-permute-start | bytes 786440 | tf_op jit(solution)/shard_map/ppermute | solution.py:48
  26.7 1.6 %collective-permute-start.11 = (bf16[256,512]{1,0:T(8,128)(2,1)S(1)}, bf16[256,512]{1,0:T(8,128)(2,1)S(1)}, u32[]{:S(2)}, u32[]{:S(2)}) collective-permute-start(bf16[256,512]{1,0:T(8,128)(2,1)S(1)} %get-tuple-element.89.refs_2_), channel_id=1, source_target_pairs={{0,8},{8,0},{16,24},{24,16},{1,9},{9,1},{17,25},{25,17},{2,10},{10... | collective-permute-start | bytes 786440 | tf_op jit(solution)/shard_map/ppermute | solution.py:48
  27.0 2.3 %collective-permute-start.12 = (bf16[256,512]{1,0:T(8,128)(2,1)S(1)}, bf16[256,512]{1,0:T(8,128)(2,1)S(1)}, u32[]{:S(2)}, u32[]{:S(2)}) collective-permute-start(bf16[256,512]{1,0:T(8,128)(2,1)S(1)} %get-tuple-element.90), channel_id=1, source_target_pairs={{0,8},{8,0},{16,24},{24,16},{1,9},{9,1},{17,25},{25,17},{2,10},{10... | collective-permute-start | bytes 786440 | tf_op jit(solution)/shard_map/ppermute | solution.py:48
  27.3 2.0 %copy-start.6 = (bf16[1024,128]{1,0:T(8,128)(2,1)S(1)}, bf16[1024,128]{1,0:T(8,128)(2,1)}, u32[]{:S(2)}) copy-start(bf16[1024,128]{1,0:T(8,128)(2,1)} %read_ref.3) | copy-start | bytes 786436
  27.3 2.0 %collective-permute-start.13 = (bf16[256,512]{1,0:T(8,128)(2,1)S(1)}, bf16[256,512]{1,0:T(8,128)(2,1)S(1)}, u32[]{:S(2)}, u32[]{:S(2)}) collective-permute-start(bf16[256,512]{1,0:T(8,128)(2,1)S(1)} %get-tuple-element.88.refs_2_), channel_id=1, source_target_pairs={{0,8},{8,0},{16,24},{24,16},{1,9},{9,1},{17,25},{25,17},{2,10},{10... | collective-permute-start | bytes 786440 | tf_op jit(solution)/shard_map/ppermute | solution.py:48
  27.5 8.2 %collective-permute-start.17 = (bf16[512,384]{1,0:T(8,128)(2,1)S(1)}, bf16[512,384]{1,0:T(8,128)(2,1)S(1)}, u32[]{:S(2)}, u32[]{:S(2)}) collective-permute-start(bf16[512,384]{1,0:T(8,128)(2,1)S(1)} %get-tuple-element.57), channel_id=1, source_target_pairs={{0,8},{8,0},{16,24},{24,16},{1,9},{9,1},{17,25},{25,17},{2,10},{10... | collective-permute-start | bytes 1179656 | tf_op jit(solution)/shard_map/ppermute | solution.py:48
  29.3 6.4 %copy-start.7 = (f32[128,128]{1,0:T(8,128)S(1)}, f32[128,128]{1,0:T(8,128)}, u32[]{:S(2)}) copy-start(f32[128,128]{1,0:T(8,128)} %target_ref.1) | copy-start | bytes 196612
  30.0 4.3 %collective-permute-start.14 = (bf16[128,128]{1,0:T(8,128)(2,1)S(1)}, bf16[128,128]{1,0:T(8,128)(2,1)S(1)}, u32[]{:S(2)}, u32[]{:S(2)}) collective-permute-start(bf16[128,128]{1,0:T(8,128)(2,1)S(1)} %get-tuple-element.58.refs_0_), channel_id=1, source_target_pairs={{0,16},{8,24},{16,0},{24,8},{1,17},{9,25},{17,1},{25,9},{2,18},{10... | collective-permute-start | bytes 98312 | tf_op jit(solution)/shard_map/ppermute | solution.py:48
  31.1 5.7 %collective-permute-start.18 = (bf16[128,512]{1,0:T(8,128)(2,1)S(1)}, bf16[128,512]{1,0:T(8,128)(2,1)S(1)}, u32[]{:S(2)}, u32[]{:S(2)}) collective-permute-start(bf16[128,512]{1,0:T(8,128)(2,1)S(1)} %attend.1.att_ref.refs_4_), channel_id=1, source_target_pairs={{0,16},{8,24},{16,0},{24,8},{1,17},{9,25},{17,1},{25,9},{2,18},{10... | collective-permute-start | bytes 393224 | tf_op jit(solution)/shard_map/ppermute | solution.py:48
  34.3 1.2 %collective-permute-start.15 = (bf16[128,128]{1,0:T(8,128)(2,1)S(1)}, bf16[128,128]{1,0:T(8,128)(2,1)S(1)}, u32[]{:S(2)}, u32[]{:S(2)}) collective-permute-start(bf16[128,128]{1,0:T(8,128)(2,1)S(1)} %get-tuple-element.58.refs_0_), channel_id=1, source_target_pairs={{0,8},{8,0},{16,24},{24,16},{1,9},{9,1},{17,25},{25,17},{2,10},{10... | collective-permute-start | bytes 98312 | tf_op jit(solution)/shard_map/ppermute | solution.py:48
  34.3 1.4 %collective-permute-start.16 = (bf16[128,128]{1,0:T(8,128)(2,1)S(1)}, bf16[128,128]{1,0:T(8,128)(2,1)S(1)}, u32[]{:S(2)}, u32[]{:S(2)}) collective-permute-start(bf16[128,128]{1,0:T(8,128)(2,1)S(1)} %collective-permute-done.14.refs_2_), channel_id=1, source_target_pairs={{0,8},{8,0},{16,24},{24,16},{1,9},{9,1},{17,25},{25,17},{2,10},{10... | collective-permute-start | bytes 98312 | tf_op jit(solution)/shard_map/ppermute | solution.py:48
  36.8 1.7 %collective-permute-start.19 = (bf16[400,512]{1,0:T(8,128)(2,1)S(1)}, bf16[400,512]{1,0:T(8,128)(2,1)S(1)}, u32[]{:S(2)}, u32[]{:S(2)}) collective-permute-start(bf16[400,512]{1,0:T(8,128)(2,1)S(1)} %backward.1.own_con), channel_id=1, source_target_pairs={{0,8},{8,0},{16,24},{24,16},{1,9},{9,1},{17,25},{25,17},{2,10},{10... | collective-permute-start | bytes 1228808 | tf_op jit(solution)/shard_map/ppermute | solution.py:48
  37.0 5.7 %collective-permute-start.23 = (bf16[128,512]{1,0:T(8,128)(2,1)S(1)}, bf16[128,512]{1,0:T(8,128)(2,1)S(1)}, u32[]{:S(2)}, u32[]{:S(2)}) collective-permute-start(bf16[128,512]{1,0:T(8,128)(2,1)S(1)} %attend.1.att_ref.refs_4_), channel_id=1, source_target_pairs={{0,8},{8,0},{16,24},{24,16},{1,9},{9,1},{17,25},{25,17},{2,10},{10... | collective-permute-start | bytes 393224 | tf_op jit(solution)/shard_map/ppermute | solution.py:48
  37.3 5.4 %collective-permute-start.24 = (bf16[128,512]{1,0:T(8,128)(2,1)S(1)}, bf16[128,512]{1,0:T(8,128)(2,1)S(1)}, u32[]{:S(2)}, u32[]{:S(2)}) collective-permute-start(bf16[128,512]{1,0:T(8,128)(2,1)S(1)} %collective-permute-done.18.refs_6_), channel_id=1, source_target_pairs={{0,8},{8,0},{16,24},{24,16},{1,9},{9,1},{17,25},{25,17},{2,10},{10... | collective-permute-start | bytes 393224 | tf_op jit(solution)/shard_map/ppermute | solution.py:48
  39.1 7.2 %collective-permute-start.20 = (bf16[528,128]{1,0:T(8,128)(2,1)S(1)}, bf16[528,128]{1,0:T(8,128)(2,1)S(1)}, u32[]{:S(2)}, u32[]{:S(2)}) collective-permute-start(bf16[528,128]{1,0:T(8,128)(2,1)S(1)} %get-tuple-element.96), channel_id=1, source_target_pairs={{0,16},{1,17},{2,18},{3,19},{4,20},{5,21},{6,22},{7,23},{8,24},{9,... | collective-permute-start | bytes 405512 | tf_op jit(solution)/shard_map/ppermute | solution.py:468
  40.2 7.8 %collective-permute-start.21 = (bf16[528,128]{1,0:T(8,128)(2,1)S(1)}, bf16[528,128]{1,0:T(8,128)(2,1)S(1)}, u32[]{:S(2)}, u32[]{:S(2)}) collective-permute-start(bf16[528,128]{1,0:T(8,128)(2,1)S(1)} %get-tuple-element.94), channel_id=1, source_target_pairs={{0,1},{1,0},{2,3},{3,2},{4,5},{5,4},{6,7},{7,6},{8,9},{9,8},{10,11... | collective-permute-start | bytes 405512 | tf_op jit(solution)/shard_map/ppermute | solution.py:468
  42.2 7.0 %collective-permute-start.22 = (bf16[528,128]{1,0:T(8,128)(2,1)S(1)}, bf16[528,128]{1,0:T(8,128)(2,1)S(1)}, u32[]{:S(2)}, u32[]{:S(2)}) collective-permute-start(bf16[528,128]{1,0:T(8,128)(2,1)S(1)} %get-tuple-element.95), channel_id=1, source_target_pairs={{0,17},{1,16},{2,19},{3,18},{4,21},{5,20},{6,23},{7,22},{8,25},{9,... | collective-permute-start | bytes 405512 | tf_op jit(solution)/shard_map/ppermute | solution.py:468
  43.2 6.1 %collective-permute-start.25 = (bf16[512,128]{1,0:T(8,128)(2,1)S(1)}, bf16[512,128]{1,0:T(8,128)(2,1)S(1)}, u32[]{:S(2)}, u32[]{:S(2)}) collective-permute-start(bf16[512,128]{1,0:T(8,128)(2,1)S(1)} %bitcast.74), channel_id=1, source_target_pairs={{0,2},{1,3},{2,0},{3,1},{4,6},{5,7},{6,4},{7,5},{8,10},{9,11},{10,... | collective-permute-start | bytes 393224 | tf_op jit(solution)/shard_map/ppermute | solution.py:48
  49.5 6.7 %collective-permute-start.26 = (bf16[272,128]{1,0:T(8,128)(2,1)S(1)}, bf16[272,128]{1,0:T(8,128)(2,1)S(1)}, u32[]{:S(2)}, u32[]{:S(2)}) collective-permute-start(bf16[272,128]{1,0:T(8,128)(2,1)S(1)} %pad_maximum_fusion.9), channel_id=1, source_target_pairs={{0,2},{1,3},{2,0},{3,1},{4,6},{5,7},{6,4},{7,5},{8,10},{9,11},{10,... | collective-permute-start | bytes 208904 | tf_op jit(solution)/shard_map/ppermute | solution.py:48
  51.8 4.3 %collective-permute-start.27 = (bf16[256,128]{1,0:T(8,128)(2,1)S(1)}, bf16[256,128]{1,0:T(8,128)(2,1)S(1)}, u32[]{:S(2)}, u32[]{:S(2)}) collective-permute-start(bf16[256,128]{1,0:T(8,128)(2,1)S(1)} %bitcast.75), channel_id=1, source_target_pairs={{0,1},{1,0},{2,3},{3,2},{4,5},{5,4},{6,7},{7,6},{8,9},{9,8},{10,11... | collective-permute-start | bytes 196616 | tf_op jit(solution)/shard_map/ppermute | solution.py:48
  56.2 7.0 %collective-permute-start.28 = (bf16[528,128]{1,0:T(8,128)(2,1)S(1)}, bf16[528,128]{1,0:T(8,128)(2,1)S(1)}, u32[]{:S(2)}, u32[]{:S(2)}) collective-permute-start(bf16[528,128]{1,0:T(8,128)(2,1)S(1)} %pad_maximum_fusion.8), channel_id=1, source_target_pairs={{0,4},{1,5},{2,6},{3,7},{4,0},{5,1},{6,2},{7,3},{8,12},{9,13},{10,... | collective-permute-start | bytes 405512 | tf_op jit(solution)/shard_map/ppermute | solution.py:48
  63.2 5.0 %collective-permute-start.29 = (bf16[1,2,256,128]{3,2,1,0:T(8,128)(2,1)S(1)}, bf16[1,2,256,128]{3,2,1,0:T(8,128)(2,1)S(1)}, u32[]{:S(2)}, u32[]{:S(2)}) collective-permute-start(bf16[1,2,256,128]{3,2,1,0:T(8,128)(2,1)S(1)} %bitcast.53), channel_id=1, source_target_pairs={{0,1},{1,0},{2,3},{3,2},{4,5},{5,4},{6,7},{7,6},{8,9},{9,8},{10,11... | collective-permute-start | bytes 393224 | tf_op jit(solution)/shard_map/ppermute | solution.py:48
  64.3 5.0 %collective-permute-start.30 = (bf16[1,2,256,128]{3,2,1,0:T(8,128)(2,1)S(1)}, bf16[1,2,256,128]{3,2,1,0:T(8,128)(2,1)S(1)}, u32[]{:S(2)}, u32[]{:S(2)}) collective-permute-start(bf16[1,2,256,128]{3,2,1,0:T(8,128)(2,1)S(1)} %bitcast.54), channel_id=1, source_target_pairs={{0,2},{1,3},{2,0},{3,1},{4,6},{5,7},{6,4},{7,5},{8,10},{9,11},{10,... | collective-permute-start | bytes 393224 | tf_op jit(solution)/shard_map/ppermute | solution.py:48
  64.3 6.9 %collective-permute-start.31 = (bf16[1,2,256,128]{3,2,1,0:T(8,128)(2,1)S(1)}, bf16[1,2,256,128]{3,2,1,0:T(8,128)(2,1)S(1)}, u32[]{:S(2)}, u32[]{:S(2)}) collective-permute-start(bf16[1,2,256,128]{3,2,1,0:T(8,128)(2,1)S(1)} %bitcast.55), channel_id=1, source_target_pairs={{0,3},{1,2},{2,1},{3,0},{4,7},{5,6},{6,5},{7,4},{8,11},{9,10},{10,... | collective-permute-start | bytes 393224 | tf_op jit(solution)/shard_map/ppermute | solution.py:48
